TPU v7x, 128 devices: a whole 4x4x4 slice. The times are simulated.
128 devices in a mesh: dp: 16 (over x_lo, y, core), tensor: 8 (over z, x_hi).
Axes of the slice: x: 4 (x_hi: 2, x_lo: 2; x = x_hi * 2 + x_lo), y: 4, z: 4, core: 2. Of those that a mesh axis runs over, the one named last changes fastest.
Arguments:
- tokens: bfloat16 [512, 8192], P(None, 'dp'), may hold values from -6 to 6
- gate_weight: bfloat16 [8192, 14336], P('dp', 'tensor'), may hold values from -0.0625 to 0.0625
- up_weight: bfloat16 [8192, 14336], P('dp', 'tensor'), may hold values from -0.0625 to 0.0625
- down_weight: bfloat16 [14336, 8192], P('tensor', 'dp'), may hold values from -0.046875 to 0.046875
- head_weight: bfloat16 [8192, 16384], P('dp', 'tensor'), may hold values from -2 to 2
- up_moment: float32 [8192, 14336], P('dp', 'tensor'), may hold values from -0.6 to 0.6
- up_curvature: float32 [8192, 14336], P('dp', 'tensor'), may hold values from 0.002 to 0.2
- true_labels: int32 [512], P('dp'), may hold values from 0 to 16383
- sampled_labels: int32 [512], P('dp'), may hold values from 0 to 16383
Outputs:
- new_moment: float32 [8192, 14336], P('dp', 'tensor')
- new_curvature: float32 [8192, 14336], P('dp', 'tensor')
- update: float32 [8192, 14336], P('dp', 'tensor')
All inputs are finite; a program needn't handle non-finite values.
Results may differ from a plain program's by a relative error of at most 0.009.
Values may be sent and summed in bfloat16 or wider, within the bound.
No kernel may reach another device: no remote copies, remote signals or barrier semaphores. Data moves between devices by JAX's collectives and lax.ppermute only.
A program may use at most 128 MiB of HBM per device.

v0:
```python
import jax
import jax.numpy as jnp
from jax import lax
from jax.sharding import PartitionSpec as P

D = 8192


beta_one = 0.965
beta_two = 0.95
rho_scale = 0.05
eps_norm = 1e-05


def partial_rows(term_fn, own_rows):
    return lax.psum_scatter(
        term_fn(jnp.int32(0), own_rows * lax.axis_size("dp")), "dp", scatter_dimension=0, tiled=True
    )


def all_tokens(stacked, row_fn):
    return row_fn(lax.all_gather(stacked, "dp", axis=0, tiled=True), jnp.int32(0))


def tensor_total(value):
    return lax.psum(value, "tensor")


def token_total(value):
    return lax.psum(value, "dp")


def keep_rows(shard_rows, first_row):
    return shard_rows


def on_device(
    tokens,
    gate_weight,
    up_weight,
    down_weight,
    head_weight,
    up_moment,
    up_curvature,
    true_labels,
    sampled_labels,
):
    own_rows = true_labels.shape[0]
    width_part = gate_weight.shape[1]
    vocab_part = head_weight.shape[1]
    paired = jnp.concatenate([gate_weight, up_weight], axis=1)

    def project_down(shard_rows, first_row):
        return jnp.einsum(
            "rkf,fd->rkd", shard_rows, down_weight, preferred_element_type=jnp.float32
        )

    def gate_up_term(first_row, row_count):
        return jnp.dot(tokens, paired, preferred_element_type=jnp.float32)

    gate_up = partial_rows(gate_up_term, own_rows)
    gate_act = gate_up[:, :width_part]
    hidden = (jax.nn.silu(gate_act) * gate_up[:, width_part:]).astype(jnp.bfloat16)
    branch_part = all_tokens(hidden[:, None, :], project_down)[:, 0, :]
    branch = tensor_total(branch_part)
    summed = tokens.astype(jnp.float32) + branch
    squares = token_total(jnp.sum(summed * summed, axis=1))
    inv_rms = lax.rsqrt(squares / D + eps_norm)[:, None]
    scaled = summed * inv_rms
    normed = scaled.astype(jnp.bfloat16)

    def logit_term(first_row, row_count):
        return jnp.dot(normed, head_weight, preferred_element_type=jnp.float32)

    logits = partial_rows(logit_term, own_rows)
    local_top = jnp.max(logits, axis=1)
    row_top = lax.pmax(local_top, "tensor")
    exp_terms = jnp.exp(logits - row_top[:, None])
    exp_total = tensor_total(jnp.sum(exp_terms, axis=1))
    probability = exp_terms / exp_total[:, None]
    vocab_start = lax.axis_index("tensor") * vocab_part
    vocab_ids = vocab_start + lax.broadcasted_iota(jnp.int32, (1, vocab_part), 1)
    true_hot = (true_labels[:, None] == vocab_ids).astype(jnp.float32)
    sample_hot = (sampled_labels[:, None] == vocab_ids).astype(jnp.float32)
    dlogits = jnp.stack([probability - true_hot, probability - sample_hot], axis=1).astype(
        jnp.bfloat16
    )

    def project_back(shard_rows, first_row):
        return jnp.einsum(
            "rkv,dv->rkd", shard_rows, head_weight, preferred_element_type=jnp.float32
        )

    dnormed = tensor_total(all_tokens(dlogits, project_back))
    inner_dot = token_total(jnp.sum(dnormed * scaled[:, None, :], axis=2)) / D
    dsummed = (inv_rms[:, :, None] * (dnormed - scaled[:, None, :] * inner_dot[:, :, None])).astype(
        jnp.bfloat16
    )

    def back_term(first_row, row_count):
        both_terms = jnp.einsum(
            "tkd,fd->tkf", dsummed, down_weight, preferred_element_type=jnp.float32
        )
        return both_terms.reshape(row_count, 2 * width_part)

    dhidden = partial_rows(back_term, own_rows).reshape(own_rows, 2, width_part)
    up_cotan = (dhidden * jax.nn.silu(gate_act)[:, None, :]).astype(jnp.bfloat16)
    cotan_all = all_tokens(up_cotan, keep_rows)
    gradients = jnp.einsum("td,tkf->kdf", tokens, cotan_all, preferred_element_type=jnp.float32)
    new_moment = beta_one * up_moment + (1.0 - beta_one) * gradients[0]
    new_curvature = beta_two * up_curvature + (1.0 - beta_two) * gradients[1] * gradients[1]
    update = jnp.clip(new_moment / (rho_scale * new_curvature), -1.0, 1.0)
    return (new_moment, new_curvature, update)


def solution(mesh):
    placed = (
        P(None, "dp"),
        P("dp", "tensor"),
        P("dp", "tensor"),
        P("tensor", "dp"),
        P("dp", "tensor"),
        P("dp", "tensor"),
        P("dp", "tensor"),
        P("dp"),
        P("dp"),
    )
    return jax.shard_map(
        on_device,
        mesh=mesh,
        in_specs=placed,
        out_specs=(P("dp", "tensor"), P("dp", "tensor"), P("dp", "tensor")),
        check_vma=False,
    )
```

profile of v0, /device:TPU:1, one launch (start us, length us, event | category | flops | bytes accessed | tf_op | source)
XLA Modules:
  0.0 705.4 jit_solution(17299578801026980290)
XLA Ops:
  7.2 7.4 %convolution_bitcast_fusion = f32[512,3584]{0,1:T(8,128)} fusion(bf16[512,512]{1,0:T(8,128)(2,1)} %param.9, bf16[512,1792]{1,0:T(8,128)(2,1)} %param.11, bf16[512,1792]{1,0:T(8,128)(2,1)} %param.10), kind=kOutput, calls=%fused_computation | convolution fusion | flops 1886388224 | bytes 11534336 | tf_op jit(solution)/shard_map/dot_general | solution.py:59
  14.7 8.4 %copy.50 = f32[512,3584]{1,0:T(8,128)} copy(f32[512,3584]{0,1:T(8,128)} %convolution_bitcast_fusion) | data formatting | bytes 14680064
  23.2 72.2 %reduce-scatter.10.cloned.1.call-done = f32[32,3584]{1,0:T(8,128)} async-done(((f32[512,3584]{1,0:T(8,128)}), f32[32,3584]{1,0:T(8,128)}) %reduce-scatter.10.cloned.1.call-update) | async-done | bytes 458768 | tf_op jit(solution)/shard_map/reduce_scatter | solution.py:16
  95.4 1.8 divide_multiply_fusion
  97.2 36.7 %all-gather.9.cloned.1.call-done = bf16[512,1792]{1,0:T(8,128)(2,1)} async-done(((bf16[32,1792]{1,0:T(8,128)(2,1)}), bf16[512,1792]{1,0:T(8,128)(2,1)}) %all-gather.9.cloned.1.call-update) | async-done | bytes 1835024 | tf_op jit(solution)/shard_map/all_gather | solution.py:22
  134.0 4.1 fusion.25
  138.2 85.5 %all-reduce.3.cloned.1.call-done = f32[512,512]{1,0:T(8,128)} async-done(((f32[512,512]{1,0:T(8,128)}), f32[512,512]{1,0:T(8,128)}) %all-reduce.3.cloned.1.call-update) | async-done | bytes 1048592 | tf_op jit(solution)/shard_map/psum | solution.py:26
  223.7 1.4 multiply_reduce_fusion.1
  225.1 32.4 %psum.36 = f32[512]{0:T(512)S(1)} all-reduce(f32[512]{0:T(512)S(1)} %multiply_reduce_fusion.1), channel_id=1, replica_groups=mesh['dp'=16,'tensor'=8] {'dp'}, use_global_device_ids=true, to_apply=%region_3.4 | all-reduce | flops 512 | bytes 4096 | tf_op jit(solution)/shard_map/psum | solution.py:30
  257.5 1.5 fusion.13
  259.0 3.2 fusion.15
  262.3 58.5 %reduce-scatter.8.cloned.1.call-done = f32[32,2048]{1,0:T(8,128)} async-done(((f32[512,2048]{1,0:T(8,128)}), f32[32,2048]{1,0:T(8,128)}) %reduce-scatter.8.cloned.1.call-update) | async-done | bytes 262160 | tf_op jit(solution)/shard_map/reduce_scatter | solution.py:16
  321.9 21.0 %pmax.7 = f32[32]{0:T(128)S(1)} all-reduce(f32[32]{0:T(128)S(1)} %reduce_max.9), channel_id=1, replica_groups=mesh['dp'=16,'tensor'=8] {'tensor'}, use_global_device_ids=true, to_apply=%region_6.7 | all-reduce | flops 32 | bytes 256 | tf_op jit(solution)/shard_map/pmax | solution.py:77
  342.9 1.2 fusion.18
  344.1 15.8 %psum.37 = f32[32]{0:T(128)S(1)} all-reduce(f32[32]{0:T(128)S(1)} %fusion.18), channel_id=1, replica_groups=mesh['dp'=16,'tensor'=8] {'tensor'}, use_global_device_ids=true, to_apply=%region_8.9 | all-reduce | flops 32 | bytes 256 | tf_op jit(solution)/shard_map/psum | solution.py:26
  361.8 44.9 %all-gather.5.cloned.1.call-done = bf16[512,2,2048]{2,0,1:T(8,128)(2,1)} async-done(((bf16[32,2,2048]{2,0,1:T(8,128)(2,1)}), bf16[512,2,2048]{2,0,1:T(8,128)(2,1)}) %all-gather.5.cloned.1.call-update) | async-done | bytes 4194320 | tf_op jit(solution)/shard_map/all_gather | solution.py:22
  406.7 5.9 fusion.6
  412.6 106.5 %all-reduce.5.cloned.1.call-done = f32[512,2,512]{2,0,1:T(8,128)} async-done(((f32[512,2,512]{2,0,1:T(8,128)}), f32[512,2,512]{2,0,1:T(8,128)}) %all-reduce.5.cloned.1.call-update) | async-done | bytes 2097168 | tf_op jit(solution)/shard_map/psum | solution.py:26
  519.1 2.0 multiply_reduce_fusion
  521.1 27.4 %psum.39 = f32[512,2]{0,1:T(2,128)S(1)} all-reduce(f32[512,2]{0,1:T(2,128)S(1)} %multiply_reduce_fusion), channel_id=1, replica_groups=mesh['dp'=16,'tensor'=8] {'dp'}, use_global_device_ids=true, to_apply=%region_11.12 | all-reduce | flops 1024 | bytes 8192 | tf_op jit(solution)/shard_map/psum | solution.py:30
  548.5 6.9 fusion.8
  555.4 8.4 %copy.52 = f32[512,3584]{1,0:T(8,128)} copy(f32[512,3584]{0,1:T(8,128)} %bitcast.37) | data formatting | bytes 14680064
  564.1 67.5 %reduce-scatter.12.cloned.1.call-done = f32[32,3584]{1,0:T(8,128)} async-done(((f32[512,3584]{1,0:T(8,128)}), f32[32,3584]{1,0:T(8,128)}) %reduce-scatter.12.cloned.1.call-update) | async-done | bytes 458768
  631.6 1.5 copy.53
  634.4 5.1 copy.37
  639.5 5.2 copy.43
  644.7 29.4 %all-gather.7.cloned.1.call-done = bf16[512,2,1792]{2,0,1:T(8,128)(2,1)} async-done(((bf16[32,2,1792]{2,0,1:T(8,128)(2,1)}), bf16[512,2,1792]{2,0,1:T(8,128)(2,1)}) %all-gather.7.cloned.1.call-update) | async-done | bytes 3670032 | tf_op jit(solution)/shard_map/all_gather | solution.py:22
  674.1 4.3 convolution_bitcast_fusion.1
  678.4 4.6 divide_clamp_fusion
  683.0 5.1 copy.44
  688.1 5.1 copy.45
  693.3 5.3 copy.46
  (42 shorter events, 4.9 us)
Async XLA Ops:
  7.2 251.9 %copy-start = (bf16[512,2048]{1,0:T(8,128)(2,1)S(1)}, bf16[512,2048]{1,0:T(8,128)(2,1)}, u32[]{:S(2)}) copy-start(bf16[512,2048]{1,0:T(8,128)(2,1)} %param.13) | copy-start | bytes 6291460
  7.2 88.2 %reduce-scatter.10.cloned.1.call-start = ((), (), s32[]{:S(2)}) async-start(), calls=%async_computation.9 | async-start | bytes 7798784 | tf_op jit(solution)/shard_map/reduce_scatter | solution.py:16
  23.1 110.9 %all-gather.9.cloned.1.call-start = ((), (), s32[]{:S(2)}) async-start(), calls=%async_computation.8 | async-start | bytes 1949696 | tf_op jit(solution)/shard_map/all_gather | solution.py:22
  97.2 126.5 %copy-start.5 = (bf16[512,512]{1,0:T(8,128)(2,1)S(1)}, bf16[512,512]{1,0:T(8,128)(2,1)}, u32[]{:S(2)}) copy-start(bf16[512,512]{1,0:T(8,128)(2,1)} %param.9) | copy-start | bytes 1572868
  97.2 126.5 %all-reduce.3.cloned.1.call-start = ((), (), s32[]{:S(2)}) async-start(), calls=%async_computation.3 | async-start | bytes 2097152 | tf_op jit(solution)/shard_map/psum | solution.py:26
  138.2 182.7 %reduce-scatter.8.cloned.1.call-start = ((), (), s32[]{:S(2)}) async-start(), calls=%async_computation.4 | async-start | bytes 4456448 | tf_op jit(solution)/shard_map/reduce_scatter | solution.py:16
  262.2 97.7 %copy-start.7 = (s32[32]{0:T(128)S(1)}, s32[32]{0:T(128)}, u32[]{:S(2)}) copy-start(s32[32]{0:T(128)} %param.16) | copy-start | bytes 388
  262.2 97.7 %copy-start.8 = (s32[32]{0:T(128)S(1)}, s32[32]{0:T(128)}, u32[]{:S(2)}) copy-start(s32[32]{0:T(128)} %param.17) | copy-start | bytes 388
  262.2 144.5 %all-gather.5.cloned.1.call-start = ((), (), s32[]{:S(2)}) async-start(), calls=%async_computation.5 | async-start | bytes 4456448 | tf_op jit(solution)/shard_map/all_gather | solution.py:22
  361.8 157.3 %all-reduce.5.cloned.1.call-start = ((), (), s32[]{:S(2)}) async-start(), calls=%async_computation.6 | async-start | bytes 4194304 | tf_op jit(solution)/shard_map/psum | solution.py:26
  412.6 219.0 %reduce-scatter.12.cloned.1.call-start = ((), (), s32[]{:S(2)}) async-start(), calls=%async_computation.10 | async-start | bytes 7798784
  519.1 29.4 %copy-start.4 = (f32[512,2,512]{2,0,1:T(8,128)S(1)}, f32[512,2,512]{2,0,1:T(8,128)}, u32[]{:S(2)}) copy-start(f32[512,2,512]{2,0,1:T(8,128)} %all-reduce.5.cloned.1.call-done) | copy-start | bytes 6291460
  563.8 110.2 %all-gather.7.cloned.1.call-start = ((), (), s32[]{:S(2)}) async-start(), calls=%async_computation.7 | async-start | bytes 3899392 | tf_op jit(solution)/shard_map/all_gather | solution.py:22
  639.5 34.5 %copy-start.6 = (bf16[512,512]{1,0:T(8,128)(2,1)S(1)}, bf16[512,512]{1,0:T(8,128)(2,1)}, u32[]{:S(2)}) copy-start(bf16[512,512]{1,0:T(8,128)(2,1)} %param.9) | copy-start | bytes 1572868
  674.1 4.3 copy-start.2
  674.1 4.3 copy-start.3
  693.3 5.3 copy-start.1
Sparse Core Ops, SparseCore 0:
  23.2 72.1 reduce-scatter.9
  97.7 36.2 all-gather.8
  138.3 85.3 all-reduce.2
  262.4 58.4 reduce-scatter.7
  361.9 44.7 all-gather.4
  412.7 106.3 all-reduce.4
  564.0 67.5 reduce-scatter.11
  634.5 39.4 all-gather.6
where the time goes:
time: 706 us; the launch traced here: 705 us
  waiting for transfers between devices  501 us (71%)
  blocking collectives  96.6 us (14%)
  local copies, waits for them, and re-layouts  44.7 us (6%)
  matrix products  31.8 us (5%)
  other arithmetic  16.2 us (2%)
  between operations  14.2 us (2%)
    psum x2, waiting for transfers between devices, tensor_total(): return lax.psum(value, 'tensor')  192 us
    reduce_scatter x2, waiting for transfers between devices, partial_rows(): lax.psum_scatter(term_fn(jnp.int32(0), own_rows * lax.axis_size('dp')), '...  131 us
    all_gather x3, waiting for transfers between devices, all_tokens(): lax.all_gather(stacked, 'dp', axis=0, tiled=True)  111 us
    unnamed x9, waiting for transfers between devices  67.6 us
    psum x2, blocking collectives, token_total(): return lax.psum(value, 'dp')  59.8 us
    unnamed x26, local copies, waits for them, and re-layouts  44.2 us
    pmax x1, blocking collectives, on_device(): row_top = lax.pmax(local_top, 'tensor')  21 us
    psum x1, blocking collectives, tensor_total(): return lax.psum(value, 'tensor')  15.8 us
  transfers between devices with their start and end apart: 8, of which 8 were waited for; matrix products, arithmetic and copies ran while one was open for 1% of the time, Pallas kernels for 0%

commit v1 on v0

v1 whole, which is shorter than its diff:
```python
import jax
import jax.numpy as jnp
from jax import lax
from jax.experimental import pallas as pl
from jax.experimental.pallas import tpu as pltpu
from jax.sharding import Mesh, PartitionSpec as P

D = 8192
FF_HALF = 896
V_HALF = 1024
BLOCK = 64
CHIPS = 8
PAD = 128

beta_one = 0.965
beta_two = 0.95
rho_scale = 0.05
eps_norm = 1e-05

WIDTH_CHIPS = ("xl", "y")
UNIT_CHIPS = ("z", "xh")
f32 = jnp.float32
bf16 = jnp.bfloat16


def other_core(value):
    return lax.ppermute(value, "core", [(0, 1), (1, 0)])


def exchange(blocks, axes):
    return lax.all_to_all(blocks, axes, split_axis=0, concat_axis=0, tiled=True)


def to_all(block, axes):
    copies = jnp.broadcast_to(block[None], (CHIPS,) + block.shape)
    return exchange(copies, axes)


def half_of(array, half, size, axis):
    return lax.dynamic_slice_in_dim(array, half * size, size, axis)


def dot(left, right):
    return jnp.dot(left, right, preferred_element_type=f32)


def dot_rows(left, right):
    return lax.dot_general(left, right, (((1,), (1,)), ((), ())), preferred_element_type=f32)


def as_three(values):
    high = lax.reduce_precision(values, 8, 7)
    rest = values - high
    middle = lax.reduce_precision(rest, 8, 7)
    return jnp.concatenate([high, middle, rest - middle], axis=1).astype(bf16)


def from_three(parts, count):
    parts = parts.astype(f32)
    return parts[..., :count] + parts[..., count : 2 * count] + parts[..., 2 * count : 3 * count]


def step_kernel(core_ref, tokens_ref, own_true, own_sampled, far_true, far_sampled, moment_ref, curve_ref, new_moment, new_curve, update):
    def work(true_ref, sampled_ref):
        dims = (((0,), (0,)), ((), ()))
        token_block = tokens_ref[...]
        grad_true = lax.dot_general(token_block, true_ref[...], dims, preferred_element_type=f32)
        grad_sampled = lax.dot_general(token_block, sampled_ref[...], dims, preferred_element_type=f32)
        moment = beta_one * moment_ref[...] + (1.0 - beta_one) * grad_true
        curve = beta_two * curve_ref[...] + (1.0 - beta_two) * grad_sampled * grad_sampled
        new_moment[...] = moment
        new_curve[...] = curve
        update[...] = jnp.clip(moment / (rho_scale * curve), -1.0, 1.0)

    half = pl.program_id(0)

    @pl.when(half == 0)
    def _():
        work(own_true, own_sampled)

    @pl.when(half == 1)
    def _():
        work(far_true, far_sampled)


def sophia_step(core, tokens, cot_own, cot_far, moment, curve):
    wide = 128
    steps = FF_HALF // wide
    rows = tokens.shape[1]

    def place(half, step, core_ref):
        return (0, (half ^ core_ref[0]) * steps + step)

    def own(shift):
        return lambda half, step, core_ref: (0, shift + jnp.where(half == 0, step, steps - 1))

    def far(shift):
        return lambda half, step, core_ref: (0, shift + jnp.where(half == 1, step, 0))

    cot_block = (tokens.shape[0], wide)
    big = pl.BlockSpec((rows, wide), place)
    shape = jax.ShapeDtypeStruct(moment.shape, f32)
    return pl.pallas_call(
        step_kernel,
        out_shape=(shape, shape, shape),
        grid_spec=pltpu.PrefetchScalarGridSpec(
            num_scalar_prefetch=1,
            grid=(2, steps),
            in_specs=[
                pl.BlockSpec(tokens.shape, lambda half, step, core_ref: (0, 0)),
                pl.BlockSpec(cot_block, own(0)),
                pl.BlockSpec(cot_block, own(steps)),
                pl.BlockSpec(cot_block, far(0)),
                pl.BlockSpec(cot_block, far(steps)),
                big,
                big,
            ],
            out_specs=(big, big, big),
        ),
        compiler_params=pltpu.CompilerParams(vmem_limit_bytes=32 * 1024 * 1024),
        cost_estimate=pl.CostEstimate(flops=1900000000, bytes_accessed=24000000, transcendentals=0),
    )(core.reshape(1), tokens, cot_own, cot_own, cot_far, cot_far, moment, curve)


def on_device(
    tokens,
    gate_weight,
    up_weight,
    down_weight,
    head_weight,
    up_moment,
    up_curvature,
    true_labels,
    sampled_labels,
):
    core = lax.axis_index("core")
    far = 1 - core
    unit_chip = lax.axis_index(UNIT_CHIPS)
    count = tokens.shape[0]

    labels = jnp.stack([true_labels, sampled_labels], axis=0)
    far_labels = other_core(labels)
    labels = jnp.where(
        core == 0,
        jnp.concatenate([labels, far_labels], axis=1),
        jnp.concatenate([far_labels, labels], axis=1),
    )

    def gate_up(half):
        gate = dot(tokens, half_of(gate_weight, half, FF_HALF, 1))
        upper = dot(tokens, half_of(up_weight, half, FF_HALF, 1))
        return gate, upper

    far_gate, far_up = gate_up(far)
    sent = jnp.concatenate([far_gate.astype(bf16), far_up.astype(bf16)], axis=1)
    got = other_core(sent)
    own_gate, own_up = gate_up(core)
    both = jnp.concatenate([own_gate, own_up], axis=1) + got.astype(f32)
    both = exchange(both.astype(bf16).reshape(CHIPS, BLOCK, 2 * FF_HALF), WIDTH_CHIPS)
    both = jnp.sum(both.astype(f32), axis=0)
    gate_act = both[:, :FF_HALF]
    silu_gate = jax.nn.silu(gate_act)
    hidden = (silu_gate * both[:, FF_HALF:]).astype(bf16)

    hidden_own = to_all(hidden, WIDTH_CHIPS).reshape(count, FF_HALF)
    hidden_far = other_core(hidden_own)
    down_own = half_of(down_weight, core, FF_HALF, 0)
    down_far = half_of(down_weight, far, FF_HALF, 0)
    branch = dot(hidden_own, down_own) + dot(hidden_far, down_far)
    width = branch.shape[1]
    branch = exchange(branch.astype(bf16).reshape(CHIPS, BLOCK, width), UNIT_CHIPS)
    branch = jnp.sum(branch.astype(f32), axis=0)
    own_tokens = half_of(tokens, unit_chip, BLOCK, 0)
    summed = own_tokens.astype(f32) + branch
    rows = to_all(summed.astype(bf16), UNIT_CHIPS).reshape(count, width)
    wide_rows = rows.astype(f32)
    squares = jnp.broadcast_to(jnp.sum(wide_rows * wide_rows, axis=1, keepdims=True), (count, PAD))

    head_own = half_of(head_weight, core, V_HALF, 1)
    head_far = half_of(head_weight, far, V_HALF, 1)
    sent = jnp.concatenate([dot(rows, head_far), squares], axis=1)
    got = other_core(sent)
    raw = jnp.concatenate([dot(rows, head_own), squares], axis=1) + got
    raw = exchange(raw.reshape(CHIPS, BLOCK, V_HALF + PAD), WIDTH_CHIPS)
    raw = jnp.sum(raw, axis=0)
    inv_rms = lax.rsqrt(raw[:, V_HALF : V_HALF + 1] / D + eps_norm)
    logits = raw[:, :V_HALF] * inv_rms
    top = jnp.max(logits, axis=1, keepdims=True)
    exp_terms = jnp.exp(logits - top)
    exp_rounded = lax.reduce_precision(exp_terms, 8, 7)
    exp_short = exp_rounded.astype(bf16)
    total = jnp.sum(exp_terms, axis=1, keepdims=True)
    pull = jnp.sum(exp_rounded * logits, axis=1, keepdims=True)
    vocab_start = (unit_chip * 2 + core) * V_HALF
    vocab_ids = vocab_start + lax.broadcasted_iota(jnp.int32, (1, V_HALF), 1)
    stats = [top, inv_rms, total, pull]
    for which in range(2):
        hot = labels[which][:, None] == vocab_ids
        stats.append(jnp.sum(jnp.where(hot, logits, 0.0), axis=1, keepdims=True))
        stats.append(jnp.sum(jnp.where(hot, exp_terms - exp_rounded, 0.0), axis=1, keepdims=True))
    label_parts = labels.T.astype(f32)
    stats.append(label_parts)
    stats = jnp.concatenate(stats, axis=1)
    n_stats = stats.shape[1]
    stat_parts = as_three(stats)
    packed = jnp.concatenate(
        [exp_short, stat_parts, jnp.zeros((BLOCK, PAD - 3 * n_stats), bf16)], axis=1
    )

    packed_own = to_all(packed, WIDTH_CHIPS).reshape(count, V_HALF + PAD)
    packed_far = other_core(packed_own)
    exp_own, exp_far = packed_own[:, :V_HALF], packed_far[:, :V_HALF]
    stats_own = from_three(packed_own[:, V_HALF:], n_stats)
    stats_far = from_three(packed_far[:, V_HALF:], n_stats)
    pair_top = jnp.maximum(stats_own[:, 0:1], stats_far[:, 0:1])
    scale_own = jnp.exp(stats_own[:, 0:1] - pair_top)
    scale_far = jnp.exp(stats_far[:, 0:1] - pair_top)
    pulled = scale_own * dot_rows(exp_own, head_own) + scale_far * dot_rows(exp_far, head_far)
    all_labels = stats_own[:, 8:10].astype(jnp.int32)
    slice_ids = unit_chip * (2 * V_HALF) + lax.broadcasted_iota(jnp.int32, (1, 2 * V_HALF), 1)

    def label_rows(which):
        hot = (all_labels[:, which : which + 1] == slice_ids).astype(bf16)
        return dot_rows(hot, head_weight).astype(bf16)

    pair_stats = jnp.concatenate(
        [
            pair_top,
            stats_own[:, 1:2],
            scale_own * stats_own[:, 2:4] + scale_far * stats_far[:, 2:4],
            stats_own[:, 4:5] + stats_far[:, 4:5],
            scale_own * stats_own[:, 5:6] + scale_far * stats_far[:, 5:6],
            stats_own[:, 6:7] + stats_far[:, 6:7],
            scale_own * stats_own[:, 7:8] + scale_far * stats_far[:, 7:8],
        ],
        axis=1,
    )
    packed = jnp.concatenate(
        [
            pulled.astype(bf16),
            label_rows(0),
            label_rows(1),
            as_three(pair_stats),
            jnp.zeros((count, PAD - 24), bf16),
        ],
        axis=1,
    )
    packed = exchange(packed.reshape(CHIPS, BLOCK, 3 * width + PAD), UNIT_CHIPS)
    stats = from_three(packed[:, :, 3 * width :], 8)
    row_top = jnp.max(stats[:, :, 0:1], axis=0, keepdims=True)
    weight = jnp.exp(stats[:, :, 0:1] - row_top)
    weight = weight / jnp.sum(weight * stats[:, :, 2:3], axis=0, keepdims=True)
    pulled = jnp.sum(weight * packed[:, :, :width].astype(f32), axis=0)
    pull = jnp.sum(weight * stats[:, :, 3:4], axis=0)
    inv_rms = stats[0, :, 1:2]
    scaled = summed * inv_rms
    dsummed = []
    for which in range(2):
        label_logit = jnp.sum(stats[:, :, 4 + 2 * which : 5 + 2 * which], axis=0)
        rest = jnp.sum(weight * stats[:, :, 5 + 2 * which : 6 + 2 * which], axis=0)
        label_row = jnp.sum(
            packed[:, :, (1 + which) * width : (2 + which) * width].astype(f32), axis=0
        )
        dnormed = pulled - (1.0 - rest) * label_row
        mean = (pull - (1.0 - rest) * label_logit) / D
        dsummed.append((inv_rms * (dnormed - scaled * mean)).astype(bf16))
    dsummed = to_all(jnp.concatenate(dsummed, axis=1), UNIT_CHIPS).reshape(count, 2 * width)

    def back(half_rows):
        return [dot_rows(dsummed[:, k * width : (k + 1) * width], half_rows) for k in range(2)]

    sent = jnp.concatenate([part.astype(bf16) for part in back(down_far)], axis=1)
    got = other_core(sent)
    dhidden = jnp.concatenate(back(down_own), axis=1) + got.astype(f32)
    dhidden = exchange(dhidden.astype(bf16).reshape(CHIPS, BLOCK, 2 * FF_HALF), WIDTH_CHIPS)
    dhidden = jnp.sum(dhidden.astype(f32), axis=0)
    cot = (dhidden * jnp.concatenate([silu_gate, silu_gate], axis=1)).astype(bf16)
    cot_own = to_all(cot, WIDTH_CHIPS).reshape(count, 2 * FF_HALF)
    cot_far = other_core(cot_own)
    return sophia_step(core, tokens, cot_own, cot_far, up_moment, up_curvature)


def solution(mesh):
    fine = Mesh(mesh.devices.reshape(2, 4, 2, 4, 2), ("xl", "y", "core", "z", "xh"))
    dp = ("xl", "y", "core")
    tensor = ("z", "xh")
    both = P(dp, tensor)
    placed = (P(None, dp), both, both, P(tensor, dp), both, both, both, P(dp), P(dp))
    return jax.shard_map(
        on_device,
        mesh=fine,
        in_specs=placed,
        out_specs=(both, both, both),
        check_vma=False,
    )
```

time: 706 us -> 321 us (0.45)
  waiting for transfers between devices: 501 us -> 62.1 us
  blocking collectives: 96.6 us -> 162 us
  local copies, waits for them, and re-layouts: 44.7 us -> 12.8 us
  starting transfers between devices: 0.51 us -> 30 us
  between operations: 14.2 us -> 1.05 us
  Pallas kernels: 0 us -> 11.2 us
  matrix products: 31.8 us -> 21.2 us
    psum x2 -> x0, waiting for transfers between devices: 192 us -> none  [tensor_total(): return lax.psum(value, 'tensor')]
    all_to_all x0 -> x7, blocking collectives: none -> 162 us  [exchange(): return lax.all_to_all(blocks, axes, split_axis=0, concat_axis=0, tiled=True)]
    reduce_scatter x2 -> x0, waiting for transfers between devices: 131 us -> none  [partial_rows(): lax.psum_scatter(term_fn(jnp.int32(0), own_rows * lax.axis_size('dp')), '...]
    all_gather x3 -> x0, waiting for transfers between devices: 111 us -> none  [all_tokens(): lax.all_gather(stacked, 'dp', axis=0, tiled=True)]
    psum x3 -> x0, blocking collectives: 75.6 us -> none  [the longest x2 59.8 us: token_total(): return lax.psum(value, 'dp')]
    unnamed x9 -> x0, waiting for transfers between devices: 67.6 us -> none
    all_to_all x0 -> x3, waiting for transfers between devices: none -> 47.8 us  [exchange(): return lax.all_to_all(blocks, axes, split_axis=0, concat_axis=0, tiled=True)]
    unnamed x26 -> x25, local copies, waits for them, and re-layouts: 44.2 us -> 0.17 us
  transfers between devices with their start and end apart: 8 -> 10, of which waited for: 8 -> 10; matrix products, arithmetic and copies ran while one was open for 1% -> 2% of each run, Pallas kernels for 0% -> 0%
where the time goes in v1:
time: 321 us; the launch traced here: 320 us
  blocking collectives  162 us (50%)
  waiting for transfers between devices  62.1 us (19%)
  starting transfers between devices  30 us (9%)
  matrix products  21.2 us (7%)
  other arithmetic  19.9 us (6%)
  local copies, waits for them, and re-layouts  12.8 us (4%)
  Pallas kernels  11.2 us (3%)
    all_to_all x7, blocking collectives, exchange(): return lax.all_to_all(blocks, axes, split_axis=0, concat_axis=0, tiled=True)  162 us
    all_to_all x3, waiting for transfers between devices, exchange(): return lax.all_to_all(blocks, axes, split_axis=0, concat_axis=0, tiled=True)  47.8 us
    all_to_all x3, starting transfers between devices, exchange(): return lax.all_to_all(blocks, axes, split_axis=0, concat_axis=0, tiled=True)  15.2 us
    ppermute x7, starting transfers between devices, other_core(): return lax.ppermute(value, 'core', [(0, 1), (1, 0)])  14.8 us
    ppermute x7, waiting for transfers between devices, other_core(): return lax.ppermute(value, 'core', [(0, 1), (1, 0)])  14.2 us
    dot_general x8, matrix products, dot_rows(): lax.dot_general(left, right, (((1,), (1,)), ((), ())), preferred_element_...  12 us
    pallas_call x1, Pallas kernels, sophia_step(): pl.pallas_call(step_kernel, out_shape=(shape, shape, shape), grid_spec=pl...  11.2 us
    dot_general x8, matrix products, dot(): return jnp.dot(left, right, preferred_element_type=f32)  9.19 us
  transfers between devices with their start and end apart: 10, of which 10 were waited for; matrix products, arithmetic and copies ran while one was open for 2% of the time, Pallas kernels for 0%

profile of v1, /device:TPU:1, one launch (start us, length us, event | category | flops | bytes accessed | tf_op | source)
XLA Modules:
  0.0 319.9 jit_solution(11768104364948742502)
XLA Ops:
  0.7 2.2 fusion.12
  6.4 2.0 convolution_bitcast_fusion.1
  10.1 3.5 %fusion.4 = bf16[512,1792]{0,1:T(8,128)(2,1)} fusion(f32[512,896]{0,1:T(8,128)S(1)} %convolution_bitcast_fusion, f32[512,896]{0,1:T(8,128)S(1)} %convolution_bitcast_fusion.1, bf16[512,1792]{0,1:T(8,128)(2,1)} %collective-permute-done), kind=kLoop, calls=%fused_computation.5 | loop fusion | flops 3670016 | bytes 7340032 | tf_op jit(solution)/shard_map/convert_element_type | solution.py:159
  13.6 3.8 %copy.69 = bf16[512,1792]{1,0:T(8,128)(2,1)} copy(bf16[512,1792]{0,1:T(8,128)(2,1)} %fusion.4) | data formatting | bytes 3670016 | tf_op jit(solution)/shard_map/convert_element_type | solution.py:159
  17.4 28.0 %all_to_all.50 = bf16[8,64,1792]{2,1,0:T(8,128)(2,1)S(1)} all-to-all(bf16[8,64,1792]{2,1,0:T(8,128)(2,1)} %bitcast.57), channel_id=1, replica_groups=mesh['xl'=2,'y'=4,'core'=2,'z'=4,'xh'=2] {'xl','y'}, dimensions={0} | all-to-all | bytes 3670016 | tf_op jit(solution)/shard_map/all_to_all | solution.py:31
  46.6 15.7 %all_to_all.51 = bf16[8,64,896]{2,1,0:T(8,128)(2,1)S(1)} all-to-all(bf16[8,64,896]{2,1,0:T(8,128)(2,1)S(1)} %broadcast_in_dim.74), channel_id=1, replica_groups=mesh['xl'=2,'y'=4,'core'=2,'z'=4,'xh'=2] {'xl','y'}, dimensions={0} | all-to-all | bytes 1835008 | tf_op jit(solution)/shard_map/all_to_all | solution.py:31
  62.3 2.9 collective-permute-start.1
  68.9 7.2 %all-to-all-start.2 = ((bf16[8,64,512]{2,1,0:T(8,128)(2,1)}), bf16[8,64,512]{2,1,0:T(8,128)(2,1)S(1)}, u32[]{:S(2)}, u32[]{:S(2)}) async-start(bf16[8,64,512]{2,1,0:T(8,128)(2,1)} %bitcast.67), calls=%async_computation.2 | async-start | bytes 1048576 | tf_op jit(solution)/shard_map/all_to_all | solution.py:31
  76.1 10.7 %all-to-all-done.2 = bf16[8,64,512]{2,1,0:T(8,128)(2,1)S(1)} async-done(((bf16[8,64,512]{2,1,0:T(8,128)(2,1)}), bf16[8,64,512]{2,1,0:T(8,128)(2,1)S(1)}, u32[]{:S(2)}, u32[]{:S(2)}) %all-to-all-start.2) | async-done | bytes 524320 | tf_op jit(solution)/shard_map/all_to_all | solution.py:31
  87.8 3.5 %all-to-all-start.3 = ((bf16[8,64,512]{2,1,0:T(8,128)(2,1)}), bf16[8,64,512]{2,1,0:T(8,128)(2,1)S(1)}, u32[]{:S(2)}, u32[]{:S(2)}) async-start(bf16[8,64,512]{2,1,0:T(8,128)(2,1)} %broadcast_in_dim.75), calls=%async_computation.3 | async-start | bytes 1048576 | tf_op jit(solution)/shard_map/all_to_all | solution.py:31
  91.3 9.5 %all-to-all-done.3 = bf16[8,64,512]{2,1,0:T(8,128)(2,1)S(1)} async-done(((bf16[8,64,512]{2,1,0:T(8,128)(2,1)}), bf16[8,64,512]{2,1,0:T(8,128)(2,1)S(1)}, u32[]{:S(2)}, u32[]{:S(2)}) %all-to-all-start.3) | async-done | bytes 524320 | tf_op jit(solution)/shard_map/all_to_all | solution.py:31
  103.4 3.0 collective-permute-start.2
  107.2 3.8 %collective-permute-done.2 = f32[512,1152]{1,0:T(8,128)} collective-permute-done((f32[512,1152]{1,0:T(8,128)}, f32[512,1152]{1,0:T(8,128)}, u32[]{:S(2)}, u32[]{:S(2)}) %collective-permute-start.2) | collective-permute-done | bytes 2359328 | tf_op jit(solution)/shard_map/ppermute | solution.py:27
  110.9 3.4 %fusion.6 = f32[512,1152]{1,0:T(8,128)} fusion(f32[512,1152]{1,0:T(8,128)} %collective-permute-done.2, f32[512,128]{1,0:T(8,128)S(1)} %broadcast_in_dim.77, f32[512,1024]{1,0:T(8,128)S(1)} %fusion.35), kind=kLoop, calls=%fused_computation.12 | loop fusion | flops 1179648 | bytes 7077888 | tf_op jit(solution)/shard_map/add | solution.py:183
  114.4 4.5 %all-to-all-start.4 = ((f32[8,64,1152]{2,1,0:T(8,128)}), f32[8,64,1152]{2,1,0:T(8,128)}, u32[]{:S(2)}, u32[]{:S(2)}) async-start(f32[8,64,1152]{2,1,0:T(8,128)} %bitcast.55), calls=%async_computation.4 | async-start | bytes 4718592 | tf_op jit(solution)/shard_map/all_to_all | solution.py:31
  120.3 27.6 %all-to-all-done.4 = f32[8,64,1152]{2,1,0:T(8,128)} async-done(((f32[8,64,1152]{2,1,0:T(8,128)}), f32[8,64,1152]{2,1,0:T(8,128)}, u32[]{:S(2)}, u32[]{:S(2)}) %all-to-all-start.4) | async-done | bytes 2359328 | tf_op jit(solution)/shard_map/all_to_all | solution.py:31
  151.0 19.7 %all_to_all.52 = bf16[8,64,1152]{2,1,0:T(8,128)(2,1)} all-to-all(bf16[8,64,1152]{2,1,0:T(8,128)(2,1)S(1)} %broadcast_in_dim.87), channel_id=1, replica_groups=mesh['xl'=2,'y'=4,'core'=2,'z'=4,'xh'=2] {'xl','y'}, dimensions={0} | all-to-all | bytes 2359296 | tf_op jit(solution)/shard_map/all_to_all | solution.py:31
  170.7 2.4 copy.74
  173.1 2.0 collective-permute-start.4
  178.9 2.0 convolution_multiply_fusion.1
  180.9 2.7 fusion.16
  183.7 2.2 fusion.20
  185.8 2.2 fusion.26
  190.5 3.6 %copy.76 = bf16[512,1664]{1,0:T(8,128)(2,1)} copy(bf16[512,1664]{0,1:T(8,128)(2,1)} %broadcast_dynamic-update-slice_fusion) | data formatting | bytes 3407872 | tf_op jit(solution)/shard_map/concatenate | solution.py:238
  194.1 27.5 %all_to_all.53 = bf16[8,64,1664]{2,1,0:T(8,128)(2,1)S(1)} all-to-all(bf16[8,64,1664]{2,1,0:T(8,128)(2,1)} %bitcast.58), channel_id=1, replica_groups=mesh['xl'=2,'y'=4,'core'=2,'z'=4,'xh'=2] {'z','xh'}, dimensions={0} | all-to-all | bytes 3407872 | tf_op jit(solution)/shard_map/all_to_all | solution.py:31
  223.6 18.2 %all_to_all.54 = bf16[8,64,1024]{2,1,0:T(8,128)(2,1)S(1)} all-to-all(bf16[8,64,1024]{2,1,0:T(8,128)(2,1)S(1)} %broadcast_in_dim.89), channel_id=1, replica_groups=mesh['xl'=2,'y'=4,'core'=2,'z'=4,'xh'=2] {'z','xh'}, dimensions={0} | all-to-all | bytes 2097152 | tf_op jit(solution)/shard_map/all_to_all | solution.py:31
  243.5 2.6 collective-permute-start.5
  249.9 25.5 %all_to_all.55 = bf16[8,64,1792]{2,1,0:T(8,128)(2,1)S(1)} all-to-all(bf16[8,64,1792]{2,1,0:T(8,128)(2,1)S(1)} %bitcast.56), channel_id=1, replica_groups=mesh['xl'=2,'y'=4,'core'=2,'z'=4,'xh'=2] {'xl','y'}, dimensions={0} | all-to-all | bytes 3670016 | tf_op jit(solution)/shard_map/all_to_all | solution.py:31
  275.8 27.1 %all_to_all.56 = bf16[8,64,1792]{2,1,0:T(8,128)(2,1)S(1)} all-to-all(bf16[8,64,1792]{2,1,0:T(8,128)(2,1)S(1)} %broadcast_in_dim.90), channel_id=1, replica_groups=mesh['xl'=2,'y'=4,'core'=2,'z'=4,'xh'=2] {'xl','y'}, dimensions={0} | all-to-all | bytes 3670016 | tf_op jit(solution)/shard_map/all_to_all | solution.py:31
  302.9 2.4 collective-permute-start.6
  305.2 3.4 %collective-permute-done.6.far_true.far_sampled = bf16[512,1792]{1,0:T(8,128)(2,1)S(1)} collective-permute-done((bf16[512,1792]{1,0:T(8,128)(2,1)S(1)}, bf16[512,1792]{1,0:T(8,128)(2,1)S(1)}, u32[]{:S(2)}, u32[]{:S(2)}) %collective-permute-start.6) | collective-permute-done | bytes 1835040 | tf_op jit(solution)/shard_map/ppermute | solution.py:27
  308.7 11.2 %shard_map.112 = (f32[512,1792]{1,0:T(8,128)}, f32[512,1792]{1,0:T(8,128)}, f32[512,1792]{1,0:T(8,128)}) custom-call(s32[1]{0:T(128)} %bitcast.core_ref, bf16[512,512]{1,0:T(8,128)(2,1)S(1)} %copy-done.2, bf16[512,1792]{1,0:T(8,128)(2,1)S(1)} %bitcast.51, bf16[512,1792]{1,0:T(8,128)(2,1)S(1)} %bitcast.52, ...), custom_call_target="tpu_custom_call" | custom-call | flops 1900000000 | bytes 24000000 | tf_op jit(solution)/shard_map/pallas_call | solution.py:103
  (100 shorter events, 32.9 us)
Async XLA Ops:
  0.6 100.3 %copy-start = (bf16[512,2048]{1,0:T(8,128)(2,1)S(1)}, bf16[512,2048]{1,0:T(8,128)(2,1)}, u32[]{:S(2)}) copy-start(bf16[512,2048]{1,0:T(8,128)(2,1)} %param.13) | copy-start | bytes 6291460
  0.6 2.2 copy-start.2
  0.7 2.2 copy-start.8
  4.9 5.2 %collective-permute-start = (bf16[512,1792]{0,1:T(8,128)(2,1)}, bf16[512,1792]{0,1:T(8,128)(2,1)}, u32[]{:S(2)}, u32[]{:S(2)}) collective-permute-start(bf16[512,1792]{0,1:T(8,128)(2,1)} %pad_maximum_fusion.2), channel_id=1, source_target_pairs={{0,8},{8,0},{1,9},{9,1},{2,10},{10,2},{3,11},{11,3},{4,12},{12,4},... | collective-permute-start | bytes 5505032 | tf_op jit(solution)/shard_map/ppermute | solution.py:27
  6.4 2.0 copy-start.9
  45.7 19.5 %copy-start.5 = (bf16[1792,512]{1,0:T(8,128)(2,1)S(1)}, bf16[1792,512]{1,0:T(8,128)(2,1)}, u32[]{:S(2)}) copy-start(bf16[1792,512]{1,0:T(8,128)(2,1)} %param.12) | copy-start | bytes 5505028
  62.3 5.0 %collective-permute-start.1 = (bf16[512,896]{1,0:T(8,128)(2,1)S(1)}, bf16[512,896]{1,0:T(8,128)(2,1)S(1)}, u32[]{:S(2)}, u32[]{:S(2)}) collective-permute-start(bf16[512,896]{1,0:T(8,128)(2,1)S(1)} %bitcast.65), channel_id=1, source_target_pairs={{0,8},{8,0},{1,9},{9,1},{2,10},{10,2},{3,11},{11,3},{4,12},{12,4},... | collective-permute-start | bytes 2752520 | tf_op jit(solution)/shard_map/ppermute | solution.py:27
  68.9 18.0 %all-to-all-start.2 = ((bf16[8,64,512]{2,1,0:T(8,128)(2,1)}), bf16[8,64,512]{2,1,0:T(8,128)(2,1)S(1)}, u32[]{:S(2)}, u32[]{:S(2)}) async-start(bf16[8,64,512]{2,1,0:T(8,128)(2,1)} %bitcast.67), calls=%async_computation.2 | async-start | bytes 1048576 | tf_op jit(solution)/shard_map/all_to_all | solution.py:31
  87.8 13.0 %all-to-all-start.3 = ((bf16[8,64,512]{2,1,0:T(8,128)(2,1)}), bf16[8,64,512]{2,1,0:T(8,128)(2,1)S(1)}, u32[]{:S(2)}, u32[]{:S(2)}) async-start(bf16[8,64,512]{2,1,0:T(8,128)(2,1)} %broadcast_in_dim.75), calls=%async_computation.3 | async-start | bytes 1048576 | tf_op jit(solution)/shard_map/all_to_all | solution.py:31
  103.4 7.5 %collective-permute-start.2 = (f32[512,1152]{1,0:T(8,128)}, f32[512,1152]{1,0:T(8,128)}, u32[]{:S(2)}, u32[]{:S(2)}) collective-permute-start(f32[512,1152]{1,0:T(8,128)} %pad_maximum_fusion), channel_id=1, source_target_pairs={{0,8},{8,0},{1,9},{9,1},{2,10},{10,2},{3,11},{11,3},{4,12},{12,4},... | collective-permute-start | bytes 7077896 | tf_op jit(solution)/shard_map/ppermute | solution.py:27
  114.4 4.5 %copy-start.10 = (s32[32]{0:T(128)S(1)}, s32[32]{0:T(128)}, u32[]{:S(2)}) copy-start(s32[32]{0:T(128)} %param.17) | copy-start | bytes 388
  114.4 4.5 %copy-start.11 = (s32[32]{0:T(128)S(1)}, s32[32]{0:T(128)}, u32[]{:S(2)}) copy-start(s32[32]{0:T(128)} %param.16) | copy-start | bytes 388
  114.4 33.5 %all-to-all-start.4 = ((f32[8,64,1152]{2,1,0:T(8,128)}), f32[8,64,1152]{2,1,0:T(8,128)}, u32[]{:S(2)}, u32[]{:S(2)}) async-start(f32[8,64,1152]{2,1,0:T(8,128)} %bitcast.55), calls=%async_computation.4 | async-start | bytes 4718592 | tf_op jit(solution)/shard_map/all_to_all | solution.py:31
  118.9 1.3 collective-permute-start.3
  173.1 4.8 %collective-permute-start.4 = (bf16[512,1152]{0,1:T(8,128)(2,1)}, bf16[512,1152]{0,1:T(8,128)(2,1)}, u32[]{:S(2)}, u32[]{:S(2)}) collective-permute-start(bf16[512,1152]{0,1:T(8,128)(2,1)} %copy.74), channel_id=1, source_target_pairs={{0,8},{8,0},{1,9},{9,1},{2,10},{10,2},{3,11},{11,3},{4,12},{12,4},... | collective-permute-start | bytes 3538952 | tf_op jit(solution)/shard_map/ppermute | solution.py:27
  223.5 18.4 %copy-start.6 = (bf16[1792,512]{1,0:T(8,128)(2,1)S(1)}, bf16[1792,512]{1,0:T(8,128)(2,1)}, u32[]{:S(2)}) copy-start(bf16[1792,512]{1,0:T(8,128)(2,1)} %param.12) | copy-start | bytes 5505028
  243.5 6.0 %collective-permute-start.5 = (bf16[512,1792]{1,0:T(8,128)(2,1)S(1)}, bf16[512,1792]{1,0:T(8,128)(2,1)S(1)}, u32[]{:S(2)}, u32[]{:S(2)}) collective-permute-start(bf16[512,1792]{1,0:T(8,128)(2,1)S(1)} %pad_maximum_fusion.3), channel_id=1, source_target_pairs={{0,8},{8,0},{1,9},{9,1},{2,10},{10,2},{3,11},{11,3},{4,12},{12,4},... | collective-permute-start | bytes 5505032 | tf_op jit(solution)/shard_map/ppermute | solution.py:27
  249.9 25.7 %copy-start.7 = (f32[64,896]{1,0:T(8,128)S(1)}, f32[64,896]{1,0:T(8,128)}, u32[]{:S(2)}) copy-start(f32[64,896]{1,0:T(8,128)} %get-tuple-element.26) | copy-start | bytes 688132
  275.3 33.3 %copy-start.4 = (f32[512,1792]{1,0:T(8,128)S(1)}, f32[512,1792]{1,0:T(8,128)}, u32[]{:S(2)}) copy-start(f32[512,1792]{1,0:T(8,128)} %curve_ref.1) | copy-start | bytes 11010052
  275.8 32.9 %copy-start.3 = (f32[512,1792]{1,0:T(8,128)S(1)}, f32[512,1792]{1,0:T(8,128)}, u32[]{:S(2)}) copy-start(f32[512,1792]{1,0:T(8,128)} %moment_ref.1) | copy-start | bytes 11010052
  302.9 5.8 %collective-permute-start.6 = (bf16[512,1792]{1,0:T(8,128)(2,1)S(1)}, bf16[512,1792]{1,0:T(8,128)(2,1)S(1)}, u32[]{:S(2)}, u32[]{:S(2)}) collective-permute-start(bf16[512,1792]{1,0:T(8,128)(2,1)S(1)} %bitcast.50), channel_id=1, source_target_pairs={{0,8},{8,0},{1,9},{9,1},{2,10},{10,2},{3,11},{11,3},{4,12},{12,4},... | collective-permute-start | bytes 5505032 | tf_op jit(solution)/shard_map/ppermute | solution.py:27
  308.7 11.2 %copy-start.1 = (bf16[512,2048]{1,0:T(8,128)(2,1)S(1)}, bf16[512,2048]{1,0:T(8,128)(2,1)}, u32[]{:S(2)}) copy-start(bf16[512,2048]{1,0:T(8,128)(2,1)} %param.13) | copy-start | bytes 6291460

commit v2 on v1

v2 whole, which is shorter than its diff:
```python
import jax
import jax.numpy as jnp
from jax import lax
from jax.experimental import pallas as pl
from jax.experimental.pallas import tpu as pltpu
from jax.sharding import Mesh, PartitionSpec as P

D = 8192
FF_HALF = 896
V_HALF = 1024
BLOCK = 64
CHIPS = 8
PAD = 128
N_STATS = 8
STEP = 16384.0
TINY = 1e-30

beta_one = 0.965
beta_two = 0.95
rho_scale = 0.05
eps_norm = 1e-05

WIDTH_CHIPS = ("xl", "y")
UNIT_CHIPS = ("z", "xh")
f32 = jnp.float32
bf16 = jnp.bfloat16
VMEM_LIMIT = 48 * 1024 * 1024


def other_core(value):
    return lax.ppermute(value, "core", [(0, 1), (1, 0)])


def exchange(blocks, axes):
    return lax.all_to_all(blocks, axes, split_axis=0, concat_axis=0, tiled=True)


def to_all(block, axes):
    copies = jnp.broadcast_to(block[None], (CHIPS,) + block.shape)
    return exchange(copies, axes)


def dot(left, right):
    return jnp.dot(left, right, preferred_element_type=f32)


def dot_rows(left, right):
    return lax.dot_general(left, right, (((1,), (1,)), ((), ())), preferred_element_type=f32)


def as_three(values):
    high = lax.reduce_precision(values, 8, 7)
    rest = values - high
    middle = lax.reduce_precision(rest, 8, 7)
    return jnp.concatenate([high, middle, rest - middle], axis=1).astype(bf16)


def from_three(parts, count):
    parts = parts.astype(f32)
    return parts[..., :count] + parts[..., count : 2 * count] + parts[..., 2 * count : 3 * count]


def whole(array):
    return pl.BlockSpec(array.shape, lambda step, half: (0,) * array.ndim)


def columns_of(array, count):
    return pl.BlockSpec((array.shape[0], count), lambda step, half: (0, half[0]))


def rows_of(array, count):
    return pl.BlockSpec((count, array.shape[1]), lambda step, half: (half[0], 0))


def on_core(kernel, half, operands, specs, shape, dtype, flops):
    size = sum(operand.size * operand.dtype.itemsize for operand in operands)
    return pl.pallas_call(
        kernel,
        out_shape=jax.ShapeDtypeStruct(shape, dtype),
        grid_spec=pltpu.PrefetchScalarGridSpec(
            num_scalar_prefetch=1,
            grid=(1,),
            in_specs=specs,
            out_specs=pl.BlockSpec(shape, lambda step, half: (0,) * len(shape)),
        ),
        compiler_params=pltpu.CompilerParams(vmem_limit_bytes=VMEM_LIMIT),
        cost_estimate=pl.CostEstimate(flops=flops, bytes_accessed=size, transcendentals=0),
    )(half.reshape(1), *operands)


def gate_up_far(half_ref, tokens, gate, up, out):
    out[:, :FF_HALF] = dot(tokens[...], gate[...]).astype(bf16)
    out[:, FF_HALF:] = dot(tokens[...], up[...]).astype(bf16)


def gate_up_own(half_ref, tokens, gate, up, got, labels, out):
    gate_sum = dot(tokens[...], gate[...]) + got[:, :FF_HALF].astype(f32)
    out[:, :FF_HALF] = gate_sum.astype(bf16)
    up_sum = dot(tokens[...], up[...]) + got[:, FF_HALF:].astype(f32)
    out[:, FF_HALF : 2 * FF_HALF] = up_sum.astype(bf16)
    for block in range(CHIPS):
        out[block * BLOCK : (block + 1) * BLOCK, 2 * FF_HALF :] = labels[...]


def squares_of(rows):
    wide = rows[...].astype(f32)
    return jnp.sum(wide * wide, axis=1, keepdims=True)


def logits_far(half_ref, rows, head, out):
    out[:, :V_HALF] = dot(rows[...], head[...])
    out[:, V_HALF:] = jnp.broadcast_to(squares_of(rows), (rows.shape[0], PAD))


def exponent_of(values):
    return jnp.ceil(jnp.log2(jnp.maximum(values, TINY)))


def logits_own(half_ref, rows, head, got, out):
    raw = dot(rows[...], head[...]) + got[:, :V_HALF]
    squares = squares_of(rows) + got[:, V_HALF : V_HALF + 1]
    level = exponent_of(jnp.max(jnp.abs(raw), axis=1, keepdims=True))
    out[:, :V_HALF] = jnp.round(raw * (STEP * jnp.exp2(-level))).astype(jnp.int32).astype(jnp.int16)
    square_level = exponent_of(squares)
    units = squares * (STEP * jnp.exp2(-square_level))
    high = jnp.floor(units)
    low = jnp.floor((units - high) * STEP)
    lane = lax.broadcasted_iota(jnp.int32, (rows.shape[0], PAD), 1)
    tail = jnp.where(lane == 0, level, jnp.where(lane == 1, high, jnp.where(lane == 2, low, square_level)))
    out[:, V_HALF:] = tail.astype(jnp.int32).astype(jnp.int16)


def pull_back(half_ref, own, far, head_own, head_far, out):
    count = own.shape[0]
    row = lax.broadcasted_iota(jnp.int32, (PAD, PAD), 0)
    lane = lax.broadcasted_iota(jnp.int32, (PAD, PAD), 1)
    gather = ((row % N_STATS == lane) & (row < 3 * N_STATS)).astype(f32).astype(bf16)
    stats_own = dot(own[:, V_HALF:], gather)
    stats_far = dot(far[:, V_HALF:], gather)
    top = jnp.maximum(stats_own[:, 0:1], stats_far[:, 0:1])
    scale_own = jnp.exp(stats_own[:, 0:1] - top)
    scale_far = jnp.exp(stats_far[:, 0:1] - top)
    pulled = scale_own * dot_rows(own[:, :V_HALF], head_own[...])
    pulled = pulled + scale_far * dot_rows(far[:, :V_HALF], head_far[...])
    width = pulled.shape[1]
    out[:, :width] = pulled.astype(bf16)
    lane = lax.broadcasted_iota(jnp.int32, (count, PAD), 1)
    is_sum = (lane == 2) | (lane == 3) | (lane == 5) | (lane == 7)
    both = jnp.where(is_sum, scale_own * stats_own + scale_far * stats_far, stats_own + stats_far)
    both = jnp.where(lane == 0, top, jnp.where(lane == 1, stats_own, both))
    both = jnp.where(lane < N_STATS, both, 0.0)
    high = both.astype(bf16)
    rest = both - high.astype(f32)
    middle = rest.astype(bf16)
    low = (rest - middle.astype(f32)).astype(bf16)
    row = lax.broadcasted_iota(jnp.int32, (PAD, PAD), 0)
    lane = lax.broadcasted_iota(jnp.int32, (PAD, PAD), 1)
    by_one = (lane == row + N_STATS).astype(f32).astype(bf16)
    by_two = (lane == row + 2 * N_STATS).astype(f32).astype(bf16)
    out[:, width:] = (high.astype(f32) + dot(middle, by_one) + dot(low, by_two)).astype(bf16)


def back_far(half_ref, dsummed, down, out):
    width = down.shape[1]
    for which in range(2):
        part = dot_rows(dsummed[:, which * width : (which + 1) * width], down[...])
        out[:, which * FF_HALF : (which + 1) * FF_HALF] = part.astype(bf16)


def back_own(half_ref, dsummed, down, got, out):
    width = down.shape[1]
    for which in range(2):
        place = slice(which * FF_HALF, (which + 1) * FF_HALF)
        part = dot_rows(dsummed[:, which * width : (which + 1) * width], down[...])
        out[:, place] = (part + got[:, place].astype(f32)).astype(bf16)


def step_kernel(half_ref, turned, cot_true, cot_sampled, moment_ref, curve_ref, *rest):
    new_moment, new_curve, update = rest[-3:]
    grad_true = dot(turned[...], cot_true[...])
    grad_sampled = dot(turned[...], cot_sampled[...])
    moment = beta_one * moment_ref[...] + (1.0 - beta_one) * grad_true
    curve = beta_two * curve_ref[...] + (1.0 - beta_two) * grad_sampled * grad_sampled
    new_moment[...] = moment
    new_curve[...] = curve
    update[...] = jnp.clip(moment / (rho_scale * curve), -1.0, 1.0)


def sophia_half(half, turned, cot, moment, curve, done):
    wide = 128
    steps = FF_HALF // wide
    rows, count = turned.shape
    big = pl.BlockSpec((rows, wide), lambda step, half: (0, half[0] * steps + step))
    shape = jax.ShapeDtypeStruct(moment.shape, f32)
    kept = [pl.BlockSpec(memory_space=pl.ANY) for _ in done]
    return pl.pallas_call(
        step_kernel,
        out_shape=(shape, shape, shape),
        grid_spec=pltpu.PrefetchScalarGridSpec(
            num_scalar_prefetch=1,
            grid=(steps,),
            in_specs=[
                pl.BlockSpec(turned.shape, lambda step, half: (0, 0)),
                pl.BlockSpec((count, wide), lambda step, half: (0, step)),
                pl.BlockSpec((count, wide), lambda step, half: (0, steps + step)),
                big,
                big,
            ]
            + kept,
            out_specs=(big, big, big),
        ),
        input_output_aliases={6 + which: which for which in range(len(done))},
        compiler_params=pltpu.CompilerParams(vmem_limit_bytes=VMEM_LIMIT),
        cost_estimate=pl.CostEstimate(flops=950000000, bytes_accessed=11000000, transcendentals=0),
    )(half.reshape(1), turned, cot, cot, moment, curve, *done)


def own_part(array, index, axis):
    keep = lax.dynamic_index_in_dim(array, index, axis, keepdims=False)
    send = lax.dynamic_index_in_dim(array, 1 - index, axis, keepdims=False)
    return keep, send


def label_rows(labels, head_weight, unit_chip):
    ids = unit_chip * (2 * V_HALF) + lax.broadcasted_iota(jnp.int32, (1, 2 * V_HALF), 1)
    parts = []
    for which in range(2):
        hot = (labels[:, which : which + 1] == ids).astype(bf16)
        parts.append(dot_rows(hot, head_weight).astype(bf16))
    rows = jnp.concatenate(parts, axis=1).reshape(2, 2, 2, BLOCK, -1)
    z = lax.axis_index("z")
    keep, send = own_part(rows, z % 2, 1)
    rows = keep + lax.ppermute(send, "z", [(0, 1), (1, 0), (2, 3), (3, 2)])
    keep, send = own_part(rows, z // 2, 0)
    rows = keep + lax.ppermute(send, "z", [(0, 2), (2, 0), (1, 3), (3, 1)])
    keep, send = own_part(rows, lax.axis_index("xh"), 0)
    return keep + lax.ppermute(send, "xh", [(0, 1), (1, 0)])


def on_device(
    tokens,
    gate_weight,
    up_weight,
    down_weight,
    head_weight,
    up_moment,
    up_curvature,
    true_labels,
    sampled_labels,
):
    core = lax.axis_index("core").astype(jnp.int32)
    far = 1 - core
    unit_chip = lax.axis_index(UNIT_CHIPS)
    count, width = tokens.shape

    labels = jnp.stack([true_labels, sampled_labels], axis=1)
    far_labels = other_core(labels)
    labels = jnp.where(
        core == 0,
        jnp.concatenate([labels, far_labels], axis=0),
        jnp.concatenate([far_labels, labels], axis=0),
    )
    digits = jnp.concatenate([labels // PAD, labels % PAD], axis=1).astype(bf16)
    digits = jnp.pad(digits, ((0, 0), (0, PAD - 4)))

    w_specs = [whole(tokens), columns_of(gate_weight, FF_HALF), columns_of(up_weight, FF_HALF)]
    gate_up_flops = 4 * count * width * FF_HALF
    sent = on_core(
        gate_up_far, far, (tokens, gate_weight, up_weight), w_specs, (count, 2 * FF_HALF), bf16, gate_up_flops
    )
    got = other_core(sent)
    both = on_core(
        gate_up_own,
        core,
        (tokens, gate_weight, up_weight, got, digits),
        w_specs + [whole(got), whole(digits)],
        (count, 2 * FF_HALF + PAD),
        bf16,
        gate_up_flops,
    )
    both = exchange(both.reshape(CHIPS, BLOCK, 2 * FF_HALF + PAD), WIDTH_CHIPS)
    digits = both[:, :, 2 * FF_HALF : 2 * FF_HALF + 4].reshape(count, 4).astype(jnp.int32)
    all_labels = digits[:, :2] * PAD + digits[:, 2:]
    both = jnp.sum(both[:, :, : 2 * FF_HALF].astype(f32), axis=0)
    silu_gate = jax.nn.silu(both[:, :FF_HALF])
    hidden = (silu_gate * both[:, FF_HALF:]).astype(bf16)

    hidden_own = to_all(hidden, WIDTH_CHIPS).reshape(count, FF_HALF)
    hidden_far = other_core(hidden_own)
    label_row = label_rows(all_labels, head_weight, unit_chip).astype(f32)
    down_own = lax.dynamic_slice_in_dim(down_weight, core * FF_HALF, FF_HALF, 0)
    down_far = lax.dynamic_slice_in_dim(down_weight, far * FF_HALF, FF_HALF, 0)
    branch = dot(hidden_own, down_own) + dot(hidden_far, down_far)
    branch = exchange(branch.astype(bf16).reshape(CHIPS, BLOCK, width), UNIT_CHIPS)
    branch = jnp.sum(branch.astype(f32), axis=0)
    own_tokens = lax.dynamic_slice_in_dim(tokens, unit_chip * BLOCK, BLOCK, 0)
    summed = own_tokens.astype(f32) + branch
    rows = to_all(summed.astype(bf16), UNIT_CHIPS).reshape(count, width)

    logit_flops = 2 * count * width * V_HALF
    head_spec = columns_of(head_weight, V_HALF)
    sent = on_core(
        logits_far, far, (rows, head_weight), [whole(rows), head_spec], (count, V_HALF + PAD), f32, logit_flops
    )
    got = other_core(sent)
    raw = on_core(
        logits_own,
        core,
        (rows, head_weight, got),
        [whole(rows), head_spec, whole(got)],
        (count, V_HALF + PAD),
        jnp.int16,
        logit_flops,
    )
    raw = exchange(raw.reshape(CHIPS, BLOCK, V_HALF + PAD), WIDTH_CHIPS).astype(f32)
    tail = raw[:, :, V_HALF : V_HALF + 4]
    raw = jnp.sum(raw[:, :, :V_HALF] * (jnp.exp2(tail[:, :, 0:1]) / STEP), axis=0)
    squares = (tail[:, :, 1:2] + tail[:, :, 2:3] / STEP) * (jnp.exp2(tail[:, :, 3:4]) / STEP)
    inv_rms = lax.rsqrt(jnp.sum(squares, axis=0) / D + eps_norm)
    logits = raw * inv_rms
    top = jnp.max(logits, axis=1, keepdims=True)
    exp_terms = jnp.exp(logits - top)
    exp_rounded = lax.reduce_precision(exp_terms, 8, 7)
    total = jnp.sum(exp_terms, axis=1, keepdims=True)
    pull = jnp.sum(exp_rounded * logits, axis=1, keepdims=True)
    vocab_start = (unit_chip * 2 + core) * V_HALF
    vocab_ids = vocab_start + lax.broadcasted_iota(jnp.int32, (1, V_HALF), 1)
    stats = [top, inv_rms, total, pull]
    for which in range(2):
        hot = labels[:, which : which + 1] == vocab_ids
        stats.append(jnp.sum(jnp.where(hot, logits, 0.0), axis=1, keepdims=True))
        stats.append(jnp.sum(jnp.where(hot, exp_terms - exp_rounded, 0.0), axis=1, keepdims=True))
    stat_parts = as_three(jnp.concatenate(stats, axis=1))
    packed = jnp.concatenate(
        [exp_rounded.astype(bf16), stat_parts, jnp.zeros((BLOCK, PAD - 3 * N_STATS), bf16)], axis=1
    )

    packed_own = to_all(packed, WIDTH_CHIPS).reshape(count, V_HALF + PAD)
    packed_far = other_core(packed_own)
    packed = pl.pallas_call(
        pull_back,
        out_shape=jax.ShapeDtypeStruct((count, width + PAD), bf16),
        grid_spec=pltpu.PrefetchScalarGridSpec(
            num_scalar_prefetch=1,
            grid=(1,),
            in_specs=[
                whole(packed_own),
                whole(packed_far),
                pl.BlockSpec((width, V_HALF), lambda step, half: (0, half[0])),
                pl.BlockSpec((width, V_HALF), lambda step, half: (0, 1 - half[0])),
            ],
            out_specs=pl.BlockSpec((count, width + PAD), lambda step, half: (0, 0)),
        ),
        compiler_params=pltpu.CompilerParams(vmem_limit_bytes=VMEM_LIMIT),
        cost_estimate=pl.CostEstimate(flops=2 * logit_flops, bytes_accessed=5000000, transcendentals=0),
    )(core.reshape(1), packed_own, packed_far, head_weight, head_weight)
    packed = exchange(packed.reshape(CHIPS, BLOCK, width + PAD), UNIT_CHIPS)
    stats = from_three(packed[:, :, width:], N_STATS)
    row_top = jnp.max(stats[:, :, 0:1], axis=0, keepdims=True)
    weight = jnp.exp(stats[:, :, 0:1] - row_top)
    weight = weight / jnp.sum(weight * stats[:, :, 2:3], axis=0, keepdims=True)
    pulled = jnp.sum(weight * packed[:, :, :width].astype(f32), axis=0)
    pull = jnp.sum(weight * stats[:, :, 3:4], axis=0)
    inv_rms = stats[0, :, 1:2]
    scaled = summed * inv_rms
    dsummed = []
    for which in range(2):
        label_logit = jnp.sum(stats[:, :, 4 + 2 * which : 5 + 2 * which], axis=0)
        rest = jnp.sum(weight * stats[:, :, 5 + 2 * which : 6 + 2 * which], axis=0)
        dnormed = pulled - (1.0 - rest) * label_row[:, which * width : (which + 1) * width]
        mean = (pull - (1.0 - rest) * label_logit) / D
        dsummed.append((inv_rms * (dnormed - scaled * mean)).astype(bf16))
    dsummed = to_all(jnp.concatenate(dsummed, axis=1), UNIT_CHIPS).reshape(count, 2 * width)

    down_spec = rows_of(down_weight, FF_HALF)
    sent = on_core(
        back_far, far, (dsummed, down_weight), [whole(dsummed), down_spec], (count, 2 * FF_HALF), bf16, gate_up_flops
    )
    got = other_core(sent)
    dhidden = on_core(
        back_own,
        core,
        (dsummed, down_weight, got),
        [whole(dsummed), down_spec, whole(got)],
        (count, 2 * FF_HALF),
        bf16,
        gate_up_flops,
    )
    dhidden = exchange(dhidden.reshape(CHIPS, BLOCK, 2 * FF_HALF), WIDTH_CHIPS)
    dhidden = jnp.sum(dhidden.astype(f32), axis=0)
    cot = (dhidden * jnp.concatenate([silu_gate, silu_gate], axis=1)).astype(bf16)
    cot_own = to_all(cot, WIDTH_CHIPS).reshape(count, 2 * FF_HALF)
    cot_far = other_core(cot_own)
    turned = tokens.T
    done = sophia_half(core, turned, cot_own, up_moment, up_curvature, ())
    return tuple(sophia_half(far, turned, cot_far, up_moment, up_curvature, done))


def solution(mesh):
    fine = Mesh(mesh.devices.reshape(2, 4, 2, 4, 2), ("xl", "y", "core", "z", "xh"))
    dp = ("xl", "y", "core")
    tensor = ("z", "xh")
    both = P(dp, tensor)
    placed = (P(None, dp), both, both, P(tensor, dp), both, both, both, P(dp), P(dp))
    return jax.shard_map(
        on_device,
        mesh=fine,
        in_specs=placed,
        out_specs=(both, both, both),
        check_vma=False,
    )
```

time: 321 us -> 311 us (0.969)
  blocking collectives: 162 us -> 129 us
  Pallas kernels: 11.2 us -> 31.8 us
  matrix products: 21.2 us -> 6.13 us
  other arithmetic: 19.9 us -> 9.46 us
  local copies, waits for them, and re-layouts: 12.8 us -> 22.9 us
  waiting for transfers between devices: 62.1 us -> 71.6 us
  starting transfers between devices: 30 us -> 37.6 us
    all_to_all x7 -> x6, blocking collectives: 162 us -> 129 us  [exchange(): return lax.all_to_all(blocks, axes, split_axis=0, concat_axis=0, tiled=True)]
    ppermute x0 -> x3, waiting for transfers between devices: none -> 22.2 us  [the longest x1 13.6 us: label_rows(): rows = keep + lax.ppermute(send, 'z', [(0, 1), (1, 0), (2, 3), (3, 2)])]
    pallas_call x1 -> x9, Pallas kernels: 11.2 us -> 31.8 us  [the longest x2 15.4 us: sophia_half(): pl.pallas_call(step_kernel, out_shape=(shape, shape, shape), grid_spec=pl...]
    unnamed x25 -> x37, local copies, waits for them, and re-layouts: 0.17 us -> 12.5 us
    all_to_all x3 -> x4, waiting for transfers between devices: 47.8 us -> 36.9 us  [exchange(): return lax.all_to_all(blocks, axes, split_axis=0, concat_axis=0, tiled=True)]
    dot_general x8 -> x2, matrix products: 12 us -> 2.75 us  [dot_rows(): lax.dot_general(left, right, (((1,), (1,)), ((), ())), preferred_element_...]
    dot_general x8 -> x2, matrix products: 9.19 us -> 3.38 us  [dot(): return jnp.dot(left, right, preferred_element_type=f32)]
    all_to_all x3 -> x4, starting transfers between devices: 15.2 us -> 19.9 us  [exchange(): return lax.all_to_all(blocks, axes, split_axis=0, concat_axis=0, tiled=True)]
  transfers between devices with their start and end apart: 10 -> 14, of which waited for: 10 -> 11; matrix products, arithmetic and copies ran while one was open for 2% -> 4% of each run, Pallas kernels for 0% -> 4%
where the time goes in v2:
time: 311 us; the launch traced here: 309 us
  blocking collectives  129 us (41%)
  waiting for transfers between devices  71.6 us (23%)
  starting transfers between devices  37.6 us (12%)
  Pallas kernels  31.8 us (10%)
  local copies, waits for them, and re-layouts  22.9 us (7%)
  other arithmetic  9.46 us (3%)
  matrix products  6.13 us (2%)
    all_to_all x6, blocking collectives, exchange(): return lax.all_to_all(blocks, axes, split_axis=0, concat_axis=0, tiled=True)  129 us
    all_to_all x4, waiting for transfers between devices, exchange(): return lax.all_to_all(blocks, axes, split_axis=0, concat_axis=0, tiled=True)  36.9 us
    all_to_all x4, starting transfers between devices, exchange(): return lax.all_to_all(blocks, axes, split_axis=0, concat_axis=0, tiled=True)  19.9 us
    pallas_call x2, Pallas kernels, sophia_half(): pl.pallas_call(step_kernel, out_shape=(shape, shape, shape), grid_spec=pl...  15.4 us
    ppermute x7, starting transfers between devices, other_core(): return lax.ppermute(value, 'core', [(0, 1), (1, 0)])  14 us
    ppermute x1, waiting for transfers between devices, label_rows(): rows = keep + lax.ppermute(send, 'z', [(0, 1), (1, 0), (2, 3), (3, 2)])  13.6 us
    pallas_call x6, Pallas kernels, on_core(): pl.pallas_call(kernel, out_shape=jax.ShapeDtypeStruct(shape, dtype), grid...  12.6 us
    ppermute x7, waiting for transfers between devices, other_core(): return lax.ppermute(value, 'core', [(0, 1), (1, 0)])  12.5 us
  transfers between devices with their start and end apart: 14, of which 11 were waited for; matrix products, arithmetic and copies ran while one was open for 4% of the time, Pallas kernels for 4%

profile of v2, /device:TPU:1, one launch (start us, length us, event | category | flops | bytes accessed | tf_op | source)
XLA Modules:
  0.0 309.2 jit_solution(9298590809907622179)
XLA Ops:
  4.7 2.5 shard_map.112
  8.8 3.1 %collective-permute-done.1 = s32[32,2]{0,1:T(2,128)S(1)} collective-permute-done((s32[32,2]{0,1:T(2,128)S(1)}, s32[32,2]{0,1:T(2,128)S(1)}, u32[]{:S(2)}, u32[]{:S(2)}) %collective-permute-start.1) | collective-permute-done | bytes 288 | tf_op jit(solution)/shard_map/ppermute | solution.py:31
  13.9 4.2 %shard_map.113 = bf16[512,1920]{1,0:T(8,128)(2,1)} custom-call(s32[1]{0:T(128)} %bitcast.2.half_ref, bf16[512,512]{1,0:T(8,128)(2,1)S(1)} %copy-done.9, bf16[512,1792]{1,0:T(8,128)(2,1)S(1)} %copy-done.5, bf16[512,1792]{1,0:T(8,128)(2,1)S(1)} %copy-done.7, bf16[512,1792]{1,0:T(8,128)(2,1)} %collective-permute-done.got, bf16[64,128]{1,0:T(8,128)(2,1)S(1)} %pad.4.labels), custom_call_target="tpu_custom_call" | custom-call | flops 939524096 | bytes 6045696 | tf_op jit(solution)/shard_map/pallas_call | solution.py:77
  18.1 29.8 %all_to_all.50 = bf16[8,64,1920]{2,1,0:T(8,128)(2,1)S(1)} all-to-all(bf16[8,64,1920]{2,1,0:T(8,128)(2,1)} %bitcast.68), channel_id=1, replica_groups=mesh['xl'=2,'y'=4,'core'=2,'z'=4,'xh'=2] {'xl','y'}, dimensions={0} | all-to-all | bytes 3932160 | tf_op jit(solution)/shard_map/all_to_all | solution.py:35
  51.1 15.2 %all_to_all.51 = bf16[8,64,896]{2,1,0:T(8,128)(2,1)S(1)} all-to-all(bf16[8,64,896]{2,1,0:T(8,128)(2,1)S(1)} %broadcast_in_dim.63), channel_id=1, replica_groups=mesh['xl'=2,'y'=4,'core'=2,'z'=4,'xh'=2] {'xl','y'}, dimensions={0} | all-to-all | bytes 1835008 | tf_op jit(solution)/shard_map/all_to_all | solution.py:35
  66.3 3.0 collective-permute-start.2
  71.5 2.7 fusion.9
  74.2 7.3 %all-to-all-start.2 = ((bf16[8,64,512]{2,1,0:T(8,128)(2,1)}), bf16[8,64,512]{2,1,0:T(8,128)(2,1)S(1)}, u32[]{:S(2)}, u32[]{:S(2)}) async-start(bf16[8,64,512]{2,1,0:T(8,128)(2,1)} %bitcast.73), calls=%async_computation.2 | async-start | bytes 1048576 | tf_op jit(solution)/shard_map/all_to_all | solution.py:35
  81.5 10.8 %all-to-all-done.2 = bf16[8,64,512]{2,1,0:T(8,128)(2,1)S(1)} async-done(((bf16[8,64,512]{2,1,0:T(8,128)(2,1)}), bf16[8,64,512]{2,1,0:T(8,128)(2,1)S(1)}, u32[]{:S(2)}, u32[]{:S(2)}) %all-to-all-start.2) | async-done | bytes 524320 | tf_op jit(solution)/shard_map/all_to_all | solution.py:35
  92.4 13.7 %all_to_all.52 = bf16[8,64,512]{2,1,0:T(8,128)(2,1)S(1)} all-to-all(bf16[8,64,512]{2,1,0:T(8,128)(2,1)S(1)} %broadcast_in_dim.64), channel_id=1, replica_groups=mesh['xl'=2,'y'=4,'core'=2,'z'=4,'xh'=2] {'z','xh'}, dimensions={0} | all-to-all | bytes 1048576 | tf_op jit(solution)/shard_map/all_to_all | solution.py:35
  106.9 2.1 collective-permute-start.3
  109.0 4.2 %collective-permute-done.3.got = f32[512,1152]{1,0:T(8,128)S(1)} collective-permute-done((f32[512,1152]{1,0:T(8,128)S(1)}, f32[512,1152]{1,0:T(8,128)S(1)}, u32[]{:S(2)}, u32[]{:S(2)}) %collective-permute-start.3) | collective-permute-done | bytes 2359328 | tf_op jit(solution)/shard_map/ppermute | solution.py:31
  115.3 4.4 %all-to-all-start.4 = ((s16[8,64,1152]{2,1,0:T(8,128)(2,1)}), s16[8,64,1152]{2,1,0:T(8,128)(2,1)}, u32[]{:S(2)}, u32[]{:S(2)}) async-start(s16[8,64,1152]{2,1,0:T(8,128)(2,1)} %bitcast.67), calls=%async_computation.4 | async-start | bytes 2359296 | tf_op jit(solution)/shard_map/all_to_all | solution.py:35
  120.0 16.1 %all-to-all-done.4 = s16[8,64,1152]{2,1,0:T(8,128)(2,1)} async-done(((s16[8,64,1152]{2,1,0:T(8,128)(2,1)}), s16[8,64,1152]{2,1,0:T(8,128)(2,1)}, u32[]{:S(2)}, u32[]{:S(2)}) %all-to-all-start.4) | async-done | bytes 1179680 | tf_op jit(solution)/shard_map/all_to_all | solution.py:35
  136.0 4.3 %copy.96 = s16[8,64,1152]{1,0,2:T(8,128)(2,1)} copy(s16[8,64,1152]{2,1,0:T(8,128)(2,1)} %all-to-all-done.4) | data formatting | bytes 2359296 | tf_op jit(solution)/shard_map/all_to_all | solution.py:35
  145.7 4.4 %all-to-all-start.5 = ((bf16[8,64,1152]{2,1,0:T(8,128)(2,1)}), bf16[8,64,1152]{2,1,0:T(8,128)(2,1)}, u32[]{:S(2)}, u32[]{:S(2)}) async-start(bf16[8,64,1152]{2,1,0:T(8,128)(2,1)} %broadcast_in_dim.74), calls=%async_computation.5 | async-start | bytes 2359296 | tf_op jit(solution)/shard_map/all_to_all | solution.py:35
  154.0 2.3 copy.101
  156.2 10.1 %all-to-all-done.5 = bf16[8,64,1152]{2,1,0:T(8,128)(2,1)} async-done(((bf16[8,64,1152]{2,1,0:T(8,128)(2,1)}), bf16[8,64,1152]{2,1,0:T(8,128)(2,1)}, u32[]{:S(2)}, u32[]{:S(2)}) %all-to-all-start.5) | async-done | bytes 1179680 | tf_op jit(solution)/shard_map/all_to_all | solution.py:35
  168.3 13.6 %collective-permute-done.5 = bf16[2,2,64,1024]{3,2,1,0:T(8,128)(2,1)} collective-permute-done((bf16[2,2,64,1024]{3,2,1,0:T(8,128)(2,1)S(1)}, bf16[2,2,64,1024]{3,2,1,0:T(8,128)(2,1)}, u32[]{:S(2)}, u32[]{:S(2)}) %collective-permute-start.5) | collective-permute-done | bytes 524320 | tf_op jit(solution)/shard_map/ppermute | solution.py:233
  184.2 3.8 %shard_map.116 = bf16[512,640]{1,0:T(8,128)(2,1)} custom-call(s32[1]{0:T(128)} %bitcast.2.half_ref, bf16[512,1152]{1,0:T(8,128)(2,1)} %bitcast.21.own, bf16[512,1152]{1,0:T(8,128)(2,1)} %collective-permute-done.4.far, bf16[512,2048]{1,0:T(8,128)(2,1)S(1)} %copy-done, bf16[512,2048]{1,0:T(8,128)(2,1)S(1)} %copy-done), custom_call_target="tpu_custom_call" | custom-call | flops 1073741824 | bytes 5000000 | tf_op jit(solution)/shard_map/pallas_call | solution.py:340
  188.0 3.7 %all-to-all-start.6 = ((bf16[8,64,640]{2,1,0:T(8,128)(2,1)}), bf16[8,64,640]{2,1,0:T(8,128)(2,1)S(1)}, u32[]{:S(2)}, u32[]{:S(2)}) async-start(bf16[8,64,640]{2,1,0:T(8,128)(2,1)} %bitcast.22), calls=%async_computation.6 | async-start | bytes 1310720 | tf_op jit(solution)/shard_map/all_to_all | solution.py:35
  193.0 2.8 collective-permute-start.7
  195.8 8.3 %collective-permute-done.7 = bf16[64,1024]{1,0:T(8,128)(2,1)S(1)} collective-permute-done((bf16[64,1024]{1,0:T(8,128)(2,1)S(1)}, bf16[64,1024]{1,0:T(8,128)(2,1)S(1)}, u32[]{:S(2)}, u32[]{:S(2)}) %collective-permute-start.7) | collective-permute-done | bytes 131104 | tf_op jit(solution)/shard_map/ppermute | solution.py:237
  205.0 18.5 %all_to_all.53 = bf16[8,64,1024]{2,1,0:T(8,128)(2,1)S(1)} all-to-all(bf16[8,64,1024]{2,1,0:T(8,128)(2,1)S(1)} %broadcast_in_dim.75), channel_id=1, replica_groups=mesh['xl'=2,'y'=4,'core'=2,'z'=4,'xh'=2] {'z','xh'}, dimensions={0} | all-to-all | bytes 2097152 | tf_op jit(solution)/shard_map/all_to_all | solution.py:35
  224.8 3.6 %collective-permute-start.8 = (bf16[512,1792]{1,0:T(8,128)(2,1)S(1)}, bf16[512,1792]{1,0:T(8,128)(2,1)S(1)}, u32[]{:S(2)}, u32[]{:S(2)}) collective-permute-start(bf16[512,1792]{1,0:T(8,128)(2,1)S(1)} %shard_map.117), channel_id=1, source_target_pairs={{0,8},{8,0},{1,9},{9,1},{2,10},{10,2},{3,11},{11,3},{4,12},{12,4},... | collective-permute-start | bytes 5505032 | tf_op jit(solution)/shard_map/ppermute | solution.py:31
  228.4 3.4 %collective-permute-done.8.got = bf16[512,1792]{1,0:T(8,128)(2,1)S(1)} collective-permute-done((bf16[512,1792]{1,0:T(8,128)(2,1)S(1)}, bf16[512,1792]{1,0:T(8,128)(2,1)S(1)}, u32[]{:S(2)}, u32[]{:S(2)}) %collective-permute-start.8) | collective-permute-done | bytes 1835040 | tf_op jit(solution)/shard_map/ppermute | solution.py:31
  233.1 2.8 shard_map.118
  235.9 25.8 %all_to_all.54 = bf16[8,64,1792]{2,1,0:T(8,128)(2,1)S(1)} all-to-all(bf16[8,64,1792]{2,1,0:T(8,128)(2,1)S(1)} %bitcast.62), channel_id=1, replica_groups=mesh['xl'=2,'y'=4,'core'=2,'z'=4,'xh'=2] {'xl','y'}, dimensions={0} | all-to-all | bytes 3670016 | tf_op jit(solution)/shard_map/all_to_all | solution.py:35
  263.2 25.5 %all_to_all.55 = bf16[8,64,1792]{2,1,0:T(8,128)(2,1)S(1)} all-to-all(bf16[8,64,1792]{2,1,0:T(8,128)(2,1)S(1)} %broadcast_in_dim.76), channel_id=1, replica_groups=mesh['xl'=2,'y'=4,'core'=2,'z'=4,'xh'=2] {'xl','y'}, dimensions={0} | all-to-all | bytes 3670016 | tf_op jit(solution)/shard_map/all_to_all | solution.py:35
  288.6 2.9 collective-permute-start.9
  293.8 7.4 %shard_map.119 = (f32[512,1792]{1,0:T(8,128)}, f32[512,1792]{1,0:T(8,128)}, f32[512,1792]{1,0:T(8,128)}) custom-call(s32[1]{0:T(128)} %bitcast.2.half_ref, bf16[512,512]{1,0:T(8,128)(2,1)S(1)} %bitcast.63, bf16[512,1792]{1,0:T(8,128)(2,1)S(1)} %bitcast.58, bf16[512,1792]{1,0:T(8,128)(2,1)S(1)} %bitcast.59, f32[512,1792]{1,0:T(8,128)S(1)} %copy-done.1, ...), custom_call_target="tpu_custom_call" | custom-call | flops 950000000 | bytes 11000000 | tf_op jit(solution)/shard_map/pallas_call | solution.py:196
  301.3 7.9 %shard_map.120 = (f32[512,1792]{1,0:T(8,128)}, f32[512,1792]{1,0:T(8,128)}, f32[512,1792]{1,0:T(8,128)}) custom-call(s32[1]{0:T(128)} %bitcast.half_ref, bf16[512,512]{1,0:T(8,128)(2,1)S(1)} %bitcast.64, bf16[512,1792]{1,0:T(8,128)(2,1)} %collective-permute-done.9.cot_true.cot_sampled, ...), custom_call_target="tpu_custom_call", output_to_operand_aliasing={{0}: (6, {}), {1}: (7, {}), {2}: (8, {})} | custom-call | flops 950000000 | bytes 11000000 | tf_op jit(solution)/shard_map/pallas_call | solution.py:196
  (115 shorter events, 37.7 us)
Async XLA Ops:
  0.6 1.5 copy-start.4
  2.1 1.5 copy-start.6
  3.6 1.0 copy-start.8
  4.7 4.0 %copy-start.14 = (s32[32]{0:T(128)S(1)}, s32[32]{0:T(128)}, u32[]{:S(2)}) copy-start(s32[32]{0:T(128)} %param.17) | copy-start | bytes 388
  4.7 4.0 %copy-start.15 = (s32[32]{0:T(128)S(1)}, s32[32]{0:T(128)}, u32[]{:S(2)}) copy-start(s32[32]{0:T(128)} %param.16) | copy-start | bytes 388
  4.7 7.7 %copy-start.5 = (bf16[512,1792]{1,0:T(8,128)(2,1)S(1)}, bf16[512,1792]{1,0:T(8,128)(2,1)}, u32[]{:S(2)}) copy-start(bf16[512,1792]{1,0:T(8,128)(2,1)} %gate.3) | copy-start | bytes 5505028
  4.7 7.7 %copy-start.9 = (bf16[512,512]{1,0:T(8,128)(2,1)S(1)}, bf16[512,512]{1,0:T(8,128)(2,1)}, u32[]{:S(2)}) copy-start(bf16[512,512]{1,0:T(8,128)(2,1)} %tokens.3) | copy-start | bytes 1572868
  7.2 5.2 %collective-permute-start = (bf16[512,1792]{1,0:T(8,128)(2,1)}, bf16[512,1792]{1,0:T(8,128)(2,1)}, u32[]{:S(2)}, u32[]{:S(2)}) collective-permute-start(bf16[512,1792]{1,0:T(8,128)(2,1)} %shard_map.112), channel_id=1, source_target_pairs={{0,8},{8,0},{1,9},{9,1},{2,10},{10,2},{3,11},{11,3},{4,12},{12,4},... | collective-permute-start | bytes 5505032 | tf_op jit(solution)/shard_map/ppermute | solution.py:31
  8.7 3.2 %collective-permute-start.1 = (s32[32,2]{0,1:T(2,128)S(1)}, s32[32,2]{0,1:T(2,128)S(1)}, u32[]{:S(2)}, u32[]{:S(2)}) collective-permute-start(s32[32,2]{0,1:T(2,128)S(1)} %pad_add_fusion), channel_id=1, source_target_pairs={{0,8},{8,0},{1,9},{9,1},{2,10},{10,2},{3,11},{11,3},{4,12},{12,4},... | collective-permute-start | bytes 776 | tf_op jit(solution)/shard_map/ppermute | solution.py:31
  12.4 1.5 copy-start.7
  47.9 1.3 copy-start.11
  49.9 19.4 %copy-start.2 = (bf16[1792,512]{1,0:T(8,128)(2,1)S(1)}, bf16[1792,512]{1,0:T(8,128)(2,1)}, u32[]{:S(2)}) copy-start(bf16[1792,512]{1,0:T(8,128)(2,1)} %down.3) | copy-start | bytes 5505028
  66.3 5.2 %collective-permute-start.2 = (bf16[512,896]{1,0:T(8,128)(2,1)S(1)}, bf16[512,896]{1,0:T(8,128)(2,1)}, u32[]{:S(2)}, u32[]{:S(2)}) collective-permute-start(bf16[512,896]{1,0:T(8,128)(2,1)S(1)} %bitcast.71), channel_id=1, source_target_pairs={{0,8},{8,0},{1,9},{9,1},{2,10},{10,2},{3,11},{11,3},{4,12},{12,4},... | collective-permute-start | bytes 2752520 | tf_op jit(solution)/shard_map/ppermute | solution.py:31
  74.2 32.0 %copy-start = (bf16[512,2048]{1,0:T(8,128)(2,1)S(1)}, bf16[512,2048]{1,0:T(8,128)(2,1)}, u32[]{:S(2)}) copy-start(bf16[512,2048]{1,0:T(8,128)(2,1)} %head_far.1) | copy-start | bytes 6291460
  74.2 18.1 %all-to-all-start.2 = ((bf16[8,64,512]{2,1,0:T(8,128)(2,1)}), bf16[8,64,512]{2,1,0:T(8,128)(2,1)S(1)}, u32[]{:S(2)}, u32[]{:S(2)}) async-start(bf16[8,64,512]{2,1,0:T(8,128)(2,1)} %bitcast.73), calls=%async_computation.2 | async-start | bytes 1048576 | tf_op jit(solution)/shard_map/all_to_all | solution.py:35
  106.9 6.3 %collective-permute-start.3 = (f32[512,1152]{1,0:T(8,128)S(1)}, f32[512,1152]{1,0:T(8,128)S(1)}, u32[]{:S(2)}, u32[]{:S(2)}) collective-permute-start(f32[512,1152]{1,0:T(8,128)S(1)} %shard_map.114), channel_id=1, source_target_pairs={{0,8},{8,0},{1,9},{9,1},{2,10},{10,2},{3,11},{11,3},{4,12},{12,4},... | collective-permute-start | bytes 7077896 | tf_op jit(solution)/shard_map/ppermute | solution.py:31
  114.2 1.0 copy-start.10
  115.3 4.5 %slice-start = ((bf16[8,64,1920]{2,1,0:T(8,128)(2,1)}), bf16[8,64,4]{2,1,0:T(8,128)(2,1)S(1)}, s32[]{:S(2)}) async-start(bf16[8,64,1920]{2,1,0:T(8,128)(2,1)} %copy-done.11), calls=%async_computation.10 | async-start | bytes 262144 | tf_op jit(solution)/shard_map/slice | solution.py:282
  115.3 20.8 %all-to-all-start.4 = ((s16[8,64,1152]{2,1,0:T(8,128)(2,1)}), s16[8,64,1152]{2,1,0:T(8,128)(2,1)}, u32[]{:S(2)}, u32[]{:S(2)}) async-start(s16[8,64,1152]{2,1,0:T(8,128)(2,1)} %bitcast.67), calls=%async_computation.4 | async-start | bytes 2359296 | tf_op jit(solution)/shard_map/all_to_all | solution.py:35
  145.7 20.6 %all-to-all-start.5 = ((bf16[8,64,1152]{2,1,0:T(8,128)(2,1)}), bf16[8,64,1152]{2,1,0:T(8,128)(2,1)}, u32[]{:S(2)}, u32[]{:S(2)}) async-start(bf16[8,64,1152]{2,1,0:T(8,128)(2,1)} %broadcast_in_dim.74), calls=%async_computation.5 | async-start | bytes 2359296 | tf_op jit(solution)/shard_map/all_to_all | solution.py:35
  166.3 17.8 %collective-permute-start.4 = (bf16[512,1152]{1,0:T(8,128)(2,1)}, bf16[512,1152]{1,0:T(8,128)(2,1)}, u32[]{:S(2)}, u32[]{:S(2)}) collective-permute-start(bf16[512,1152]{1,0:T(8,128)(2,1)} %bitcast.21.own), channel_id=1, source_target_pairs={{0,8},{8,0},{1,9},{9,1},{2,10},{10,2},{3,11},{11,3},{4,12},{12,4},... | collective-permute-start | bytes 3538952 | tf_op jit(solution)/shard_map/ppermute | solution.py:31
  168.2 13.7 %collective-permute-start.5 = (bf16[2,2,64,1024]{3,2,1,0:T(8,128)(2,1)S(1)}, bf16[2,2,64,1024]{3,2,1,0:T(8,128)(2,1)}, u32[]{:S(2)}, u32[]{:S(2)}) collective-permute-start(bf16[2,2,64,1024]{3,2,1,0:T(8,128)(2,1)S(1)} %dynamic-slice_bitcast_fusion), channel_id=1, source_target_pairs={{0,2},{2,0},{4,6},{6,4},{1,3},{3,1},{5,7},{7,5},{8,10},{10,8},{12,... | collective-permute-start | bytes 1572872 | tf_op jit(solution)/shard_map/ppermute | solution.py:233
  183.3 8.7 %collective-permute-start.6 = (bf16[2,64,1024]{2,1,0:T(8,128)(2,1)S(1)}, bf16[2,64,1024]{2,1,0:T(8,128)(2,1)}, u32[]{:S(2)}, u32[]{:S(2)}) collective-permute-start(bf16[2,64,1024]{2,1,0:T(8,128)(2,1)S(1)} %dynamic-slice_bitcast_fusion.1), channel_id=1, source_target_pairs={{0,4},{4,0},{2,6},{6,2},{1,5},{5,1},{3,7},{7,3},{8,12},{12,8},{10,... | collective-permute-start | bytes 786440 | tf_op jit(solution)/shard_map/ppermute | solution.py:235
  188.0 16.1 %all-to-all-start.6 = ((bf16[8,64,640]{2,1,0:T(8,128)(2,1)}), bf16[8,64,640]{2,1,0:T(8,128)(2,1)S(1)}, u32[]{:S(2)}, u32[]{:S(2)}) async-start(bf16[8,64,640]{2,1,0:T(8,128)(2,1)} %bitcast.22), calls=%async_computation.6 | async-start | bytes 1310720 | tf_op jit(solution)/shard_map/all_to_all | solution.py:35
  193.0 11.1 %collective-permute-start.7 = (bf16[64,1024]{1,0:T(8,128)(2,1)S(1)}, bf16[64,1024]{1,0:T(8,128)(2,1)S(1)}, u32[]{:S(2)}, u32[]{:S(2)}) collective-permute-start(bf16[64,1024]{1,0:T(8,128)(2,1)S(1)} %dynamic-slice_bitcast_fusion.2), channel_id=1, source_target_pairs={{0,1},{1,0},{2,3},{3,2},{4,5},{5,4},{6,7},{7,6},{8,9},{9,8},{10,11... | collective-permute-start | bytes 393224 | tf_op jit(solution)/shard_map/ppermute | solution.py:237
  204.7 18.9 %copy-start.3 = (bf16[1792,512]{1,0:T(8,128)(2,1)S(1)}, bf16[1792,512]{1,0:T(8,128)(2,1)}, u32[]{:S(2)}) copy-start(bf16[1792,512]{1,0:T(8,128)(2,1)} %down.3) | copy-start | bytes 5505028
  224.8 7.0 %collective-permute-start.8 = (bf16[512,1792]{1,0:T(8,128)(2,1)S(1)}, bf16[512,1792]{1,0:T(8,128)(2,1)S(1)}, u32[]{:S(2)}, u32[]{:S(2)}) collective-permute-start(bf16[512,1792]{1,0:T(8,128)(2,1)S(1)} %shard_map.117), channel_id=1, source_target_pairs={{0,8},{8,0},{1,9},{9,1},{2,10},{10,2},{3,11},{11,3},{4,12},{12,4},... | collective-permute-start | bytes 5505032 | tf_op jit(solution)/shard_map/ppermute | solution.py:31
  231.8 1.2 copy-start.13
  261.7 1.0 copy-start.12
  288.6 12.6 %collective-permute-start.9 = (bf16[512,1792]{1,0:T(8,128)(2,1)S(1)}, bf16[512,1792]{1,0:T(8,128)(2,1)}, u32[]{:S(2)}, u32[]{:S(2)}) collective-permute-start(bf16[512,1792]{1,0:T(8,128)(2,1)S(1)} %bitcast.57), channel_id=1, source_target_pairs={{0,8},{8,0},{1,9},{9,1},{2,10},{10,2},{3,11},{11,3},{4,12},{12,4},... | collective-permute-start | bytes 5505032 | tf_op jit(solution)/shard_map/ppermute | solution.py:31
  291.8 2.0 copy-start.1

commit v3 on v2

v3 whole, which is shorter than its diff:
```python
import jax
import jax.numpy as jnp
from jax import lax
from jax.experimental import pallas as pl
from jax.experimental.pallas import tpu as pltpu
from jax.sharding import Mesh, PartitionSpec as P

D = 8192
FF_HALF = 896
V_HALF = 1024
BLOCK = 64
CHIPS = 8
PAD = 128
N_STATS = 8
STEP = 16384.0
TINY = 1e-30

beta_one = 0.965
beta_two = 0.95
rho_scale = 0.05
eps_norm = 1e-05

WIDTH_CHIPS = ("xl", "y")
UNIT_CHIPS = ("z", "xh")
f32 = jnp.float32
bf16 = jnp.bfloat16
VMEM_LIMIT = 48 * 1024 * 1024
FIRST_LIMIT = 60 * 1024 * 1024


def other_core(value):
    return lax.ppermute(value, "core", [(0, 1), (1, 0)])


def exchange(blocks, axes):
    return lax.all_to_all(blocks, axes, split_axis=0, concat_axis=0, tiled=True)


def to_all(block, axes):
    copies = jnp.broadcast_to(block[None], (CHIPS,) + block.shape)
    return exchange(copies, axes)


def together(*values):
    return lax.optimization_barrier(values)


def dot(left, right):
    return jnp.dot(left, right, preferred_element_type=f32)


def dot_rows(left, right):
    return lax.dot_general(left, right, (((1,), (1,)), ((), ())), preferred_element_type=f32)


def from_three(parts, count):
    parts = parts.astype(f32)
    return parts[..., :count] + parts[..., count : 2 * count] + parts[..., 2 * count : 3 * count]


def whole(array):
    return pl.BlockSpec(array.shape, lambda step, half: (0,) * array.ndim)


def columns_of(array, count):
    return pl.BlockSpec((array.shape[0], count), lambda step, half: (0, half[0]))


def rows_of(array, count):
    return pl.BlockSpec((count, array.shape[1]), lambda step, half: (half[0], 0))


def on_core(kernel, half, operands, specs, outs, flops, limit=VMEM_LIMIT):
    size = sum(operand.size * operand.dtype.itemsize for operand in operands)
    results = pl.pallas_call(
        kernel,
        out_shape=tuple(jax.ShapeDtypeStruct(shape, dtype) for shape, dtype in outs),
        grid_spec=pltpu.PrefetchScalarGridSpec(
            num_scalar_prefetch=1,
            grid=(1,),
            in_specs=specs,
            out_specs=tuple(whole(jax.ShapeDtypeStruct(shape, dtype)) for shape, dtype in outs),
        ),
        compiler_params=pltpu.CompilerParams(vmem_limit_bytes=limit),
        cost_estimate=pl.CostEstimate(flops=flops, bytes_accessed=size, transcendentals=0),
    )(half.reshape(1), *operands)
    return results if len(outs) > 1 else results[0]


def gate_up_far(half_ref, tokens, gate, up, out):
    out[:, :FF_HALF] = dot(tokens[...], gate[...]).astype(bf16)
    out[:, FF_HALF:] = dot(tokens[...], up[...]).astype(bf16)


def gate_up_own(half_ref, tokens, gate, up, got, labels, out):
    gate_sum = dot(tokens[...], gate[...]) + got[:, :FF_HALF].astype(f32)
    out[:, :FF_HALF] = gate_sum.astype(bf16)
    up_sum = dot(tokens[...], up[...]) + got[:, FF_HALF:].astype(f32)
    out[:, FF_HALF : 2 * FF_HALF] = up_sum.astype(bf16)
    for block in range(CHIPS):
        out[block * BLOCK : (block + 1) * BLOCK, 2 * FF_HALF :] = labels[...]


def hidden_kernel(half_ref, both, hidden, silu_out):
    gate = jnp.zeros((BLOCK, FF_HALF), f32)
    upper = jnp.zeros((BLOCK, FF_HALF), f32)
    for chip in range(CHIPS):
        gate = gate + both[chip, :, :FF_HALF].astype(f32)
        upper = upper + both[chip, :, FF_HALF : 2 * FF_HALF].astype(f32)
    silu_gate = gate / (1.0 + jnp.exp(-gate))
    silu_out[...] = silu_gate
    rounded = (silu_gate * upper).astype(bf16)
    for chip in range(CHIPS):
        hidden[chip] = rounded


def squares_of(rows):
    wide = rows[...].astype(f32)
    return jnp.sum(wide * wide, axis=1, keepdims=True)


def exponent_of(values):
    return jnp.ceil(jnp.log2(jnp.maximum(values, TINY)))


def logits_kernel(half_ref, rows, far_rows, head, head_got, out):
    raw = dot(rows[...], head[...]) + dot(far_rows[...], head_got[...])
    squares = squares_of(rows) + squares_of(far_rows)
    level = exponent_of(jnp.max(jnp.abs(raw), axis=1, keepdims=True))
    out[:, :V_HALF] = jnp.round(raw * (STEP * jnp.exp2(-level))).astype(jnp.int32).astype(jnp.int16)
    square_level = exponent_of(squares)
    units = squares * (STEP * jnp.exp2(-square_level))
    high = jnp.floor(units)
    low = jnp.floor((units - high) * STEP)
    lane = lax.broadcasted_iota(jnp.int32, (rows.shape[0], PAD), 1)
    tail = jnp.where(lane == 0, level, jnp.where(lane == 1, high, jnp.where(lane == 2, low, square_level)))
    out[:, V_HALF:] = tail.astype(jnp.int32).astype(jnp.int16)


def pack_three(values):
    lane = lax.broadcasted_iota(jnp.int32, values.shape, 1)
    values = jnp.where(lane < N_STATS, values, 0.0)
    high = values.astype(bf16)
    rest = values - high.astype(f32)
    middle = rest.astype(bf16)
    low = (rest - middle.astype(f32)).astype(bf16)
    row = lax.broadcasted_iota(jnp.int32, (PAD, PAD), 0)
    lane = lax.broadcasted_iota(jnp.int32, (PAD, PAD), 1)
    by_one = (lane == row + N_STATS).astype(f32).astype(bf16)
    by_two = (lane == row + 2 * N_STATS).astype(f32).astype(bf16)
    return (high.astype(f32) + dot(middle, by_one) + dot(low, by_two)).astype(bf16)


def softmax_kernel(start_ref, raw, labels, out):
    total = jnp.zeros((BLOCK, V_HALF), f32)
    squares = jnp.zeros((BLOCK, 1), f32)
    for chip in range(CHIPS):
        tail = raw[chip, :, V_HALF:].astype(jnp.int32).astype(f32)
        scale = jnp.exp2(tail[:, 0:1]) / STEP
        total = total + raw[chip, :, :V_HALF].astype(jnp.int32).astype(f32) * scale
        square_scale = jnp.exp2(tail[:, 3:4]) / STEP
        squares = squares + (tail[:, 1:2] + tail[:, 2:3] / STEP) * square_scale
    inv_rms = lax.rsqrt(squares / D + eps_norm)
    logits = total * inv_rms
    top = jnp.max(logits, axis=1, keepdims=True)
    exp_terms = jnp.exp(logits - top)
    short = exp_terms.astype(bf16)
    rounded = short.astype(f32)
    ids = start_ref[0] + lax.broadcasted_iota(jnp.int32, (BLOCK, V_HALF), 1)
    stats = [
        top,
        inv_rms,
        jnp.sum(exp_terms, axis=1, keepdims=True),
        jnp.sum(rounded * logits, axis=1, keepdims=True),
    ]
    for which in range(2):
        hot = labels[:, which : which + 1] == ids
        stats.append(jnp.sum(jnp.where(hot, logits, 0.0), axis=1, keepdims=True))
        stats.append(jnp.sum(jnp.where(hot, exp_terms - rounded, 0.0), axis=1, keepdims=True))
    lane = lax.broadcasted_iota(jnp.int32, (BLOCK, PAD), 1)
    table = jnp.zeros((BLOCK, PAD), f32)
    for place, value in enumerate(stats):
        table = jnp.where(lane == place, value, table)
    packed = pack_three(table)
    for chip in range(CHIPS):
        out[chip, :, :V_HALF] = short
        out[chip, :, V_HALF:] = packed


def pull_back(half_ref, own, far, head_own, head_far, out):
    count = own.shape[0]
    row = lax.broadcasted_iota(jnp.int32, (PAD, PAD), 0)
    lane = lax.broadcasted_iota(jnp.int32, (PAD, PAD), 1)
    gather = ((row % N_STATS == lane) & (row < 3 * N_STATS)).astype(f32).astype(bf16)
    stats_own = dot(own[:, V_HALF:], gather)
    stats_far = dot(far[:, V_HALF:], gather)
    top = jnp.maximum(stats_own[:, 0:1], stats_far[:, 0:1])
    scale_own = jnp.exp(stats_own[:, 0:1] - top)
    scale_far = jnp.exp(stats_far[:, 0:1] - top)
    pulled = scale_own * dot_rows(own[:, :V_HALF], head_own[...])
    pulled = pulled + scale_far * dot_rows(far[:, :V_HALF], head_far[...])
    width = pulled.shape[1]
    out[:, :width] = pulled.astype(bf16)
    lane = lax.broadcasted_iota(jnp.int32, (count, PAD), 1)
    is_sum = (lane == 2) | (lane == 3) | (lane == 5) | (lane == 7)
    both = jnp.where(is_sum, scale_own * stats_own + scale_far * stats_far, stats_own + stats_far)
    both = jnp.where(lane == 0, top, jnp.where(lane == 1, stats_own, both))
    out[:, width:] = pack_three(both)


def back_kernel(half_ref, dsummed, far_dsummed, down, down_got, out):
    width = down.shape[1]
    for which in range(2):
        place = slice(which * width, (which + 1) * width)
        part = dot_rows(dsummed[:, place], down[...]) + dot_rows(far_dsummed[:, place], down_got[...])
        out[:, which * FF_HALF : (which + 1) * FF_HALF] = part.astype(bf16)


def step_kernel(half_ref, turned, cot, moment_ref, curve_ref, *rest):
    new_moment, new_curve, update = rest[-3:]
    grad_true = dot(turned[...], cot[:, :FF_HALF])
    grad_sampled = dot(turned[...], cot[:, FF_HALF:])
    moment = beta_one * moment_ref[...] + (1.0 - beta_one) * grad_true
    curve = beta_two * curve_ref[...] + (1.0 - beta_two) * grad_sampled * grad_sampled
    new_moment[...] = moment
    new_curve[...] = curve
    update[...] = jnp.clip(moment / (rho_scale * curve), -1.0, 1.0)


def sophia_half(half, turned, cot, moment, curve, done):
    tall = 128
    rows, count = turned.shape
    big = pl.BlockSpec((tall, FF_HALF), lambda step, half: (step, half[0]))
    shape = jax.ShapeDtypeStruct(moment.shape, f32)
    kept = [pl.BlockSpec(memory_space=pl.ANY) for _ in done]
    return pl.pallas_call(
        step_kernel,
        out_shape=(shape, shape, shape),
        grid_spec=pltpu.PrefetchScalarGridSpec(
            num_scalar_prefetch=1,
            grid=(rows // tall,),
            in_specs=[
                pl.BlockSpec((tall, count), lambda step, half: (step, 0)),
                whole(cot),
                big,
                big,
            ]
            + kept,
            out_specs=(big, big, big),
        ),
        input_output_aliases={5 + which: which for which in range(len(done))},
        compiler_params=pltpu.CompilerParams(vmem_limit_bytes=VMEM_LIMIT),
        cost_estimate=pl.CostEstimate(flops=950000000, bytes_accessed=11000000, transcendentals=0),
    )(half.reshape(1), turned, cot, moment, curve, *done)


def own_part(array, index, axis):
    keep = lax.dynamic_index_in_dim(array, index, axis, keepdims=False)
    send = lax.dynamic_index_in_dim(array, 1 - index, axis, keepdims=False)
    return keep, send


def label_rows(labels, head_weight, unit_chip):
    ids = unit_chip * (2 * V_HALF) + lax.broadcasted_iota(jnp.int32, (1, 2 * V_HALF), 1)
    parts = []
    for which in range(2):
        hot = (labels[:, which : which + 1] == ids).astype(bf16)
        parts.append(dot_rows(hot, head_weight).astype(bf16))
    rows = jnp.concatenate(parts, axis=1).reshape(2, 2, 2, BLOCK, -1)
    keep, send = own_part(rows, lax.axis_index("z") % 2, 1)
    return keep + lax.ppermute(send, "z", [(0, 1), (1, 0), (2, 3), (3, 2)])


def own_label_rows(rows):
    keep, send = own_part(rows, lax.axis_index("z") // 2, 0)
    rows = keep + lax.ppermute(send, "z", [(0, 2), (2, 0), (1, 3), (3, 1)])
    keep, send = own_part(rows, lax.axis_index("xh"), 0)
    return keep + lax.ppermute(send, "xh", [(0, 1), (1, 0)])


def on_device(
    tokens,
    gate_weight,
    up_weight,
    down_weight,
    head_weight,
    up_moment,
    up_curvature,
    true_labels,
    sampled_labels,
):
    core = lax.axis_index("core").astype(jnp.int32)
    far = 1 - core
    unit_chip = lax.axis_index(UNIT_CHIPS)
    count, width = tokens.shape

    labels = jnp.stack([true_labels, sampled_labels], axis=1)
    far_labels = other_core(labels)
    labels = jnp.where(
        core == 0,
        jnp.concatenate([labels, far_labels], axis=0),
        jnp.concatenate([far_labels, labels], axis=0),
    )
    digits = jnp.concatenate([labels // PAD, labels % PAD], axis=1).astype(bf16)
    digits = jnp.pad(digits, ((0, 0), (0, PAD - 4)))

    w_specs = [whole(tokens), columns_of(gate_weight, FF_HALF), columns_of(up_weight, FF_HALF)]
    gate_up_flops = 4 * count * width * FF_HALF
    sent = on_core(
        gate_up_far,
        far,
        (tokens, gate_weight, up_weight),
        w_specs,
        [((count, 2 * FF_HALF), bf16)],
        gate_up_flops,
        FIRST_LIMIT,
    )
    got = other_core(sent)
    both = on_core(
        gate_up_own,
        core,
        (tokens, gate_weight, up_weight, got, digits),
        w_specs + [whole(got), whole(digits)],
        [((count, 2 * FF_HALF + PAD), bf16)],
        gate_up_flops,
        FIRST_LIMIT,
    )
    head_send = lax.dynamic_slice_in_dim(head_weight, far * V_HALF, V_HALF, 1)
    down_send = lax.dynamic_slice_in_dim(down_weight, far * FF_HALF, FF_HALF, 0)
    both, head_send, down_send = together(both, head_send, down_send)
    both, head_got, down_got = together(
        exchange(both.reshape(CHIPS, BLOCK, 2 * FF_HALF + PAD), WIDTH_CHIPS),
        other_core(head_send),
        other_core(down_send),
    )
    hidden, silu_gate = on_core(
        hidden_kernel,
        core,
        (both,),
        [whole(both)],
        [((CHIPS, BLOCK, FF_HALF), bf16), ((BLOCK, FF_HALF), f32)],
        1000000,
    )
    digits = both[:, :, 2 * FF_HALF : 2 * FF_HALF + 4].reshape(count, 4)

    hidden, digits = together(hidden, digits)
    digits = digits.astype(jnp.int32)
    all_labels = digits[:, :2] * PAD + digits[:, 2:]
    hidden_own, label_row = together(
        exchange(hidden, WIDTH_CHIPS), label_rows(all_labels, head_weight, unit_chip)
    )
    hidden_own = hidden_own.reshape(count, FF_HALF)
    hidden_far = other_core(hidden_own)
    down_own = lax.dynamic_slice_in_dim(down_weight, core * FF_HALF, FF_HALF, 0)
    down_far = lax.dynamic_slice_in_dim(down_weight, far * FF_HALF, FF_HALF, 0)
    branch = dot(hidden_own, down_own) + dot(hidden_far, down_far)
    branch = exchange(branch.astype(bf16).reshape(CHIPS, BLOCK, width), UNIT_CHIPS)
    branch = jnp.sum(branch.astype(f32), axis=0)
    own_tokens = lax.dynamic_slice_in_dim(tokens, unit_chip * BLOCK, BLOCK, 0)
    summed = own_tokens.astype(f32) + branch
    rows = to_all(summed.astype(bf16), UNIT_CHIPS).reshape(count, width)

    far_rows = other_core(rows)
    logit_flops = 4 * count * width * V_HALF
    raw = on_core(
        logits_kernel,
        core,
        (rows, far_rows, head_weight, head_got),
        [whole(rows), whole(far_rows), columns_of(head_weight, V_HALF), whole(head_got)],
        [((count, V_HALF + PAD), jnp.int16)],
        logit_flops,
    )
    raw, label_row = together(raw, label_row)
    raw, label_row = together(
        exchange(raw.reshape(CHIPS, BLOCK, V_HALF + PAD), WIDTH_CHIPS), own_label_rows(label_row)
    )
    label_row = label_row.astype(f32)
    vocab_start = ((unit_chip * 2 + core) * V_HALF).astype(jnp.int32)
    packed = on_core(
        softmax_kernel,
        vocab_start,
        (raw, labels),
        [whole(raw), whole(labels)],
        [((CHIPS, BLOCK, V_HALF + PAD), bf16)],
        1000000,
    )
    packed, token_rows = together(packed, tokens)
    packed_own, turned = together(exchange(packed, WIDTH_CHIPS), token_rows.T)
    packed_own = packed_own.reshape(count, V_HALF + PAD)
    packed_far = other_core(packed_own)
    packed = on_core(
        pull_back,
        core,
        (packed_own, packed_far, head_weight, head_weight),
        [
            whole(packed_own),
            whole(packed_far),
            pl.BlockSpec((width, V_HALF), lambda step, half: (0, half[0])),
            pl.BlockSpec((width, V_HALF), lambda step, half: (0, 1 - half[0])),
        ],
        [((count, width + PAD), bf16)],
        logit_flops,
    )
    packed = exchange(packed.reshape(CHIPS, BLOCK, width + PAD), UNIT_CHIPS)
    stats = from_three(packed[:, :, width:], N_STATS)
    row_top = jnp.max(stats[:, :, 0:1], axis=0, keepdims=True)
    weight = jnp.exp(stats[:, :, 0:1] - row_top)
    weight = weight / jnp.sum(weight * stats[:, :, 2:3], axis=0, keepdims=True)
    pulled = jnp.sum(weight * packed[:, :, :width].astype(f32), axis=0)
    pull = jnp.sum(weight * stats[:, :, 3:4], axis=0)
    inv_rms = stats[0, :, 1:2]
    scaled = summed * inv_rms
    dsummed = []
    for which in range(2):
        label_logit = jnp.sum(stats[:, :, 4 + 2 * which : 5 + 2 * which], axis=0)
        rest = jnp.sum(weight * stats[:, :, 5 + 2 * which : 6 + 2 * which], axis=0)
        dnormed = pulled - (1.0 - rest) * label_row[:, which * width : (which + 1) * width]
        mean = (pull - (1.0 - rest) * label_logit) / D
        dsummed.append((inv_rms * (dnormed - scaled * mean)).astype(bf16))
    dsummed = to_all(jnp.concatenate(dsummed, axis=1), UNIT_CHIPS).reshape(count, 2 * width)

    far_dsummed = other_core(dsummed)
    dhidden = on_core(
        back_kernel,
        core,
        (dsummed, far_dsummed, down_weight, down_got),
        [whole(dsummed), whole(far_dsummed), rows_of(down_weight, FF_HALF), whole(down_got)],
        [((count, 2 * FF_HALF), bf16)],
        2 * gate_up_flops,
    )
    dhidden = exchange(dhidden.reshape(CHIPS, BLOCK, 2 * FF_HALF), WIDTH_CHIPS)
    dhidden = jnp.sum(dhidden.astype(f32), axis=0)
    cot = (dhidden * jnp.concatenate([silu_gate, silu_gate], axis=1)).astype(bf16)
    cot_own = to_all(cot, WIDTH_CHIPS).reshape(count, 2 * FF_HALF)
    cot_far = other_core(cot_own)
    done = sophia_half(core, turned, cot_own, up_moment, up_curvature, ())
    return tuple(sophia_half(far, turned, cot_far, up_moment, up_curvature, done))


def solution(mesh):
    fine = Mesh(mesh.devices.reshape(2, 4, 2, 4, 2), ("xl", "y", "core", "z", "xh"))
    dp = ("xl", "y", "core")
    tensor = ("z", "xh")
    both = P(dp, tensor)
    placed = (P(None, dp), both, both, P(tensor, dp), both, both, both, P(dp), P(dp))
    return jax.shard_map(
        on_device,
        mesh=fine,
        in_specs=placed,
        out_specs=(both, both, both),
        check_vma=False,
    )
```

time: 311 us -> 289 us (0.929)
  blocking collectives: 129 us -> 84.7 us
  waiting for transfers between devices: 71.6 us -> 90.9 us
  starting transfers between devices: 37.6 us -> 48.9 us
  local copies, waits for them, and re-layouts: 22.9 us -> 15.9 us
    all_to_all x6 -> x4, blocking collectives: 129 us -> 84.7 us  [exchange(): return lax.all_to_all(blocks, axes, split_axis=0, concat_axis=0, tiled=True)]
    all_to_all x4 -> x6, waiting for transfers between devices: 36.9 us -> 55.6 us  [exchange(): return lax.all_to_all(blocks, axes, split_axis=0, concat_axis=0, tiled=True)]
    all_to_all x4 -> x6, starting transfers between devices: 19.9 us -> 29.5 us  [exchange(): return lax.all_to_all(blocks, axes, split_axis=0, concat_axis=0, tiled=True)]
    unnamed x37 -> x33, local copies, waits for them, and re-layouts: 12.5 us -> 6.52 us
    pallas_call x2, Pallas kernels: 15.4 us -> 10.3 us  [sophia_half(): pl.pallas_call(step_kernel, out_shape=(shape, shape, shape), grid_spec=pl...]
    all_to_all x1 -> x0, local copies, waits for them, and re-layouts: 4.31 us -> none  [exchange(): return lax.all_to_all(blocks, axes, split_axis=0, concat_axis=0, tiled=True)]
    pallas_call x7, Pallas kernels: 16.4 us -> 20.5 us  [on_core(): pl.pallas_call(kernel, out_shape=tuple((jax.ShapeDtypeStruct(shape, dtype...]
    ppermute x7 -> x9, starting transfers between devices: 14 us -> 15.7 us  [other_core(): return lax.ppermute(value, 'core', [(0, 1), (1, 0)])]
  transfers between devices with their start and end apart: 14 -> 18, of which waited for: 11 -> 13; matrix products, arithmetic and copies ran while one was open for 4% -> 7% of each run, Pallas kernels for 4% -> 2%
where the time goes in v3:
time: 289 us; the launch traced here: 287 us
  waiting for transfers between devices  90.9 us (31%)
  blocking collectives  84.7 us (29%)
  starting transfers between devices  48.9 us (17%)
  Pallas kernels  30.8 us (11%)
  local copies, waits for them, and re-layouts  15.9 us (6%)
  matrix products  7.59 us (3%)
  other arithmetic  7.49 us (3%)
    all_to_all x4, blocking collectives, exchange(): return lax.all_to_all(blocks, axes, split_axis=0, concat_axis=0, tiled=True)  84.7 us
    all_to_all x6, waiting for transfers between devices, exchange(): return lax.all_to_all(blocks, axes, split_axis=0, concat_axis=0, tiled=True)  55.6 us
    all_to_all x6, starting transfers between devices, exchange(): return lax.all_to_all(blocks, axes, split_axis=0, concat_axis=0, tiled=True)  29.5 us
    pallas_call x7, Pallas kernels, on_core(): pl.pallas_call(kernel, out_shape=tuple((jax.ShapeDtypeStruct(shape, dtype...  20.5 us
    ppermute x9, starting transfers between devices, other_core(): return lax.ppermute(value, 'core', [(0, 1), (1, 0)])  15.7 us
    ppermute x1, waiting for transfers between devices, label_rows(): return keep + lax.ppermute(send, 'z', [(0, 1), (1, 0), (2, 3), (3, 2)])  11.7 us
    ppermute x9, waiting for transfers between devices, other_core(): return lax.ppermute(value, 'core', [(0, 1), (1, 0)])  10.9 us
    pallas_call x2, Pallas kernels, sophia_half(): pl.pallas_call(step_kernel, out_shape=(shape, shape, shape), grid_spec=pl...  10.3 us
  transfers between devices with their start and end apart: 18, of which 13 were waited for; matrix products, arithmetic and copies ran while one was open for 7% of the time, Pallas kernels for 2%

profile of v3, /device:TPU:1, one launch (start us, length us, event | category | flops | bytes accessed | tf_op | source)
XLA Modules:
  0.0 287.3 jit_solution(75977492954424182)
XLA Ops:
  0.7 4.3 %shard_map.112 = bf16[512,1792]{1,0:T(8,128)(2,1)} custom-call(s32[1]{0:T(128)} %bitcast.half_ref, bf16[512,512]{1,0:T(8,128)(2,1)} %tokens.3, bf16[512,1792]{1,0:T(8,128)(2,1)} %gate.3, bf16[512,1792]{1,0:T(8,128)(2,1)} %up.3), custom_call_target="tpu_custom_call" | custom-call | flops 939524096 | bytes 4194304 | tf_op jit(solution)/shard_map/pallas_call | solution.py:75
  10.8 4.7 %shard_map.113 = bf16[512,1920]{1,0:T(8,128)(2,1)} custom-call(s32[1]{0:T(128)} %bitcast.2.half_ref, bf16[512,512]{1,0:T(8,128)(2,1)} %tokens.3, bf16[512,1792]{1,0:T(8,128)(2,1)} %gate.3, bf16[512,1792]{1,0:T(8,128)(2,1)} %up.3, bf16[512,1792]{1,0:T(8,128)(2,1)} %collective-permute-done.got, bf16[64,128]{1,0:T(8,128)(2,1)} %pad.4.labels), custom_call_target="tpu_custom_call" | custom-call | flops 939524096 | bytes 6045696 | tf_op jit(solution)/shard_map/pallas_call | solution.py:75
  15.5 5.2 %all-to-all-start = ((bf16[8,64,1920]{2,1,0:T(8,128)(2,1)}), bf16[8,64,1920]{2,1,0:T(8,128)(2,1)}, u32[]{:S(2)}, u32[]{:S(2)}) async-start(bf16[8,64,1920]{2,1,0:T(8,128)(2,1)} %bitcast.51), calls=%async_computation | async-start | bytes 3932160 | tf_op jit(solution)/shard_map/all_to_all | solution.py:36
  21.4 3.8 %collective-permute-done.3.down_got = bf16[896,512]{1,0:T(8,128)(2,1)} collective-permute-done((bf16[896,512]{1,0:T(8,128)(2,1)}, bf16[896,512]{1,0:T(8,128)(2,1)}, u32[]{:S(2)}, u32[]{:S(2)}) %collective-permute-start.3) | collective-permute-done | bytes 917536 | tf_op jit(solution)/shard_map/ppermute | solution.py:32
  25.2 20.4 %all-to-all-done.both = bf16[8,64,1920]{2,1,0:T(8,128)(2,1)} async-done(((bf16[8,64,1920]{2,1,0:T(8,128)(2,1)}), bf16[8,64,1920]{2,1,0:T(8,128)(2,1)}, u32[]{:S(2)}, u32[]{:S(2)}) %all-to-all-start) | async-done | bytes 1966112 | tf_op jit(solution)/shard_map/all_to_all | solution.py:36
  49.5 4.2 %all-to-all-start.1 = ((bf16[8,64,896]{2,1,0:T(8,128)(2,1)}), bf16[8,64,896]{2,1,0:T(8,128)(2,1)}, u32[]{:S(2)}, u32[]{:S(2)}) async-start(bf16[8,64,896]{2,1,0:T(8,128)(2,1)} %copy-done.6), calls=%async_computation.1 | async-start | bytes 1835008 | tf_op jit(solution)/shard_map/all_to_all | solution.py:36
  61.5 11.7 %collective-permute-done.4 = bf16[2,2,64,1024]{3,2,1,0:T(8,128)(2,1)} collective-permute-done((bf16[2,2,64,1024]{3,2,1,0:T(8,128)(2,1)}, bf16[2,2,64,1024]{3,2,1,0:T(8,128)(2,1)}, u32[]{:S(2)}, u32[]{:S(2)}) %collective-permute-start.4) | collective-permute-done | bytes 524320 | tf_op jit(solution)/shard_map/ppermute | solution.py:271
  76.6 2.2 fusion.15
  79.0 2.7 fusion.8
  81.7 7.0 %all-to-all-start.2 = ((bf16[8,64,512]{2,1,0:T(8,128)(2,1)}), bf16[8,64,512]{2,1,0:T(8,128)(2,1)S(1)}, u32[]{:S(2)}, u32[]{:S(2)}) async-start(bf16[8,64,512]{2,1,0:T(8,128)(2,1)} %bitcast.54), calls=%async_computation.2 | async-start | bytes 1048576 | tf_op jit(solution)/shard_map/all_to_all | solution.py:36
  88.7 10.8 %all-to-all-done.2 = bf16[8,64,512]{2,1,0:T(8,128)(2,1)S(1)} async-done(((bf16[8,64,512]{2,1,0:T(8,128)(2,1)}), bf16[8,64,512]{2,1,0:T(8,128)(2,1)S(1)}, u32[]{:S(2)}, u32[]{:S(2)}) %all-to-all-start.2) | async-done | bytes 524320 | tf_op jit(solution)/shard_map/all_to_all | solution.py:36
  101.1 13.7 %all_to_all.50 = bf16[8,64,512]{2,1,0:T(8,128)(2,1)S(1)} all-to-all(bf16[8,64,512]{2,1,0:T(8,128)(2,1)S(1)} %broadcast_in_dim.6), channel_id=1, replica_groups=mesh['xl'=2,'y'=4,'core'=2,'z'=4,'xh'=2] {'z','xh'}, dimensions={0} | all-to-all | bytes 1048576 | tf_op jit(solution)/shard_map/all_to_all | solution.py:36
  114.9 2.0 collective-permute-start.6
  122.2 4.4 %all-to-all-start.4 = ((s16[8,64,1152]{2,1,0:T(8,128)(2,1)}), s16[8,64,1152]{2,1,0:T(8,128)(2,1)S(1)}, u32[]{:S(2)}, u32[]{:S(2)}) async-start(s16[8,64,1152]{2,1,0:T(8,128)(2,1)} %bitcast.45), calls=%async_computation.4 | async-start | bytes 2359296 | tf_op jit(solution)/shard_map/all_to_all | solution.py:36
  129.1 8.2 %collective-permute-done.7 = bf16[2,64,1024]{2,1,0:T(8,128)(2,1)} collective-permute-done((bf16[2,64,1024]{2,1,0:T(8,128)(2,1)}, bf16[2,64,1024]{2,1,0:T(8,128)(2,1)}, u32[]{:S(2)}, u32[]{:S(2)}) %collective-permute-start.7) | collective-permute-done | bytes 262176 | tf_op jit(solution)/shard_map/ppermute | solution.py:276
  140.9 4.5 %collective-permute-done.8 = bf16[64,1024]{1,0:T(8,128)(2,1)} collective-permute-done((bf16[64,1024]{1,0:T(8,128)(2,1)}, bf16[64,1024]{1,0:T(8,128)(2,1)}, u32[]{:S(2)}, u32[]{:S(2)}) %collective-permute-start.8) | collective-permute-done | bytes 131104 | tf_op jit(solution)/shard_map/ppermute | solution.py:278
  149.0 5.0 %all-to-all-start.5 = ((bf16[8,64,1152]{2,1,0:T(8,128)(2,1)}), bf16[8,64,1152]{2,1,0:T(8,128)(2,1)}, u32[]{:S(2)}, u32[]{:S(2)}) async-start(bf16[8,64,1152]{2,1,0:T(8,128)(2,1)} %copy-done.2), calls=%async_computation.5 | async-start | bytes 2359296 | tf_op jit(solution)/shard_map/all_to_all | solution.py:36
  154.2 11.8 %all-to-all-done.5 = bf16[8,64,1152]{2,1,0:T(8,128)(2,1)} async-done(((bf16[8,64,1152]{2,1,0:T(8,128)(2,1)}), bf16[8,64,1152]{2,1,0:T(8,128)(2,1)}, u32[]{:S(2)}, u32[]{:S(2)}) %all-to-all-start.5) | async-done | bytes 1179680 | tf_op jit(solution)/shard_map/all_to_all | solution.py:36
  166.0 5.2 %collective-permute-start.9 = (bf16[512,1152]{1,0:T(8,128)(2,1)}, bf16[512,1152]{1,0:T(8,128)(2,1)S(1)}, u32[]{:S(2)}, u32[]{:S(2)}) collective-permute-start(bf16[512,1152]{1,0:T(8,128)(2,1)} %bitcast.21.own), channel_id=1, source_target_pairs={{0,8},{8,0},{1,9},{9,1},{2,10},{10,2},{3,11},{11,3},{4,12},{12,4},... | collective-permute-start | bytes 3538952 | tf_op jit(solution)/shard_map/ppermute | solution.py:32
  171.2 2.7 collective-permute-done.9.far
  173.9 3.5 %shard_map.117 = bf16[512,640]{1,0:T(8,128)(2,1)} custom-call(s32[1]{0:T(128)} %bitcast.2.half_ref, bf16[512,1152]{1,0:T(8,128)(2,1)} %bitcast.21.own, bf16[512,1152]{1,0:T(8,128)(2,1)S(1)} %collective-permute-done.9.far, bf16[512,2048]{1,0:T(8,128)(2,1)S(1)} %copy-done, bf16[512,2048]{1,0:T(8,128)(2,1)S(1)} %copy-done), custom_call_target="tpu_custom_call" | custom-call | flops 1073741824 | bytes 6553600 | tf_op jit(solution)/shard_map/pallas_call | solution.py:75
  177.4 3.7 %all-to-all-start.6 = ((bf16[8,64,640]{2,1,0:T(8,128)(2,1)}), bf16[8,64,640]{2,1,0:T(8,128)(2,1)S(1)}, u32[]{:S(2)}, u32[]{:S(2)}) async-start(bf16[8,64,640]{2,1,0:T(8,128)(2,1)} %bitcast.22), calls=%async_computation.6 | async-start | bytes 1310720 | tf_op jit(solution)/shard_map/all_to_all | solution.py:36
  181.1 12.6 %all-to-all-done.6 = bf16[8,64,640]{2,1,0:T(8,128)(2,1)S(1)} async-done(((bf16[8,64,640]{2,1,0:T(8,128)(2,1)}), bf16[8,64,640]{2,1,0:T(8,128)(2,1)S(1)}, u32[]{:S(2)}, u32[]{:S(2)}) %all-to-all-start.6) | async-done | bytes 655392 | tf_op jit(solution)/shard_map/all_to_all | solution.py:36
  194.6 19.2 %all_to_all.51 = bf16[8,64,1024]{2,1,0:T(8,128)(2,1)S(1)} all-to-all(bf16[8,64,1024]{2,1,0:T(8,128)(2,1)S(1)} %broadcast_in_dim.7), channel_id=1, replica_groups=mesh['xl'=2,'y'=4,'core'=2,'z'=4,'xh'=2] {'z','xh'}, dimensions={0} | all-to-all | bytes 2097152 | tf_op jit(solution)/shard_map/all_to_all | solution.py:36
  213.8 1.9 collective-permute-start.10
  215.7 2.3 collective-permute-done.10.far_dsummed
  218.0 3.8 %shard_map.118 = bf16[512,1792]{1,0:T(8,128)(2,1)S(1)} custom-call(s32[1]{0:T(128)} %bitcast.2.half_ref, bf16[512,1024]{1,0:T(8,128)(2,1)S(1)} %bitcast.50, bf16[512,1024]{1,0:T(8,128)(2,1)S(1)} %collective-permute-done.10.far_dsummed, bf16[1792,512]{1,0:T(8,128)(2,1)} %down.1, bf16[896,512]{1,0:T(8,128)(2,1)} %collective-permute-done.3.down_got), custom_call_target="tpu_custom_call" | custom-call | flops 1879048192 | bytes 4849664 | tf_op jit(solution)/shard_map/pallas_call | solution.py:75
  221.8 26.1 %all_to_all.52 = bf16[8,64,1792]{2,1,0:T(8,128)(2,1)S(1)} all-to-all(bf16[8,64,1792]{2,1,0:T(8,128)(2,1)S(1)} %bitcast.48), channel_id=1, replica_groups=mesh['xl'=2,'y'=4,'core'=2,'z'=4,'xh'=2] {'xl','y'}, dimensions={0} | all-to-all | bytes 3670016 | tf_op jit(solution)/shard_map/all_to_all | solution.py:36
  248.3 25.7 %all_to_all.53 = bf16[8,64,1792]{2,1,0:T(8,128)(2,1)S(1)} all-to-all(bf16[8,64,1792]{2,1,0:T(8,128)(2,1)S(1)} %broadcast_in_dim.8), channel_id=1, replica_groups=mesh['xl'=2,'y'=4,'core'=2,'z'=4,'xh'=2] {'xl','y'}, dimensions={0} | all-to-all | bytes 3670016 | tf_op jit(solution)/shard_map/all_to_all | solution.py:36
  274.1 2.9 %collective-permute-start.11 = (bf16[512,1792]{1,0:T(8,128)(2,1)S(1)}, bf16[512,1792]{1,0:T(8,128)(2,1)S(1)}, u32[]{:S(2)}, u32[]{:S(2)}) collective-permute-start(bf16[512,1792]{1,0:T(8,128)(2,1)S(1)} %bitcast.41), channel_id=1, source_target_pairs={{0,8},{8,0},{1,9},{9,1},{2,10},{10,2},{3,11},{11,3},{4,12},{12,4},... | collective-permute-start | bytes 5505032 | tf_op jit(solution)/shard_map/ppermute | solution.py:32
  277.0 5.1 %shard_map.119 = (f32[512,1792]{1,0:T(8,128)}, f32[512,1792]{1,0:T(8,128)}, f32[512,1792]{1,0:T(8,128)}) custom-call(s32[1]{0:T(128)} %bitcast.2.half_ref, bf16[512,512]{1,0:T(8,128)(2,1)S(1)} %bitcast.43, bf16[512,1792]{1,0:T(8,128)(2,1)S(1)} %bitcast.42, f32[512,1792]{1,0:T(8,128)S(1)} %copy-done.1, f32[512,1792]{1,0:T(8,128)} %curve_ref.3), custom_call_target="tpu_custom_call" | custom-call | flops 950000000 | bytes 11000000 | tf_op jit(solution)/shard_map/pallas_call | solution.py:236
  282.1 5.2 %shard_map.120 = (f32[512,1792]{1,0:T(8,128)}, f32[512,1792]{1,0:T(8,128)}, f32[512,1792]{1,0:T(8,128)}) custom-call(s32[1]{0:T(128)} %bitcast.half_ref, bf16[512,512]{1,0:T(8,128)(2,1)S(1)} %bitcast.44, bf16[512,1792]{1,0:T(8,128)(2,1)S(1)} %collective-permute-done.11.cot, ...), custom_call_target="tpu_custom_call", output_to_operand_aliasing={{0}: (5, {}), {1}: (6, {}), {2}: (7, {})} | custom-call | flops 950000000 | bytes 11000000 | tf_op jit(solution)/shard_map/pallas_call | solution.py:236
  (103 shorter events, 39.7 us)
Async XLA Ops:
  0.6 5.7 %copy-start.14 = (s32[32]{0:T(128)S(1)}, s32[32]{0:T(128)}, u32[]{:S(2)}) copy-start(s32[32]{0:T(128)} %param.17) | copy-start | bytes 388
  0.6 5.7 %copy-start.15 = (s32[32]{0:T(128)S(1)}, s32[32]{0:T(128)}, u32[]{:S(2)}) copy-start(s32[32]{0:T(128)} %param.16) | copy-start | bytes 388
  0.7 5.8 %copy-start = (bf16[512,2048]{1,0:T(8,128)(2,1)S(1)}, bf16[512,2048]{1,0:T(8,128)(2,1)}, u32[]{:S(2)}) copy-start(bf16[512,2048]{1,0:T(8,128)(2,1)} %head_far.1) | copy-start | bytes 6291460
  4.9 5.9 %collective-permute-start = (bf16[512,1792]{1,0:T(8,128)(2,1)}, bf16[512,1792]{1,0:T(8,128)(2,1)}, u32[]{:S(2)}, u32[]{:S(2)}) collective-permute-start(bf16[512,1792]{1,0:T(8,128)(2,1)} %shard_map.112), channel_id=1, source_target_pairs={{0,8},{8,0},{1,9},{9,1},{2,10},{10,2},{3,11},{11,3},{4,12},{12,4},... | collective-permute-start | bytes 5505032 | tf_op jit(solution)/shard_map/ppermute | solution.py:32
  6.4 3.2 %collective-permute-start.1 = (s32[32,2]{0,1:T(2,128)S(1)}, s32[32,2]{0,1:T(2,128)S(1)}, u32[]{:S(2)}, u32[]{:S(2)}) collective-permute-start(s32[32,2]{0,1:T(2,128)S(1)} %pad_add_fusion), channel_id=1, source_target_pairs={{0,8},{8,0},{1,9},{9,1},{2,10},{10,2},{3,11},{11,3},{4,12},{12,4},... | collective-permute-start | bytes 776 | tf_op jit(solution)/shard_map/ppermute | solution.py:32
  6.5 1.9 copy-start.13
  15.5 30.1 %all-to-all-start = ((bf16[8,64,1920]{2,1,0:T(8,128)(2,1)}), bf16[8,64,1920]{2,1,0:T(8,128)(2,1)}, u32[]{:S(2)}, u32[]{:S(2)}) async-start(bf16[8,64,1920]{2,1,0:T(8,128)(2,1)} %bitcast.51), calls=%async_computation | async-start | bytes 3932160 | tf_op jit(solution)/shard_map/all_to_all | solution.py:36
  20.7 4.5 %collective-permute-start.2 = (bf16[512,1024]{1,0:T(8,128)(2,1)}, bf16[512,1024]{1,0:T(8,128)(2,1)S(1)}, u32[]{:S(2)}, u32[]{:S(2)}) collective-permute-start(bf16[512,1024]{1,0:T(8,128)(2,1)} %constant_dynamic-slice_fusion.1), channel_id=1, source_target_pairs={{0,8},{8,0},{1,9},{9,1},{2,10},{10,2},{3,11},{11,3},{4,12},{12,4},... | collective-permute-start | bytes 3145736 | tf_op jit(solution)/shard_map/ppermute | solution.py:32
  21.3 3.9 %collective-permute-start.3 = (bf16[896,512]{1,0:T(8,128)(2,1)}, bf16[896,512]{1,0:T(8,128)(2,1)}, u32[]{:S(2)}, u32[]{:S(2)}) collective-permute-start(bf16[896,512]{1,0:T(8,128)(2,1)} %constant_dynamic-slice_fusion), channel_id=1, source_target_pairs={{0,8},{8,0},{1,9},{9,1},{2,10},{10,2},{3,11},{11,3},{4,12},{12,4},... | collective-permute-start | bytes 2752520 | tf_op jit(solution)/shard_map/ppermute | solution.py:32
  25.2 24.3 %copy-start.4 = (bf16[512,1024]{1,0:T(8,128)(2,1)}, bf16[512,1024]{1,0:T(8,128)(2,1)S(1)}, u32[]{:S(2)}) copy-start(bf16[512,1024]{1,0:T(8,128)(2,1)S(1)} %collective-permute-done.2.head_got) | copy-start | bytes 3145732
  48.4 0.9 copy-start.6
  49.5 25.6 %all-to-all-start.1 = ((bf16[8,64,896]{2,1,0:T(8,128)(2,1)}), bf16[8,64,896]{2,1,0:T(8,128)(2,1)}, u32[]{:S(2)}, u32[]{:S(2)}) async-start(bf16[8,64,896]{2,1,0:T(8,128)(2,1)} %copy-done.6), calls=%async_computation.1 | async-start | bytes 1835008 | tf_op jit(solution)/shard_map/all_to_all | solution.py:36
  59.9 13.4 %collective-permute-start.4 = (bf16[2,2,64,1024]{3,2,1,0:T(8,128)(2,1)}, bf16[2,2,64,1024]{3,2,1,0:T(8,128)(2,1)}, u32[]{:S(2)}, u32[]{:S(2)}) collective-permute-start(bf16[2,2,64,1024]{3,2,1,0:T(8,128)(2,1)} %dynamic-slice_bitcast_fusion), channel_id=1, source_target_pairs={{0,2},{2,0},{4,6},{6,4},{1,3},{3,1},{5,7},{7,5},{8,10},{10,8},{12,... | collective-permute-start | bytes 1572872 | tf_op jit(solution)/shard_map/ppermute | solution.py:271
  75.1 3.9 %copy-start.11 = (bf16[896,512]{1,0:T(8,128)(2,1)S(1)}, bf16[896,512]{1,0:T(8,128)(2,1)}, u32[]{:S(2)}) copy-start(bf16[896,512]{1,0:T(8,128)(2,1)} %constant_dynamic-slice_fusion) | copy-start | bytes 2752516
  75.1 3.9 %collective-permute-start.5 = (bf16[512,896]{1,0:T(8,128)(2,1)}, bf16[512,896]{1,0:T(8,128)(2,1)}, u32[]{:S(2)}, u32[]{:S(2)}) collective-permute-start(bf16[512,896]{1,0:T(8,128)(2,1)} %bitcast.12), channel_id=1, source_target_pairs={{0,8},{8,0},{1,9},{9,1},{2,10},{10,2},{3,11},{11,3},{4,12},{12,4},... | collective-permute-start | bytes 2752520 | tf_op jit(solution)/shard_map/ppermute | solution.py:32
  81.7 17.8 %all-to-all-start.2 = ((bf16[8,64,512]{2,1,0:T(8,128)(2,1)}), bf16[8,64,512]{2,1,0:T(8,128)(2,1)S(1)}, u32[]{:S(2)}, u32[]{:S(2)}) async-start(bf16[8,64,512]{2,1,0:T(8,128)(2,1)} %bitcast.54), calls=%async_computation.2 | async-start | bytes 1048576 | tf_op jit(solution)/shard_map/all_to_all | solution.py:36
  114.9 3.6 %collective-permute-start.6 = (bf16[512,512]{1,0:T(8,128)(2,1)S(1)}, bf16[512,512]{1,0:T(8,128)(2,1)S(1)}, u32[]{:S(2)}, u32[]{:S(2)}) collective-permute-start(bf16[512,512]{1,0:T(8,128)(2,1)S(1)} %bitcast.46), channel_id=1, source_target_pairs={{0,8},{8,0},{1,9},{9,1},{2,10},{10,2},{3,11},{11,3},{4,12},{12,4},... | collective-permute-start | bytes 1572872 | tf_op jit(solution)/shard_map/ppermute | solution.py:32
  118.4 1.2 copy-start.5
  121.2 1.0 copy-start.3
  122.2 24.8 %all-to-all-start.4 = ((s16[8,64,1152]{2,1,0:T(8,128)(2,1)}), s16[8,64,1152]{2,1,0:T(8,128)(2,1)S(1)}, u32[]{:S(2)}, u32[]{:S(2)}) async-start(s16[8,64,1152]{2,1,0:T(8,128)(2,1)} %bitcast.45), calls=%async_computation.4 | async-start | bytes 2359296 | tf_op jit(solution)/shard_map/all_to_all | solution.py:36
  128.3 9.0 %collective-permute-start.7 = (bf16[2,64,1024]{2,1,0:T(8,128)(2,1)}, bf16[2,64,1024]{2,1,0:T(8,128)(2,1)}, u32[]{:S(2)}, u32[]{:S(2)}) collective-permute-start(bf16[2,64,1024]{2,1,0:T(8,128)(2,1)} %dynamic-slice_bitcast_fusion.1), channel_id=1, source_target_pairs={{0,4},{4,0},{2,6},{6,2},{1,5},{5,1},{3,7},{7,3},{8,12},{12,8},{10,... | collective-permute-start | bytes 786440 | tf_op jit(solution)/shard_map/ppermute | solution.py:276
  139.8 5.6 %collective-permute-start.8 = (bf16[64,1024]{1,0:T(8,128)(2,1)}, bf16[64,1024]{1,0:T(8,128)(2,1)}, u32[]{:S(2)}, u32[]{:S(2)}) collective-permute-start(bf16[64,1024]{1,0:T(8,128)(2,1)} %dynamic-slice_bitcast_fusion.2), channel_id=1, source_target_pairs={{0,1},{1,0},{2,3},{3,2},{4,5},{5,4},{6,7},{7,6},{8,9},{9,8},{10,11... | collective-permute-start | bytes 393224 | tf_op jit(solution)/shard_map/ppermute | solution.py:278
  148.0 1.0 copy-start.2
  149.0 5.0 %copy-start.7 = (bf16[512,512]{1,0:T(8,128)(2,1)S(1)}, bf16[512,512]{1,0:T(8,128)(2,1)}, u32[]{:S(2)}) copy-start(bf16[512,512]{1,0:T(8,128)(2,1)} %tokens.3) | copy-start | bytes 1572868
  149.0 17.0 %all-to-all-start.5 = ((bf16[8,64,1152]{2,1,0:T(8,128)(2,1)}), bf16[8,64,1152]{2,1,0:T(8,128)(2,1)}, u32[]{:S(2)}, u32[]{:S(2)}) async-start(bf16[8,64,1152]{2,1,0:T(8,128)(2,1)} %copy-done.2), calls=%async_computation.5 | async-start | bytes 2359296 | tf_op jit(solution)/shard_map/all_to_all | solution.py:36
  166.0 15.1 %copy-start.12 = (bf16[64,1024]{1,0:T(8,128)(2,1)S(1)}, bf16[64,1024]{1,0:T(8,128)(2,1)}, u32[]{:S(2)}) copy-start(bf16[64,1024]{1,0:T(8,128)(2,1)} %bitcast_add_fusion.2) | copy-start | bytes 393220
  166.0 7.9 %collective-permute-start.9 = (bf16[512,1152]{1,0:T(8,128)(2,1)}, bf16[512,1152]{1,0:T(8,128)(2,1)S(1)}, u32[]{:S(2)}, u32[]{:S(2)}) collective-permute-start(bf16[512,1152]{1,0:T(8,128)(2,1)} %bitcast.21.own), channel_id=1, source_target_pairs={{0,8},{8,0},{1,9},{9,1},{2,10},{10,2},{3,11},{11,3},{4,12},{12,4},... | collective-permute-start | bytes 3538952 | tf_op jit(solution)/shard_map/ppermute | solution.py:32
  177.4 16.9 %copy-start.9 = (f32[64,512]{1,0:T(8,128)S(1)}, f32[64,512]{1,0:T(8,128)}, u32[]{:S(2)}) copy-start(f32[64,512]{1,0:T(8,128)} %copy-done.8) | copy-start | bytes 393220
  177.4 16.4 %all-to-all-start.6 = ((bf16[8,64,640]{2,1,0:T(8,128)(2,1)}), bf16[8,64,640]{2,1,0:T(8,128)(2,1)S(1)}, u32[]{:S(2)}, u32[]{:S(2)}) async-start(bf16[8,64,640]{2,1,0:T(8,128)(2,1)} %bitcast.22), calls=%async_computation.6 | async-start | bytes 1310720 | tf_op jit(solution)/shard_map/all_to_all | solution.py:36
  213.8 4.2 %collective-permute-start.10 = (bf16[512,1024]{1,0:T(8,128)(2,1)S(1)}, bf16[512,1024]{1,0:T(8,128)(2,1)S(1)}, u32[]{:S(2)}, u32[]{:S(2)}) collective-permute-start(bf16[512,1024]{1,0:T(8,128)(2,1)S(1)} %bitcast.49), channel_id=1, source_target_pairs={{0,8},{8,0},{1,9},{9,1},{2,10},{10,2},{3,11},{11,3},{4,12},{12,4},... | collective-permute-start | bytes 3145736 | tf_op jit(solution)/shard_map/ppermute | solution.py:32
  248.3 28.7 %copy-start.1 = (f32[512,1792]{1,0:T(8,128)S(1)}, f32[512,1792]{1,0:T(8,128)}, u32[]{:S(2)}) copy-start(f32[512,1792]{1,0:T(8,128)} %moment_ref.3) | copy-start | bytes 11010052
  274.1 8.1 %collective-permute-start.11 = (bf16[512,1792]{1,0:T(8,128)(2,1)S(1)}, bf16[512,1792]{1,0:T(8,128)(2,1)S(1)}, u32[]{:S(2)}, u32[]{:S(2)}) collective-permute-start(bf16[512,1792]{1,0:T(8,128)(2,1)S(1)} %bitcast.41), channel_id=1, source_target_pairs={{0,8},{8,0},{1,9},{9,1},{2,10},{10,2},{3,11},{11,3},{4,12},{12,4},... | collective-permute-start | bytes 5505032 | tf_op jit(solution)/shard_map/ppermute | solution.py:32
  (2 other events, 1.4 us)

commit v4 on v3

--- a/solution.py
+++ b/solution.py
@@ -20,12 +20,12 @@
 rho_scale = 0.05
 eps_norm = 1e-05
 
-WIDTH_CHIPS = ("xl", "y")
+WIDTH_CHIPS = ("y", "xl")
 UNIT_CHIPS = ("z", "xh")
 f32 = jnp.float32
 bf16 = jnp.bfloat16
-VMEM_LIMIT = 48 * 1024 * 1024
-FIRST_LIMIT = 60 * 1024 * 1024
+VMEM_LIMIT = 60 * 1024 * 1024
+STEPS = 4
 
 
 def other_core(value):
@@ -70,18 +70,22 @@
     return pl.BlockSpec((count, array.shape[1]), lambda step, half: (half[0], 0))
 
 
-def on_core(kernel, half, operands, specs, outs, flops, limit=VMEM_LIMIT):
+def row_blocks(array):
+    return pl.BlockSpec((array.shape[0] // STEPS,) + array.shape[1:], lambda step, half: (step,) + (0,) * (array.ndim - 1))
+
+
+def on_core(kernel, half, operands, specs, outs, flops, steps=1):
     size = sum(operand.size * operand.dtype.itemsize for operand in operands)
     results = pl.pallas_call(
         kernel,
         out_shape=tuple(jax.ShapeDtypeStruct(shape, dtype) for shape, dtype in outs),
         grid_spec=pltpu.PrefetchScalarGridSpec(
             num_scalar_prefetch=1,
-            grid=(1,),
+            grid=(steps,),
             in_specs=specs,
-            out_specs=tuple(whole(jax.ShapeDtypeStruct(shape, dtype)) for shape, dtype in outs),
+            out_specs=tuple((whole if steps == 1 else row_blocks)(jax.ShapeDtypeStruct(*out)) for out in outs),
         ),
-        compiler_params=pltpu.CompilerParams(vmem_limit_bytes=limit),
+        compiler_params=pltpu.CompilerParams(vmem_limit_bytes=VMEM_LIMIT),
         cost_estimate=pl.CostEstimate(flops=flops, bytes_accessed=size, transcendentals=0),
     )(half.reshape(1), *operands)
     return results if len(outs) > 1 else results[0]
@@ -97,7 +101,7 @@
     out[:, :FF_HALF] = gate_sum.astype(bf16)
     up_sum = dot(tokens[...], up[...]) + got[:, FF_HALF:].astype(f32)
     out[:, FF_HALF : 2 * FF_HALF] = up_sum.astype(bf16)
-    for block in range(CHIPS):
+    for block in range(CHIPS // STEPS):
         out[block * BLOCK : (block + 1) * BLOCK, 2 * FF_HALF :] = labels[...]
 
 
@@ -266,7 +270,10 @@
     for which in range(2):
         hot = (labels[:, which : which + 1] == ids).astype(bf16)
         parts.append(dot_rows(hot, head_weight).astype(bf16))
-    rows = jnp.concatenate(parts, axis=1).reshape(2, 2, 2, BLOCK, -1)
+    return jnp.concatenate(parts, axis=1).reshape(2, 2, 2, BLOCK, -1)
+
+
+def pair_label_rows(rows):
     keep, send = own_part(rows, lax.axis_index("z") % 2, 1)
     return keep + lax.ppermute(send, "z", [(0, 1), (1, 0), (2, 3), (3, 2)])
 
@@ -304,7 +311,7 @@
     digits = jnp.concatenate([labels // PAD, labels % PAD], axis=1).astype(bf16)
     digits = jnp.pad(digits, ((0, 0), (0, PAD - 4)))
 
-    w_specs = [whole(tokens), columns_of(gate_weight, FF_HALF), columns_of(up_weight, FF_HALF)]
+    w_specs = [row_blocks(tokens), columns_of(gate_weight, FF_HALF), columns_of(up_weight, FF_HALF)]
     gate_up_flops = 4 * count * width * FF_HALF
     sent = on_core(
         gate_up_far,
@@ -313,17 +320,17 @@
         w_specs,
         [((count, 2 * FF_HALF), bf16)],
         gate_up_flops,
-        FIRST_LIMIT,
+        STEPS,
     )
     got = other_core(sent)
     both = on_core(
         gate_up_own,
         core,
         (tokens, gate_weight, up_weight, got, digits),
-        w_specs + [whole(got), whole(digits)],
+        w_specs + [row_blocks(got), whole(digits)],
         [((count, 2 * FF_HALF + PAD), bf16)],
         gate_up_flops,
-        FIRST_LIMIT,
+        STEPS,
     )
     head_send = lax.dynamic_slice_in_dim(head_weight, far * V_HALF, V_HALF, 1)
     down_send = lax.dynamic_slice_in_dim(down_weight, far * FF_HALF, FF_HALF, 0)
@@ -341,18 +348,21 @@
         [((CHIPS, BLOCK, FF_HALF), bf16), ((BLOCK, FF_HALF), f32)],
         1000000,
     )
-    digits = both[:, :, 2 * FF_HALF : 2 * FF_HALF + 4].reshape(count, 4)
-
-    hidden, digits = together(hidden, digits)
-    digits = digits.astype(jnp.int32)
-    all_labels = digits[:, :2] * PAD + digits[:, 2:]
-    hidden_own, label_row = together(
-        exchange(hidden, WIDTH_CHIPS), label_rows(all_labels, head_weight, unit_chip)
+
+    hidden, digits = together(hidden, both)
+    digits = digits[:, :, 2 * FF_HALF : 2 * FF_HALF + 4].astype(jnp.int32)
+    all_labels = digits[:, :, :2] * PAD + digits[:, :, 2:]
+    all_labels = all_labels.reshape(4, 2, BLOCK, 2).transpose(1, 0, 2, 3).reshape(count, 2)
+    width_chip = lax.axis_index(WIDTH_CHIPS)
+    hidden_own, label_row, labels, down_own, down_far = together(
+        exchange(hidden, WIDTH_CHIPS),
+        label_rows(all_labels, head_weight, unit_chip),
+        lax.dynamic_slice_in_dim(all_labels, width_chip * BLOCK, BLOCK, 0),
+        lax.dynamic_slice_in_dim(down_weight, core * FF_HALF, FF_HALF, 0),
+        lax.dynamic_slice_in_dim(down_weight, far * FF_HALF, FF_HALF, 0),
     )
     hidden_own = hidden_own.reshape(count, FF_HALF)
     hidden_far = other_core(hidden_own)
-    down_own = lax.dynamic_slice_in_dim(down_weight, core * FF_HALF, FF_HALF, 0)
-    down_far = lax.dynamic_slice_in_dim(down_weight, far * FF_HALF, FF_HALF, 0)
     branch = dot(hidden_own, down_own) + dot(hidden_far, down_far)
     branch = exchange(branch.astype(bf16).reshape(CHIPS, BLOCK, width), UNIT_CHIPS)
     branch = jnp.sum(branch.astype(f32), axis=0)
@@ -372,9 +382,8 @@
     )
     raw, label_row = together(raw, label_row)
     raw, label_row = together(
-        exchange(raw.reshape(CHIPS, BLOCK, V_HALF + PAD), WIDTH_CHIPS), own_label_rows(label_row)
-    )
-    label_row = label_row.astype(f32)
+        exchange(raw.reshape(CHIPS, BLOCK, V_HALF + PAD), WIDTH_CHIPS), pair_label_rows(label_row)
+    )
     vocab_start = ((unit_chip * 2 + core) * V_HALF).astype(jnp.int32)
     packed = on_core(
         softmax_kernel,
@@ -384,8 +393,11 @@
         [((CHIPS, BLOCK, V_HALF + PAD), bf16)],
         1000000,
     )
-    packed, token_rows = together(packed, tokens)
-    packed_own, turned = together(exchange(packed, WIDTH_CHIPS), token_rows.T)
+    packed, token_rows, label_row = together(packed, tokens, label_row)
+    packed_own, turned, label_row = together(
+        exchange(packed, WIDTH_CHIPS), token_rows.T, own_label_rows(label_row)
+    )
+    label_row = label_row.astype(f32)
     packed_own = packed_own.reshape(count, V_HALF + PAD)
     packed_far = other_core(packed_own)
     packed = on_core(
@@ -393,13 +405,14 @@
         core,
         (packed_own, packed_far, head_weight, head_weight),
         [
-            whole(packed_own),
-            whole(packed_far),
+            row_blocks(packed_own),
+            row_blocks(packed_far),
             pl.BlockSpec((width, V_HALF), lambda step, half: (0, half[0])),
             pl.BlockSpec((width, V_HALF), lambda step, half: (0, 1 - half[0])),
         ],
         [((count, width + PAD), bf16)],
         logit_flops,
+        STEPS,
     )
     packed = exchange(packed.reshape(CHIPS, BLOCK, width + PAD), UNIT_CHIPS)
     stats = from_three(packed[:, :, width:], N_STATS)
@@ -424,9 +437,10 @@
         back_kernel,
         core,
         (dsummed, far_dsummed, down_weight, down_got),
-        [whole(dsummed), whole(far_dsummed), rows_of(down_weight, FF_HALF), whole(down_got)],
+        [row_blocks(dsummed), row_blocks(far_dsummed), rows_of(down_weight, FF_HALF), whole(down_got)],
         [((count, 2 * FF_HALF), bf16)],
         2 * gate_up_flops,
+        STEPS,
     )
     dhidden = exchange(dhidden.reshape(CHIPS, BLOCK, 2 * FF_HALF), WIDTH_CHIPS)
     dhidden = jnp.sum(dhidden.astype(f32), axis=0)

time: 289 us -> 292 us (1.010)
  Pallas kernels: 30.8 us -> 47.6 us
  starting transfers between devices: 48.9 us -> 43.6 us
  other arithmetic: 7.49 us -> 3.25 us
  local copies, waits for them, and re-layouts: 15.9 us -> 11.8 us
    pallas_call x7, Pallas kernels: 20.5 us -> 34.3 us  [on_core(): pl.pallas_call(kernel, out_shape=tuple((jax.ShapeDtypeStruct(shape, dtype...]
    squeeze x3, local copies, waits for them, and re-layouts: 3.17 us -> 0.09 us  [own_part(): send = lax.dynamic_index_in_dim(array, 1 - index, axis, keepdims=False)]
    pallas_call x2, Pallas kernels: 10.3 us -> 13.3 us  [sophia_half(): pl.pallas_call(step_kernel, out_shape=(shape, shape, shape), grid_spec=pl...]
    unnamed x33 -> x31, local copies, waits for them, and re-layouts: 6.52 us -> 5.28 us
  transfers between devices with their start and end apart: 18 -> 18, of which waited for: 13 -> 14; matrix products, arithmetic and copies ran while one was open for 7% -> 5% of each run, Pallas kernels for 2% -> 2%
where the time goes in v4:
time: 292 us; the launch traced here: 291 us
  waiting for transfers between devices  90.6 us (31%)
  blocking collectives  86.4 us (30%)
  Pallas kernels  47.6 us (16%)
  starting transfers between devices  43.6 us (15%)
  local copies, waits for them, and re-layouts  11.8 us (4%)
  matrix products  6.41 us (2%)
  other arithmetic  3.25 us (1%)
    all_to_all x4, blocking collectives, exchange(): return lax.all_to_all(blocks, axes, split_axis=0, concat_axis=0, tiled=True)  86.4 us
    all_to_all x6, waiting for transfers between devices, exchange(): return lax.all_to_all(blocks, axes, split_axis=0, concat_axis=0, tiled=True)  53.8 us
    pallas_call x7, Pallas kernels, on_core(): pl.pallas_call(kernel, out_shape=tuple((jax.ShapeDtypeStruct(shape, dtype...  34.3 us
    all_to_all x6, starting transfers between devices, exchange(): return lax.all_to_all(blocks, axes, split_axis=0, concat_axis=0, tiled=True)  27.3 us
    ppermute x9, starting transfers between devices, other_core(): return lax.ppermute(value, 'core', [(0, 1), (1, 0)])  14.6 us
    pallas_call x2, Pallas kernels, sophia_half(): pl.pallas_call(step_kernel, out_shape=(shape, shape, shape), grid_spec=pl...  13.3 us
    ppermute x1, waiting for transfers between devices, pair_label_rows(): return keep + lax.ppermute(send, 'z', [(0, 1), (1, 0), (2, 3), (3, 2)])  13.2 us
    ppermute x9, waiting for transfers between devices, other_core(): return lax.ppermute(value, 'core', [(0, 1), (1, 0)])  10.5 us
  transfers between devices with their start and end apart: 18, of which 14 were waited for; matrix products, arithmetic and copies ran while one was open for 5% of the time, Pallas kernels for 2%

profile of v4, /device:TPU:1, one launch (start us, length us, event | category | flops | bytes accessed | tf_op | source)
XLA Modules:
  0.0 290.7 jit_solution(15250580644142567864)
XLA Ops:
  0.7 4.9 %shard_map.112 = bf16[512,1792]{1,0:T(8,128)(2,1)} custom-call(s32[1]{0:T(128)} %bitcast.half_ref, bf16[512,512]{1,0:T(8,128)(2,1)} %tokens.3, bf16[512,1792]{1,0:T(8,128)(2,1)} %gate.3, bf16[512,1792]{1,0:T(8,128)(2,1)} %up.3), custom_call_target="tpu_custom_call" | custom-call | flops 939524096 | bytes 4194304 | tf_op jit(solution)/shard_map/pallas_call | solution.py:79
  7.1 2.8 constant_dynamic-slice_fusion
  11.1 5.2 %shard_map.113 = bf16[512,1920]{1,0:T(8,128)(2,1)} custom-call(s32[1]{0:T(128)} %bitcast.2.half_ref, bf16[512,512]{1,0:T(8,128)(2,1)} %tokens.3, bf16[512,1792]{1,0:T(8,128)(2,1)} %gate.3, bf16[512,1792]{1,0:T(8,128)(2,1)} %up.3, bf16[512,1792]{1,0:T(8,128)(2,1)} %collective-permute-done.got, bf16[64,128]{1,0:T(8,128)(2,1)} %pad.4.labels), custom_call_target="tpu_custom_call" | custom-call | flops 939524096 | bytes 6045696 | tf_op jit(solution)/shard_map/pallas_call | solution.py:79
  16.3 5.2 %all-to-all-start = ((bf16[8,64,1920]{2,1,0:T(8,128)(2,1)}), bf16[8,64,1920]{2,1,0:T(8,128)(2,1)}, u32[]{:S(2)}, u32[]{:S(2)}) async-start(bf16[8,64,1920]{2,1,0:T(8,128)(2,1)} %bitcast.43), calls=%async_computation | async-start | bytes 3932160 | tf_op jit(solution)/shard_map/all_to_all | solution.py:36
  22.2 3.8 %collective-permute-done.3.down_got = bf16[896,512]{1,0:T(8,128)(2,1)} collective-permute-done((bf16[896,512]{1,0:T(8,128)(2,1)}, bf16[896,512]{1,0:T(8,128)(2,1)}, u32[]{:S(2)}, u32[]{:S(2)}) %collective-permute-start.3) | collective-permute-done | bytes 917536 | tf_op jit(solution)/shard_map/ppermute | solution.py:32
  26.1 20.7 %all-to-all-done.both = bf16[8,64,1920]{2,1,0:T(8,128)(2,1)} async-done(((bf16[8,64,1920]{2,1,0:T(8,128)(2,1)}), bf16[8,64,1920]{2,1,0:T(8,128)(2,1)}, u32[]{:S(2)}, u32[]{:S(2)}) %all-to-all-start) | async-done | bytes 1966112 | tf_op jit(solution)/shard_map/all_to_all | solution.py:36
  46.7 2.8 shard_map.114
  49.6 4.2 %all-to-all-start.1 = ((bf16[8,64,896]{2,1,0:T(8,128)(2,1)}), bf16[8,64,896]{2,1,0:T(8,128)(2,1)}, u32[]{:S(2)}, u32[]{:S(2)}) async-start(bf16[8,64,896]{2,1,0:T(8,128)(2,1)} %get-tuple-element.36), calls=%async_computation.1 | async-start | bytes 1835008 | tf_op jit(solution)/shard_map/all_to_all | solution.py:36
  59.2 7.4 %all-to-all-done.1 = bf16[8,64,896]{2,1,0:T(8,128)(2,1)} async-done(((bf16[8,64,896]{2,1,0:T(8,128)(2,1)}), bf16[8,64,896]{2,1,0:T(8,128)(2,1)}, u32[]{:S(2)}, u32[]{:S(2)}) %all-to-all-start.1) | async-done | bytes 917536 | tf_op jit(solution)/shard_map/all_to_all | solution.py:36
  66.6 2.5 collective-permute-start.4
  72.9 7.2 %all-to-all-start.2 = ((bf16[8,64,512]{2,1,0:T(8,128)(2,1)}), bf16[8,64,512]{2,1,0:T(8,128)(2,1)S(1)}, u32[]{:S(2)}, u32[]{:S(2)}) async-start(bf16[8,64,512]{2,1,0:T(8,128)(2,1)} %bitcast.12), calls=%async_computation.2 | async-start | bytes 1048576 | tf_op jit(solution)/shard_map/all_to_all | solution.py:36
  80.1 10.8 %all-to-all-done.2 = bf16[8,64,512]{2,1,0:T(8,128)(2,1)S(1)} async-done(((bf16[8,64,512]{2,1,0:T(8,128)(2,1)}), bf16[8,64,512]{2,1,0:T(8,128)(2,1)S(1)}, u32[]{:S(2)}, u32[]{:S(2)}) %all-to-all-start.2) | async-done | bytes 524320 | tf_op jit(solution)/shard_map/all_to_all | solution.py:36
  91.0 13.7 %all_to_all.50 = bf16[8,64,512]{2,1,0:T(8,128)(2,1)S(1)} all-to-all(bf16[8,64,512]{2,1,0:T(8,128)(2,1)S(1)} %broadcast_in_dim.6), channel_id=1, replica_groups=mesh['xl'=2,'y'=4,'core'=2,'z'=4,'xh'=2] {'z','xh'}, dimensions={0} | all-to-all | bytes 1048576 | tf_op jit(solution)/shard_map/all_to_all | solution.py:36
  109.1 4.4 %shard_map.115 = s16[512,1152]{1,0:T(8,128)(2,1)} custom-call(s32[1]{0:T(128)} %bitcast.2.half_ref, bf16[512,512]{1,0:T(8,128)(2,1)} %bitcast.57, bf16[512,512]{1,0:T(8,128)(2,1)} %copy-done.10, bf16[512,2048]{1,0:T(8,128)(2,1)} %head_far.1, bf16[512,1024]{1,0:T(8,128)(2,1)} %collective-permute-done.2.head_got), custom_call_target="tpu_custom_call" | custom-call | flops 1073741824 | bytes 4194304 | tf_op jit(solution)/shard_map/pallas_call | solution.py:79
  113.5 3.6 %all-to-all-start.4 = ((s16[8,64,1152]{2,1,0:T(8,128)(2,1)}), s16[8,64,1152]{2,1,0:T(8,128)(2,1)S(1)}, u32[]{:S(2)}, u32[]{:S(2)}) async-start(s16[8,64,1152]{2,1,0:T(8,128)(2,1)} %bitcast.50), calls=%async_computation.4 | async-start | bytes 2359296 | tf_op jit(solution)/shard_map/all_to_all | solution.py:36
  117.3 13.2 %collective-permute-done.6 = bf16[2,2,64,1024]{3,2,1,0:T(8,128)(2,1)} collective-permute-done((bf16[2,2,64,1024]{3,2,1,0:T(8,128)(2,1)S(1)}, bf16[2,2,64,1024]{3,2,1,0:T(8,128)(2,1)}, u32[]{:S(2)}, u32[]{:S(2)}) %collective-permute-start.6) | collective-permute-done | bytes 524320 | tf_op jit(solution)/shard_map/ppermute | solution.py:278
  134.9 3.2 %shard_map.116 = bf16[8,64,1152]{2,1,0:T(8,128)(2,1)} custom-call(s32[1]{0:T(128)} %bitcast.1.start_ref, s16[8,64,1152]{2,1,0:T(8,128)(2,1)} %copy-done.4, s32[64,2]{1,0:T(8,128)} %constant_dynamic-slice_fusion.1.labels), custom_call_target="tpu_custom_call" | custom-call | flops 1000000 | bytes 1180160 | tf_op jit(solution)/shard_map/pallas_call | solution.py:79
  138.1 3.6 %all-to-all-start.5 = ((bf16[8,64,1152]{2,1,0:T(8,128)(2,1)}), bf16[8,64,1152]{2,1,0:T(8,128)(2,1)S(1)}, u32[]{:S(2)}, u32[]{:S(2)}) async-start(bf16[8,64,1152]{2,1,0:T(8,128)(2,1)} %shard_map.116), calls=%async_computation.5 | async-start | bytes 2359296 | tf_op jit(solution)/shard_map/all_to_all | solution.py:36
  142.7 7.3 %collective-permute-done.7 = bf16[2,64,1024]{2,1,0:T(8,128)(2,1)S(1)} collective-permute-done((bf16[2,64,1024]{2,1,0:T(8,128)(2,1)S(1)}, bf16[2,64,1024]{2,1,0:T(8,128)(2,1)S(1)}, u32[]{:S(2)}, u32[]{:S(2)}) %collective-permute-start.7) | collective-permute-done | bytes 262176 | tf_op jit(solution)/shard_map/ppermute | solution.py:283
  151.6 5.8 %collective-permute-done.8 = bf16[64,1024]{1,0:T(8,128)(2,1)S(1)} collective-permute-done((bf16[64,1024]{1,0:T(8,128)(2,1)S(1)}, bf16[64,1024]{1,0:T(8,128)(2,1)S(1)}, u32[]{:S(2)}, u32[]{:S(2)}) %collective-permute-start.8) | collective-permute-done | bytes 131104 | tf_op jit(solution)/shard_map/ppermute | solution.py:285
  157.5 3.6 %collective-permute-start.9 = (bf16[512,1152]{1,0:T(8,128)(2,1)S(1)}, bf16[512,1152]{1,0:T(8,128)(2,1)S(1)}, u32[]{:S(2)}, u32[]{:S(2)}) collective-permute-start(bf16[512,1152]{1,0:T(8,128)(2,1)S(1)} %bitcast.48), channel_id=1, source_target_pairs={{0,8},{8,0},{1,9},{9,1},{2,10},{10,2},{3,11},{11,3},{4,12},{12,4},... | collective-permute-start | bytes 3538952 | tf_op jit(solution)/shard_map/ppermute | solution.py:32
  161.1 2.5 collective-permute-done.9.far
  164.6 6.2 %shard_map.117 = bf16[512,640]{1,0:T(8,128)(2,1)} custom-call(s32[1]{0:T(128)} %bitcast.2.half_ref, bf16[512,1152]{1,0:T(8,128)(2,1)} %bitcast.49, bf16[512,1152]{1,0:T(8,128)(2,1)} %copy-done.7, bf16[512,2048]{1,0:T(8,128)(2,1)} %head_far.1, bf16[512,2048]{1,0:T(8,128)(2,1)} %head_far.1), custom_call_target="tpu_custom_call" | custom-call | flops 1073741824 | bytes 6553600 | tf_op jit(solution)/shard_map/pallas_call | solution.py:79
  170.8 3.5 %all-to-all-start.6 = ((bf16[8,64,640]{2,1,0:T(8,128)(2,1)}), bf16[8,64,640]{2,1,0:T(8,128)(2,1)S(1)}, u32[]{:S(2)}, u32[]{:S(2)}) async-start(bf16[8,64,640]{2,1,0:T(8,128)(2,1)} %bitcast.53), calls=%async_computation.6 | async-start | bytes 1310720 | tf_op jit(solution)/shard_map/all_to_all | solution.py:36
  174.4 12.6 %all-to-all-done.6 = bf16[8,64,640]{2,1,0:T(8,128)(2,1)S(1)} async-done(((bf16[8,64,640]{2,1,0:T(8,128)(2,1)}), bf16[8,64,640]{2,1,0:T(8,128)(2,1)S(1)}, u32[]{:S(2)}, u32[]{:S(2)}) %all-to-all-start.6) | async-done | bytes 655392 | tf_op jit(solution)/shard_map/all_to_all | solution.py:36
  187.9 19.2 %all_to_all.51 = bf16[8,64,1024]{2,1,0:T(8,128)(2,1)S(1)} all-to-all(bf16[8,64,1024]{2,1,0:T(8,128)(2,1)S(1)} %broadcast_in_dim.7), channel_id=1, replica_groups=mesh['xl'=2,'y'=4,'core'=2,'z'=4,'xh'=2] {'z','xh'}, dimensions={0} | all-to-all | bytes 2097152 | tf_op jit(solution)/shard_map/all_to_all | solution.py:36
  212.2 7.5 %shard_map.118 = bf16[512,1792]{1,0:T(8,128)(2,1)} custom-call(s32[1]{0:T(128)} %bitcast.2.half_ref, bf16[512,1024]{1,0:T(8,128)(2,1)} %bitcast.61, bf16[512,1024]{1,0:T(8,128)(2,1)} %copy-done.14, bf16[1792,512]{1,0:T(8,128)(2,1)} %down.1, bf16[896,512]{1,0:T(8,128)(2,1)} %collective-permute-done.3.down_got), custom_call_target="tpu_custom_call" | custom-call | flops 1879048192 | bytes 4849664 | tf_op jit(solution)/shard_map/pallas_call | solution.py:79
  219.7 27.9 %all_to_all.52 = bf16[8,64,1792]{2,1,0:T(8,128)(2,1)S(1)} all-to-all(bf16[8,64,1792]{2,1,0:T(8,128)(2,1)} %bitcast.58), channel_id=1, replica_groups=mesh['xl'=2,'y'=4,'core'=2,'z'=4,'xh'=2] {'y','xl'}, dimensions={0} | all-to-all | bytes 3670016 | tf_op jit(solution)/shard_map/all_to_all | solution.py:36
  248.1 25.6 %all_to_all.53 = bf16[8,64,1792]{2,1,0:T(8,128)(2,1)S(1)} all-to-all(bf16[8,64,1792]{2,1,0:T(8,128)(2,1)S(1)} %broadcast_in_dim.8), channel_id=1, replica_groups=mesh['xl'=2,'y'=4,'core'=2,'z'=4,'xh'=2] {'y','xl'}, dimensions={0} | all-to-all | bytes 3670016 | tf_op jit(solution)/shard_map/all_to_all | solution.py:36
  273.7 2.4 collective-permute-start.11
  276.1 6.7 %shard_map.119 = (f32[512,1792]{1,0:T(8,128)}, f32[512,1792]{1,0:T(8,128)}, f32[512,1792]{1,0:T(8,128)}) custom-call(s32[1]{0:T(128)} %bitcast.2.half_ref, bf16[512,512]{1,0:T(8,128)(2,1)} %bitcast.46, bf16[512,1792]{1,0:T(8,128)(2,1)} %bitcast.45, f32[512,1792]{1,0:T(8,128)} %moment_ref.3, f32[512,1792]{1,0:T(8,128)} %curve_ref.3), custom_call_target="tpu_custom_call" | custom-call | flops 950000000 | bytes 11000000 | tf_op jit(solution)/shard_map/pallas_call | solution.py:240
  284.0 6.6 %shard_map.120 = (f32[512,1792]{1,0:T(8,128)}, f32[512,1792]{1,0:T(8,128)}, f32[512,1792]{1,0:T(8,128)}) custom-call(s32[1]{0:T(128)} %bitcast.half_ref, bf16[512,512]{1,0:T(8,128)(2,1)} %bitcast.47, bf16[512,1792]{1,0:T(8,128)(2,1)} %copy-done.6, f32[512,1792]{1,0:T(8,128)} %moment_ref.3, ...), custom_call_target="tpu_custom_call", output_to_operand_aliasing={{0}: (5, {}), {1}: (6, {}), {2}: (7, {})} | custom-call | flops 950000000 | bytes 11000000 | tf_op jit(solution)/shard_map/pallas_call | solution.py:240
  (94 shorter events, 33.0 us)
Async XLA Ops:
  0.6 6.4 %copy-start.12 = (s32[32]{0:T(128)S(1)}, s32[32]{0:T(128)}, u32[]{:S(2)}) copy-start(s32[32]{0:T(128)} %param.17) | copy-start | bytes 388
  0.6 6.4 %copy-start.13 = (s32[32]{0:T(128)S(1)}, s32[32]{0:T(128)}, u32[]{:S(2)}) copy-start(s32[32]{0:T(128)} %param.16) | copy-start | bytes 388
  5.6 4.4 %copy-start = (bf16[512,2048]{1,0:T(8,128)(2,1)S(1)}, bf16[512,2048]{1,0:T(8,128)(2,1)}, u32[]{:S(2)}) copy-start(bf16[512,2048]{1,0:T(8,128)(2,1)} %head_far.1) | copy-start | bytes 6291460
  5.6 5.5 %collective-permute-start = (bf16[512,1792]{1,0:T(8,128)(2,1)}, bf16[512,1792]{1,0:T(8,128)(2,1)}, u32[]{:S(2)}, u32[]{:S(2)}) collective-permute-start(bf16[512,1792]{1,0:T(8,128)(2,1)} %shard_map.112), channel_id=1, source_target_pairs={{0,8},{8,0},{1,9},{9,1},{2,10},{10,2},{3,11},{11,3},{4,12},{12,4},... | collective-permute-start | bytes 5505032 | tf_op jit(solution)/shard_map/ppermute | solution.py:32
  7.0 3.2 %collective-permute-start.1 = (s32[32,2]{0,1:T(2,128)S(1)}, s32[32,2]{0,1:T(2,128)S(1)}, u32[]{:S(2)}, u32[]{:S(2)}) collective-permute-start(s32[32,2]{0,1:T(2,128)S(1)} %pad_add_fusion), channel_id=1, source_target_pairs={{0,8},{8,0},{1,9},{9,1},{2,10},{10,2},{3,11},{11,3},{4,12},{12,4},... | collective-permute-start | bytes 776 | tf_op jit(solution)/shard_map/ppermute | solution.py:32
  16.3 30.4 %all-to-all-start = ((bf16[8,64,1920]{2,1,0:T(8,128)(2,1)}), bf16[8,64,1920]{2,1,0:T(8,128)(2,1)}, u32[]{:S(2)}, u32[]{:S(2)}) async-start(bf16[8,64,1920]{2,1,0:T(8,128)(2,1)} %bitcast.43), calls=%async_computation | async-start | bytes 3932160 | tf_op jit(solution)/shard_map/all_to_all | solution.py:36
  21.5 4.5 %collective-permute-start.2 = (bf16[512,1024]{1,0:T(8,128)(2,1)S(1)}, bf16[512,1024]{1,0:T(8,128)(2,1)}, u32[]{:S(2)}, u32[]{:S(2)}) collective-permute-start(bf16[512,1024]{1,0:T(8,128)(2,1)S(1)} %constant_dynamic-slice_fusion.3), channel_id=1, source_target_pairs={{0,8},{8,0},{1,9},{9,1},{2,10},{10,2},{3,11},{11,3},{4,12},{12,4},... | collective-permute-start | bytes 3145736 | tf_op jit(solution)/shard_map/ppermute | solution.py:32
  22.1 3.9 %collective-permute-start.3 = (bf16[896,512]{1,0:T(8,128)(2,1)}, bf16[896,512]{1,0:T(8,128)(2,1)}, u32[]{:S(2)}, u32[]{:S(2)}) collective-permute-start(bf16[896,512]{1,0:T(8,128)(2,1)} %get-tuple-element.40), channel_id=1, source_target_pairs={{0,8},{8,0},{1,9},{9,1},{2,10},{10,2},{3,11},{11,3},{4,12},{12,4},... | collective-permute-start | bytes 2752520 | tf_op jit(solution)/shard_map/ppermute | solution.py:32
  49.6 17.1 %all-to-all-start.1 = ((bf16[8,64,896]{2,1,0:T(8,128)(2,1)}), bf16[8,64,896]{2,1,0:T(8,128)(2,1)}, u32[]{:S(2)}, u32[]{:S(2)}) async-start(bf16[8,64,896]{2,1,0:T(8,128)(2,1)} %get-tuple-element.36), calls=%async_computation.1 | async-start | bytes 1835008 | tf_op jit(solution)/shard_map/all_to_all | solution.py:36
  58.6 12.8 %copy-start.9 = (bf16[896,512]{1,0:T(8,128)(2,1)S(1)}, bf16[896,512]{1,0:T(8,128)(2,1)}, u32[]{:S(2)}) copy-start(bf16[896,512]{1,0:T(8,128)(2,1)} %get-tuple-element.40) | copy-start | bytes 2752516
  66.6 4.8 %collective-permute-start.4 = (bf16[512,896]{1,0:T(8,128)(2,1)}, bf16[512,896]{1,0:T(8,128)(2,1)S(1)}, u32[]{:S(2)}, u32[]{:S(2)}) collective-permute-start(bf16[512,896]{1,0:T(8,128)(2,1)} %bitcast.11), channel_id=1, source_target_pairs={{0,8},{8,0},{1,9},{9,1},{2,10},{10,2},{3,11},{11,3},{4,12},{12,4},... | collective-permute-start | bytes 2752520 | tf_op jit(solution)/shard_map/ppermute | solution.py:32
  71.2 19.7 %copy-start.2 = (bf16[512,512]{1,0:T(8,128)(2,1)S(1)}, bf16[512,512]{1,0:T(8,128)(2,1)}, u32[]{:S(2)}) copy-start(bf16[512,512]{1,0:T(8,128)(2,1)} %tokens.3) | copy-start | bytes 1572868
  72.9 18.0 %all-to-all-start.2 = ((bf16[8,64,512]{2,1,0:T(8,128)(2,1)}), bf16[8,64,512]{2,1,0:T(8,128)(2,1)S(1)}, u32[]{:S(2)}, u32[]{:S(2)}) async-start(bf16[8,64,512]{2,1,0:T(8,128)(2,1)} %bitcast.12), calls=%async_computation.2 | async-start | bytes 1048576 | tf_op jit(solution)/shard_map/all_to_all | solution.py:36
  104.7 3.6 %copy-start.5 = (bf16[8,64,512]{2,1,0:T(8,128)(2,1)}, bf16[8,64,512]{2,1,0:T(8,128)(2,1)S(1)}, u32[]{:S(2)}) copy-start(bf16[8,64,512]{2,1,0:T(8,128)(2,1)S(1)} %all_to_all.50) | copy-start | bytes 1572868
  104.7 3.6 %collective-permute-start.5 = (bf16[512,512]{1,0:T(8,128)(2,1)S(1)}, bf16[512,512]{1,0:T(8,128)(2,1)S(1)}, u32[]{:S(2)}, u32[]{:S(2)}) collective-permute-start(bf16[512,512]{1,0:T(8,128)(2,1)S(1)} %bitcast.56), channel_id=1, source_target_pairs={{0,8},{8,0},{1,9},{9,1},{2,10},{10,2},{3,11},{11,3},{4,12},{12,4},... | collective-permute-start | bytes 1572872 | tf_op jit(solution)/shard_map/ppermute | solution.py:32
  113.5 20.4 %all-to-all-start.4 = ((s16[8,64,1152]{2,1,0:T(8,128)(2,1)}), s16[8,64,1152]{2,1,0:T(8,128)(2,1)S(1)}, u32[]{:S(2)}, u32[]{:S(2)}) async-start(s16[8,64,1152]{2,1,0:T(8,128)(2,1)} %bitcast.50), calls=%async_computation.4 | async-start | bytes 2359296 | tf_op jit(solution)/shard_map/all_to_all | solution.py:36
  117.2 13.3 %collective-permute-start.6 = (bf16[2,2,64,1024]{3,2,1,0:T(8,128)(2,1)S(1)}, bf16[2,2,64,1024]{3,2,1,0:T(8,128)(2,1)}, u32[]{:S(2)}, u32[]{:S(2)}) collective-permute-start(bf16[2,2,64,1024]{3,2,1,0:T(8,128)(2,1)S(1)} %dynamic-slice_bitcast_fusion), channel_id=1, source_target_pairs={{0,2},{2,0},{4,6},{6,4},{1,3},{3,1},{5,7},{7,5},{8,10},{10,8},{12,... | collective-permute-start | bytes 1572872 | tf_op jit(solution)/shard_map/ppermute | solution.py:278
  133.9 1.0 copy-start.4
  138.1 19.3 %all-to-all-start.5 = ((bf16[8,64,1152]{2,1,0:T(8,128)(2,1)}), bf16[8,64,1152]{2,1,0:T(8,128)(2,1)S(1)}, u32[]{:S(2)}, u32[]{:S(2)}) async-start(bf16[8,64,1152]{2,1,0:T(8,128)(2,1)} %shard_map.116), calls=%async_computation.5 | async-start | bytes 2359296 | tf_op jit(solution)/shard_map/all_to_all | solution.py:36
  141.7 8.2 %collective-permute-start.7 = (bf16[2,64,1024]{2,1,0:T(8,128)(2,1)S(1)}, bf16[2,64,1024]{2,1,0:T(8,128)(2,1)S(1)}, u32[]{:S(2)}, u32[]{:S(2)}) collective-permute-start(bf16[2,64,1024]{2,1,0:T(8,128)(2,1)S(1)} %dynamic-slice_bitcast_fusion.1), channel_id=1, source_target_pairs={{0,4},{4,0},{2,6},{6,2},{1,5},{5,1},{3,7},{7,3},{8,12},{12,8},{10,... | collective-permute-start | bytes 786440 | tf_op jit(solution)/shard_map/ppermute | solution.py:283
  150.0 7.5 %collective-permute-start.8 = (bf16[64,1024]{1,0:T(8,128)(2,1)S(1)}, bf16[64,1024]{1,0:T(8,128)(2,1)S(1)}, u32[]{:S(2)}, u32[]{:S(2)}) collective-permute-start(bf16[64,1024]{1,0:T(8,128)(2,1)S(1)} %dynamic-slice_bitcast_fusion.2), channel_id=1, source_target_pairs={{0,1},{1,0},{2,3},{3,2},{4,5},{5,4},{6,7},{7,6},{8,9},{9,8},{10,11... | collective-permute-start | bytes 393224 | tf_op jit(solution)/shard_map/ppermute | solution.py:285
  157.5 6.1 %copy-start.3 = (bf16[8,64,1152]{2,1,0:T(8,128)(2,1)}, bf16[8,64,1152]{2,1,0:T(8,128)(2,1)S(1)}, u32[]{:S(2)}) copy-start(bf16[8,64,1152]{2,1,0:T(8,128)(2,1)S(1)} %all-to-all-done.5) | copy-start | bytes 3538948
  157.5 6.1 %collective-permute-start.9 = (bf16[512,1152]{1,0:T(8,128)(2,1)S(1)}, bf16[512,1152]{1,0:T(8,128)(2,1)S(1)}, u32[]{:S(2)}, u32[]{:S(2)}) collective-permute-start(bf16[512,1152]{1,0:T(8,128)(2,1)S(1)} %bitcast.48), channel_id=1, source_target_pairs={{0,8},{8,0},{1,9},{9,1},{2,10},{10,2},{3,11},{11,3},{4,12},{12,4},... | collective-permute-start | bytes 3538952 | tf_op jit(solution)/shard_map/ppermute | solution.py:32
  163.6 1.0 copy-start.7
  170.8 16.2 %all-to-all-start.6 = ((bf16[8,64,640]{2,1,0:T(8,128)(2,1)}), bf16[8,64,640]{2,1,0:T(8,128)(2,1)S(1)}, u32[]{:S(2)}, u32[]{:S(2)}) async-start(bf16[8,64,640]{2,1,0:T(8,128)(2,1)} %bitcast.53), calls=%async_computation.6 | async-start | bytes 1310720 | tf_op jit(solution)/shard_map/all_to_all | solution.py:36
  207.1 4.2 %copy-start.8 = (bf16[8,64,1024]{2,1,0:T(8,128)(2,1)}, bf16[8,64,1024]{2,1,0:T(8,128)(2,1)S(1)}, u32[]{:S(2)}) copy-start(bf16[8,64,1024]{2,1,0:T(8,128)(2,1)S(1)} %all_to_all.51) | copy-start | bytes 3145732
  207.1 4.2 %collective-permute-start.10 = (bf16[512,1024]{1,0:T(8,128)(2,1)S(1)}, bf16[512,1024]{1,0:T(8,128)(2,1)S(1)}, u32[]{:S(2)}, u32[]{:S(2)}) collective-permute-start(bf16[512,1024]{1,0:T(8,128)(2,1)S(1)} %bitcast.60), channel_id=1, source_target_pairs={{0,8},{8,0},{1,9},{9,1},{2,10},{10,2},{3,11},{11,3},{4,12},{12,4},... | collective-permute-start | bytes 3145736 | tf_op jit(solution)/shard_map/ppermute | solution.py:32
  211.3 1.0 copy-start.14
  219.7 28.2 %copy-start.11 = (f32[64,896]{1,0:T(8,128)S(1)}, f32[64,896]{1,0:T(8,128)}, u32[]{:S(2)}) copy-start(f32[64,896]{1,0:T(8,128)} %get-tuple-element.55) | copy-start | bytes 688132
  273.7 2.4 copy-start.1
  273.7 9.1 %collective-permute-start.11 = (bf16[512,1792]{1,0:T(8,128)(2,1)S(1)}, bf16[512,1792]{1,0:T(8,128)(2,1)S(1)}, u32[]{:S(2)}, u32[]{:S(2)}) collective-permute-start(bf16[512,1792]{1,0:T(8,128)(2,1)S(1)} %bitcast.44), channel_id=1, source_target_pairs={{0,8},{8,0},{1,9},{9,1},{2,10},{10,2},{3,11},{11,3},{4,12},{12,4},... | collective-permute-start | bytes 5505032 | tf_op jit(solution)/shard_map/ppermute | solution.py:32
  282.8 1.3 copy-start.6
  (1 other events, 0.8 us)

commit v5 on v4

--- a/solution.py
+++ b/solution.py
@@ -24,8 +24,7 @@
 UNIT_CHIPS = ("z", "xh")
 f32 = jnp.float32
 bf16 = jnp.bfloat16
-VMEM_LIMIT = 60 * 1024 * 1024
-STEPS = 4
+VMEM_LIMIT = 24 * 1024 * 1024
 
 
 def other_core(value):
@@ -70,20 +69,16 @@
     return pl.BlockSpec((count, array.shape[1]), lambda step, half: (half[0], 0))
 
 
-def row_blocks(array):
-    return pl.BlockSpec((array.shape[0] // STEPS,) + array.shape[1:], lambda step, half: (step,) + (0,) * (array.ndim - 1))
-
-
-def on_core(kernel, half, operands, specs, outs, flops, steps=1):
+def on_core(kernel, half, operands, specs, outs, flops):
     size = sum(operand.size * operand.dtype.itemsize for operand in operands)
     results = pl.pallas_call(
         kernel,
         out_shape=tuple(jax.ShapeDtypeStruct(shape, dtype) for shape, dtype in outs),
         grid_spec=pltpu.PrefetchScalarGridSpec(
             num_scalar_prefetch=1,
-            grid=(steps,),
+            grid=(1,),
             in_specs=specs,
-            out_specs=tuple((whole if steps == 1 else row_blocks)(jax.ShapeDtypeStruct(*out)) for out in outs),
+            out_specs=tuple(whole(jax.ShapeDtypeStruct(*out)) for out in outs),
         ),
         compiler_params=pltpu.CompilerParams(vmem_limit_bytes=VMEM_LIMIT),
         cost_estimate=pl.CostEstimate(flops=flops, bytes_accessed=size, transcendentals=0),
@@ -91,17 +86,12 @@
     return results if len(outs) > 1 else results[0]
 
 
-def gate_up_far(half_ref, tokens, gate, up, out):
-    out[:, :FF_HALF] = dot(tokens[...], gate[...]).astype(bf16)
-    out[:, FF_HALF:] = dot(tokens[...], up[...]).astype(bf16)
-
-
-def gate_up_own(half_ref, tokens, gate, up, got, labels, out):
-    gate_sum = dot(tokens[...], gate[...]) + got[:, :FF_HALF].astype(f32)
+def gate_up_own(half_ref, tokens, gate, up, got_gate, got_up, labels, out):
+    gate_sum = dot(tokens[...], gate[...]) + got_gate[...].astype(f32)
     out[:, :FF_HALF] = gate_sum.astype(bf16)
-    up_sum = dot(tokens[...], up[...]) + got[:, FF_HALF:].astype(f32)
+    up_sum = dot(tokens[...], up[...]) + got_up[...].astype(f32)
     out[:, FF_HALF : 2 * FF_HALF] = up_sum.astype(bf16)
-    for block in range(CHIPS // STEPS):
+    for block in range(CHIPS):
         out[block * BLOCK : (block + 1) * BLOCK, 2 * FF_HALF :] = labels[...]
 
 
@@ -311,26 +301,19 @@
     digits = jnp.concatenate([labels // PAD, labels % PAD], axis=1).astype(bf16)
     digits = jnp.pad(digits, ((0, 0), (0, PAD - 4)))
 
-    w_specs = [row_blocks(tokens), columns_of(gate_weight, FF_HALF), columns_of(up_weight, FF_HALF)]
+    w_specs = [whole(tokens), columns_of(gate_weight, FF_HALF), columns_of(up_weight, FF_HALF)]
     gate_up_flops = 4 * count * width * FF_HALF
-    sent = on_core(
-        gate_up_far,
-        far,
-        (tokens, gate_weight, up_weight),
-        w_specs,
-        [((count, 2 * FF_HALF), bf16)],
-        gate_up_flops,
-        STEPS,
-    )
-    got = other_core(sent)
+    far_gate = lax.dynamic_slice_in_dim(gate_weight, far * FF_HALF, FF_HALF, 1)
+    far_up = lax.dynamic_slice_in_dim(up_weight, far * FF_HALF, FF_HALF, 1)
+    got_gate = other_core(dot(tokens, far_gate).astype(bf16))
+    got_up = other_core(dot(tokens, far_up).astype(bf16))
     both = on_core(
         gate_up_own,
         core,
-        (tokens, gate_weight, up_weight, got, digits),
-        w_specs + [row_blocks(got), whole(digits)],
+        (tokens, gate_weight, up_weight, got_gate, got_up, digits),
+        w_specs + [whole(got_gate), whole(got_up), whole(digits)],
         [((count, 2 * FF_HALF + PAD), bf16)],
         gate_up_flops,
-        STEPS,
     )
     head_send = lax.dynamic_slice_in_dim(head_weight, far * V_HALF, V_HALF, 1)
     down_send = lax.dynamic_slice_in_dim(down_weight, far * FF_HALF, FF_HALF, 0)
@@ -405,14 +388,13 @@
         core,
         (packed_own, packed_far, head_weight, head_weight),
         [
-            row_blocks(packed_own),
-            row_blocks(packed_far),
+            whole(packed_own),
+            whole(packed_far),
             pl.BlockSpec((width, V_HALF), lambda step, half: (0, half[0])),
             pl.BlockSpec((width, V_HALF), lambda step, half: (0, 1 - half[0])),
         ],
         [((count, width + PAD), bf16)],
         logit_flops,
-        STEPS,
     )
     packed = exchange(packed.reshape(CHIPS, BLOCK, width + PAD), UNIT_CHIPS)
     stats = from_three(packed[:, :, width:], N_STATS)
@@ -437,10 +419,9 @@
         back_kernel,
         core,
         (dsummed, far_dsummed, down_weight, down_got),
-        [row_blocks(dsummed), row_blocks(far_dsummed), rows_of(down_weight, FF_HALF), whole(down_got)],
+        [whole(dsummed), whole(far_dsummed), rows_of(down_weight, FF_HALF), whole(down_got)],
         [((count, 2 * FF_HALF), bf16)],
         2 * gate_up_flops,
-        STEPS,
     )
     dhidden = exchange(dhidden.reshape(CHIPS, BLOCK, 2 * FF_HALF), WIDTH_CHIPS)
     dhidden = jnp.sum(dhidden.astype(f32), axis=0)

time: 292 us -> 280 us (0.959)
  Pallas kernels: 47.6 us -> 21.6 us
  local copies, waits for them, and re-layouts: 11.8 us -> 20.1 us
  waiting for transfers between devices: 90.6 us -> 84.2 us
  other arithmetic: 3.25 us -> 9.17 us
  matrix products: 6.41 us -> 11.2 us
    pallas_call x7 -> x6, Pallas kernels: 34.3 us -> 14.1 us  [on_core(): pl.pallas_call(kernel, out_shape=tuple((jax.ShapeDtypeStruct(shape, dtype...]
    pallas_call x2, Pallas kernels: 13.3 us -> 7.5 us  [sophia_half(): pl.pallas_call(step_kernel, out_shape=(shape, shape, shape), grid_spec=pl...]
    all_to_all x6, waiting for transfers between devices: 53.8 us -> 48.3 us  [exchange(): return lax.all_to_all(blocks, axes, split_axis=0, concat_axis=0, tiled=True)]
    dot_general x2 -> x4, matrix products: 3.66 us -> 8.42 us  [dot(): return jnp.dot(left, right, preferred_element_type=f32)]
    unnamed x31 -> x45, local copies, waits for them, and re-layouts: 5.28 us -> 9.01 us
    squeeze x3, local copies, waits for them, and re-layouts: 0.09 us -> 3.27 us  [own_part(): send = lax.dynamic_index_in_dim(array, 1 - index, axis, keepdims=False)]
    ppermute x9 -> x10, waiting for transfers between devices: 10.5 us -> 10.3 us  [other_core(): return lax.ppermute(value, 'core', [(0, 1), (1, 0)])]
    ppermute x9 -> x10, starting transfers between devices: 14.6 us -> 14.7 us  [other_core(): return lax.ppermute(value, 'core', [(0, 1), (1, 0)])]
  transfers between devices with their start and end apart: 18 -> 19, of which waited for: 14 -> 12; matrix products, arithmetic and copies ran while one was open for 5% -> 9% of each run, Pallas kernels for 2% -> 1%
where the time goes in v5:
time: 280 us; the launch traced here: 279 us
  blocking collectives  87.1 us (31%)
  waiting for transfers between devices  84.2 us (30%)
  starting transfers between devices  44.9 us (16%)
  Pallas kernels  21.6 us (8%)
  local copies, waits for them, and re-layouts  20.1 us (7%)
  matrix products  11.2 us (4%)
  other arithmetic  9.17 us (3%)
    all_to_all x4, blocking collectives, exchange(): return lax.all_to_all(blocks, axes, split_axis=0, concat_axis=0, tiled=True)  87.1 us
    all_to_all x6, waiting for transfers between devices, exchange(): return lax.all_to_all(blocks, axes, split_axis=0, concat_axis=0, tiled=True)  48.3 us
    all_to_all x6, starting transfers between devices, exchange(): return lax.all_to_all(blocks, axes, split_axis=0, concat_axis=0, tiled=True)  28.7 us
    ppermute x10, starting transfers between devices, other_core(): return lax.ppermute(value, 'core', [(0, 1), (1, 0)])  14.7 us
    pallas_call x6, Pallas kernels, on_core(): pl.pallas_call(kernel, out_shape=tuple((jax.ShapeDtypeStruct(shape, dtype...  14.1 us
    ppermute x1, waiting for transfers between devices, pair_label_rows(): return keep + lax.ppermute(send, 'z', [(0, 1), (1, 0), (2, 3), (3, 2)])  13.4 us
    ppermute x10, waiting for transfers between devices, other_core(): return lax.ppermute(value, 'core', [(0, 1), (1, 0)])  10.3 us
    unnamed x45, local copies, waits for them, and re-layouts  9.01 us
  transfers between devices with their start and end apart: 19, of which 12 were waited for; matrix products, arithmetic and copies ran while one was open for 9% of the time, Pallas kernels for 1%

profile of v5, /device:TPU:1, one launch (start us, length us, event | category | flops | bytes accessed | tf_op | source)
XLA Modules:
  0.0 279.3 jit_solution(325172216088866598)
XLA Ops:
  0.7 3.1 %fusion.9 = bf16[512,896]{1,0:T(8,128)(2,1)} fusion(bf16[512,512]{1,0:T(8,128)(2,1)} %tokens.1, bf16[512,1792]{1,0:T(8,128)(2,1)} %up.1, s32[]{:T(128)S(6)} %select_n.70), kind=kOutput, calls=%fused_computation.13 | convolution fusion | flops 470220800 | bytes 2359300 | tf_op jit(solution)/shard_map/dot_general | solution.py:48
  7.5 2.8 %constant_dynamic-slice_fusion = (bf16[896,512]{1,0:T(8,128)(2,1)}, bf16[896,512]{1,0:T(8,128)(2,1)}) fusion(bf16[1792,512]{1,0:T(8,128)(2,1)} %down.1, s32[]{:T(128)S(6)} %select_n.77, s32[]{:T(128)S(6)} %select_n.70), kind=kLoop, calls=%fused_computation.64 | loop fusion | bytes 3670024 | tf_op jit(solution)/shard_map/dynamic_slice | solution.py:344
  15.9 2.6 shard_map.112
  19.8 5.2 %all-to-all-start = ((bf16[8,64,1920]{2,1,0:T(8,128)(2,1)}), bf16[8,64,1920]{2,1,0:T(8,128)(2,1)}, u32[]{:S(2)}, u32[]{:S(2)}) async-start(bf16[8,64,1920]{2,1,0:T(8,128)(2,1)} %bitcast.49), calls=%async_computation | async-start | bytes 3932160 | tf_op jit(solution)/shard_map/all_to_all | solution.py:35
  25.5 3.7 %collective-permute-done.4.down_got = bf16[896,512]{1,0:T(8,128)(2,1)S(1)} collective-permute-done((bf16[896,512]{1,0:T(8,128)(2,1)}, bf16[896,512]{1,0:T(8,128)(2,1)S(1)}, u32[]{:S(2)}, u32[]{:S(2)}) %collective-permute-start.4) | collective-permute-done | bytes 917536 | tf_op jit(solution)/shard_map/ppermute | solution.py:31
  30.1 20.4 %all-to-all-done.both = bf16[8,64,1920]{2,1,0:T(8,128)(2,1)} async-done(((bf16[8,64,1920]{2,1,0:T(8,128)(2,1)}), bf16[8,64,1920]{2,1,0:T(8,128)(2,1)}, u32[]{:S(2)}, u32[]{:S(2)}) %all-to-all-start) | async-done | bytes 1966112 | tf_op jit(solution)/shard_map/all_to_all | solution.py:35
  50.5 2.8 shard_map.113
  53.2 4.2 %all-to-all-start.1 = ((bf16[8,64,896]{2,1,0:T(8,128)(2,1)}), bf16[8,64,896]{2,1,0:T(8,128)(2,1)}, u32[]{:S(2)}, u32[]{:S(2)}) async-start(bf16[8,64,896]{2,1,0:T(8,128)(2,1)} %get-tuple-element.36), calls=%async_computation.1 | async-start | bytes 1835008 | tf_op jit(solution)/shard_map/all_to_all | solution.py:35
  65.0 5.4 %all-to-all-done.1 = bf16[8,64,896]{2,1,0:T(8,128)(2,1)} async-done(((bf16[8,64,896]{2,1,0:T(8,128)(2,1)}), bf16[8,64,896]{2,1,0:T(8,128)(2,1)}, u32[]{:S(2)}, u32[]{:S(2)}) %all-to-all-start.1) | async-done | bytes 917536 | tf_op jit(solution)/shard_map/all_to_all | solution.py:35
  70.4 2.3 collective-permute-start.5
  76.6 7.2 %all-to-all-start.2 = ((bf16[8,64,512]{2,1,0:T(8,128)(2,1)}), bf16[8,64,512]{2,1,0:T(8,128)(2,1)S(1)}, u32[]{:S(2)}, u32[]{:S(2)}) async-start(bf16[8,64,512]{2,1,0:T(8,128)(2,1)} %bitcast.66), calls=%async_computation.2 | async-start | bytes 1048576 | tf_op jit(solution)/shard_map/all_to_all | solution.py:35
  83.8 10.8 %all-to-all-done.2 = bf16[8,64,512]{2,1,0:T(8,128)(2,1)S(1)} async-done(((bf16[8,64,512]{2,1,0:T(8,128)(2,1)}), bf16[8,64,512]{2,1,0:T(8,128)(2,1)S(1)}, u32[]{:S(2)}, u32[]{:S(2)}) %all-to-all-start.2) | async-done | bytes 524320 | tf_op jit(solution)/shard_map/all_to_all | solution.py:35
  94.7 13.7 %all_to_all.50 = bf16[8,64,512]{2,1,0:T(8,128)(2,1)S(1)} all-to-all(bf16[8,64,512]{2,1,0:T(8,128)(2,1)S(1)} %broadcast_in_dim.6), channel_id=1, replica_groups=mesh['xl'=2,'y'=4,'core'=2,'z'=4,'xh'=2] {'z','xh'}, dimensions={0} | all-to-all | bytes 1048576 | tf_op jit(solution)/shard_map/all_to_all | solution.py:35
  112.0 2.8 %shard_map.114 = s16[512,1152]{1,0:T(8,128)(2,1)S(1)} custom-call(s32[1]{0:T(128)} %bitcast.2.half_ref, bf16[512,512]{1,0:T(8,128)(2,1)S(1)} %bitcast.57, bf16[512,512]{1,0:T(8,128)(2,1)S(1)} %collective-permute-done.6.far_rows, bf16[512,2048]{1,0:T(8,128)(2,1)S(1)} %copy-done, bf16[512,1024]{1,0:T(8,128)(2,1)} %collective-permute-done.3.head_got), custom_call_target="tpu_custom_call" | custom-call | flops 1073741824 | bytes 4194304 | tf_op jit(solution)/shard_map/pallas_call | solution.py:74
  115.8 3.6 %all-to-all-start.4 = ((s16[8,64,1152]{2,1,0:T(8,128)(2,1)}), s16[8,64,1152]{2,1,0:T(8,128)(2,1)S(1)}, u32[]{:S(2)}, u32[]{:S(2)}) async-start(s16[8,64,1152]{2,1,0:T(8,128)(2,1)} %bitcast.54), calls=%async_computation.4 | async-start | bytes 2359296 | tf_op jit(solution)/shard_map/all_to_all | solution.py:35
  121.3 13.4 %collective-permute-done.7 = bf16[2,2,64,1024]{3,2,1,0:T(8,128)(2,1)} collective-permute-done((bf16[2,2,64,1024]{3,2,1,0:T(8,128)(2,1)}, bf16[2,2,64,1024]{3,2,1,0:T(8,128)(2,1)}, u32[]{:S(2)}, u32[]{:S(2)}) %collective-permute-start.7) | collective-permute-done | bytes 524320 | tf_op jit(solution)/shard_map/ppermute | solution.py:268
  138.8 4.8 %all-to-all-start.5 = ((bf16[8,64,1152]{2,1,0:T(8,128)(2,1)}), bf16[8,64,1152]{2,1,0:T(8,128)(2,1)}, u32[]{:S(2)}, u32[]{:S(2)}) async-start(bf16[8,64,1152]{2,1,0:T(8,128)(2,1)} %copy-done.4), calls=%async_computation.5 | async-start | bytes 2359296 | tf_op jit(solution)/shard_map/all_to_all | solution.py:35
  145.2 7.0 %collective-permute-done.8 = bf16[2,64,1024]{2,1,0:T(8,128)(2,1)} collective-permute-done((bf16[2,64,1024]{2,1,0:T(8,128)(2,1)}, bf16[2,64,1024]{2,1,0:T(8,128)(2,1)}, u32[]{:S(2)}, u32[]{:S(2)}) %collective-permute-start.8) | collective-permute-done | bytes 262176 | tf_op jit(solution)/shard_map/ppermute | solution.py:273
  155.3 5.1 %collective-permute-done.9 = bf16[64,1024]{1,0:T(8,128)(2,1)S(1)} collective-permute-done((bf16[64,1024]{1,0:T(8,128)(2,1)}, bf16[64,1024]{1,0:T(8,128)(2,1)S(1)}, u32[]{:S(2)}, u32[]{:S(2)}) %collective-permute-start.9) | collective-permute-done | bytes 131104 | tf_op jit(solution)/shard_map/ppermute | solution.py:275
  162.0 3.5 %collective-permute-start.10 = (bf16[512,1152]{1,0:T(8,128)(2,1)}, bf16[512,1152]{1,0:T(8,128)(2,1)S(1)}, u32[]{:S(2)}, u32[]{:S(2)}) collective-permute-start(bf16[512,1152]{1,0:T(8,128)(2,1)} %bitcast.24.own), channel_id=1, source_target_pairs={{0,8},{8,0},{1,9},{9,1},{2,10},{10,2},{3,11},{11,3},{4,12},{12,4},... | collective-permute-start | bytes 3538952 | tf_op jit(solution)/shard_map/ppermute | solution.py:31
  165.5 2.7 collective-permute-done.10.far
  168.2 2.7 shard_map.116
  171.7 3.7 %all-to-all-start.6 = ((bf16[8,64,640]{2,1,0:T(8,128)(2,1)}), bf16[8,64,640]{2,1,0:T(8,128)(2,1)S(1)}, u32[]{:S(2)}, u32[]{:S(2)}) async-start(bf16[8,64,640]{2,1,0:T(8,128)(2,1)} %bitcast.55), calls=%async_computation.6 | async-start | bytes 1310720 | tf_op jit(solution)/shard_map/all_to_all | solution.py:35
  176.3 11.8 %all-to-all-done.6 = bf16[8,64,640]{2,1,0:T(8,128)(2,1)S(1)} async-done(((bf16[8,64,640]{2,1,0:T(8,128)(2,1)}), bf16[8,64,640]{2,1,0:T(8,128)(2,1)S(1)}, u32[]{:S(2)}, u32[]{:S(2)}) %all-to-all-start.6) | async-done | bytes 655392 | tf_op jit(solution)/shard_map/all_to_all | solution.py:35
  188.9 19.3 %all_to_all.51 = bf16[8,64,1024]{2,1,0:T(8,128)(2,1)S(1)} all-to-all(bf16[8,64,1024]{2,1,0:T(8,128)(2,1)S(1)} %broadcast_in_dim.7), channel_id=1, replica_groups=mesh['xl'=2,'y'=4,'core'=2,'z'=4,'xh'=2] {'z','xh'}, dimensions={0} | all-to-all | bytes 2097152 | tf_op jit(solution)/shard_map/all_to_all | solution.py:35
  210.2 2.3 collective-permute-done.11.far_dsummed
  212.5 2.4 shard_map.117
  214.8 28.3 %all_to_all.52 = bf16[8,64,1792]{2,1,0:T(8,128)(2,1)S(1)} all-to-all(bf16[8,64,1792]{2,1,0:T(8,128)(2,1)S(1)} %bitcast.58), channel_id=1, replica_groups=mesh['xl'=2,'y'=4,'core'=2,'z'=4,'xh'=2] {'y','xl'}, dimensions={0} | all-to-all | bytes 3670016 | tf_op jit(solution)/shard_map/all_to_all | solution.py:35
  243.6 25.8 %all_to_all.53 = bf16[8,64,1792]{2,1,0:T(8,128)(2,1)S(1)} all-to-all(bf16[8,64,1792]{2,1,0:T(8,128)(2,1)S(1)} %broadcast_in_dim.8), channel_id=1, replica_groups=mesh['xl'=2,'y'=4,'core'=2,'z'=4,'xh'=2] {'y','xl'}, dimensions={0} | all-to-all | bytes 3670016 | tf_op jit(solution)/shard_map/all_to_all | solution.py:35
  269.4 2.4 collective-permute-start.12
  271.8 3.7 %shard_map.118 = (f32[512,1792]{1,0:T(8,128)}, f32[512,1792]{1,0:T(8,128)}, f32[512,1792]{1,0:T(8,128)}) custom-call(s32[1]{0:T(128)} %bitcast.2.half_ref, bf16[512,512]{1,0:T(8,128)(2,1)S(1)} %bitcast.52, bf16[512,1792]{1,0:T(8,128)(2,1)S(1)} %bitcast.51, f32[512,1792]{1,0:T(8,128)S(1)} %copy-done.1, f32[512,1792]{1,0:T(8,128)S(1)} %copy-done.2), custom_call_target="tpu_custom_call" | custom-call | flops 950000000 | bytes 11000000 | tf_op jit(solution)/shard_map/pallas_call | solution.py:230
  275.6 3.7 %shard_map.119 = (f32[512,1792]{1,0:T(8,128)}, f32[512,1792]{1,0:T(8,128)}, f32[512,1792]{1,0:T(8,128)}) custom-call(s32[1]{0:T(128)} %bitcast.half_ref, bf16[512,512]{1,0:T(8,128)(2,1)S(1)} %bitcast.53, bf16[512,1792]{1,0:T(8,128)(2,1)S(1)} %collective-permute-done.12.cot, ...), custom_call_target="tpu_custom_call", output_to_operand_aliasing={{0}: (5, {}), {1}: (6, {}), {2}: (7, {})} | custom-call | flops 950000000 | bytes 11000000 | tf_op jit(solution)/shard_map/pallas_call | solution.py:230
  (111 shorter events, 45.0 us)
Async XLA Ops:
  0.6 4.6 %copy-start.6 = (bf16[512,512]{1,0:T(8,128)(2,1)S(1)}, bf16[512,512]{1,0:T(8,128)(2,1)}, u32[]{:S(2)}) copy-start(bf16[512,512]{1,0:T(8,128)(2,1)} %tokens.1) | copy-start | bytes 1572868
  0.6 4.6 %copy-start.10 = (bf16[512,1792]{1,0:T(8,128)(2,1)S(1)}, bf16[512,1792]{1,0:T(8,128)(2,1)}, u32[]{:S(2)}) copy-start(bf16[512,1792]{1,0:T(8,128)(2,1)} %gate.1) | copy-start | bytes 5505028
  0.7 6.2 %copy-start.20 = (s32[32]{0:T(128)S(1)}, s32[32]{0:T(128)}, u32[]{:S(2)}) copy-start(s32[32]{0:T(128)} %param.17) | copy-start | bytes 388
  0.7 6.2 %copy-start.21 = (s32[32]{0:T(128)S(1)}, s32[32]{0:T(128)}, u32[]{:S(2)}) copy-start(s32[32]{0:T(128)} %param.16) | copy-start | bytes 388
  3.8 9.1 %collective-permute-start.1 = (bf16[512,896]{1,0:T(8,128)(2,1)}, bf16[512,896]{1,0:T(8,128)(2,1)S(1)}, u32[]{:S(2)}, u32[]{:S(2)}) collective-permute-start(bf16[512,896]{1,0:T(8,128)(2,1)} %fusion.9), channel_id=1, source_target_pairs={{0,8},{8,0},{1,9},{9,1},{2,10},{10,2},{3,11},{11,3},{4,12},{12,4},... | collective-permute-start | bytes 2752520 | tf_op jit(solution)/shard_map/ppermute | solution.py:31
  6.9 6.0 %collective-permute-start = (bf16[512,896]{1,0:T(8,128)(2,1)}, bf16[512,896]{1,0:T(8,128)(2,1)}, u32[]{:S(2)}, u32[]{:S(2)}) collective-permute-start(bf16[512,896]{1,0:T(8,128)(2,1)} %fusion.8), channel_id=1, source_target_pairs={{0,8},{8,0},{1,9},{9,1},{2,10},{10,2},{3,11},{11,3},{4,12},{12,4},... | collective-permute-start | bytes 2752520 | tf_op jit(solution)/shard_map/ppermute | solution.py:31
  6.9 4.5 %collective-permute-start.2 = (s32[32,2]{0,1:T(2,128)S(1)}, s32[32,2]{0,1:T(2,128)S(1)}, u32[]{:S(2)}, u32[]{:S(2)}) collective-permute-start(s32[32,2]{0,1:T(2,128)S(1)} %pad_add_fusion), channel_id=1, source_target_pairs={{0,8},{8,0},{1,9},{9,1},{2,10},{10,2},{3,11},{11,3},{4,12},{12,4},... | collective-permute-start | bytes 776 | tf_op jit(solution)/shard_map/ppermute | solution.py:31
  19.8 30.7 %all-to-all-start = ((bf16[8,64,1920]{2,1,0:T(8,128)(2,1)}), bf16[8,64,1920]{2,1,0:T(8,128)(2,1)}, u32[]{:S(2)}, u32[]{:S(2)}) async-start(bf16[8,64,1920]{2,1,0:T(8,128)(2,1)} %bitcast.49), calls=%async_computation | async-start | bytes 3932160 | tf_op jit(solution)/shard_map/all_to_all | solution.py:35
  25.0 5.1 %collective-permute-start.3 = (bf16[512,1024]{1,0:T(8,128)(2,1)}, bf16[512,1024]{1,0:T(8,128)(2,1)}, u32[]{:S(2)}, u32[]{:S(2)}) collective-permute-start(bf16[512,1024]{1,0:T(8,128)(2,1)} %constant_dynamic-slice_fusion.3), channel_id=1, source_target_pairs={{0,8},{8,0},{1,9},{9,1},{2,10},{10,2},{3,11},{11,3},{4,12},{12,4},... | collective-permute-start | bytes 3145736 | tf_op jit(solution)/shard_map/ppermute | solution.py:31
  25.3 3.9 %collective-permute-start.4 = (bf16[896,512]{1,0:T(8,128)(2,1)}, bf16[896,512]{1,0:T(8,128)(2,1)S(1)}, u32[]{:S(2)}, u32[]{:S(2)}) collective-permute-start(bf16[896,512]{1,0:T(8,128)(2,1)} %get-tuple-element.40), channel_id=1, source_target_pairs={{0,8},{8,0},{1,9},{9,1},{2,10},{10,2},{3,11},{11,3},{4,12},{12,4},... | collective-permute-start | bytes 2752520 | tf_op jit(solution)/shard_map/ppermute | solution.py:31
  53.2 17.2 %all-to-all-start.1 = ((bf16[8,64,896]{2,1,0:T(8,128)(2,1)}), bf16[8,64,896]{2,1,0:T(8,128)(2,1)}, u32[]{:S(2)}, u32[]{:S(2)}) async-start(bf16[8,64,896]{2,1,0:T(8,128)(2,1)} %get-tuple-element.36), calls=%async_computation.1 | async-start | bytes 1835008 | tf_op jit(solution)/shard_map/all_to_all | solution.py:35
  70.4 4.7 %copy-start.19 = (bf16[896,512]{1,0:T(8,128)(2,1)S(1)}, bf16[896,512]{1,0:T(8,128)(2,1)}, u32[]{:S(2)}) copy-start(bf16[896,512]{1,0:T(8,128)(2,1)} %get-tuple-element.40) | copy-start | bytes 2752516
  70.4 4.7 %collective-permute-start.5 = (bf16[512,896]{1,0:T(8,128)(2,1)}, bf16[512,896]{1,0:T(8,128)(2,1)S(1)}, u32[]{:S(2)}, u32[]{:S(2)}) collective-permute-start(bf16[512,896]{1,0:T(8,128)(2,1)} %bitcast.13), channel_id=1, source_target_pairs={{0,8},{8,0},{1,9},{9,1},{2,10},{10,2},{3,11},{11,3},{4,12},{12,4},... | collective-permute-start | bytes 2752520 | tf_op jit(solution)/shard_map/ppermute | solution.py:31
  76.6 18.0 %all-to-all-start.2 = ((bf16[8,64,512]{2,1,0:T(8,128)(2,1)}), bf16[8,64,512]{2,1,0:T(8,128)(2,1)S(1)}, u32[]{:S(2)}, u32[]{:S(2)}) async-start(bf16[8,64,512]{2,1,0:T(8,128)(2,1)} %bitcast.66), calls=%async_computation.2 | async-start | bytes 1048576 | tf_op jit(solution)/shard_map/all_to_all | solution.py:35
  94.6 20.2 %copy-start.16 = (f32[64,512]{1,0:T(8,128)}, f32[64,512]{1,0:T(8,128)S(1)}, u32[]{:S(2)}) copy-start(f32[64,512]{1,0:T(8,128)S(1)} %convert_reduce_fusion.1) | copy-start | bytes 393220
  108.4 3.6 %collective-permute-start.6 = (bf16[512,512]{1,0:T(8,128)(2,1)S(1)}, bf16[512,512]{1,0:T(8,128)(2,1)S(1)}, u32[]{:S(2)}, u32[]{:S(2)}) collective-permute-start(bf16[512,512]{1,0:T(8,128)(2,1)S(1)} %bitcast.56), channel_id=1, source_target_pairs={{0,8},{8,0},{1,9},{9,1},{2,10},{10,2},{3,11},{11,3},{4,12},{12,4},... | collective-permute-start | bytes 1572872 | tf_op jit(solution)/shard_map/ppermute | solution.py:31
  115.8 21.0 %all-to-all-start.4 = ((s16[8,64,1152]{2,1,0:T(8,128)(2,1)}), s16[8,64,1152]{2,1,0:T(8,128)(2,1)S(1)}, u32[]{:S(2)}, u32[]{:S(2)}) async-start(s16[8,64,1152]{2,1,0:T(8,128)(2,1)} %bitcast.54), calls=%async_computation.4 | async-start | bytes 2359296 | tf_op jit(solution)/shard_map/all_to_all | solution.py:35
  121.3 13.5 %collective-permute-start.7 = (bf16[2,2,64,1024]{3,2,1,0:T(8,128)(2,1)}, bf16[2,2,64,1024]{3,2,1,0:T(8,128)(2,1)}, u32[]{:S(2)}, u32[]{:S(2)}) collective-permute-start(bf16[2,2,64,1024]{3,2,1,0:T(8,128)(2,1)} %dynamic-slice_bitcast_fusion), channel_id=1, source_target_pairs={{0,2},{2,0},{4,6},{6,4},{1,3},{3,1},{5,7},{7,5},{8,10},{10,8},{12,... | collective-permute-start | bytes 1572872 | tf_op jit(solution)/shard_map/ppermute | solution.py:268
  138.8 4.9 %copy-start.15 = (bf16[2,2,64,1024]{3,2,1,0:T(8,128)(2,1)S(1)}, bf16[2,2,64,1024]{3,2,1,0:T(8,128)(2,1)}, u32[]{:S(2)}) copy-start(bf16[2,2,64,1024]{3,2,1,0:T(8,128)(2,1)} %bitcast_add_fusion) | copy-start | bytes 1572868
  138.8 16.3 %copy-start.7 = (bf16[512,512]{1,0:T(8,128)(2,1)S(1)}, bf16[512,512]{1,0:T(8,128)(2,1)}, u32[]{:S(2)}) copy-start(bf16[512,512]{1,0:T(8,128)(2,1)} %tokens.1) | copy-start | bytes 1572868
  138.8 23.3 %all-to-all-start.5 = ((bf16[8,64,1152]{2,1,0:T(8,128)(2,1)}), bf16[8,64,1152]{2,1,0:T(8,128)(2,1)}, u32[]{:S(2)}, u32[]{:S(2)}) async-start(bf16[8,64,1152]{2,1,0:T(8,128)(2,1)} %copy-done.4), calls=%async_computation.5 | async-start | bytes 2359296 | tf_op jit(solution)/shard_map/all_to_all | solution.py:35
  144.4 7.8 %collective-permute-start.8 = (bf16[2,64,1024]{2,1,0:T(8,128)(2,1)}, bf16[2,64,1024]{2,1,0:T(8,128)(2,1)}, u32[]{:S(2)}, u32[]{:S(2)}) collective-permute-start(bf16[2,64,1024]{2,1,0:T(8,128)(2,1)} %dynamic-slice_bitcast_fusion.1), channel_id=1, source_target_pairs={{0,4},{4,0},{2,6},{6,2},{1,5},{5,1},{3,7},{7,3},{8,12},{12,8},{10,... | collective-permute-start | bytes 786440 | tf_op jit(solution)/shard_map/ppermute | solution.py:273
  154.5 5.9 %collective-permute-start.9 = (bf16[64,1024]{1,0:T(8,128)(2,1)}, bf16[64,1024]{1,0:T(8,128)(2,1)S(1)}, u32[]{:S(2)}, u32[]{:S(2)}) collective-permute-start(bf16[64,1024]{1,0:T(8,128)(2,1)} %dynamic-slice_bitcast_fusion.2), channel_id=1, source_target_pairs={{0,1},{1,0},{2,3},{3,2},{4,5},{5,4},{6,7},{7,6},{8,9},{9,8},{10,11... | collective-permute-start | bytes 393224 | tf_op jit(solution)/shard_map/ppermute | solution.py:275
  162.0 6.2 %collective-permute-start.10 = (bf16[512,1152]{1,0:T(8,128)(2,1)}, bf16[512,1152]{1,0:T(8,128)(2,1)S(1)}, u32[]{:S(2)}, u32[]{:S(2)}) collective-permute-start(bf16[512,1152]{1,0:T(8,128)(2,1)} %bitcast.24.own), channel_id=1, source_target_pairs={{0,8},{8,0},{1,9},{9,1},{2,10},{10,2},{3,11},{11,3},{4,12},{12,4},... | collective-permute-start | bytes 3538952 | tf_op jit(solution)/shard_map/ppermute | solution.py:31
  171.7 16.9 %copy-start.17 = (f32[64,512]{1,0:T(8,128)S(1)}, f32[64,512]{1,0:T(8,128)}, u32[]{:S(2)}) copy-start(f32[64,512]{1,0:T(8,128)} %copy-done.16) | copy-start | bytes 393220
  171.7 16.4 %all-to-all-start.6 = ((bf16[8,64,640]{2,1,0:T(8,128)(2,1)}), bf16[8,64,640]{2,1,0:T(8,128)(2,1)S(1)}, u32[]{:S(2)}, u32[]{:S(2)}) async-start(bf16[8,64,640]{2,1,0:T(8,128)(2,1)} %bitcast.55), calls=%async_computation.6 | async-start | bytes 1310720 | tf_op jit(solution)/shard_map/all_to_all | solution.py:35
  188.6 23.8 %copy-start.9 = (bf16[1792,512]{1,0:T(8,128)(2,1)S(1)}, bf16[1792,512]{1,0:T(8,128)(2,1)}, u32[]{:S(2)}) copy-start(bf16[1792,512]{1,0:T(8,128)(2,1)} %down.1) | copy-start | bytes 5505028
  188.6 23.8 %copy-start.14 = (bf16[896,512]{1,0:T(8,128)(2,1)S(1)}, bf16[896,512]{1,0:T(8,128)(2,1)}, u32[]{:S(2)}) copy-start(bf16[896,512]{1,0:T(8,128)(2,1)} %copy-done.13) | copy-start | bytes 2752516
  208.2 4.2 %collective-permute-start.11 = (bf16[512,1024]{1,0:T(8,128)(2,1)S(1)}, bf16[512,1024]{1,0:T(8,128)(2,1)S(1)}, u32[]{:S(2)}, u32[]{:S(2)}) collective-permute-start(bf16[512,1024]{1,0:T(8,128)(2,1)S(1)} %bitcast.59), channel_id=1, source_target_pairs={{0,8},{8,0},{1,9},{9,1},{2,10},{10,2},{3,11},{11,3},{4,12},{12,4},... | collective-permute-start | bytes 3145736 | tf_op jit(solution)/shard_map/ppermute | solution.py:31
  243.1 28.7 %copy-start.2 = (f32[512,1792]{1,0:T(8,128)S(1)}, f32[512,1792]{1,0:T(8,128)}, u32[]{:S(2)}) copy-start(f32[512,1792]{1,0:T(8,128)} %curve_ref.3) | copy-start | bytes 11010052
  243.5 28.3 %copy-start.1 = (f32[512,1792]{1,0:T(8,128)S(1)}, f32[512,1792]{1,0:T(8,128)}, u32[]{:S(2)}) copy-start(f32[512,1792]{1,0:T(8,128)} %moment_ref.3) | copy-start | bytes 11010052
  269.4 6.2 %collective-permute-start.12 = (bf16[512,1792]{1,0:T(8,128)(2,1)S(1)}, bf16[512,1792]{1,0:T(8,128)(2,1)S(1)}, u32[]{:S(2)}, u32[]{:S(2)}) collective-permute-start(bf16[512,1792]{1,0:T(8,128)(2,1)S(1)} %bitcast.50), channel_id=1, source_target_pairs={{0,8},{8,0},{1,9},{9,1},{2,10},{10,2},{3,11},{11,3},{4,12},{12,4},... | collective-permute-start | bytes 5505032 | tf_op jit(solution)/shard_map/ppermute | solution.py:31
  (9 other events, 12.2 us)

commit v6 on v5

--- a/solution.py
+++ b/solution.py
@@ -1,3 +1,5 @@
+import itertools
+
 import jax
 import jax.numpy as jnp
 from jax import lax
@@ -20,8 +22,9 @@
 rho_scale = 0.05
 eps_norm = 1e-05
 
-WIDTH_CHIPS = ("y", "xl")
+WIDTH_CHIPS = ("xl", "y")
 UNIT_CHIPS = ("z", "xh")
+MESH_SIZES = {"xl": 2, "y": 4, "core": 2, "z": 4, "xh": 2}
 f32 = jnp.float32
 bf16 = jnp.bfloat16
 VMEM_LIMIT = 24 * 1024 * 1024
@@ -31,8 +34,21 @@
     return lax.ppermute(value, "core", [(0, 1), (1, 0)])
 
 
+def partners(axes):
+    names = tuple(MESH_SIZES)
+    places = list(itertools.product(*(range(size) for size in MESH_SIZES.values())))
+    groups = {}
+    for number, place in enumerate(places):
+        fixed = tuple(value for name, value in zip(names, place) if name not in axes)
+        groups.setdefault(fixed, []).append(number)
+    core = names.index("core")
+    return [members[::-1] if places[members[0]][core] else members for members in groups.values()]
+
+
 def exchange(blocks, axes):
-    return lax.all_to_all(blocks, axes, split_axis=0, concat_axis=0, tiled=True)
+    return lax.all_to_all(
+        blocks, tuple(MESH_SIZES), split_axis=0, concat_axis=0, tiled=True, axis_index_groups=partners(axes)
+    )
 
 
 def to_all(block, axes):
@@ -40,6 +56,24 @@
     return exchange(copies, axes)
 
 
+def block_rows(block):
+    return slice(block * BLOCK, (block + 1) * BLOCK)
+
+
+def join_cores(own, far):
+    return jnp.concatenate(
+        [own[block_rows(block)] + far[block_rows(CHIPS - 1 - block)] for block in range(CHIPS)], axis=0
+    )
+
+
+def reverse_rows(rows):
+    return jnp.concatenate([rows[block_rows(CHIPS - 1 - block)] for block in range(CHIPS)], axis=0)
+
+
+def reverse_blocks(rows):
+    return rows.reshape((CHIPS, BLOCK) + rows.shape[1:])[::-1].reshape(rows.shape)
+
+
 def together(*values):
     return lax.optimization_barrier(values)
 
@@ -69,7 +103,7 @@
     return pl.BlockSpec((count, array.shape[1]), lambda step, half: (half[0], 0))
 
 
-def on_core(kernel, half, operands, specs, outs, flops):
+def on_core(kernel, half, operands, specs, outs, flops, limit=VMEM_LIMIT):
     size = sum(operand.size * operand.dtype.itemsize for operand in operands)
     results = pl.pallas_call(
         kernel,
@@ -80,19 +114,26 @@
             in_specs=specs,
             out_specs=tuple(whole(jax.ShapeDtypeStruct(*out)) for out in outs),
         ),
-        compiler_params=pltpu.CompilerParams(vmem_limit_bytes=VMEM_LIMIT),
+        compiler_params=pltpu.CompilerParams(vmem_limit_bytes=limit),
         cost_estimate=pl.CostEstimate(flops=flops, bytes_accessed=size, transcendentals=0),
     )(half.reshape(1), *operands)
     return results if len(outs) > 1 else results[0]
 
 
 def gate_up_own(half_ref, tokens, gate, up, got_gate, got_up, labels, out):
-    gate_sum = dot(tokens[...], gate[...]) + got_gate[...].astype(f32)
-    out[:, :FF_HALF] = gate_sum.astype(bf16)
-    up_sum = dot(tokens[...], up[...]) + got_up[...].astype(f32)
-    out[:, FF_HALF : 2 * FF_HALF] = up_sum.astype(bf16)
+    core = half_ref[0]
+    gate_sum = (dot(tokens[...], gate[...]) + got_gate[...].astype(f32)).astype(bf16)
+    up_sum = (dot(tokens[...], up[...]) + got_up[...].astype(f32)).astype(bf16)
     for block in range(CHIPS):
-        out[block * BLOCK : (block + 1) * BLOCK, 2 * FF_HALF :] = labels[...]
+        place = block + core * (CHIPS - 1 - 2 * block)
+        rows = pl.ds(pl.multiple_of(place * BLOCK, BLOCK), BLOCK)
+        out[rows, :FF_HALF] = gate_sum[block_rows(block)]
+        out[rows, FF_HALF : 2 * FF_HALF] = up_sum[block_rows(block)]
+        out[rows, 2 * FF_HALF :] = labels[...]
+
+
+def branch_kernel(half_ref, own, far, down_own, down_far, out):
+    out[...] = join_cores(dot(own[...], down_own[...]), dot(far[...], down_far[...])).astype(bf16)
 
 
 def hidden_kernel(half_ref, both, hidden, silu_out):
@@ -118,8 +159,8 @@
 
 
 def logits_kernel(half_ref, rows, far_rows, head, head_got, out):
-    raw = dot(rows[...], head[...]) + dot(far_rows[...], head_got[...])
-    squares = squares_of(rows) + squares_of(far_rows)
+    raw = join_cores(dot(rows[...], head[...]), dot(far_rows[...], head_got[...]))
+    squares = join_cores(squares_of(rows), squares_of(far_rows))
     level = exponent_of(jnp.max(jnp.abs(raw), axis=1, keepdims=True))
     out[:, :V_HALF] = jnp.round(raw * (STEP * jnp.exp2(-level))).astype(jnp.int32).astype(jnp.int16)
     square_level = exponent_of(squares)
@@ -187,12 +228,12 @@
     lane = lax.broadcasted_iota(jnp.int32, (PAD, PAD), 1)
     gather = ((row % N_STATS == lane) & (row < 3 * N_STATS)).astype(f32).astype(bf16)
     stats_own = dot(own[:, V_HALF:], gather)
-    stats_far = dot(far[:, V_HALF:], gather)
+    stats_far = reverse_rows(dot(far[:, V_HALF:], gather))
     top = jnp.maximum(stats_own[:, 0:1], stats_far[:, 0:1])
     scale_own = jnp.exp(stats_own[:, 0:1] - top)
     scale_far = jnp.exp(stats_far[:, 0:1] - top)
     pulled = scale_own * dot_rows(own[:, :V_HALF], head_own[...])
-    pulled = pulled + scale_far * dot_rows(far[:, :V_HALF], head_far[...])
+    pulled = pulled + scale_far * reverse_rows(dot_rows(far[:, :V_HALF], head_far[...]))
     width = pulled.shape[1]
     out[:, :width] = pulled.astype(bf16)
     lane = lax.broadcasted_iota(jnp.int32, (count, PAD), 1)
@@ -206,7 +247,7 @@
     width = down.shape[1]
     for which in range(2):
         place = slice(which * width, (which + 1) * width)
-        part = dot_rows(dsummed[:, place], down[...]) + dot_rows(far_dsummed[:, place], down_got[...])
+        part = join_cores(dot_rows(dsummed[:, place], down[...]), dot_rows(far_dsummed[:, place], down_got[...]))
         out[:, which * FF_HALF : (which + 1) * FF_HALF] = part.astype(bf16)
 
 
@@ -260,17 +301,19 @@
     for which in range(2):
         hot = (labels[:, which : which + 1] == ids).astype(bf16)
         parts.append(dot_rows(hot, head_weight).astype(bf16))
-    return jnp.concatenate(parts, axis=1).reshape(2, 2, 2, BLOCK, -1)
-
-
-def pair_label_rows(rows):
-    keep, send = own_part(rows, lax.axis_index("z") % 2, 1)
-    return keep + lax.ppermute(send, "z", [(0, 1), (1, 0), (2, 3), (3, 2)])
+    return jnp.concatenate(parts, axis=1).reshape(4, 2, BLOCK, -1)
+
+
+def plane_label_rows(rows):
+    z = lax.axis_index("z")
+    total = lax.dynamic_index_in_dim(rows, z, 0, keepdims=False)
+    for shift in (1, 3, 2):
+        sent = lax.dynamic_index_in_dim(rows, (z + shift) % 4, 0, keepdims=False)
+        total = total + lax.ppermute(sent, "z", [(place, (place + shift) % 4) for place in range(4)])
+    return total
 
 
 def own_label_rows(rows):
-    keep, send = own_part(rows, lax.axis_index("z") // 2, 0)
-    rows = keep + lax.ppermute(send, "z", [(0, 2), (2, 0), (1, 3), (3, 1)])
     keep, send = own_part(rows, lax.axis_index("xh"), 0)
     return keep + lax.ppermute(send, "xh", [(0, 1), (1, 0)])
 
@@ -314,6 +357,7 @@
         w_specs + [whole(got_gate), whole(got_up), whole(digits)],
         [((count, 2 * FF_HALF + PAD), bf16)],
         gate_up_flops,
+        60 * 1024 * 1024,
     )
     head_send = lax.dynamic_slice_in_dim(head_weight, far * V_HALF, V_HALF, 1)
     down_send = lax.dynamic_slice_in_dim(down_weight, far * FF_HALF, FF_HALF, 0)
@@ -335,19 +379,29 @@
     hidden, digits = together(hidden, both)
     digits = digits[:, :, 2 * FF_HALF : 2 * FF_HALF + 4].astype(jnp.int32)
     all_labels = digits[:, :, :2] * PAD + digits[:, :, 2:]
-    all_labels = all_labels.reshape(4, 2, BLOCK, 2).transpose(1, 0, 2, 3).reshape(count, 2)
+    all_labels = jnp.where(core == 0, all_labels, all_labels[::-1]).reshape(count, 2)
     width_chip = lax.axis_index(WIDTH_CHIPS)
-    hidden_own, label_row, labels, down_own, down_far = together(
+    hidden_own, label_row, labels = together(
         exchange(hidden, WIDTH_CHIPS),
         label_rows(all_labels, head_weight, unit_chip),
         lax.dynamic_slice_in_dim(all_labels, width_chip * BLOCK, BLOCK, 0),
-        lax.dynamic_slice_in_dim(down_weight, core * FF_HALF, FF_HALF, 0),
-        lax.dynamic_slice_in_dim(down_weight, far * FF_HALF, FF_HALF, 0),
     )
     hidden_own = hidden_own.reshape(count, FF_HALF)
     hidden_far = other_core(hidden_own)
-    branch = dot(hidden_own, down_own) + dot(hidden_far, down_far)
-    branch = exchange(branch.astype(bf16).reshape(CHIPS, BLOCK, width), UNIT_CHIPS)
+    branch = on_core(
+        branch_kernel,
+        core,
+        (hidden_own, hidden_far, down_weight, down_weight),
+        [
+            whole(hidden_own),
+            whole(hidden_far),
+            rows_of(down_weight, FF_HALF),
+            pl.BlockSpec((FF_HALF, width), lambda step, half: (1 - half[0], 0)),
+        ],
+        [((count, width), bf16)],
+        gate_up_flops,
+    )
+    branch = exchange(branch.reshape(CHIPS, BLOCK, width), UNIT_CHIPS)
     branch = jnp.sum(branch.astype(f32), axis=0)
     own_tokens = lax.dynamic_slice_in_dim(tokens, unit_chip * BLOCK, BLOCK, 0)
     summed = own_tokens.astype(f32) + branch
@@ -365,7 +419,7 @@
     )
     raw, label_row = together(raw, label_row)
     raw, label_row = together(
-        exchange(raw.reshape(CHIPS, BLOCK, V_HALF + PAD), WIDTH_CHIPS), pair_label_rows(label_row)
+        exchange(raw.reshape(CHIPS, BLOCK, V_HALF + PAD), WIDTH_CHIPS), plane_label_rows(label_row)
     )
     vocab_start = ((unit_chip * 2 + core) * V_HALF).astype(jnp.int32)
     packed = on_core(
@@ -377,8 +431,13 @@
         1000000,
     )
     packed, token_rows, label_row = together(packed, tokens, label_row)
-    packed_own, turned, label_row = together(
-        exchange(packed, WIDTH_CHIPS), token_rows.T, own_label_rows(label_row)
+    turned = token_rows.T
+    turned_reverse = reverse_blocks(token_rows).T
+    packed_own, turned_own, turned_far, label_row = together(
+        exchange(packed, WIDTH_CHIPS),
+        jnp.where(core == 0, turned, turned_reverse),
+        jnp.where(core == 0, turned_reverse, turned),
+        own_label_rows(label_row),
     )
     label_row = label_row.astype(f32)
     packed_own = packed_own.reshape(count, V_HALF + PAD)
@@ -428,8 +487,8 @@
     cot = (dhidden * jnp.concatenate([silu_gate, silu_gate], axis=1)).astype(bf16)
     cot_own = to_all(cot, WIDTH_CHIPS).reshape(count, 2 * FF_HALF)
     cot_far = other_core(cot_own)
-    done = sophia_half(core, turned, cot_own, up_moment, up_curvature, ())
-    return tuple(sophia_half(far, turned, cot_far, up_moment, up_curvature, done))
+    done = sophia_half(core, turned_own, cot_own, up_moment, up_curvature, ())
+    return tuple(sophia_half(far, turned_far, cot_far, up_moment, up_curvature, done))
 
 
 def solution(mesh):

time: 280 us -> 279 us (level)
  waiting for transfers between devices: 84.2 us -> 70.5 us
  starting transfers between devices: 44.9 us -> 52.7 us
  other arithmetic: 9.17 us -> 12.7 us
    all_to_all x6, starting transfers between devices: 28.7 us -> 40.2 us  [exchange(): lax.all_to_all(blocks, tuple(MESH_SIZES), split_axis=0, concat_axis=0, ti...]
    ppermute x10, starting transfers between devices: 14.7 us -> 6.44 us  [other_core(): return lax.ppermute(value, 'core', [(0, 1), (1, 0)])]
    all_to_all x6, waiting for transfers between devices: 48.3 us -> 40.1 us  [exchange(): lax.all_to_all(blocks, tuple(MESH_SIZES), split_axis=0, concat_axis=0, ti...]
    ppermute x2 -> x3, waiting for transfers between devices: 20.4 us -> 12.2 us  [plane_label_rows(): lax.ppermute(sent, 'z', [(place, (place + shift) % 4) for place in range(...]
    dot_general x4 -> x2, matrix products: 8.42 us -> 5.94 us  [dot(): return jnp.dot(left, right, preferred_element_type=f32)]
    pallas_call x6 -> x7, Pallas kernels: 14.1 us -> 16.1 us  [on_core(): pl.pallas_call(kernel, out_shape=tuple((jax.ShapeDtypeStruct(shape, dtype...]
    unnamed x45 -> x43, local copies, waits for them, and re-layouts: 9.01 us -> 7.26 us
  transfers between devices with their start and end apart: 19 -> 20, of which waited for: 12 -> 13; matrix products, arithmetic and copies ran while one was open for 9% -> 11% of each run, Pallas kernels for 1% -> 1%
where the time goes in v6:
time: 279 us; the launch traced here: 278 us
  blocking collectives  86 us (31%)
  waiting for transfers between devices  70.5 us (25%)
  starting transfers between devices  52.7 us (19%)
  Pallas kernels  23.7 us (8%)
  local copies, waits for them, and re-layouts  22.5 us (8%)
  other arithmetic  12.7 us (5%)
  matrix products  8.68 us (3%)
    all_to_all x4, blocking collectives, exchange(): lax.all_to_all(blocks, tuple(MESH_SIZES), split_axis=0, concat_axis=0, ti...  86 us
    all_to_all x6, starting transfers between devices, exchange(): lax.all_to_all(blocks, tuple(MESH_SIZES), split_axis=0, concat_axis=0, ti...  40.2 us
    all_to_all x6, waiting for transfers between devices, exchange(): lax.all_to_all(blocks, tuple(MESH_SIZES), split_axis=0, concat_axis=0, ti...  40.1 us
    pallas_call x7, Pallas kernels, on_core(): pl.pallas_call(kernel, out_shape=tuple((jax.ShapeDtypeStruct(shape, dtype...  16.1 us
    ppermute x10, waiting for transfers between devices, other_core(): return lax.ppermute(value, 'core', [(0, 1), (1, 0)])  12.8 us
    ppermute x3, waiting for transfers between devices, plane_label_rows(): lax.ppermute(sent, 'z', [(place, (place + shift) % 4) for place in range(...  12.2 us
    pallas_call x2, Pallas kernels, sophia_half(): pl.pallas_call(step_kernel, out_shape=(shape, shape, shape), grid_spec=pl...  7.55 us
    unnamed x43, local copies, waits for them, and re-layouts  7.26 us
  transfers between devices with their start and end apart: 20, of which 13 were waited for; matrix products, arithmetic and copies ran while one was open for 11% of the time, Pallas kernels for 1%

profile of v6, /device:TPU:1, one launch (start us, length us, event | category | flops | bytes accessed | tf_op | source)
XLA Modules:
  0.0 277.7 jit_solution(10790285721953792712)
XLA Ops:
  0.7 3.1 %fusion.9 = bf16[512,896]{1,0:T(8,128)(2,1)} fusion(bf16[512,512]{1,0:T(8,128)(2,1)} %tokens.1, bf16[512,1792]{1,0:T(8,128)(2,1)} %up.1, s32[]{:T(128)S(6)} %select_n.95), kind=kOutput, calls=%fused_computation.12 | convolution fusion | flops 470220800 | bytes 2359300 | tf_op jit(solution)/shard_map/dot_general | solution.py:82
  5.2 2.8 %fusion.8 = bf16[512,896]{1,0:T(8,128)(2,1)} fusion(bf16[512,512]{1,0:T(8,128)(2,1)S(1)} %copy-done.14, bf16[512,1792]{1,0:T(8,128)(2,1)} %gate.1, s32[]{:T(128)S(6)} %select_n.95), kind=kOutput, calls=%fused_computation.11 | convolution fusion | flops 470220800 | bytes 2359300 | tf_op jit(solution)/shard_map/dot_general | solution.py:82
  13.3 4.8 %shard_map.112 = bf16[512,1920]{1,0:T(8,128)(2,1)} custom-call(s32[1]{0:T(128)} %bitcast.2.half_ref, bf16[512,512]{1,0:T(8,128)(2,1)} %tokens.1, bf16[512,1792]{1,0:T(8,128)(2,1)} %gate.1, bf16[512,1792]{1,0:T(8,128)(2,1)} %up.1, bf16[512,896]{1,0:T(8,128)(2,1)} %collective-permute-done.got_gate, bf16[512,896]{1,0:T(8,128)(2,1)} %copy-done.18, ...), custom_call_target="tpu_custom_call" | custom-call | flops 939524096 | bytes 6045696 | tf_op jit(solution)/shard_map/pallas_call | solution.py:108
  18.1 8.0 %all-to-all-start = ((bf16[8,64,1920]{2,1,0:T(8,128)(2,1)}), bf16[8,64,1920]{2,1,0:T(8,128)(2,1)}, u32[]{:S(2)}, u32[]{:S(2)}) async-start(bf16[8,64,1920]{2,1,0:T(8,128)(2,1)} %bitcast.64), calls=%async_computation | async-start | bytes 3932160 | tf_op jit(solution)/shard_map/all_to_all | solution.py:49
  26.6 3.6 %collective-permute-done.4.down_got = bf16[896,512]{1,0:T(8,128)(2,1)} collective-permute-done((bf16[896,512]{1,0:T(8,128)(2,1)}, bf16[896,512]{1,0:T(8,128)(2,1)}, u32[]{:S(2)}, u32[]{:S(2)}) %collective-permute-start.4) | collective-permute-done | bytes 917536 | tf_op jit(solution)/shard_map/ppermute | solution.py:34
  30.2 19.1 %all-to-all-done.both = bf16[8,64,1920]{2,1,0:T(8,128)(2,1)} async-done(((bf16[8,64,1920]{2,1,0:T(8,128)(2,1)}), bf16[8,64,1920]{2,1,0:T(8,128)(2,1)}, u32[]{:S(2)}, u32[]{:S(2)}) %all-to-all-start) | async-done | bytes 1966112 | tf_op jit(solution)/shard_map/all_to_all | solution.py:49
  52.1 4.9 %all-to-all-start.1 = ((bf16[8,64,896]{2,1,0:T(8,128)(2,1)}), bf16[8,64,896]{2,1,0:T(8,128)(2,1)S(1)}, u32[]{:S(2)}, u32[]{:S(2)}) async-start(bf16[8,64,896]{2,1,0:T(8,128)(2,1)} %copy-done.13), calls=%async_computation.1 | async-start | bytes 1835008 | tf_op jit(solution)/shard_map/all_to_all | solution.py:49
  62.2 2.3 copy.65
  64.4 4.6 %all-to-all-done.1 = bf16[8,64,896]{2,1,0:T(8,128)(2,1)S(1)} async-done(((bf16[8,64,896]{2,1,0:T(8,128)(2,1)}), bf16[8,64,896]{2,1,0:T(8,128)(2,1)S(1)}, u32[]{:S(2)}, u32[]{:S(2)}) %all-to-all-start.1) | async-done | bytes 917536 | tf_op jit(solution)/shard_map/all_to_all | solution.py:49
  69.1 2.5 collective-permute-done.5.far
  75.1 10.1 %all-to-all-start.2 = ((bf16[8,64,512]{2,1,0:T(8,128)(2,1)}), bf16[8,64,512]{2,1,0:T(8,128)(2,1)}, u32[]{:S(2)}, u32[]{:S(2)}) async-start(bf16[8,64,512]{2,1,0:T(8,128)(2,1)} %bitcast.11), calls=%async_computation.2 | async-start | bytes 1048576 | tf_op jit(solution)/shard_map/all_to_all | solution.py:49
  85.2 7.9 %all-to-all-done.2 = bf16[8,64,512]{2,1,0:T(8,128)(2,1)} async-done(((bf16[8,64,512]{2,1,0:T(8,128)(2,1)}), bf16[8,64,512]{2,1,0:T(8,128)(2,1)}, u32[]{:S(2)}, u32[]{:S(2)}) %all-to-all-start.2) | async-done | bytes 524320 | tf_op jit(solution)/shard_map/all_to_all | solution.py:49
  95.2 13.4 %all_to_all.50 = bf16[8,64,512]{2,1,0:T(8,128)(2,1)S(1)} all-to-all(bf16[8,64,512]{2,1,0:T(8,128)(2,1)S(1)} %broadcast_in_dim.6), channel_id=1, replica_groups={{0,1,2,3,4,5,6,7},{15,14,13,12,11,10,9,8},{16,17,18,19,20,21,22,23},{31..., dimensions={0} | all-to-all | bytes 1048576 | tf_op jit(solution)/shard_map/all_to_all | solution.py:49
  114.3 5.5 %all-to-all-start.4 = ((s16[8,64,1152]{2,1,0:T(8,128)(2,1)}), s16[8,64,1152]{2,1,0:T(8,128)(2,1)S(1)}, u32[]{:S(2)}, u32[]{:S(2)}) async-start(s16[8,64,1152]{2,1,0:T(8,128)(2,1)} %bitcast.55), calls=%async_computation.4 | async-start | bytes 2359296 | tf_op jit(solution)/shard_map/all_to_all | solution.py:49
  121.8 2.6 collective-permute-start.9
  125.0 6.7 %collective-permute-done.7 = bf16[2,64,1024]{2,1,0:T(8,128)(2,1)} collective-permute-done((bf16[2,64,1024]{2,1,0:T(8,128)(2,1)}, bf16[2,64,1024]{2,1,0:T(8,128)(2,1)}, u32[]{:S(2)}, u32[]{:S(2)}) %collective-permute-start.7) | collective-permute-done | bytes 262176 | tf_op jit(solution)/shard_map/ppermute | solution.py:312
  131.6 4.6 %collective-permute-done.9 = bf16[2,64,1024]{2,1,0:T(8,128)(2,1)} collective-permute-done((bf16[2,64,1024]{2,1,0:T(8,128)(2,1)}, bf16[2,64,1024]{2,1,0:T(8,128)(2,1)}, u32[]{:S(2)}, u32[]{:S(2)}) %collective-permute-start.9) | collective-permute-done | bytes 262176 | tf_op jit(solution)/shard_map/ppermute | solution.py:312
  141.1 5.3 %all-to-all-start.5 = ((bf16[8,64,1152]{2,1,0:T(8,128)(2,1)}), bf16[8,64,1152]{2,1,0:T(8,128)(2,1)S(1)}, u32[]{:S(2)}, u32[]{:S(2)}) async-start(bf16[8,64,1152]{2,1,0:T(8,128)(2,1)} %copy-done.6), calls=%async_computation.5 | async-start | bytes 2359296 | tf_op jit(solution)/shard_map/all_to_all | solution.py:49
  147.9 2.9 %collective-permute-start.10 = (bf16[64,1024]{1,0:T(8,128)(2,1)}, bf16[64,1024]{1,0:T(8,128)(2,1)}, u32[]{:S(2)}, u32[]{:S(2)}) collective-permute-start(bf16[64,1024]{1,0:T(8,128)(2,1)} %dynamic-slice_bitcast_fusion.3), channel_id=1, source_target_pairs={{0,1},{1,0},{2,3},{3,2},{4,5},{5,4},{6,7},{7,6},{8,9},{9,8},{10,11... | collective-permute-start | bytes 393224 | tf_op jit(solution)/shard_map/ppermute | solution.py:318
  154.7 2.0 copy.67
  156.7 2.3 select_bitcast_fusion
  159.0 5.5 %collective-permute-done.10 = bf16[64,1024]{1,0:T(8,128)(2,1)} collective-permute-done((bf16[64,1024]{1,0:T(8,128)(2,1)}, bf16[64,1024]{1,0:T(8,128)(2,1)}, u32[]{:S(2)}, u32[]{:S(2)}) %collective-permute-start.10) | collective-permute-done | bytes 131104 | tf_op jit(solution)/shard_map/ppermute | solution.py:318
  166.0 2.8 %collective-permute-done.11.far = bf16[512,1152]{1,0:T(8,128)(2,1)S(1)} collective-permute-done((bf16[512,1152]{1,0:T(8,128)(2,1)S(1)}, bf16[512,1152]{1,0:T(8,128)(2,1)S(1)}, u32[]{:S(2)}, u32[]{:S(2)}) %collective-permute-start.11) | collective-permute-done | bytes 1179680 | tf_op jit(solution)/shard_map/ppermute | solution.py:34
  171.1 6.5 %all-to-all-start.6 = ((bf16[8,64,640]{2,1,0:T(8,128)(2,1)}), bf16[8,64,640]{2,1,0:T(8,128)(2,1)S(1)}, u32[]{:S(2)}, u32[]{:S(2)}) async-start(bf16[8,64,640]{2,1,0:T(8,128)(2,1)} %bitcast.58), calls=%async_computation.6 | async-start | bytes 1310720 | tf_op jit(solution)/shard_map/all_to_all | solution.py:49
  178.5 8.4 %all-to-all-done.6 = bf16[8,64,640]{2,1,0:T(8,128)(2,1)S(1)} async-done(((bf16[8,64,640]{2,1,0:T(8,128)(2,1)}), bf16[8,64,640]{2,1,0:T(8,128)(2,1)S(1)}, u32[]{:S(2)}, u32[]{:S(2)}) %all-to-all-start.6) | async-done | bytes 655392 | tf_op jit(solution)/shard_map/all_to_all | solution.py:49
  188.8 19.3 %all_to_all.51 = bf16[8,64,1024]{2,1,0:T(8,128)(2,1)S(1)} all-to-all(bf16[8,64,1024]{2,1,0:T(8,128)(2,1)S(1)} %broadcast_in_dim.7), channel_id=1, replica_groups={{0,1,2,3,4,5,6,7},{15,14,13,12,11,10,9,8},{16,17,18,19,20,21,22,23},{31..., dimensions={0} | all-to-all | bytes 2097152 | tf_op jit(solution)/shard_map/all_to_all | solution.py:49
  208.9 2.3 collective-permute-done.12.far_dsummed
  211.2 3.5 %shard_map.118 = bf16[512,1792]{1,0:T(8,128)(2,1)S(1)} custom-call(s32[1]{0:T(128)} %bitcast.2.half_ref, bf16[512,1024]{1,0:T(8,128)(2,1)S(1)} %bitcast.63, bf16[512,1024]{1,0:T(8,128)(2,1)S(1)} %collective-permute-done.12.far_dsummed, bf16[1792,512]{1,0:T(8,128)(2,1)S(1)} %copy-done.5, bf16[896,512]{1,0:T(8,128)(2,1)} %collective-permute-done.4.down_got), custom_call_target="tpu_custom_call" | custom-call | flops 1879048192 | bytes 4849664 | tf_op jit(solution)/shard_map/pallas_call | solution.py:108
  214.7 27.7 %all_to_all.52 = bf16[8,64,1792]{2,1,0:T(8,128)(2,1)S(1)} all-to-all(bf16[8,64,1792]{2,1,0:T(8,128)(2,1)S(1)} %bitcast.61), channel_id=1, replica_groups={{0,16,32,48,64,80,96,112},{1,17,33,49,65,81,97,113},{2,18,34,50,66,82,9..., dimensions={0} | all-to-all | bytes 3670016 | tf_op jit(solution)/shard_map/all_to_all | solution.py:49
  242.9 25.5 %all_to_all.53 = bf16[8,64,1792]{2,1,0:T(8,128)(2,1)S(1)} all-to-all(bf16[8,64,1792]{2,1,0:T(8,128)(2,1)S(1)} %broadcast_in_dim.8), channel_id=1, replica_groups={{0,16,32,48,64,80,96,112},{1,17,33,49,65,81,97,113},{2,18,34,50,66,82,9..., dimensions={0} | all-to-all | bytes 3670016 | tf_op jit(solution)/shard_map/all_to_all | solution.py:49
  270.1 3.8 %shard_map.119 = (f32[512,1792]{1,0:T(8,128)}, f32[512,1792]{1,0:T(8,128)}, f32[512,1792]{1,0:T(8,128)}) custom-call(s32[1]{0:T(128)} %bitcast.2.half_ref, bf16[512,512]{1,0:T(8,128)(2,1)S(1)} %copy-done.10, bf16[512,1792]{1,0:T(8,128)(2,1)S(1)} %bitcast.52, f32[512,1792]{1,0:T(8,128)S(1)} %copy-done.1, f32[512,1792]{1,0:T(8,128)S(1)} %copy-done.2), custom_call_target="tpu_custom_call" | custom-call | flops 950000000 | bytes 11000000 | tf_op jit(solution)/shard_map/pallas_call | solution.py:271
  273.9 3.8 %shard_map.120 = (f32[512,1792]{1,0:T(8,128)}, f32[512,1792]{1,0:T(8,128)}, f32[512,1792]{1,0:T(8,128)}) custom-call(s32[1]{0:T(128)} %bitcast.half_ref, bf16[512,512]{1,0:T(8,128)(2,1)S(1)} %copy-done.9, bf16[512,1792]{1,0:T(8,128)(2,1)S(1)} %collective-permute-done.13.cot, ...), custom_call_target="tpu_custom_call", output_to_operand_aliasing={{0}: (5, {}), {1}: (6, {}), {2}: (7, {})} | custom-call | flops 950000000 | bytes 11000000 | tf_op jit(solution)/shard_map/pallas_call | solution.py:271
  (111 shorter events, 48.6 us)
Async XLA Ops:
  0.7 7.4 %copy-start.19 = (s32[32]{0:T(128)S(1)}, s32[32]{0:T(128)}, u32[]{:S(2)}) copy-start(s32[32]{0:T(128)} %param.17) | copy-start | bytes 388
  0.7 7.4 %copy-start.20 = (s32[32]{0:T(128)S(1)}, s32[32]{0:T(128)}, u32[]{:S(2)}) copy-start(s32[32]{0:T(128)} %param.16) | copy-start | bytes 388
  0.7 8.0 %copy-start = (bf16[512,2048]{1,0:T(8,128)(2,1)S(1)}, bf16[512,2048]{1,0:T(8,128)(2,1)}, u32[]{:S(2)}) copy-start(bf16[512,2048]{1,0:T(8,128)(2,1)} %head_far.1) | copy-start | bytes 6291460
  3.8 8.6 %collective-permute-start.1 = (bf16[512,896]{1,0:T(8,128)(2,1)}, bf16[512,896]{1,0:T(8,128)(2,1)S(1)}, u32[]{:S(2)}, u32[]{:S(2)}) collective-permute-start(bf16[512,896]{1,0:T(8,128)(2,1)} %fusion.9), channel_id=1, source_target_pairs={{0,8},{8,0},{1,9},{9,1},{2,10},{10,2},{3,11},{11,3},{4,12},{12,4},... | collective-permute-start | bytes 2752520 | tf_op jit(solution)/shard_map/ppermute | solution.py:34
  8.0 4.3 %collective-permute-start = (bf16[512,896]{1,0:T(8,128)(2,1)}, bf16[512,896]{1,0:T(8,128)(2,1)}, u32[]{:S(2)}, u32[]{:S(2)}) collective-permute-start(bf16[512,896]{1,0:T(8,128)(2,1)} %fusion.8), channel_id=1, source_target_pairs={{0,8},{8,0},{1,9},{9,1},{2,10},{10,2},{3,11},{11,3},{4,12},{12,4},... | collective-permute-start | bytes 2752520 | tf_op jit(solution)/shard_map/ppermute | solution.py:34
  8.1 3.5 %collective-permute-start.2 = (s32[32,2]{0,1:T(2,128)S(1)}, s32[32,2]{0,1:T(2,128)S(1)}, u32[]{:S(2)}, u32[]{:S(2)}) collective-permute-start(s32[32,2]{0,1:T(2,128)S(1)} %pad_add_fusion), channel_id=1, source_target_pairs={{0,8},{8,0},{1,9},{9,1},{2,10},{10,2},{3,11},{11,3},{4,12},{12,4},... | collective-permute-start | bytes 776 | tf_op jit(solution)/shard_map/ppermute | solution.py:34
  18.1 31.3 %all-to-all-start = ((bf16[8,64,1920]{2,1,0:T(8,128)(2,1)}), bf16[8,64,1920]{2,1,0:T(8,128)(2,1)}, u32[]{:S(2)}, u32[]{:S(2)}) async-start(bf16[8,64,1920]{2,1,0:T(8,128)(2,1)} %bitcast.64), calls=%async_computation | async-start | bytes 3932160 | tf_op jit(solution)/shard_map/all_to_all | solution.py:49
  26.0 4.2 %collective-permute-start.3 = (bf16[512,1024]{1,0:T(8,128)(2,1)}, bf16[512,1024]{1,0:T(8,128)(2,1)S(1)}, u32[]{:S(2)}, u32[]{:S(2)}) collective-permute-start(bf16[512,1024]{1,0:T(8,128)(2,1)} %constant_dynamic-slice_fusion.2), channel_id=1, source_target_pairs={{0,8},{8,0},{1,9},{9,1},{2,10},{10,2},{3,11},{11,3},{4,12},{12,4},... | collective-permute-start | bytes 3145736 | tf_op jit(solution)/shard_map/ppermute | solution.py:34
  26.0 4.2 %collective-permute-start.4 = (bf16[896,512]{1,0:T(8,128)(2,1)}, bf16[896,512]{1,0:T(8,128)(2,1)}, u32[]{:S(2)}, u32[]{:S(2)}) collective-permute-start(bf16[896,512]{1,0:T(8,128)(2,1)} %constant_dynamic-slice_fusion.1), channel_id=1, source_target_pairs={{0,8},{8,0},{1,9},{9,1},{2,10},{10,2},{3,11},{11,3},{4,12},{12,4},... | collective-permute-start | bytes 2752520 | tf_op jit(solution)/shard_map/ppermute | solution.py:34
  30.2 21.9 %copy-start.11 = (bf16[512,1024]{1,0:T(8,128)(2,1)}, bf16[512,1024]{1,0:T(8,128)(2,1)S(1)}, u32[]{:S(2)}) copy-start(bf16[512,1024]{1,0:T(8,128)(2,1)S(1)} %collective-permute-done.3.head_got) | copy-start | bytes 3145732
  52.1 17.0 %all-to-all-start.1 = ((bf16[8,64,896]{2,1,0:T(8,128)(2,1)}), bf16[8,64,896]{2,1,0:T(8,128)(2,1)S(1)}, u32[]{:S(2)}, u32[]{:S(2)}) async-start(bf16[8,64,896]{2,1,0:T(8,128)(2,1)} %copy-done.13), calls=%async_computation.1 | async-start | bytes 1835008 | tf_op jit(solution)/shard_map/all_to_all | solution.py:49
  69.1 2.5 collective-permute-start.5
  75.1 36.5 %copy-start.12 = (bf16[512,1024]{1,0:T(8,128)(2,1)S(1)}, bf16[512,1024]{1,0:T(8,128)(2,1)}, u32[]{:S(2)}) copy-start(bf16[512,1024]{1,0:T(8,128)(2,1)} %copy-done.11) | copy-start | bytes 3145732
  75.1 18.0 %all-to-all-start.2 = ((bf16[8,64,512]{2,1,0:T(8,128)(2,1)}), bf16[8,64,512]{2,1,0:T(8,128)(2,1)}, u32[]{:S(2)}, u32[]{:S(2)}) async-start(bf16[8,64,512]{2,1,0:T(8,128)(2,1)} %bitcast.11), calls=%async_computation.2 | async-start | bytes 1048576 | tf_op jit(solution)/shard_map/all_to_all | solution.py:49
  94.3 19.0 %copy-start.15 = (f32[64,512]{1,0:T(8,128)}, f32[64,512]{1,0:T(8,128)S(1)}, u32[]{:S(2)}) copy-start(f32[64,512]{1,0:T(8,128)S(1)} %convert_reduce_fusion.1) | copy-start | bytes 393220
  108.6 3.0 %collective-permute-start.6 = (bf16[512,512]{1,0:T(8,128)(2,1)S(1)}, bf16[512,512]{1,0:T(8,128)(2,1)S(1)}, u32[]{:S(2)}, u32[]{:S(2)}) collective-permute-start(bf16[512,512]{1,0:T(8,128)(2,1)S(1)} %bitcast.59), channel_id=1, source_target_pairs={{0,8},{8,0},{1,9},{9,1},{2,10},{10,2},{3,11},{11,3},{4,12},{12,4},... | collective-permute-start | bytes 1572872 | tf_op jit(solution)/shard_map/ppermute | solution.py:34
  114.3 24.8 %all-to-all-start.4 = ((s16[8,64,1152]{2,1,0:T(8,128)(2,1)}), s16[8,64,1152]{2,1,0:T(8,128)(2,1)S(1)}, u32[]{:S(2)}, u32[]{:S(2)}) async-start(s16[8,64,1152]{2,1,0:T(8,128)(2,1)} %bitcast.55), calls=%async_computation.4 | async-start | bytes 2359296 | tf_op jit(solution)/shard_map/all_to_all | solution.py:49
  121.8 9.8 %collective-permute-start.7 = (bf16[2,64,1024]{2,1,0:T(8,128)(2,1)}, bf16[2,64,1024]{2,1,0:T(8,128)(2,1)}, u32[]{:S(2)}, u32[]{:S(2)}) collective-permute-start(bf16[2,64,1024]{2,1,0:T(8,128)(2,1)} %get-tuple-element.70), channel_id=1, source_target_pairs={{0,2},{2,4},{4,6},{6,0},{1,3},{3,5},{5,7},{7,1},{8,10},{10,12},{12... | collective-permute-start | bytes 786440 | tf_op jit(solution)/shard_map/ppermute | solution.py:312
  121.8 14.4 %collective-permute-start.9 = (bf16[2,64,1024]{2,1,0:T(8,128)(2,1)}, bf16[2,64,1024]{2,1,0:T(8,128)(2,1)}, u32[]{:S(2)}, u32[]{:S(2)}) collective-permute-start(bf16[2,64,1024]{2,1,0:T(8,128)(2,1)} %get-tuple-element.71), channel_id=1, source_target_pairs={{0,4},{2,6},{4,0},{6,2},{1,5},{3,7},{5,1},{7,3},{8,12},{10,14},{12... | collective-permute-start | bytes 786440 | tf_op jit(solution)/shard_map/ppermute | solution.py:312
  124.4 12.7 %collective-permute-start.8 = (bf16[2,64,1024]{2,1,0:T(8,128)(2,1)}, bf16[2,64,1024]{2,1,0:T(8,128)(2,1)}, u32[]{:S(2)}, u32[]{:S(2)}) collective-permute-start(bf16[2,64,1024]{2,1,0:T(8,128)(2,1)} %get-tuple-element.72), channel_id=1, source_target_pairs={{0,6},{2,0},{4,2},{6,4},{1,7},{3,1},{5,3},{7,5},{8,14},{10,8},{12,... | collective-permute-start | bytes 786440 | tf_op jit(solution)/shard_map/ppermute | solution.py:312
  141.1 25.0 %all-to-all-start.5 = ((bf16[8,64,1152]{2,1,0:T(8,128)(2,1)}), bf16[8,64,1152]{2,1,0:T(8,128)(2,1)S(1)}, u32[]{:S(2)}, u32[]{:S(2)}) async-start(bf16[8,64,1152]{2,1,0:T(8,128)(2,1)} %copy-done.6), calls=%async_computation.5 | async-start | bytes 2359296 | tf_op jit(solution)/shard_map/all_to_all | solution.py:49
  147.9 16.6 %collective-permute-start.10 = (bf16[64,1024]{1,0:T(8,128)(2,1)}, bf16[64,1024]{1,0:T(8,128)(2,1)}, u32[]{:S(2)}, u32[]{:S(2)}) collective-permute-start(bf16[64,1024]{1,0:T(8,128)(2,1)} %dynamic-slice_bitcast_fusion.3), channel_id=1, source_target_pairs={{0,1},{1,0},{2,3},{3,2},{4,5},{5,4},{6,7},{7,6},{8,9},{9,8},{10,11... | collective-permute-start | bytes 393224 | tf_op jit(solution)/shard_map/ppermute | solution.py:318
  156.7 7.7 %copy-start.17 = (bf16[2,64,1024]{2,1,0:T(8,128)(2,1)S(1)}, bf16[2,64,1024]{2,1,0:T(8,128)(2,1)}, u32[]{:S(2)}) copy-start(bf16[2,64,1024]{2,1,0:T(8,128)(2,1)} %fusion.20) | copy-start | bytes 786436
  166.0 2.8 %collective-permute-start.11 = (bf16[512,1152]{1,0:T(8,128)(2,1)S(1)}, bf16[512,1152]{1,0:T(8,128)(2,1)S(1)}, u32[]{:S(2)}, u32[]{:S(2)}) collective-permute-start(bf16[512,1152]{1,0:T(8,128)(2,1)S(1)} %bitcast.53), channel_id=1, source_target_pairs={{0,8},{8,0},{1,9},{9,1},{2,10},{10,2},{3,11},{11,3},{4,12},{12,4},... | collective-permute-start | bytes 3538952 | tf_op jit(solution)/shard_map/ppermute | solution.py:34
  171.1 16.4 %copy-start.16 = (f32[64,512]{1,0:T(8,128)S(1)}, f32[64,512]{1,0:T(8,128)}, u32[]{:S(2)}) copy-start(f32[64,512]{1,0:T(8,128)} %copy-done.15) | copy-start | bytes 393220
  171.1 15.8 %all-to-all-start.6 = ((bf16[8,64,640]{2,1,0:T(8,128)(2,1)}), bf16[8,64,640]{2,1,0:T(8,128)(2,1)S(1)}, u32[]{:S(2)}, u32[]{:S(2)}) async-start(bf16[8,64,640]{2,1,0:T(8,128)(2,1)} %bitcast.58), calls=%async_computation.6 | async-start | bytes 1310720 | tf_op jit(solution)/shard_map/all_to_all | solution.py:49
  187.5 23.7 %copy-start.5 = (bf16[1792,512]{1,0:T(8,128)(2,1)S(1)}, bf16[1792,512]{1,0:T(8,128)(2,1)}, u32[]{:S(2)}) copy-start(bf16[1792,512]{1,0:T(8,128)(2,1)} %down.1) | copy-start | bytes 5505028
  208.1 3.1 %collective-permute-start.12 = (bf16[512,1024]{1,0:T(8,128)(2,1)S(1)}, bf16[512,1024]{1,0:T(8,128)(2,1)S(1)}, u32[]{:S(2)}, u32[]{:S(2)}) collective-permute-start(bf16[512,1024]{1,0:T(8,128)(2,1)S(1)} %bitcast.62), channel_id=1, source_target_pairs={{0,8},{8,0},{1,9},{9,1},{2,10},{10,2},{3,11},{11,3},{4,12},{12,4},... | collective-permute-start | bytes 3145736 | tf_op jit(solution)/shard_map/ppermute | solution.py:34
  242.5 27.7 %copy-start.2 = (f32[512,1792]{1,0:T(8,128)S(1)}, f32[512,1792]{1,0:T(8,128)}, u32[]{:S(2)}) copy-start(f32[512,1792]{1,0:T(8,128)} %curve_ref.3) | copy-start | bytes 11010052
  242.8 27.4 %copy-start.10 = (bf16[512,512]{1,0:T(8,128)(2,1)S(1)}, bf16[512,512]{1,0:T(8,128)(2,1)}, u32[]{:S(2)}) copy-start(bf16[512,512]{1,0:T(8,128)(2,1)} %get-tuple-element.53.turned) | copy-start | bytes 1572868
  242.9 27.2 %copy-start.1 = (f32[512,1792]{1,0:T(8,128)S(1)}, f32[512,1792]{1,0:T(8,128)}, u32[]{:S(2)}) copy-start(f32[512,1792]{1,0:T(8,128)} %moment_ref.3) | copy-start | bytes 11010052
  268.5 5.5 %collective-permute-start.13 = (bf16[512,1792]{1,0:T(8,128)(2,1)S(1)}, bf16[512,1792]{1,0:T(8,128)(2,1)S(1)}, u32[]{:S(2)}, u32[]{:S(2)}) collective-permute-start(bf16[512,1792]{1,0:T(8,128)(2,1)S(1)} %bitcast.51), channel_id=1, source_target_pairs={{0,8},{8,0},{1,9},{9,1},{2,10},{10,2},{3,11},{11,3},{4,12},{12,4},... | collective-permute-start | bytes 5505032 | tf_op jit(solution)/shard_map/ppermute | solution.py:34
  (9 other events, 18.2 us)

commit v7 on v6

--- a/solution.py
+++ b/solution.py
@@ -295,22 +295,22 @@
     return keep, send
 
 
-def label_rows(labels, head_weight, unit_chip):
+def label_parts(labels, head_weight, unit_chip):
     ids = unit_chip * (2 * V_HALF) + lax.broadcasted_iota(jnp.int32, (1, 2 * V_HALF), 1)
     parts = []
     for which in range(2):
         hot = (labels[:, which : which + 1] == ids).astype(bf16)
         parts.append(dot_rows(hot, head_weight).astype(bf16))
-    return jnp.concatenate(parts, axis=1).reshape(4, 2, BLOCK, -1)
-
-
-def plane_label_rows(rows):
+    return plane_parts(jnp.concatenate(parts, axis=1).reshape(4, 2, BLOCK, -1))
+
+
+def plane_parts(rows):
     z = lax.axis_index("z")
-    total = lax.dynamic_index_in_dim(rows, z, 0, keepdims=False)
-    for shift in (1, 3, 2):
-        sent = lax.dynamic_index_in_dim(rows, (z + shift) % 4, 0, keepdims=False)
-        total = total + lax.ppermute(sent, "z", [(place, (place + shift) % 4) for place in range(4)])
-    return total
+    return [lax.dynamic_index_in_dim(rows, (z + shift) % 4, 0, keepdims=False) for shift in range(4)]
+
+
+def along_z(value, shift):
+    return lax.ppermute(value, "z", [(place, (place + shift) % 4) for place in range(4)])
 
 
 def own_label_rows(rows):
@@ -381,9 +381,9 @@
     all_labels = digits[:, :, :2] * PAD + digits[:, :, 2:]
     all_labels = jnp.where(core == 0, all_labels, all_labels[::-1]).reshape(count, 2)
     width_chip = lax.axis_index(WIDTH_CHIPS)
-    hidden_own, label_row, labels = together(
+    hidden_own, parts, labels = together(
         exchange(hidden, WIDTH_CHIPS),
-        label_rows(all_labels, head_weight, unit_chip),
+        label_parts(all_labels, head_weight, unit_chip),
         lax.dynamic_slice_in_dim(all_labels, width_chip * BLOCK, BLOCK, 0),
     )
     hidden_own = hidden_own.reshape(count, FF_HALF)
@@ -401,11 +401,17 @@
         [((count, width), bf16)],
         gate_up_flops,
     )
-    branch = exchange(branch.reshape(CHIPS, BLOCK, width), UNIT_CHIPS)
+    branch, parts[1] = together(branch, parts[1])
+    branch, parts[1] = together(
+        exchange(branch.reshape(CHIPS, BLOCK, width), UNIT_CHIPS), along_z(parts[1], 1)
+    )
     branch = jnp.sum(branch.astype(f32), axis=0)
     own_tokens = lax.dynamic_slice_in_dim(tokens, unit_chip * BLOCK, BLOCK, 0)
     summed = own_tokens.astype(f32) + branch
-    rows = to_all(summed.astype(bf16), UNIT_CHIPS).reshape(count, width)
+    rows = jnp.broadcast_to(summed.astype(bf16)[None], (CHIPS, BLOCK, width))
+    rows, parts[3] = together(rows, parts[3])
+    rows, parts[3] = together(exchange(rows, UNIT_CHIPS), along_z(parts[3], 3))
+    rows = rows.reshape(count, width)
 
     far_rows = other_core(rows)
     logit_flops = 4 * count * width * V_HALF
@@ -417,9 +423,9 @@
         [((count, V_HALF + PAD), jnp.int16)],
         logit_flops,
     )
-    raw, label_row = together(raw, label_row)
-    raw, label_row = together(
-        exchange(raw.reshape(CHIPS, BLOCK, V_HALF + PAD), WIDTH_CHIPS), plane_label_rows(label_row)
+    raw, parts[2] = together(raw, parts[2])
+    raw, parts[2] = together(
+        exchange(raw.reshape(CHIPS, BLOCK, V_HALF + PAD), WIDTH_CHIPS), along_z(parts[2], 2)
     )
     vocab_start = ((unit_chip * 2 + core) * V_HALF).astype(jnp.int32)
     packed = on_core(
@@ -430,14 +436,9 @@
         [((CHIPS, BLOCK, V_HALF + PAD), bf16)],
         1000000,
     )
-    packed, token_rows, label_row = together(packed, tokens, label_row)
-    turned = token_rows.T
-    turned_reverse = reverse_blocks(token_rows).T
-    packed_own, turned_own, turned_far, label_row = together(
-        exchange(packed, WIDTH_CHIPS),
-        jnp.where(core == 0, turned, turned_reverse),
-        jnp.where(core == 0, turned_reverse, turned),
-        own_label_rows(label_row),
+    packed, parts = together(packed, parts)
+    packed_own, label_row = together(
+        exchange(packed, WIDTH_CHIPS), own_label_rows(parts[0] + parts[1] + parts[2] + parts[3])
     )
     label_row = label_row.astype(f32)
     packed_own = packed_own.reshape(count, V_HALF + PAD)
@@ -482,7 +483,14 @@
         [((count, 2 * FF_HALF), bf16)],
         2 * gate_up_flops,
     )
-    dhidden = exchange(dhidden.reshape(CHIPS, BLOCK, 2 * FF_HALF), WIDTH_CHIPS)
+    dhidden, token_rows = together(dhidden, tokens)
+    turned = token_rows.T
+    turned_reverse = reverse_blocks(token_rows).T
+    dhidden, turned_own, turned_far = together(
+        exchange(dhidden.reshape(CHIPS, BLOCK, 2 * FF_HALF), WIDTH_CHIPS),
+        jnp.where(core == 0, turned, turned_reverse),
+        jnp.where(core == 0, turned_reverse, turned),
+    )
     dhidden = jnp.sum(dhidden.astype(f32), axis=0)
     cot = (dhidden * jnp.concatenate([silu_gate, silu_gate], axis=1)).astype(bf16)
     cot_own = to_all(cot, WIDTH_CHIPS).reshape(count, 2 * FF_HALF)

time: 279 us -> 287 us (1.029)
  waiting for transfers between devices: 70.5 us -> 114 us
  blocking collectives: 86 us -> 44.5 us
  starting transfers between devices: 52.7 us -> 61.8 us
    all_to_all x4 -> x2, blocking collectives: 86 us -> 44.5 us  [exchange(): lax.all_to_all(blocks, tuple(MESH_SIZES), split_axis=0, concat_axis=0, ti...]
    ppermute x3, waiting for transfers between devices: 12.2 us -> 31.6 us  [along_z(): lax.ppermute(value, 'z', [(place, (place + shift) % 4) for place in range...]
    all_to_all x6 -> x8, waiting for transfers between devices: 40.1 us -> 56 us  [exchange(): lax.all_to_all(blocks, tuple(MESH_SIZES), split_axis=0, concat_axis=0, ti...]
    all_to_all x6 -> x8, starting transfers between devices: 40.2 us -> 51.4 us  [exchange(): lax.all_to_all(blocks, tuple(MESH_SIZES), split_axis=0, concat_axis=0, ti...]
    ppermute x1, waiting for transfers between devices: 5.45 us -> 13.5 us  [own_label_rows(): return keep + lax.ppermute(send, 'xh', [(0, 1), (1, 0)])]
    unnamed x43 -> x47, local copies, waits for them, and re-layouts: 7.26 us -> 11.1 us
  transfers between devices with their start and end apart: 20 -> 22, of which waited for: 13 -> 14; matrix products, arithmetic and copies ran while one was open for 11% -> 7% of each run, Pallas kernels for 1% -> 1%
where the time goes in v7:
time: 287 us; the launch traced here: 286 us
  waiting for transfers between devices  114 us (40%)
  starting transfers between devices  61.8 us (22%)
  blocking collectives  44.5 us (16%)
  Pallas kernels  23.7 us (8%)
  local copies, waits for them, and re-layouts  20.8 us (7%)
  other arithmetic  11.3 us (4%)
  matrix products  8.69 us (3%)
    all_to_all x8, waiting for transfers between devices, exchange(): lax.all_to_all(blocks, tuple(MESH_SIZES), split_axis=0, concat_axis=0, ti...  56 us
    all_to_all x8, starting transfers between devices, exchange(): lax.all_to_all(blocks, tuple(MESH_SIZES), split_axis=0, concat_axis=0, ti...  51.4 us
    all_to_all x2, blocking collectives, exchange(): lax.all_to_all(blocks, tuple(MESH_SIZES), split_axis=0, concat_axis=0, ti...  44.5 us
    ppermute x3, waiting for transfers between devices, along_z(): lax.ppermute(value, 'z', [(place, (place + shift) % 4) for place in range...  31.6 us
    pallas_call x7, Pallas kernels, on_core(): pl.pallas_call(kernel, out_shape=tuple((jax.ShapeDtypeStruct(shape, dtype...  16.2 us
    ppermute x1, waiting for transfers between devices, own_label_rows(): return keep + lax.ppermute(send, 'xh', [(0, 1), (1, 0)])  13.5 us
    ppermute x10, waiting for transfers between devices, other_core(): return lax.ppermute(value, 'core', [(0, 1), (1, 0)])  12.7 us
    unnamed x47, local copies, waits for them, and re-layouts  11.1 us
  transfers between devices with their start and end apart: 22, of which 14 were waited for; matrix products, arithmetic and copies ran while one was open for 7% of the time, Pallas kernels for 1%

profile of v7, /device:TPU:1, one launch (start us, length us, event | category | flops | bytes accessed | tf_op | source)
XLA Modules:
  0.0 285.6 jit_solution(1169202567601363486)
XLA Ops:
  0.7 3.1 %fusion.9 = bf16[512,896]{1,0:T(8,128)(2,1)} fusion(bf16[512,512]{1,0:T(8,128)(2,1)} %tokens.1, bf16[512,1792]{1,0:T(8,128)(2,1)} %up.1, s32[]{:T(128)S(6)} %select_n.99), kind=kOutput, calls=%fused_computation.12 | convolution fusion | flops 470220800 | bytes 2359300 | tf_op jit(solution)/shard_map/dot_general | solution.py:82
  5.2 2.8 fusion.8
  13.3 4.8 %shard_map.112 = bf16[512,1920]{1,0:T(8,128)(2,1)} custom-call(s32[1]{0:T(128)} %bitcast.1.half_ref, bf16[512,512]{1,0:T(8,128)(2,1)} %tokens.1, bf16[512,1792]{1,0:T(8,128)(2,1)} %gate.1, bf16[512,1792]{1,0:T(8,128)(2,1)} %up.1, bf16[512,896]{1,0:T(8,128)(2,1)} %collective-permute-done.got_gate, bf16[512,896]{1,0:T(8,128)(2,1)} %copy-done.18, ...), custom_call_target="tpu_custom_call" | custom-call | flops 939524096 | bytes 6045696 | tf_op jit(solution)/shard_map/pallas_call | solution.py:108
  18.1 8.0 %all-to-all-start = ((bf16[8,64,1920]{2,1,0:T(8,128)(2,1)}), bf16[8,64,1920]{2,1,0:T(8,128)(2,1)}, u32[]{:S(2)}, u32[]{:S(2)}) async-start(bf16[8,64,1920]{2,1,0:T(8,128)(2,1)} %bitcast.60), calls=%async_computation | async-start | bytes 3932160 | tf_op jit(solution)/shard_map/all_to_all | solution.py:49
  26.6 3.6 %collective-permute-done.4.down_got = bf16[896,512]{1,0:T(8,128)(2,1)} collective-permute-done((bf16[896,512]{1,0:T(8,128)(2,1)}, bf16[896,512]{1,0:T(8,128)(2,1)}, u32[]{:S(2)}, u32[]{:S(2)}) %collective-permute-start.4) | collective-permute-done | bytes 917536 | tf_op jit(solution)/shard_map/ppermute | solution.py:34
  30.2 19.1 %all-to-all-done.both = bf16[8,64,1920]{2,1,0:T(8,128)(2,1)} async-done(((bf16[8,64,1920]{2,1,0:T(8,128)(2,1)}), bf16[8,64,1920]{2,1,0:T(8,128)(2,1)}, u32[]{:S(2)}, u32[]{:S(2)}) %all-to-all-start) | async-done | bytes 1966112 | tf_op jit(solution)/shard_map/all_to_all | solution.py:49
  52.1 4.9 %all-to-all-start.1 = ((bf16[8,64,896]{2,1,0:T(8,128)(2,1)}), bf16[8,64,896]{2,1,0:T(8,128)(2,1)S(1)}, u32[]{:S(2)}, u32[]{:S(2)}) async-start(bf16[8,64,896]{2,1,0:T(8,128)(2,1)} %copy-done.12), calls=%async_computation.1 | async-start | bytes 1835008 | tf_op jit(solution)/shard_map/all_to_all | solution.py:49
  62.2 2.3 copy.65
  64.4 2.1 dynamic-slice_bitcast_fusion
  66.5 2.5 all-to-all-done.1
  69.1 2.5 collective-permute-done.5.far
  73.0 2.0 shard_map.114
  75.1 9.4 %all-to-all-start.2 = ((bf16[8,64,512]{2,1,0:T(8,128)(2,1)}), bf16[8,64,512]{2,1,0:T(8,128)(2,1)S(1)}, u32[]{:S(2)}, u32[]{:S(2)}) async-start(bf16[8,64,512]{2,1,0:T(8,128)(2,1)} %bitcast.15), calls=%async_computation.2 | async-start | bytes 1048576 | tf_op jit(solution)/shard_map/all_to_all | solution.py:49
  85.0 11.8 %collective-permute-done.6 = bf16[2,64,1024]{2,1,0:T(8,128)(2,1)S(1)} collective-permute-done((bf16[2,64,1024]{2,1,0:T(8,128)(2,1)}, bf16[2,64,1024]{2,1,0:T(8,128)(2,1)S(1)}, u32[]{:S(2)}, u32[]{:S(2)}) %collective-permute-start.6) | collective-permute-done | bytes 262176 | tf_op jit(solution)/shard_map/ppermute | solution.py:313
  99.4 6.4 %all-to-all-start.3 = ((bf16[8,64,512]{2,1,0:T(8,128)(2,1)}), bf16[8,64,512]{2,1,0:T(8,128)(2,1)S(1)}, u32[]{:S(2)}, u32[]{:S(2)}) async-start(bf16[8,64,512]{2,1,0:T(8,128)(2,1)} %broadcast_in_dim.6), calls=%async_computation.3 | async-start | bytes 1048576 | tf_op jit(solution)/shard_map/all_to_all | solution.py:49
  106.0 12.3 %collective-permute-done.7 = bf16[2,64,1024]{2,1,0:T(8,128)(2,1)S(1)} collective-permute-done((bf16[2,64,1024]{2,1,0:T(8,128)(2,1)S(1)}, bf16[2,64,1024]{2,1,0:T(8,128)(2,1)S(1)}, u32[]{:S(2)}, u32[]{:S(2)}) %collective-permute-start.7) | collective-permute-done | bytes 262176 | tf_op jit(solution)/shard_map/ppermute | solution.py:313
  124.1 5.3 %all-to-all-start.4 = ((s16[8,64,1152]{2,1,0:T(8,128)(2,1)}), s16[8,64,1152]{2,1,0:T(8,128)(2,1)S(1)}, u32[]{:S(2)}, u32[]{:S(2)}) async-start(s16[8,64,1152]{2,1,0:T(8,128)(2,1)} %bitcast.51), calls=%async_computation.4 | async-start | bytes 2359296 | tf_op jit(solution)/shard_map/all_to_all | solution.py:49
  131.3 7.5 %collective-permute-done.9 = bf16[2,64,1024]{2,1,0:T(8,128)(2,1)} collective-permute-done((bf16[2,64,1024]{2,1,0:T(8,128)(2,1)}, bf16[2,64,1024]{2,1,0:T(8,128)(2,1)}, u32[]{:S(2)}, u32[]{:S(2)}) %collective-permute-start.9) | collective-permute-done | bytes 262176 | tf_op jit(solution)/shard_map/ppermute | solution.py:313
  138.8 5.5 %all-to-all-done.4.raw = s16[8,64,1152]{2,1,0:T(8,128)(2,1)S(1)} async-done(((s16[8,64,1152]{2,1,0:T(8,128)(2,1)}), s16[8,64,1152]{2,1,0:T(8,128)(2,1)S(1)}, u32[]{:S(2)}, u32[]{:S(2)}) %all-to-all-start.4) | async-done | bytes 1179680 | tf_op jit(solution)/shard_map/all_to_all | solution.py:49
  146.2 4.8 %all-to-all-start.5 = ((bf16[8,64,1152]{2,1,0:T(8,128)(2,1)}), bf16[8,64,1152]{2,1,0:T(8,128)(2,1)S(1)}, u32[]{:S(2)}, u32[]{:S(2)}) async-start(bf16[8,64,1152]{2,1,0:T(8,128)(2,1)} %copy-done.6), calls=%async_computation.5 | async-start | bytes 2359296 | tf_op jit(solution)/shard_map/all_to_all | solution.py:49
  155.5 13.5 %collective-permute-done.10 = bf16[64,1024]{1,0:T(8,128)(2,1)} collective-permute-done((bf16[64,1024]{1,0:T(8,128)(2,1)}, bf16[64,1024]{1,0:T(8,128)(2,1)}, u32[]{:S(2)}, u32[]{:S(2)}) %collective-permute-start.10) | collective-permute-done | bytes 131104 | tf_op jit(solution)/shard_map/ppermute | solution.py:318
  170.9 2.7 collective-permute-done.11.far
  175.8 6.9 %all-to-all-start.6 = ((bf16[8,64,640]{2,1,0:T(8,128)(2,1)}), bf16[8,64,640]{2,1,0:T(8,128)(2,1)S(1)}, u32[]{:S(2)}, u32[]{:S(2)}) async-start(bf16[8,64,640]{2,1,0:T(8,128)(2,1)} %bitcast.54), calls=%async_computation.6 | async-start | bytes 1310720 | tf_op jit(solution)/shard_map/all_to_all | solution.py:49
  184.3 7.5 %all-to-all-done.6 = bf16[8,64,640]{2,1,0:T(8,128)(2,1)S(1)} async-done(((bf16[8,64,640]{2,1,0:T(8,128)(2,1)}), bf16[8,64,640]{2,1,0:T(8,128)(2,1)S(1)}, u32[]{:S(2)}, u32[]{:S(2)}) %all-to-all-start.6) | async-done | bytes 655392 | tf_op jit(solution)/shard_map/all_to_all | solution.py:49
  193.8 18.9 %all_to_all.50 = bf16[8,64,1024]{2,1,0:T(8,128)(2,1)S(1)} all-to-all(bf16[8,64,1024]{2,1,0:T(8,128)(2,1)S(1)} %broadcast_in_dim.7), channel_id=1, replica_groups={{0,1,2,3,4,5,6,7},{15,14,13,12,11,10,9,8},{16,17,18,19,20,21,22,23},{31..., dimensions={0} | all-to-all | bytes 2097152 | tf_op jit(solution)/shard_map/all_to_all | solution.py:49
  213.9 2.3 collective-permute-done.12.far_dsummed
  216.1 3.5 %shard_map.118 = bf16[512,1792]{1,0:T(8,128)(2,1)S(1)} custom-call(s32[1]{0:T(128)} %bitcast.1.half_ref, bf16[512,1024]{1,0:T(8,128)(2,1)S(1)} %bitcast.59, bf16[512,1024]{1,0:T(8,128)(2,1)S(1)} %collective-permute-done.12.far_dsummed, bf16[1792,512]{1,0:T(8,128)(2,1)S(1)} %copy-done.5, bf16[896,512]{1,0:T(8,128)(2,1)} %collective-permute-done.4.down_got), custom_call_target="tpu_custom_call" | custom-call | flops 1879048192 | bytes 4849664 | tf_op jit(solution)/shard_map/pallas_call | solution.py:108
  220.9 5.8 %all-to-all-start.8 = ((bf16[8,64,1792]{2,1,0:T(8,128)(2,1)}), bf16[8,64,1792]{2,1,0:T(8,128)(2,1)}, u32[]{:S(2)}, u32[]{:S(2)}) async-start(bf16[8,64,1792]{2,1,0:T(8,128)(2,1)} %bitcast.57), calls=%async_computation.8 | async-start | bytes 3670016 | tf_op jit(solution)/shard_map/all_to_all | solution.py:49
  227.3 21.4 %all-to-all-done.8 = bf16[8,64,1792]{2,1,0:T(8,128)(2,1)} async-done(((bf16[8,64,1792]{2,1,0:T(8,128)(2,1)}), bf16[8,64,1792]{2,1,0:T(8,128)(2,1)}, u32[]{:S(2)}, u32[]{:S(2)}) %all-to-all-start.8) | async-done | bytes 1835040 | tf_op jit(solution)/shard_map/all_to_all | solution.py:49
  250.9 25.6 %all_to_all.51 = bf16[8,64,1792]{2,1,0:T(8,128)(2,1)S(1)} all-to-all(bf16[8,64,1792]{2,1,0:T(8,128)(2,1)S(1)} %broadcast_in_dim.8), channel_id=1, replica_groups={{0,16,32,48,64,80,96,112},{1,17,33,49,65,81,97,113},{2,18,34,50,66,82,9..., dimensions={0} | all-to-all | bytes 3670016 | tf_op jit(solution)/shard_map/all_to_all | solution.py:49
  278.1 3.7 %shard_map.119 = (f32[512,1792]{1,0:T(8,128)}, f32[512,1792]{1,0:T(8,128)}, f32[512,1792]{1,0:T(8,128)}) custom-call(s32[1]{0:T(128)} %bitcast.1.half_ref, bf16[512,512]{1,0:T(8,128)(2,1)S(1)} %get-tuple-element.85.turned, bf16[512,1792]{1,0:T(8,128)(2,1)S(1)} %bitcast.48, f32[512,1792]{1,0:T(8,128)S(1)} %copy-done.1, f32[512,1792]{1,0:T(8,128)S(1)} %copy-done.2), custom_call_target="tpu_custom_call" | custom-call | flops 950000000 | bytes 11000000 | tf_op jit(solution)/shard_map/pallas_call | solution.py:271
  281.9 3.7 %shard_map.120 = (f32[512,1792]{1,0:T(8,128)}, f32[512,1792]{1,0:T(8,128)}, f32[512,1792]{1,0:T(8,128)}) custom-call(s32[1]{0:T(128)} %bitcast.half_ref, bf16[512,512]{1,0:T(8,128)(2,1)S(1)} %get-tuple-element.82.turned, bf16[512,1792]{1,0:T(8,128)(2,1)S(1)} %collective-permute-done.13.cot, ...), custom_call_target="tpu_custom_call", output_to_operand_aliasing={{0}: (5, {}), {1}: (6, {}), {2}: (7, {})} | custom-call | flops 950000000 | bytes 11000000 | tf_op jit(solution)/shard_map/pallas_call | solution.py:271
  (117 shorter events, 48.3 us)
Async XLA Ops:
  0.7 7.4 %copy-start.21 = (s32[32]{0:T(128)S(1)}, s32[32]{0:T(128)}, u32[]{:S(2)}) copy-start(s32[32]{0:T(128)} %param.17) | copy-start | bytes 388
  0.7 7.4 %copy-start.22 = (s32[32]{0:T(128)S(1)}, s32[32]{0:T(128)}, u32[]{:S(2)}) copy-start(s32[32]{0:T(128)} %param.16) | copy-start | bytes 388
  0.7 8.0 %copy-start = (bf16[512,2048]{1,0:T(8,128)(2,1)S(1)}, bf16[512,2048]{1,0:T(8,128)(2,1)}, u32[]{:S(2)}) copy-start(bf16[512,2048]{1,0:T(8,128)(2,1)} %head_far.1) | copy-start | bytes 6291460
  3.8 8.6 %collective-permute-start.1 = (bf16[512,896]{1,0:T(8,128)(2,1)}, bf16[512,896]{1,0:T(8,128)(2,1)S(1)}, u32[]{:S(2)}, u32[]{:S(2)}) collective-permute-start(bf16[512,896]{1,0:T(8,128)(2,1)} %fusion.9), channel_id=1, source_target_pairs={{0,8},{8,0},{1,9},{9,1},{2,10},{10,2},{3,11},{11,3},{4,12},{12,4},... | collective-permute-start | bytes 2752520 | tf_op jit(solution)/shard_map/ppermute | solution.py:34
  8.0 4.3 %collective-permute-start = (bf16[512,896]{1,0:T(8,128)(2,1)}, bf16[512,896]{1,0:T(8,128)(2,1)}, u32[]{:S(2)}, u32[]{:S(2)}) collective-permute-start(bf16[512,896]{1,0:T(8,128)(2,1)} %fusion.8), channel_id=1, source_target_pairs={{0,8},{8,0},{1,9},{9,1},{2,10},{10,2},{3,11},{11,3},{4,12},{12,4},... | collective-permute-start | bytes 2752520 | tf_op jit(solution)/shard_map/ppermute | solution.py:34
  8.1 3.5 %collective-permute-start.2 = (s32[32,2]{0,1:T(2,128)S(1)}, s32[32,2]{0,1:T(2,128)S(1)}, u32[]{:S(2)}, u32[]{:S(2)}) collective-permute-start(s32[32,2]{0,1:T(2,128)S(1)} %pad_add_fusion), channel_id=1, source_target_pairs={{0,8},{8,0},{1,9},{9,1},{2,10},{10,2},{3,11},{11,3},{4,12},{12,4},... | collective-permute-start | bytes 776 | tf_op jit(solution)/shard_map/ppermute | solution.py:34
  18.1 31.3 %all-to-all-start = ((bf16[8,64,1920]{2,1,0:T(8,128)(2,1)}), bf16[8,64,1920]{2,1,0:T(8,128)(2,1)}, u32[]{:S(2)}, u32[]{:S(2)}) async-start(bf16[8,64,1920]{2,1,0:T(8,128)(2,1)} %bitcast.60), calls=%async_computation | async-start | bytes 3932160 | tf_op jit(solution)/shard_map/all_to_all | solution.py:49
  26.1 4.2 %collective-permute-start.3 = (bf16[512,1024]{1,0:T(8,128)(2,1)}, bf16[512,1024]{1,0:T(8,128)(2,1)S(1)}, u32[]{:S(2)}, u32[]{:S(2)}) collective-permute-start(bf16[512,1024]{1,0:T(8,128)(2,1)} %constant_dynamic-slice_fusion.2), channel_id=1, source_target_pairs={{0,8},{8,0},{1,9},{9,1},{2,10},{10,2},{3,11},{11,3},{4,12},{12,4},... | collective-permute-start | bytes 3145736 | tf_op jit(solution)/shard_map/ppermute | solution.py:34
  26.1 4.2 %collective-permute-start.4 = (bf16[896,512]{1,0:T(8,128)(2,1)}, bf16[896,512]{1,0:T(8,128)(2,1)}, u32[]{:S(2)}, u32[]{:S(2)}) collective-permute-start(bf16[896,512]{1,0:T(8,128)(2,1)} %constant_dynamic-slice_fusion.1), channel_id=1, source_target_pairs={{0,8},{8,0},{1,9},{9,1},{2,10},{10,2},{3,11},{11,3},{4,12},{12,4},... | collective-permute-start | bytes 2752520 | tf_op jit(solution)/shard_map/ppermute | solution.py:34
  30.2 21.9 %copy-start.10 = (bf16[512,1024]{1,0:T(8,128)(2,1)}, bf16[512,1024]{1,0:T(8,128)(2,1)S(1)}, u32[]{:S(2)}) copy-start(bf16[512,1024]{1,0:T(8,128)(2,1)S(1)} %collective-permute-done.3.head_got) | copy-start | bytes 3145732
  52.1 17.0 %all-to-all-start.1 = ((bf16[8,64,896]{2,1,0:T(8,128)(2,1)}), bf16[8,64,896]{2,1,0:T(8,128)(2,1)S(1)}, u32[]{:S(2)}, u32[]{:S(2)}) async-start(bf16[8,64,896]{2,1,0:T(8,128)(2,1)} %copy-done.12), calls=%async_computation.1 | async-start | bytes 1835008 | tf_op jit(solution)/shard_map/all_to_all | solution.py:49
  69.1 2.5 collective-permute-start.5
  75.1 22.5 %all-to-all-start.2 = ((bf16[8,64,512]{2,1,0:T(8,128)(2,1)}), bf16[8,64,512]{2,1,0:T(8,128)(2,1)S(1)}, u32[]{:S(2)}, u32[]{:S(2)}) async-start(bf16[8,64,512]{2,1,0:T(8,128)(2,1)} %bitcast.15), calls=%async_computation.2 | async-start | bytes 1048576 | tf_op jit(solution)/shard_map/all_to_all | solution.py:49
  84.4 12.4 %collective-permute-start.6 = (bf16[2,64,1024]{2,1,0:T(8,128)(2,1)}, bf16[2,64,1024]{2,1,0:T(8,128)(2,1)S(1)}, u32[]{:S(2)}, u32[]{:S(2)}) collective-permute-start(bf16[2,64,1024]{2,1,0:T(8,128)(2,1)} %get-tuple-element.56), channel_id=1, source_target_pairs={{0,2},{2,4},{4,6},{6,0},{1,3},{3,5},{5,7},{7,1},{8,10},{10,12},{12... | collective-permute-start | bytes 786440 | tf_op jit(solution)/shard_map/ppermute | solution.py:313
  97.6 25.5 %copy-start.15 = (f32[64,512]{1,0:T(8,128)}, f32[64,512]{1,0:T(8,128)S(1)}, u32[]{:S(2)}) copy-start(f32[64,512]{1,0:T(8,128)S(1)} %convert_reduce_fusion.1) | copy-start | bytes 393220
  99.4 18.9 %all-to-all-start.3 = ((bf16[8,64,512]{2,1,0:T(8,128)(2,1)}), bf16[8,64,512]{2,1,0:T(8,128)(2,1)S(1)}, u32[]{:S(2)}, u32[]{:S(2)}) async-start(bf16[8,64,512]{2,1,0:T(8,128)(2,1)} %broadcast_in_dim.6), calls=%async_computation.3 | async-start | bytes 1048576 | tf_op jit(solution)/shard_map/all_to_all | solution.py:49
  105.7 12.5 %collective-permute-start.7 = (bf16[2,64,1024]{2,1,0:T(8,128)(2,1)S(1)}, bf16[2,64,1024]{2,1,0:T(8,128)(2,1)S(1)}, u32[]{:S(2)}, u32[]{:S(2)}) collective-permute-start(bf16[2,64,1024]{2,1,0:T(8,128)(2,1)S(1)} %get-tuple-element.60), channel_id=1, source_target_pairs={{0,6},{2,0},{4,2},{6,4},{1,7},{3,1},{5,3},{7,5},{8,14},{10,8},{12,... | collective-permute-start | bytes 786440 | tf_op jit(solution)/shard_map/ppermute | solution.py:313
  118.3 1.9 collective-permute-start.8
  124.1 20.2 %all-to-all-start.4 = ((s16[8,64,1152]{2,1,0:T(8,128)(2,1)}), s16[8,64,1152]{2,1,0:T(8,128)(2,1)S(1)}, u32[]{:S(2)}, u32[]{:S(2)}) async-start(s16[8,64,1152]{2,1,0:T(8,128)(2,1)} %bitcast.51), calls=%async_computation.4 | async-start | bytes 2359296 | tf_op jit(solution)/shard_map/all_to_all | solution.py:49
  129.4 9.4 %collective-permute-start.9 = (bf16[2,64,1024]{2,1,0:T(8,128)(2,1)}, bf16[2,64,1024]{2,1,0:T(8,128)(2,1)}, u32[]{:S(2)}, u32[]{:S(2)}) collective-permute-start(bf16[2,64,1024]{2,1,0:T(8,128)(2,1)} %get-tuple-element.65), channel_id=1, source_target_pairs={{0,4},{2,6},{4,0},{6,2},{1,5},{3,7},{5,1},{7,3},{8,12},{10,14},{12... | collective-permute-start | bytes 786440 | tf_op jit(solution)/shard_map/ppermute | solution.py:313
  146.2 24.5 %all-to-all-start.5 = ((bf16[8,64,1152]{2,1,0:T(8,128)(2,1)}), bf16[8,64,1152]{2,1,0:T(8,128)(2,1)S(1)}, u32[]{:S(2)}, u32[]{:S(2)}) async-start(bf16[8,64,1152]{2,1,0:T(8,128)(2,1)} %copy-done.6), calls=%async_computation.5 | async-start | bytes 2359296 | tf_op jit(solution)/shard_map/all_to_all | solution.py:49
  153.7 15.4 %collective-permute-start.10 = (bf16[64,1024]{1,0:T(8,128)(2,1)}, bf16[64,1024]{1,0:T(8,128)(2,1)}, u32[]{:S(2)}, u32[]{:S(2)}) collective-permute-start(bf16[64,1024]{1,0:T(8,128)(2,1)} %dynamic-slice_bitcast_fusion.4), channel_id=1, source_target_pairs={{0,1},{1,0},{2,3},{3,2},{4,5},{5,4},{6,7},{7,6},{8,9},{9,8},{10,11... | collective-permute-start | bytes 393224 | tf_op jit(solution)/shard_map/ppermute | solution.py:318
  170.7 2.8 collective-permute-start.11
  175.8 16.5 %copy-start.14 = (bf16[512,512]{1,0:T(8,128)(2,1)S(1)}, bf16[512,512]{1,0:T(8,128)(2,1)}, u32[]{:S(2)}) copy-start(bf16[512,512]{1,0:T(8,128)(2,1)} %tokens.1) | copy-start | bytes 1572868
  175.8 16.5 %copy-start.16 = (f32[64,512]{1,0:T(8,128)S(1)}, f32[64,512]{1,0:T(8,128)}, u32[]{:S(2)}) copy-start(f32[64,512]{1,0:T(8,128)} %copy-done.15) | copy-start | bytes 393220
  175.8 16.0 %all-to-all-start.6 = ((bf16[8,64,640]{2,1,0:T(8,128)(2,1)}), bf16[8,64,640]{2,1,0:T(8,128)(2,1)S(1)}, u32[]{:S(2)}, u32[]{:S(2)}) async-start(bf16[8,64,640]{2,1,0:T(8,128)(2,1)} %bitcast.54), calls=%async_computation.6 | async-start | bytes 1310720 | tf_op jit(solution)/shard_map/all_to_all | solution.py:49
  192.4 23.8 %copy-start.5 = (bf16[1792,512]{1,0:T(8,128)(2,1)S(1)}, bf16[1792,512]{1,0:T(8,128)(2,1)}, u32[]{:S(2)}) copy-start(bf16[1792,512]{1,0:T(8,128)(2,1)} %down.1) | copy-start | bytes 5505028
  212.7 3.5 %collective-permute-start.12 = (bf16[512,1024]{1,0:T(8,128)(2,1)S(1)}, bf16[512,1024]{1,0:T(8,128)(2,1)S(1)}, u32[]{:S(2)}, u32[]{:S(2)}) collective-permute-start(bf16[512,1024]{1,0:T(8,128)(2,1)S(1)} %bitcast.58), channel_id=1, source_target_pairs={{0,8},{8,0},{1,9},{9,1},{2,10},{10,2},{3,11},{11,3},{4,12},{12,4},... | collective-permute-start | bytes 3145736 | tf_op jit(solution)/shard_map/ppermute | solution.py:34
  220.9 27.8 %all-to-all-start.8 = ((bf16[8,64,1792]{2,1,0:T(8,128)(2,1)}), bf16[8,64,1792]{2,1,0:T(8,128)(2,1)}, u32[]{:S(2)}, u32[]{:S(2)}) async-start(bf16[8,64,1792]{2,1,0:T(8,128)(2,1)} %bitcast.57), calls=%async_computation.8 | async-start | bytes 3670016 | tf_op jit(solution)/shard_map/all_to_all | solution.py:49
  248.7 29.4 %copy-start.2 = (f32[512,1792]{1,0:T(8,128)S(1)}, f32[512,1792]{1,0:T(8,128)}, u32[]{:S(2)}) copy-start(f32[512,1792]{1,0:T(8,128)} %curve_ref.3) | copy-start | bytes 11010052
  250.9 27.2 %copy-start.1 = (f32[512,1792]{1,0:T(8,128)S(1)}, f32[512,1792]{1,0:T(8,128)}, u32[]{:S(2)}) copy-start(f32[512,1792]{1,0:T(8,128)} %moment_ref.3) | copy-start | bytes 11010052
  276.5 5.3 %collective-permute-start.13 = (bf16[512,1792]{1,0:T(8,128)(2,1)S(1)}, bf16[512,1792]{1,0:T(8,128)(2,1)S(1)}, u32[]{:S(2)}, u32[]{:S(2)}) collective-permute-start(bf16[512,1792]{1,0:T(8,128)(2,1)S(1)} %bitcast.47), channel_id=1, source_target_pairs={{0,8},{8,0},{1,9},{9,1},{2,10},{10,2},{3,11},{11,3},{4,12},{12,4},... | collective-permute-start | bytes 5505032 | tf_op jit(solution)/shard_map/ppermute | solution.py:34
  (13 other events, 21.4 us)

commit v8 on v6

--- a/solution.py
+++ b/solution.py
@@ -289,33 +289,13 @@
     )(half.reshape(1), turned, cot, moment, curve, *done)
 
 
-def own_part(array, index, axis):
-    keep = lax.dynamic_index_in_dim(array, index, axis, keepdims=False)
-    send = lax.dynamic_index_in_dim(array, 1 - index, axis, keepdims=False)
-    return keep, send
-
-
 def label_rows(labels, head_weight, unit_chip):
     ids = unit_chip * (2 * V_HALF) + lax.broadcasted_iota(jnp.int32, (1, 2 * V_HALF), 1)
     parts = []
     for which in range(2):
         hot = (labels[:, which : which + 1] == ids).astype(bf16)
         parts.append(dot_rows(hot, head_weight).astype(bf16))
-    return jnp.concatenate(parts, axis=1).reshape(4, 2, BLOCK, -1)
-
-
-def plane_label_rows(rows):
-    z = lax.axis_index("z")
-    total = lax.dynamic_index_in_dim(rows, z, 0, keepdims=False)
-    for shift in (1, 3, 2):
-        sent = lax.dynamic_index_in_dim(rows, (z + shift) % 4, 0, keepdims=False)
-        total = total + lax.ppermute(sent, "z", [(place, (place + shift) % 4) for place in range(4)])
-    return total
-
-
-def own_label_rows(rows):
-    keep, send = own_part(rows, lax.axis_index("xh"), 0)
-    return keep + lax.ppermute(send, "xh", [(0, 1), (1, 0)])
+    return jnp.concatenate(parts, axis=1)
 
 
 def on_device(
@@ -386,6 +366,7 @@
         label_rows(all_labels, head_weight, unit_chip),
         lax.dynamic_slice_in_dim(all_labels, width_chip * BLOCK, BLOCK, 0),
     )
+    label_row = lax.psum_scatter(label_row, UNIT_CHIPS, scatter_dimension=0, tiled=True)
     hidden_own = hidden_own.reshape(count, FF_HALF)
     hidden_far = other_core(hidden_own)
     branch = on_core(
@@ -417,10 +398,7 @@
         [((count, V_HALF + PAD), jnp.int16)],
         logit_flops,
     )
-    raw, label_row = together(raw, label_row)
-    raw, label_row = together(
-        exchange(raw.reshape(CHIPS, BLOCK, V_HALF + PAD), WIDTH_CHIPS), plane_label_rows(label_row)
-    )
+    raw = exchange(raw.reshape(CHIPS, BLOCK, V_HALF + PAD), WIDTH_CHIPS)
     vocab_start = ((unit_chip * 2 + core) * V_HALF).astype(jnp.int32)
     packed = on_core(
         softmax_kernel,
@@ -430,16 +408,14 @@
         [((CHIPS, BLOCK, V_HALF + PAD), bf16)],
         1000000,
     )
-    packed, token_rows, label_row = together(packed, tokens, label_row)
+    packed, token_rows = together(packed, tokens)
     turned = token_rows.T
     turned_reverse = reverse_blocks(token_rows).T
-    packed_own, turned_own, turned_far, label_row = together(
+    packed_own, turned_own, turned_far = together(
         exchange(packed, WIDTH_CHIPS),
         jnp.where(core == 0, turned, turned_reverse),
         jnp.where(core == 0, turned_reverse, turned),
-        own_label_rows(label_row),
-    )
-    label_row = label_row.astype(f32)
+    )
     packed_own = packed_own.reshape(count, V_HALF + PAD)
     packed_far = other_core(packed_own)
     packed = on_core(
@@ -456,6 +432,8 @@
         logit_flops,
     )
     packed = exchange(packed.reshape(CHIPS, BLOCK, width + PAD), UNIT_CHIPS)
+    packed, label_row = together(packed, label_row)
+    label_row = label_row.astype(f32)
     stats = from_three(packed[:, :, width:], N_STATS)
     row_top = jnp.max(stats[:, :, 0:1], axis=0, keepdims=True)
     weight = jnp.exp(stats[:, :, 0:1] - row_top)

time: 279 us -> 326 us (1.17)
  waiting for transfers between devices: 70.5 us -> 115 us
  between operations: 0.99 us -> 14.4 us
  starting transfers between devices: 52.7 us -> 47.6 us
  other arithmetic: 12.7 us -> 8.25 us
    unnamed x0 -> x2, waiting for transfers between devices: none -> 49.3 us
    ppermute x4 -> x0, waiting for transfers between devices: 17.6 us -> none  [the longest x3 12.2 us: plane_label_rows(): lax.ppermute(sent, 'z', [(place, (place + shift) % 4) for place in range(...]
    all_to_all x6, waiting for transfers between devices: 40.1 us -> 53.2 us  [exchange(): lax.all_to_all(blocks, tuple(MESH_SIZES), split_axis=0, concat_axis=0, ti...]
    ppermute x4 -> x0, starting transfers between devices: 6 us -> none  [the longest x3 3.12 us: plane_label_rows(): lax.ppermute(sent, 'z', [(place, (place + shift) % 4) for place in range(...]
    squeeze x2 -> x0, local copies, waits for them, and re-layouts: 3.57 us -> none  [the longest x1 2.02 us: plane_label_rows(): sent = lax.dynamic_index_in_dim(rows, (z + shift) % 4, 0, keepdims=False)]
    add x2 -> x0, other arithmetic: 3.52 us -> none  [the longest x1 1.94 us: plane_label_rows(): total + lax.ppermute(sent, 'z', [(place, (place + shift) % 4) for place i...]
    unnamed x43 -> x41, local copies, waits for them, and re-layouts: 7.26 us -> 9.32 us
  transfers between devices with their start and end apart: 20 -> 17, of which waited for: 13 -> 11; matrix products, arithmetic and copies ran while one was open for 11% -> 7% of each run, Pallas kernels for 1% -> 2%
where the time goes in v8:
time: 326 us; the launch traced here: 325 us
  waiting for transfers between devices  115 us (35%)
  blocking collectives  85.6 us (26%)
  starting transfers between devices  47.6 us (15%)
  Pallas kernels  23.7 us (7%)
  local copies, waits for them, and re-layouts  21.2 us (7%)
  between operations  14.4 us (4%)
  matrix products  8.68 us (3%)
  other arithmetic  8.25 us (3%)
    all_to_all x4, blocking collectives, exchange(): lax.all_to_all(blocks, tuple(MESH_SIZES), split_axis=0, concat_axis=0, ti...  85.6 us
    all_to_all x6, waiting for transfers between devices, exchange(): lax.all_to_all(blocks, tuple(MESH_SIZES), split_axis=0, concat_axis=0, ti...  53.2 us
    unnamed x2, waiting for transfers between devices  49.3 us
    all_to_all x6, starting transfers between devices, exchange(): lax.all_to_all(blocks, tuple(MESH_SIZES), split_axis=0, concat_axis=0, ti...  40.7 us
    pallas_call x7, Pallas kernels, on_core(): pl.pallas_call(kernel, out_shape=tuple((jax.ShapeDtypeStruct(shape, dtype...  16.1 us
    ppermute x10, waiting for transfers between devices, other_core(): return lax.ppermute(value, 'core', [(0, 1), (1, 0)])  12.8 us
    unnamed x41, local copies, waits for them, and re-layouts  9.32 us
    pallas_call x2, Pallas kernels, sophia_half(): pl.pallas_call(step_kernel, out_shape=(shape, shape, shape), grid_spec=pl...  7.55 us
  transfers between devices with their start and end apart: 17, of which 11 were waited for; matrix products, arithmetic and copies ran while one was open for 7% of the time, Pallas kernels for 2%

profile of v8, /device:TPU:1, one launch (start us, length us, event | category | flops | bytes accessed | tf_op | source)
XLA Modules:
  0.0 324.7 jit_solution(16440251874624518591)
XLA Ops:
  7.2 3.1 fusion.9
  11.8 2.8 fusion.8
  19.8 4.8 %shard_map.112 = bf16[512,1920]{1,0:T(8,128)(2,1)} custom-call(s32[1]{0:T(128)} %bitcast.2.half_ref, bf16[512,512]{1,0:T(8,128)(2,1)} %tokens.1, bf16[512,1792]{1,0:T(8,128)(2,1)} %gate.1, bf16[512,1792]{1,0:T(8,128)(2,1)} %up.1, bf16[512,896]{1,0:T(8,128)(2,1)} %collective-permute-done.got_gate, bf16[512,896]{1,0:T(8,128)(2,1)} %copy-done.17, ...), custom_call_target="tpu_custom_call" | custom-call | flops 939524096 | bytes 6045696 | tf_op jit(solution)/shard_map/pallas_call | solution.py:108
  24.6 8.0 %all-to-all-start = ((bf16[8,64,1920]{2,1,0:T(8,128)(2,1)}), bf16[8,64,1920]{2,1,0:T(8,128)(2,1)}, u32[]{:S(2)}, u32[]{:S(2)}) async-start(bf16[8,64,1920]{2,1,0:T(8,128)(2,1)} %bitcast.48), calls=%async_computation | async-start | bytes 3932160 | tf_op jit(solution)/shard_map/all_to_all | solution.py:49
  33.1 3.6 %collective-permute-done.4.down_got = bf16[896,512]{1,0:T(8,128)(2,1)} collective-permute-done((bf16[896,512]{1,0:T(8,128)(2,1)}, bf16[896,512]{1,0:T(8,128)(2,1)}, u32[]{:S(2)}, u32[]{:S(2)}) %collective-permute-start.4) | collective-permute-done | bytes 917536 | tf_op jit(solution)/shard_map/ppermute | solution.py:34
  36.8 19.1 %all-to-all-done.both = bf16[8,64,1920]{2,1,0:T(8,128)(2,1)} async-done(((bf16[8,64,1920]{2,1,0:T(8,128)(2,1)}), bf16[8,64,1920]{2,1,0:T(8,128)(2,1)}, u32[]{:S(2)}, u32[]{:S(2)}) %all-to-all-start) | async-done | bytes 1966112 | tf_op jit(solution)/shard_map/all_to_all | solution.py:49
  58.6 4.9 %all-to-all-start.1 = ((bf16[8,64,896]{2,1,0:T(8,128)(2,1)}), bf16[8,64,896]{2,1,0:T(8,128)(2,1)S(1)}, u32[]{:S(2)}, u32[]{:S(2)}) async-start(bf16[8,64,896]{2,1,0:T(8,128)(2,1)} %copy-done.13), calls=%async_computation.1 | async-start | bytes 1835008 | tf_op jit(solution)/shard_map/all_to_all | solution.py:49
  68.7 6.9 %all-to-all-done.1 = bf16[8,64,896]{2,1,0:T(8,128)(2,1)S(1)} async-done(((bf16[8,64,896]{2,1,0:T(8,128)(2,1)}), bf16[8,64,896]{2,1,0:T(8,128)(2,1)S(1)}, u32[]{:S(2)}, u32[]{:S(2)}) %all-to-all-start.1) | async-done | bytes 917536 | tf_op jit(solution)/shard_map/all_to_all | solution.py:49
  75.6 2.5 collective-permute-done.5.far
  79.5 2.0 shard_map.114
  81.6 10.1 %all-to-all-start.2 = ((bf16[8,64,512]{2,1,0:T(8,128)(2,1)}), bf16[8,64,512]{2,1,0:T(8,128)(2,1)}, u32[]{:S(2)}, u32[]{:S(2)}) async-start(bf16[8,64,512]{2,1,0:T(8,128)(2,1)} %bitcast.10), calls=%async_computation.2 | async-start | bytes 1048576 | tf_op jit(solution)/shard_map/all_to_all | solution.py:49
  91.7 7.9 %all-to-all-done.2 = bf16[8,64,512]{2,1,0:T(8,128)(2,1)} async-done(((bf16[8,64,512]{2,1,0:T(8,128)(2,1)}), bf16[8,64,512]{2,1,0:T(8,128)(2,1)}, u32[]{:S(2)}, u32[]{:S(2)}) %all-to-all-start.2) | async-done | bytes 524320 | tf_op jit(solution)/shard_map/all_to_all | solution.py:49
  101.7 13.4 %all_to_all.50 = bf16[8,64,512]{2,1,0:T(8,128)(2,1)S(1)} all-to-all(bf16[8,64,512]{2,1,0:T(8,128)(2,1)S(1)} %broadcast_in_dim.6), channel_id=1, replica_groups={{0,1,2,3,4,5,6,7},{15,14,13,12,11,10,9,8},{16,17,18,19,20,21,22,23},{31..., dimensions={0} | all-to-all | bytes 1048576 | tf_op jit(solution)/shard_map/all_to_all | solution.py:49
  120.8 5.5 %all-to-all-start.4 = ((s16[8,64,1152]{2,1,0:T(8,128)(2,1)}), s16[8,64,1152]{2,1,0:T(8,128)(2,1)S(1)}, u32[]{:S(2)}, u32[]{:S(2)}) async-start(s16[8,64,1152]{2,1,0:T(8,128)(2,1)} %bitcast.39), calls=%async_computation.4 | async-start | bytes 2359296 | tf_op jit(solution)/shard_map/all_to_all | solution.py:49
  126.3 14.8 %all-to-all-done.4.raw = s16[8,64,1152]{2,1,0:T(8,128)(2,1)S(1)} async-done(((s16[8,64,1152]{2,1,0:T(8,128)(2,1)}), s16[8,64,1152]{2,1,0:T(8,128)(2,1)S(1)}, u32[]{:S(2)}, u32[]{:S(2)}) %all-to-all-start.4) | async-done | bytes 1179680 | tf_op jit(solution)/shard_map/all_to_all | solution.py:49
  143.1 4.8 %all-to-all-start.5 = ((bf16[8,64,1152]{2,1,0:T(8,128)(2,1)}), bf16[8,64,1152]{2,1,0:T(8,128)(2,1)S(1)}, u32[]{:S(2)}, u32[]{:S(2)}) async-start(bf16[8,64,1152]{2,1,0:T(8,128)(2,1)} %copy-done.6), calls=%async_computation.5 | async-start | bytes 2359296 | tf_op jit(solution)/shard_map/all_to_all | solution.py:49
  148.0 2.3 copy.57
  150.3 2.0 copy.49
  154.2 2.1 copy.50
  156.2 2.2 select_bitcast_fusion
  158.5 4.4 %all-to-all-done.5 = bf16[8,64,1152]{2,1,0:T(8,128)(2,1)S(1)} async-done(((bf16[8,64,1152]{2,1,0:T(8,128)(2,1)}), bf16[8,64,1152]{2,1,0:T(8,128)(2,1)S(1)}, u32[]{:S(2)}, u32[]{:S(2)}) %all-to-all-start.5) | async-done | bytes 1179680 | tf_op jit(solution)/shard_map/all_to_all | solution.py:49
  162.9 2.8 collective-permute-done.7.far
  168.0 7.4 %all-to-all-start.6 = ((bf16[8,64,640]{2,1,0:T(8,128)(2,1)}), bf16[8,64,640]{2,1,0:T(8,128)(2,1)S(1)}, u32[]{:S(2)}, u32[]{:S(2)}) async-start(bf16[8,64,640]{2,1,0:T(8,128)(2,1)} %bitcast.42), calls=%async_computation.6 | async-start | bytes 1310720 | tf_op jit(solution)/shard_map/all_to_all | solution.py:49
  175.4 49.3 %reduce-scatter.4.cloned.1.call-done = bf16[64,1024]{1,0:T(8,128)(2,1)} async-done(((bf16[512,1024]{1,0:T(8,128)(2,1)}), bf16[64,1024]{1,0:T(8,128)(2,1)}) %reduce-scatter.4.cloned.1.call-update) | async-done | bytes 131088
  228.9 18.8 %all_to_all.51 = bf16[8,64,1024]{2,1,0:T(8,128)(2,1)S(1)} all-to-all(bf16[8,64,1024]{2,1,0:T(8,128)(2,1)S(1)} %broadcast_in_dim.7), channel_id=1, replica_groups={{0,1,2,3,4,5,6,7},{15,14,13,12,11,10,9,8},{16,17,18,19,20,21,22,23},{31..., dimensions={0} | all-to-all | bytes 2097152 | tf_op jit(solution)/shard_map/all_to_all | solution.py:49
  247.7 2.0 collective-permute-start.8
  249.8 2.3 collective-permute-done.8.far_dsummed
  252.1 3.5 %shard_map.118 = bf16[512,1792]{1,0:T(8,128)(2,1)S(1)} custom-call(s32[1]{0:T(128)} %bitcast.2.half_ref, bf16[512,1024]{1,0:T(8,128)(2,1)S(1)} %bitcast.47, bf16[512,1024]{1,0:T(8,128)(2,1)S(1)} %collective-permute-done.8.far_dsummed, bf16[1792,512]{1,0:T(8,128)(2,1)S(1)} %copy-done.5, bf16[896,512]{1,0:T(8,128)(2,1)} %collective-permute-done.4.down_got), custom_call_target="tpu_custom_call" | custom-call | flops 1879048192 | bytes 4849664 | tf_op jit(solution)/shard_map/pallas_call | solution.py:108
  255.6 27.0 %all_to_all.52 = bf16[8,64,1792]{2,1,0:T(8,128)(2,1)S(1)} all-to-all(bf16[8,64,1792]{2,1,0:T(8,128)(2,1)S(1)} %bitcast.45), channel_id=1, replica_groups={{0,16,32,48,64,80,96,112},{1,17,33,49,65,81,97,113},{2,18,34,50,66,82,9..., dimensions={0} | all-to-all | bytes 3670016 | tf_op jit(solution)/shard_map/all_to_all | solution.py:49
  283.1 26.4 %all_to_all.53 = bf16[8,64,1792]{2,1,0:T(8,128)(2,1)S(1)} all-to-all(bf16[8,64,1792]{2,1,0:T(8,128)(2,1)S(1)} %broadcast_in_dim.8), channel_id=1, replica_groups={{0,16,32,48,64,80,96,112},{1,17,33,49,65,81,97,113},{2,18,34,50,66,82,9..., dimensions={0} | all-to-all | bytes 3670016 | tf_op jit(solution)/shard_map/all_to_all | solution.py:49
  310.3 3.8 %shard_map.119 = (f32[512,1792]{1,0:T(8,128)}, f32[512,1792]{1,0:T(8,128)}, f32[512,1792]{1,0:T(8,128)}) custom-call(s32[1]{0:T(128)} %bitcast.2.half_ref, bf16[512,512]{1,0:T(8,128)(2,1)S(1)} %copy-done.10, bf16[512,1792]{1,0:T(8,128)(2,1)S(1)} %bitcast.36, f32[512,1792]{1,0:T(8,128)S(1)} %copy-done.1, f32[512,1792]{1,0:T(8,128)S(1)} %copy-done.2), custom_call_target="tpu_custom_call" | custom-call | flops 950000000 | bytes 11000000 | tf_op jit(solution)/shard_map/pallas_call | solution.py:271
  314.1 3.8 %shard_map.120 = (f32[512,1792]{1,0:T(8,128)}, f32[512,1792]{1,0:T(8,128)}, f32[512,1792]{1,0:T(8,128)}) custom-call(s32[1]{0:T(128)} %bitcast.half_ref, bf16[512,512]{1,0:T(8,128)(2,1)S(1)} %copy-done.9, bf16[512,1792]{1,0:T(8,128)(2,1)S(1)} %collective-permute-done.9.cot, ...), custom_call_target="tpu_custom_call", output_to_operand_aliasing={{0}: (5, {}), {1}: (6, {}), {2}: (7, {})} | custom-call | flops 950000000 | bytes 11000000 | tf_op jit(solution)/shard_map/pallas_call | solution.py:271
  (101 shorter events, 35.8 us)
Async XLA Ops:
  7.2 4.6 %copy-start.14 = (bf16[512,512]{1,0:T(8,128)(2,1)S(1)}, bf16[512,512]{1,0:T(8,128)(2,1)}, u32[]{:S(2)}) copy-start(bf16[512,512]{1,0:T(8,128)(2,1)} %tokens.1) | copy-start | bytes 1572868
  7.2 7.4 %copy-start.18 = (s32[32]{0:T(128)S(1)}, s32[32]{0:T(128)}, u32[]{:S(2)}) copy-start(s32[32]{0:T(128)} %param.17) | copy-start | bytes 388
  7.2 7.4 %copy-start.19 = (s32[32]{0:T(128)S(1)}, s32[32]{0:T(128)}, u32[]{:S(2)}) copy-start(s32[32]{0:T(128)} %param.16) | copy-start | bytes 388
  7.2 8.0 %copy-start = (bf16[512,2048]{1,0:T(8,128)(2,1)S(1)}, bf16[512,2048]{1,0:T(8,128)(2,1)}, u32[]{:S(2)}) copy-start(bf16[512,2048]{1,0:T(8,128)(2,1)} %head_far.1) | copy-start | bytes 6291460
  10.3 8.6 %collective-permute-start.1 = (bf16[512,896]{1,0:T(8,128)(2,1)}, bf16[512,896]{1,0:T(8,128)(2,1)S(1)}, u32[]{:S(2)}, u32[]{:S(2)}) collective-permute-start(bf16[512,896]{1,0:T(8,128)(2,1)} %fusion.9), channel_id=1, source_target_pairs={{0,8},{8,0},{1,9},{9,1},{2,10},{10,2},{3,11},{11,3},{4,12},{12,4},... | collective-permute-start | bytes 2752520 | tf_op jit(solution)/shard_map/ppermute | solution.py:34
  14.6 4.3 %collective-permute-start = (bf16[512,896]{1,0:T(8,128)(2,1)}, bf16[512,896]{1,0:T(8,128)(2,1)}, u32[]{:S(2)}, u32[]{:S(2)}) collective-permute-start(bf16[512,896]{1,0:T(8,128)(2,1)} %fusion.8), channel_id=1, source_target_pairs={{0,8},{8,0},{1,9},{9,1},{2,10},{10,2},{3,11},{11,3},{4,12},{12,4},... | collective-permute-start | bytes 2752520 | tf_op jit(solution)/shard_map/ppermute | solution.py:34
  14.6 3.4 %collective-permute-start.2 = (s32[32,2]{0,1:T(2,128)S(1)}, s32[32,2]{0,1:T(2,128)S(1)}, u32[]{:S(2)}, u32[]{:S(2)}) collective-permute-start(s32[32,2]{0,1:T(2,128)S(1)} %pad_add_fusion), channel_id=1, source_target_pairs={{0,8},{8,0},{1,9},{9,1},{2,10},{10,2},{3,11},{11,3},{4,12},{12,4},... | collective-permute-start | bytes 776 | tf_op jit(solution)/shard_map/ppermute | solution.py:34
  15.2 1.9 copy-start.3
  24.6 31.3 %all-to-all-start = ((bf16[8,64,1920]{2,1,0:T(8,128)(2,1)}), bf16[8,64,1920]{2,1,0:T(8,128)(2,1)}, u32[]{:S(2)}, u32[]{:S(2)}) async-start(bf16[8,64,1920]{2,1,0:T(8,128)(2,1)} %bitcast.48), calls=%async_computation | async-start | bytes 3932160 | tf_op jit(solution)/shard_map/all_to_all | solution.py:49
  32.6 4.2 %collective-permute-start.3 = (bf16[512,1024]{1,0:T(8,128)(2,1)}, bf16[512,1024]{1,0:T(8,128)(2,1)S(1)}, u32[]{:S(2)}, u32[]{:S(2)}) collective-permute-start(bf16[512,1024]{1,0:T(8,128)(2,1)} %constant_dynamic-slice_fusion.2), channel_id=1, source_target_pairs={{0,8},{8,0},{1,9},{9,1},{2,10},{10,2},{3,11},{11,3},{4,12},{12,4},... | collective-permute-start | bytes 3145736 | tf_op jit(solution)/shard_map/ppermute | solution.py:34
  32.6 4.2 %collective-permute-start.4 = (bf16[896,512]{1,0:T(8,128)(2,1)}, bf16[896,512]{1,0:T(8,128)(2,1)}, u32[]{:S(2)}, u32[]{:S(2)}) collective-permute-start(bf16[896,512]{1,0:T(8,128)(2,1)} %constant_dynamic-slice_fusion.1), channel_id=1, source_target_pairs={{0,8},{8,0},{1,9},{9,1},{2,10},{10,2},{3,11},{11,3},{4,12},{12,4},... | collective-permute-start | bytes 2752520 | tf_op jit(solution)/shard_map/ppermute | solution.py:34
  36.7 21.9 %copy-start.11 = (bf16[512,1024]{1,0:T(8,128)(2,1)}, bf16[512,1024]{1,0:T(8,128)(2,1)S(1)}, u32[]{:S(2)}) copy-start(bf16[512,1024]{1,0:T(8,128)(2,1)S(1)} %collective-permute-done.3.head_got) | copy-start | bytes 3145732
  58.6 17.0 %all-to-all-start.1 = ((bf16[8,64,896]{2,1,0:T(8,128)(2,1)}), bf16[8,64,896]{2,1,0:T(8,128)(2,1)S(1)}, u32[]{:S(2)}, u32[]{:S(2)}) async-start(bf16[8,64,896]{2,1,0:T(8,128)(2,1)} %copy-done.13), calls=%async_computation.1 | async-start | bytes 1835008 | tf_op jit(solution)/shard_map/all_to_all | solution.py:49
  75.6 2.5 collective-permute-start.5
  78.0 1.5 copy-start.4
  81.6 36.5 %copy-start.12 = (bf16[512,1024]{1,0:T(8,128)(2,1)S(1)}, bf16[512,1024]{1,0:T(8,128)(2,1)}, u32[]{:S(2)}) copy-start(bf16[512,1024]{1,0:T(8,128)(2,1)} %copy-done.11) | copy-start | bytes 3145732
  81.6 18.0 %all-to-all-start.2 = ((bf16[8,64,512]{2,1,0:T(8,128)(2,1)}), bf16[8,64,512]{2,1,0:T(8,128)(2,1)}, u32[]{:S(2)}, u32[]{:S(2)}) async-start(bf16[8,64,512]{2,1,0:T(8,128)(2,1)} %bitcast.10), calls=%async_computation.2 | async-start | bytes 1048576 | tf_op jit(solution)/shard_map/all_to_all | solution.py:49
  100.8 19.0 %copy-start.15 = (f32[64,512]{1,0:T(8,128)}, f32[64,512]{1,0:T(8,128)S(1)}, u32[]{:S(2)}) copy-start(f32[64,512]{1,0:T(8,128)S(1)} %convert_reduce_fusion.1) | copy-start | bytes 393220
  115.1 3.0 collective-permute-start.6
  120.8 20.4 %all-to-all-start.4 = ((s16[8,64,1152]{2,1,0:T(8,128)(2,1)}), s16[8,64,1152]{2,1,0:T(8,128)(2,1)S(1)}, u32[]{:S(2)}, u32[]{:S(2)}) async-start(s16[8,64,1152]{2,1,0:T(8,128)(2,1)} %bitcast.39), calls=%async_computation.4 | async-start | bytes 2359296 | tf_op jit(solution)/shard_map/all_to_all | solution.py:49
  143.1 19.8 %all-to-all-start.5 = ((bf16[8,64,1152]{2,1,0:T(8,128)(2,1)}), bf16[8,64,1152]{2,1,0:T(8,128)(2,1)S(1)}, u32[]{:S(2)}, u32[]{:S(2)}) async-start(bf16[8,64,1152]{2,1,0:T(8,128)(2,1)} %copy-done.6), calls=%async_computation.5 | async-start | bytes 2359296 | tf_op jit(solution)/shard_map/all_to_all | solution.py:49
  148.0 76.7 %reduce-scatter.4.cloned.1.call-start = ((), (), s32[]{:S(2)}) async-start(), calls=%async_computation.11 | async-start | bytes 1179648
  162.9 2.8 collective-permute-start.7
  168.0 57.8 %all-to-all-start.6 = ((bf16[8,64,640]{2,1,0:T(8,128)(2,1)}), bf16[8,64,640]{2,1,0:T(8,128)(2,1)S(1)}, u32[]{:S(2)}, u32[]{:S(2)}) async-start(bf16[8,64,640]{2,1,0:T(8,128)(2,1)} %bitcast.42), calls=%async_computation.6 | async-start | bytes 1310720 | tf_op jit(solution)/shard_map/all_to_all | solution.py:49
  225.7 1.9 copy-start.16
  227.6 24.5 %copy-start.5 = (bf16[1792,512]{1,0:T(8,128)(2,1)S(1)}, bf16[1792,512]{1,0:T(8,128)(2,1)}, u32[]{:S(2)}) copy-start(bf16[1792,512]{1,0:T(8,128)(2,1)} %down.1) | copy-start | bytes 5505028
  247.7 4.3 %collective-permute-start.8 = (bf16[512,1024]{1,0:T(8,128)(2,1)S(1)}, bf16[512,1024]{1,0:T(8,128)(2,1)S(1)}, u32[]{:S(2)}, u32[]{:S(2)}) collective-permute-start(bf16[512,1024]{1,0:T(8,128)(2,1)S(1)} %bitcast.46), channel_id=1, source_target_pairs={{0,8},{8,0},{1,9},{9,1},{2,10},{10,2},{3,11},{11,3},{4,12},{12,4},... | collective-permute-start | bytes 3145736 | tf_op jit(solution)/shard_map/ppermute | solution.py:34
  282.6 27.7 %copy-start.2 = (f32[512,1792]{1,0:T(8,128)S(1)}, f32[512,1792]{1,0:T(8,128)}, u32[]{:S(2)}) copy-start(f32[512,1792]{1,0:T(8,128)} %curve_ref.3) | copy-start | bytes 11010052
  282.9 27.4 %copy-start.10 = (bf16[512,512]{1,0:T(8,128)(2,1)S(1)}, bf16[512,512]{1,0:T(8,128)(2,1)}, u32[]{:S(2)}) copy-start(bf16[512,512]{1,0:T(8,128)(2,1)} %get-tuple-element.45.turned) | copy-start | bytes 1572868
  283.1 27.3 %copy-start.1 = (f32[512,1792]{1,0:T(8,128)S(1)}, f32[512,1792]{1,0:T(8,128)}, u32[]{:S(2)}) copy-start(f32[512,1792]{1,0:T(8,128)} %moment_ref.3) | copy-start | bytes 11010052
  309.5 4.6 %copy-start.9 = (bf16[512,512]{1,0:T(8,128)(2,1)S(1)}, bf16[512,512]{1,0:T(8,128)(2,1)}, u32[]{:S(2)}) copy-start(bf16[512,512]{1,0:T(8,128)(2,1)} %get-tuple-element.38.turned) | copy-start | bytes 1572868
  309.5 4.6 %collective-permute-start.9 = (bf16[512,1792]{1,0:T(8,128)(2,1)S(1)}, bf16[512,1792]{1,0:T(8,128)(2,1)S(1)}, u32[]{:S(2)}, u32[]{:S(2)}) collective-permute-start(bf16[512,1792]{1,0:T(8,128)(2,1)S(1)} %bitcast.35), channel_id=1, source_target_pairs={{0,8},{8,0},{1,9},{9,1},{2,10},{10,2},{3,11},{11,3},{4,12},{12,4},... | collective-permute-start | bytes 5505032 | tf_op jit(solution)/shard_map/ppermute | solution.py:34
  (5 other events, 4.7 us)
Sparse Core Ops, SparseCore 0:
  153.0 71.6 reduce-scatter.3

commit v9 on v6

--- a/solution.py
+++ b/solution.py
@@ -120,10 +120,10 @@
     return results if len(outs) > 1 else results[0]
 
 
-def gate_up_own(half_ref, tokens, gate, up, got_gate, got_up, labels, out):
+def gate_up_pack(half_ref, own_gate, own_up, got_gate, got_up, labels, out):
     core = half_ref[0]
-    gate_sum = (dot(tokens[...], gate[...]) + got_gate[...].astype(f32)).astype(bf16)
-    up_sum = (dot(tokens[...], up[...]) + got_up[...].astype(f32)).astype(bf16)
+    gate_sum = (own_gate[...] + got_gate[...].astype(f32)).astype(bf16)
+    up_sum = (own_up[...] + got_up[...].astype(f32)).astype(bf16)
     for block in range(CHIPS):
         place = block + core * (CHIPS - 1 - 2 * block)
         rows = pl.ds(pl.multiple_of(place * BLOCK, BLOCK), BLOCK)
@@ -301,21 +301,22 @@
     for which in range(2):
         hot = (labels[:, which : which + 1] == ids).astype(bf16)
         parts.append(dot_rows(hot, head_weight).astype(bf16))
-    return jnp.concatenate(parts, axis=1).reshape(4, 2, BLOCK, -1)
+    return jnp.concatenate(parts, axis=1).reshape(2, 2, 2, BLOCK, -1)
+
+
+def near_label_rows(rows):
+    keep, send = own_part(rows, lax.axis_index("z") % 2, 1)
+    return keep + lax.ppermute(send, "z", [(0, 1), (1, 0), (2, 3), (3, 2)])
 
 
 def plane_label_rows(rows):
-    z = lax.axis_index("z")
-    total = lax.dynamic_index_in_dim(rows, z, 0, keepdims=False)
-    for shift in (1, 3, 2):
-        sent = lax.dynamic_index_in_dim(rows, (z + shift) % 4, 0, keepdims=False)
-        total = total + lax.ppermute(sent, "z", [(place, (place + shift) % 4) for place in range(4)])
-    return total
-
-
-def own_label_rows(rows):
-    keep, send = own_part(rows, lax.axis_index("xh"), 0)
-    return keep + lax.ppermute(send, "xh", [(0, 1), (1, 0)])
+    keep, send = own_part(rows, lax.axis_index("z") // 2, 0)
+    rows = keep + lax.ppermute(send, "z", [(0, 2), (2, 0), (1, 3), (3, 1)])
+    return own_part(rows, lax.axis_index("xh"), 0)
+
+
+def other_plane(rows):
+    return lax.ppermute(rows, "xh", [(0, 1), (1, 0)])
 
 
 def on_device(
@@ -344,24 +345,28 @@
     digits = jnp.concatenate([labels // PAD, labels % PAD], axis=1).astype(bf16)
     digits = jnp.pad(digits, ((0, 0), (0, PAD - 4)))
 
-    w_specs = [whole(tokens), columns_of(gate_weight, FF_HALF), columns_of(up_weight, FF_HALF)]
     gate_up_flops = 4 * count * width * FF_HALF
-    far_gate = lax.dynamic_slice_in_dim(gate_weight, far * FF_HALF, FF_HALF, 1)
-    far_up = lax.dynamic_slice_in_dim(up_weight, far * FF_HALF, FF_HALF, 1)
-    got_gate = other_core(dot(tokens, far_gate).astype(bf16))
-    got_up = other_core(dot(tokens, far_up).astype(bf16))
+
+    def gate_up(half):
+        gate = lax.dynamic_slice_in_dim(gate_weight, half * FF_HALF, FF_HALF, 1)
+        upper = lax.dynamic_slice_in_dim(up_weight, half * FF_HALF, FF_HALF, 1)
+        return dot(tokens, gate), dot(tokens, upper)
+
+    far_gate, far_up = gate_up(far)
+    got_gate, got_up = other_core(far_gate.astype(bf16)), other_core(far_up.astype(bf16))
+    own_gate, own_up = gate_up(core)
+    operands = (own_gate, own_up, got_gate, got_up, digits)
     both = on_core(
-        gate_up_own,
+        gate_up_pack,
         core,
-        (tokens, gate_weight, up_weight, got_gate, got_up, digits),
-        w_specs + [whole(got_gate), whole(got_up), whole(digits)],
+        operands,
+        [whole(operand) for operand in operands],
         [((count, 2 * FF_HALF + PAD), bf16)],
-        gate_up_flops,
-        60 * 1024 * 1024,
-    )
-    head_send = lax.dynamic_slice_in_dim(head_weight, far * V_HALF, V_HALF, 1)
-    down_send = lax.dynamic_slice_in_dim(down_weight, far * FF_HALF, FF_HALF, 0)
-    both, head_send, down_send = together(both, head_send, down_send)
+        1000000,
+    )
+    both, sent_head, sent_down = together(both, head_weight, down_weight)
+    head_send = lax.dynamic_slice_in_dim(sent_head, far * V_HALF, V_HALF, 1)
+    down_send = lax.dynamic_slice_in_dim(sent_down, far * FF_HALF, FF_HALF, 0)
     both, head_got, down_got = together(
         exchange(both.reshape(CHIPS, BLOCK, 2 * FF_HALF + PAD), WIDTH_CHIPS),
         other_core(head_send),
@@ -419,7 +424,7 @@
     )
     raw, label_row = together(raw, label_row)
     raw, label_row = together(
-        exchange(raw.reshape(CHIPS, BLOCK, V_HALF + PAD), WIDTH_CHIPS), plane_label_rows(label_row)
+        exchange(raw.reshape(CHIPS, BLOCK, V_HALF + PAD), WIDTH_CHIPS), near_label_rows(label_row)
     )
     vocab_start = ((unit_chip * 2 + core) * V_HALF).astype(jnp.int32)
     packed = on_core(
@@ -437,9 +442,10 @@
         exchange(packed, WIDTH_CHIPS),
         jnp.where(core == 0, turned, turned_reverse),
         jnp.where(core == 0, turned_reverse, turned),
-        own_label_rows(label_row),
-    )
-    label_row = label_row.astype(f32)
+        plane_label_rows(label_row),
+    )
+    label_row, label_sent = label_row
+    label_row = label_row.astype(f32) + other_plane(label_sent).astype(f32)
     packed_own = packed_own.reshape(count, V_HALF + PAD)
     packed_far = other_core(packed_own)
     packed = on_core(
@@ -455,6 +461,7 @@
         [((count, width + PAD), bf16)],
         logit_flops,
     )
+    packed, label_row = together(packed, label_row)
     packed = exchange(packed.reshape(CHIPS, BLOCK, width + PAD), UNIT_CHIPS)
     stats = from_three(packed[:, :, width:], N_STATS)
     row_top = jnp.max(stats[:, :, 0:1], axis=0, keepdims=True)

time: 279 us -> 277 us (level)
  blocking collectives: 86 us -> 101 us
  waiting for transfers between devices: 70.5 us -> 57.9 us
  starting transfers between devices: 52.7 us -> 45.8 us
  Pallas kernels: 23.7 us -> 20.4 us
    all_to_all x4 -> x5, blocking collectives: 86 us -> 101 us  [exchange(): lax.all_to_all(blocks, tuple(MESH_SIZES), split_axis=0, concat_axis=0, ti...]
    all_to_all x6 -> x5, waiting for transfers between devices: 40.1 us -> 32.2 us  [exchange(): lax.all_to_all(blocks, tuple(MESH_SIZES), split_axis=0, concat_axis=0, ti...]
    all_to_all x6 -> x5, starting transfers between devices: 40.2 us -> 34.5 us  [exchange(): lax.all_to_all(blocks, tuple(MESH_SIZES), split_axis=0, concat_axis=0, ti...]
    ppermute x10, waiting for transfers between devices: 12.8 us -> 9.12 us  [other_core(): return lax.ppermute(value, 'core', [(0, 1), (1, 0)])]
    pallas_call x7, Pallas kernels: 16.1 us -> 12.9 us  [on_core(): pl.pallas_call(kernel, out_shape=tuple((jax.ShapeDtypeStruct(shape, dtype...]
    dot_general x2 -> x4, matrix products: 5.94 us -> 8.57 us  [dot(): return jnp.dot(left, right, preferred_element_type=f32)]
    unnamed x43 -> x53, local copies, waits for them, and re-layouts: 7.26 us -> 9.79 us
    ppermute x4 -> x3, starting transfers between devices: 6 us -> 4.07 us  [the longest x1 2.87 us: other_plane(): return lax.ppermute(rows, 'xh', [(0, 1), (1, 0)])]
  transfers between devices with their start and end apart: 20 -> 18, of which waited for: 13 -> 10; matrix products, arithmetic and copies ran while one was open for 11% -> 13% of each run, Pallas kernels for 1% -> 1%
where the time goes in v9:
time: 277 us; the launch traced here: 276 us
  blocking collectives  101 us (36%)
  waiting for transfers between devices  57.9 us (21%)
  starting transfers between devices  45.8 us (17%)
  local copies, waits for them, and re-layouts  25.1 us (9%)
  Pallas kernels  20.4 us (7%)
  other arithmetic  13.7 us (5%)
  matrix products  11.3 us (4%)
    all_to_all x5, blocking collectives, exchange(): lax.all_to_all(blocks, tuple(MESH_SIZES), split_axis=0, concat_axis=0, ti...  101 us
    all_to_all x5, starting transfers between devices, exchange(): lax.all_to_all(blocks, tuple(MESH_SIZES), split_axis=0, concat_axis=0, ti...  34.5 us
    all_to_all x5, waiting for transfers between devices, exchange(): lax.all_to_all(blocks, tuple(MESH_SIZES), split_axis=0, concat_axis=0, ti...  32.2 us
    ppermute x1, waiting for transfers between devices, near_label_rows(): return keep + lax.ppermute(send, 'z', [(0, 1), (1, 0), (2, 3), (3, 2)])  13.2 us
    pallas_call x7, Pallas kernels, on_core(): pl.pallas_call(kernel, out_shape=tuple((jax.ShapeDtypeStruct(shape, dtype...  12.9 us
    unnamed x53, local copies, waits for them, and re-layouts  9.79 us
    ppermute x10, waiting for transfers between devices, other_core(): return lax.ppermute(value, 'core', [(0, 1), (1, 0)])  9.12 us
    dot_general x4, matrix products, dot(): return jnp.dot(left, right, preferred_element_type=f32)  8.57 us
  transfers between devices with their start and end apart: 18, of which 10 were waited for; matrix products, arithmetic and copies ran while one was open for 13% of the time, Pallas kernels for 1%

profile of v9, /device:TPU:1, one launch (start us, length us, event | category | flops | bytes accessed | tf_op | source)
XLA Modules:
  0.0 275.8 jit_solution(10493386759317176565)
XLA Ops:
  2.9 3.0 %fusion.9 = bf16[512,896]{1,0:T(8,128)(2,1)} fusion(bf16[512,512]{1,0:T(8,128)(2,1)} %param.9, bf16[512,1792]{1,0:T(8,128)(2,1)} %param.11, s32[]{:T(128)S(6)} %select_n.97), kind=kOutput, calls=%fused_computation.14 | convolution fusion | flops 470220800 | bytes 2359300 | tf_op jit(solution)/shard_map/dot_general | solution.py:82
  10.1 1.9 convolution_bitcast_fusion.own_up
  18.1 8.1 %all-to-all-start = ((bf16[8,64,1920]{2,1,0:T(8,128)(2,1)}), bf16[8,64,1920]{2,1,0:T(8,128)(2,1)}, u32[]{:S(2)}, u32[]{:S(2)}) async-start(bf16[8,64,1920]{2,1,0:T(8,128)(2,1)} %bitcast.53), calls=%async_computation | async-start | bytes 3932160 | tf_op jit(solution)/shard_map/all_to_all | solution.py:49
  29.1 2.8 %collective-permute-done.4.down_got = bf16[896,512]{1,0:T(8,128)(2,1)} collective-permute-done((bf16[896,512]{1,0:T(8,128)(2,1)}, bf16[896,512]{1,0:T(8,128)(2,1)}, u32[]{:S(2)}, u32[]{:S(2)}) %collective-permute-start.4) | collective-permute-done | bytes 917536 | tf_op jit(solution)/shard_map/ppermute | solution.py:34
  31.9 17.6 %all-to-all-done.both = bf16[8,64,1920]{2,1,0:T(8,128)(2,1)} async-done(((bf16[8,64,1920]{2,1,0:T(8,128)(2,1)}), bf16[8,64,1920]{2,1,0:T(8,128)(2,1)}, u32[]{:S(2)}, u32[]{:S(2)}) %all-to-all-start) | async-done | bytes 1966112 | tf_op jit(solution)/shard_map/all_to_all | solution.py:49
  52.2 4.9 %all-to-all-start.1 = ((bf16[8,64,896]{2,1,0:T(8,128)(2,1)}), bf16[8,64,896]{2,1,0:T(8,128)(2,1)S(1)}, u32[]{:S(2)}, u32[]{:S(2)}) async-start(bf16[8,64,896]{2,1,0:T(8,128)(2,1)} %copy-done.17), calls=%async_computation.1 | async-start | bytes 1835008 | tf_op jit(solution)/shard_map/all_to_all | solution.py:49
  62.3 2.3 copy.77
  64.5 4.6 %all-to-all-done.1 = bf16[8,64,896]{2,1,0:T(8,128)(2,1)S(1)} async-done(((bf16[8,64,896]{2,1,0:T(8,128)(2,1)}), bf16[8,64,896]{2,1,0:T(8,128)(2,1)S(1)}, u32[]{:S(2)}, u32[]{:S(2)}) %all-to-all-start.1) | async-done | bytes 917536 | tf_op jit(solution)/shard_map/all_to_all | solution.py:49
  69.2 2.5 collective-permute-done.5.far
  73.1 2.0 shard_map.114
  75.2 10.1 %all-to-all-start.2 = ((bf16[8,64,512]{2,1,0:T(8,128)(2,1)}), bf16[8,64,512]{2,1,0:T(8,128)(2,1)}, u32[]{:S(2)}, u32[]{:S(2)}) async-start(bf16[8,64,512]{2,1,0:T(8,128)(2,1)} %bitcast.13), calls=%async_computation.2 | async-start | bytes 1048576 | tf_op jit(solution)/shard_map/all_to_all | solution.py:49
  85.3 7.9 %all-to-all-done.2 = bf16[8,64,512]{2,1,0:T(8,128)(2,1)} async-done(((bf16[8,64,512]{2,1,0:T(8,128)(2,1)}), bf16[8,64,512]{2,1,0:T(8,128)(2,1)}, u32[]{:S(2)}, u32[]{:S(2)}) %all-to-all-start.2) | async-done | bytes 524320 | tf_op jit(solution)/shard_map/all_to_all | solution.py:49
  95.3 13.4 %all_to_all.50 = bf16[8,64,512]{2,1,0:T(8,128)(2,1)S(1)} all-to-all(bf16[8,64,512]{2,1,0:T(8,128)(2,1)S(1)} %broadcast_in_dim.6), channel_id=1, replica_groups={{0,1,2,3,4,5,6,7},{15,14,13,12,11,10,9,8},{16,17,18,19,20,21,22,23},{31..., dimensions={0} | all-to-all | bytes 1048576 | tf_op jit(solution)/shard_map/all_to_all | solution.py:49
  114.4 5.6 %all-to-all-start.4 = ((s16[8,64,1152]{2,1,0:T(8,128)(2,1)}), s16[8,64,1152]{2,1,0:T(8,128)(2,1)S(1)}, u32[]{:S(2)}, u32[]{:S(2)}) async-start(s16[8,64,1152]{2,1,0:T(8,128)(2,1)} %bitcast.58), calls=%async_computation.4 | async-start | bytes 2359296 | tf_op jit(solution)/shard_map/all_to_all | solution.py:49
  121.8 13.2 %collective-permute-done.7 = bf16[2,2,64,1024]{3,2,1,0:T(8,128)(2,1)} collective-permute-done((bf16[2,2,64,1024]{3,2,1,0:T(8,128)(2,1)}, bf16[2,2,64,1024]{3,2,1,0:T(8,128)(2,1)}, u32[]{:S(2)}, u32[]{:S(2)}) %collective-permute-start.7) | collective-permute-done | bytes 524320 | tf_op jit(solution)/shard_map/ppermute | solution.py:309
  135.0 2.1 bitcast_add_fusion
  139.0 5.9 %all-to-all-start.5 = ((bf16[8,64,1152]{2,1,0:T(8,128)(2,1)}), bf16[8,64,1152]{2,1,0:T(8,128)(2,1)S(1)}, u32[]{:S(2)}, u32[]{:S(2)}) async-start(bf16[8,64,1152]{2,1,0:T(8,128)(2,1)} %copy-done.11), calls=%async_computation.5 | async-start | bytes 2359296 | tf_op jit(solution)/shard_map/all_to_all | solution.py:49
  147.7 2.1 copy.78
  151.6 2.0 copy.79
  153.7 2.3 select_bitcast_fusion
  157.7 2.1 all-to-all-done.5
  159.8 2.9 %collective-permute-start.10 = (bf16[64,1024]{1,0:T(8,128)(2,1)}, bf16[64,1024]{1,0:T(8,128)(2,1)S(1)}, u32[]{:S(2)}, u32[]{:S(2)}) collective-permute-start(bf16[64,1024]{1,0:T(8,128)(2,1)} %get-tuple-element.54), channel_id=1, source_target_pairs={{0,1},{1,0},{2,3},{3,2},{4,5},{5,4},{6,7},{7,6},{8,9},{9,8},{10,11... | collective-permute-start | bytes 393224 | tf_op jit(solution)/shard_map/ppermute | solution.py:319
  162.7 3.4 %collective-permute-done.10 = bf16[64,1024]{1,0:T(8,128)(2,1)S(1)} collective-permute-done((bf16[64,1024]{1,0:T(8,128)(2,1)}, bf16[64,1024]{1,0:T(8,128)(2,1)S(1)}, u32[]{:S(2)}, u32[]{:S(2)}) %collective-permute-start.10) | collective-permute-done | bytes 131104 | tf_op jit(solution)/shard_map/ppermute | solution.py:319
  169.1 14.0 %all_to_all.51 = bf16[8,64,640]{2,1,0:T(8,128)(2,1)S(1)} all-to-all(bf16[8,64,640]{2,1,0:T(8,128)(2,1)S(1)} %bitcast.61), channel_id=1, replica_groups={{0,1,2,3,4,5,6,7},{15,14,13,12,11,10,9,8},{16,17,18,19,20,21,22,23},{31..., dimensions={0} | all-to-all | bytes 1310720 | tf_op jit(solution)/shard_map/all_to_all | solution.py:49
  184.9 19.9 %all_to_all.52 = bf16[8,64,1024]{2,1,0:T(8,128)(2,1)S(1)} all-to-all(bf16[8,64,1024]{2,1,0:T(8,128)(2,1)S(1)} %broadcast_in_dim.7), channel_id=1, replica_groups={{0,1,2,3,4,5,6,7},{15,14,13,12,11,10,9,8},{16,17,18,19,20,21,22,23},{31..., dimensions={0} | all-to-all | bytes 2097152 | tf_op jit(solution)/shard_map/all_to_all | solution.py:49
  204.7 2.2 collective-permute-start.11
  207.0 2.3 collective-permute-done.11.far_dsummed
  209.2 3.5 %shard_map.118 = bf16[512,1792]{1,0:T(8,128)(2,1)S(1)} custom-call(s32[1]{0:T(128)} %bitcast.2.half_ref, bf16[512,1024]{1,0:T(8,128)(2,1)S(1)} %bitcast.66, bf16[512,1024]{1,0:T(8,128)(2,1)S(1)} %collective-permute-done.11.far_dsummed, bf16[1792,512]{1,0:T(8,128)(2,1)S(1)} %copy-done.7, bf16[896,512]{1,0:T(8,128)(2,1)} %collective-permute-done.4.down_got), custom_call_target="tpu_custom_call" | custom-call | flops 1879048192 | bytes 4849664 | tf_op jit(solution)/shard_map/pallas_call | solution.py:108
  212.8 27.5 %all_to_all.53 = bf16[8,64,1792]{2,1,0:T(8,128)(2,1)S(1)} all-to-all(bf16[8,64,1792]{2,1,0:T(8,128)(2,1)S(1)} %bitcast.64), channel_id=1, replica_groups={{0,16,32,48,64,80,96,112},{1,17,33,49,65,81,97,113},{2,18,34,50,66,82,9..., dimensions={0} | all-to-all | bytes 3670016 | tf_op jit(solution)/shard_map/all_to_all | solution.py:49
  240.8 25.8 %all_to_all.54 = bf16[8,64,1792]{2,1,0:T(8,128)(2,1)S(1)} all-to-all(bf16[8,64,1792]{2,1,0:T(8,128)(2,1)S(1)} %broadcast_in_dim.8), channel_id=1, replica_groups={{0,16,32,48,64,80,96,112},{1,17,33,49,65,81,97,113},{2,18,34,50,66,82,9..., dimensions={0} | all-to-all | bytes 3670016 | tf_op jit(solution)/shard_map/all_to_all | solution.py:49
  268.3 3.8 %shard_map.119 = (f32[512,1792]{1,0:T(8,128)}, f32[512,1792]{1,0:T(8,128)}, f32[512,1792]{1,0:T(8,128)}) custom-call(s32[1]{0:T(128)} %bitcast.2.half_ref, bf16[512,512]{1,0:T(8,128)(2,1)S(1)} %copy-done.14, bf16[512,1792]{1,0:T(8,128)(2,1)S(1)} %bitcast.55, f32[512,1792]{1,0:T(8,128)S(1)} %copy-done.3, f32[512,1792]{1,0:T(8,128)S(1)} %copy-done.4), custom_call_target="tpu_custom_call" | custom-call | flops 950000000 | bytes 11000000 | tf_op jit(solution)/shard_map/pallas_call | solution.py:271
  272.1 3.8 %shard_map.120 = (f32[512,1792]{1,0:T(8,128)}, f32[512,1792]{1,0:T(8,128)}, f32[512,1792]{1,0:T(8,128)}) custom-call(s32[1]{0:T(128)} %bitcast.half_ref, bf16[512,512]{1,0:T(8,128)(2,1)S(1)} %copy-done.13, bf16[512,1792]{1,0:T(8,128)(2,1)S(1)} %collective-permute-done.12.cot, ...), custom_call_target="tpu_custom_call", output_to_operand_aliasing={{0}: (5, {}), {1}: (6, {}), {2}: (7, {})} | custom-call | flops 950000000 | bytes 11000000 | tf_op jit(solution)/shard_map/pallas_call | solution.py:271
  (121 shorter events, 49.4 us)
Async XLA Ops:
  0.6 5.3 %copy-start = (bf16[512,1792]{1,0:T(8,128)(2,1)S(1)}, bf16[512,1792]{1,0:T(8,128)(2,1)}, u32[]{:S(2)}) copy-start(bf16[512,1792]{1,0:T(8,128)(2,1)} %param.10) | copy-start | bytes 5505028
  0.6 5.3 %copy-start.18 = (bf16[512,512]{1,0:T(8,128)(2,1)S(1)}, bf16[512,512]{1,0:T(8,128)(2,1)}, u32[]{:S(2)}) copy-start(bf16[512,512]{1,0:T(8,128)(2,1)} %param.9) | copy-start | bytes 1572868
  1.5 10.5 %collective-permute-start.2 = (s32[32,2]{0,1:T(2,128)S(1)}, s32[32,2]{0,1:T(2,128)S(1)}, u32[]{:S(2)}, u32[]{:S(2)}) collective-permute-start(s32[32,2]{0,1:T(2,128)S(1)} %pad_add_fusion), channel_id=1, source_target_pairs={{0,8},{8,0},{1,9},{9,1},{2,10},{10,2},{3,11},{11,3},{4,12},{12,4},... | collective-permute-start | bytes 776 | tf_op jit(solution)/shard_map/ppermute | solution.py:34
  5.9 6.3 %collective-permute-start.1 = (bf16[512,896]{1,0:T(8,128)(2,1)}, bf16[512,896]{1,0:T(8,128)(2,1)S(1)}, u32[]{:S(2)}, u32[]{:S(2)}) collective-permute-start(bf16[512,896]{1,0:T(8,128)(2,1)} %fusion.9), channel_id=1, source_target_pairs={{0,8},{8,0},{1,9},{9,1},{2,10},{10,2},{3,11},{11,3},{4,12},{12,4},... | collective-permute-start | bytes 2752520 | tf_op jit(solution)/shard_map/ppermute | solution.py:34
  7.6 4.7 %collective-permute-start = (bf16[512,896]{1,0:T(8,128)(2,1)}, bf16[512,896]{1,0:T(8,128)(2,1)}, u32[]{:S(2)}, u32[]{:S(2)}) collective-permute-start(bf16[512,896]{1,0:T(8,128)(2,1)} %fusion.8), channel_id=1, source_target_pairs={{0,8},{8,0},{1,9},{9,1},{2,10},{10,2},{3,11},{11,3},{4,12},{12,4},... | collective-permute-start | bytes 2752520 | tf_op jit(solution)/shard_map/ppermute | solution.py:34
  18.1 8.1 %copy-start.2 = (bf16[512,2048]{1,0:T(8,128)(2,1)S(1)}, bf16[512,2048]{1,0:T(8,128)(2,1)}, u32[]{:S(2)}) copy-start(bf16[512,2048]{1,0:T(8,128)(2,1)} %head_far.1) | copy-start | bytes 6291460
  18.1 31.4 %all-to-all-start = ((bf16[8,64,1920]{2,1,0:T(8,128)(2,1)}), bf16[8,64,1920]{2,1,0:T(8,128)(2,1)}, u32[]{:S(2)}, u32[]{:S(2)}) async-start(bf16[8,64,1920]{2,1,0:T(8,128)(2,1)} %bitcast.53), calls=%async_computation | async-start | bytes 3932160 | tf_op jit(solution)/shard_map/all_to_all | solution.py:49
  27.3 4.6 %collective-permute-start.3 = (bf16[512,1024]{1,0:T(8,128)(2,1)}, bf16[512,1024]{1,0:T(8,128)(2,1)S(1)}, u32[]{:S(2)}, u32[]{:S(2)}) collective-permute-start(bf16[512,1024]{1,0:T(8,128)(2,1)} %constant_dynamic-slice_fusion.2), channel_id=1, source_target_pairs={{0,8},{8,0},{1,9},{9,1},{2,10},{10,2},{3,11},{11,3},{4,12},{12,4},... | collective-permute-start | bytes 3145736 | tf_op jit(solution)/shard_map/ppermute | solution.py:34
  29.0 2.8 %collective-permute-start.4 = (bf16[896,512]{1,0:T(8,128)(2,1)}, bf16[896,512]{1,0:T(8,128)(2,1)}, u32[]{:S(2)}, u32[]{:S(2)}) collective-permute-start(bf16[896,512]{1,0:T(8,128)(2,1)} %constant_dynamic-slice_fusion.1), channel_id=1, source_target_pairs={{0,8},{8,0},{1,9},{9,1},{2,10},{10,2},{3,11},{11,3},{4,12},{12,4},... | collective-permute-start | bytes 2752520 | tf_op jit(solution)/shard_map/ppermute | solution.py:34
  31.9 20.3 %copy-start.15 = (bf16[512,1024]{1,0:T(8,128)(2,1)}, bf16[512,1024]{1,0:T(8,128)(2,1)S(1)}, u32[]{:S(2)}) copy-start(bf16[512,1024]{1,0:T(8,128)(2,1)S(1)} %collective-permute-done.3.head_got) | copy-start | bytes 3145732
  52.2 17.0 %all-to-all-start.1 = ((bf16[8,64,896]{2,1,0:T(8,128)(2,1)}), bf16[8,64,896]{2,1,0:T(8,128)(2,1)S(1)}, u32[]{:S(2)}, u32[]{:S(2)}) async-start(bf16[8,64,896]{2,1,0:T(8,128)(2,1)} %copy-done.17), calls=%async_computation.1 | async-start | bytes 1835008 | tf_op jit(solution)/shard_map/all_to_all | solution.py:49
  69.2 2.5 collective-permute-start.5
  75.2 36.5 %copy-start.16 = (bf16[512,1024]{1,0:T(8,128)(2,1)S(1)}, bf16[512,1024]{1,0:T(8,128)(2,1)}, u32[]{:S(2)}) copy-start(bf16[512,1024]{1,0:T(8,128)(2,1)} %copy-done.15) | copy-start | bytes 3145732
  75.2 18.0 %all-to-all-start.2 = ((bf16[8,64,512]{2,1,0:T(8,128)(2,1)}), bf16[8,64,512]{2,1,0:T(8,128)(2,1)}, u32[]{:S(2)}, u32[]{:S(2)}) async-start(bf16[8,64,512]{2,1,0:T(8,128)(2,1)} %bitcast.13), calls=%async_computation.2 | async-start | bytes 1048576 | tf_op jit(solution)/shard_map/all_to_all | solution.py:49
  94.4 19.0 %copy-start.20 = (f32[64,512]{1,0:T(8,128)}, f32[64,512]{1,0:T(8,128)S(1)}, u32[]{:S(2)}) copy-start(f32[64,512]{1,0:T(8,128)S(1)} %convert_reduce_fusion.1) | copy-start | bytes 393220
  108.7 3.0 %collective-permute-start.6 = (bf16[512,512]{1,0:T(8,128)(2,1)S(1)}, bf16[512,512]{1,0:T(8,128)(2,1)S(1)}, u32[]{:S(2)}, u32[]{:S(2)}) collective-permute-start(bf16[512,512]{1,0:T(8,128)(2,1)S(1)} %bitcast.62), channel_id=1, source_target_pairs={{0,8},{8,0},{1,9},{9,1},{2,10},{10,2},{3,11},{11,3},{4,12},{12,4},... | collective-permute-start | bytes 1572872 | tf_op jit(solution)/shard_map/ppermute | solution.py:34
  114.4 22.7 %all-to-all-start.4 = ((s16[8,64,1152]{2,1,0:T(8,128)(2,1)}), s16[8,64,1152]{2,1,0:T(8,128)(2,1)S(1)}, u32[]{:S(2)}, u32[]{:S(2)}) async-start(s16[8,64,1152]{2,1,0:T(8,128)(2,1)} %bitcast.58), calls=%async_computation.4 | async-start | bytes 2359296 | tf_op jit(solution)/shard_map/all_to_all | solution.py:49
  121.8 13.2 %collective-permute-start.7 = (bf16[2,2,64,1024]{3,2,1,0:T(8,128)(2,1)}, bf16[2,2,64,1024]{3,2,1,0:T(8,128)(2,1)}, u32[]{:S(2)}, u32[]{:S(2)}) collective-permute-start(bf16[2,2,64,1024]{3,2,1,0:T(8,128)(2,1)} %dynamic-slice_bitcast_fusion), channel_id=1, source_target_pairs={{0,2},{2,0},{4,6},{6,4},{1,3},{3,1},{5,7},{7,5},{8,10},{10,8},{12,... | collective-permute-start | bytes 1572872 | tf_op jit(solution)/shard_map/ppermute | solution.py:309
  139.0 20.8 %all-to-all-start.5 = ((bf16[8,64,1152]{2,1,0:T(8,128)(2,1)}), bf16[8,64,1152]{2,1,0:T(8,128)(2,1)S(1)}, u32[]{:S(2)}, u32[]{:S(2)}) async-start(bf16[8,64,1152]{2,1,0:T(8,128)(2,1)} %copy-done.11), calls=%async_computation.5 | async-start | bytes 2359296 | tf_op jit(solution)/shard_map/all_to_all | solution.py:49
  146.5 9.5 %collective-permute-start.8 = (bf16[2,64,1024]{2,1,0:T(8,128)(2,1)}, bf16[2,64,1024]{2,1,0:T(8,128)(2,1)}, u32[]{:S(2)}, u32[]{:S(2)}) collective-permute-start(bf16[2,64,1024]{2,1,0:T(8,128)(2,1)} %dynamic-slice_bitcast_fusion.1), channel_id=1, source_target_pairs={{0,4},{4,0},{2,6},{6,2},{1,5},{5,1},{3,7},{7,3},{8,12},{12,8},{10,... | collective-permute-start | bytes 786440 | tf_op jit(solution)/shard_map/ppermute | solution.py:314
  159.8 7.9 %collective-permute-start.9 = (bf16[512,1152]{1,0:T(8,128)(2,1)S(1)}, bf16[512,1152]{1,0:T(8,128)(2,1)S(1)}, u32[]{:S(2)}, u32[]{:S(2)}) collective-permute-start(bf16[512,1152]{1,0:T(8,128)(2,1)S(1)} %bitcast.56), channel_id=1, source_target_pairs={{0,8},{8,0},{1,9},{9,1},{2,10},{10,2},{3,11},{11,3},{4,12},{12,4},... | collective-permute-start | bytes 3538952 | tf_op jit(solution)/shard_map/ppermute | solution.py:34
  159.8 6.3 %collective-permute-start.10 = (bf16[64,1024]{1,0:T(8,128)(2,1)}, bf16[64,1024]{1,0:T(8,128)(2,1)S(1)}, u32[]{:S(2)}, u32[]{:S(2)}) collective-permute-start(bf16[64,1024]{1,0:T(8,128)(2,1)} %get-tuple-element.54), channel_id=1, source_target_pairs={{0,1},{1,0},{2,3},{3,2},{4,5},{5,4},{6,7},{7,6},{8,9},{9,8},{10,11... | collective-permute-start | bytes 393224 | tf_op jit(solution)/shard_map/ppermute | solution.py:319
  169.1 14.6 %copy-start.21 = (f32[64,512]{1,0:T(8,128)S(1)}, f32[64,512]{1,0:T(8,128)}, u32[]{:S(2)}) copy-start(f32[64,512]{1,0:T(8,128)} %copy-done.20) | copy-start | bytes 393220
  169.1 14.6 %copy-start.22 = (f32[64,1024]{1,0:T(8,128)S(1)}, f32[64,1024]{1,0:T(8,128)}, u32[]{:S(2)}) copy-start(f32[64,1024]{1,0:T(8,128)} %convert_add_fusion) | copy-start | bytes 786436
  184.7 24.5 %copy-start.7 = (bf16[1792,512]{1,0:T(8,128)(2,1)S(1)}, bf16[1792,512]{1,0:T(8,128)(2,1)}, u32[]{:S(2)}) copy-start(bf16[1792,512]{1,0:T(8,128)(2,1)} %down.1) | copy-start | bytes 5505028
  204.7 4.5 %collective-permute-start.11 = (bf16[512,1024]{1,0:T(8,128)(2,1)S(1)}, bf16[512,1024]{1,0:T(8,128)(2,1)S(1)}, u32[]{:S(2)}, u32[]{:S(2)}) collective-permute-start(bf16[512,1024]{1,0:T(8,128)(2,1)S(1)} %bitcast.65), channel_id=1, source_target_pairs={{0,8},{8,0},{1,9},{9,1},{2,10},{10,2},{3,11},{11,3},{4,12},{12,4},... | collective-permute-start | bytes 3145736 | tf_op jit(solution)/shard_map/ppermute | solution.py:34
  240.3 27.9 %copy-start.4 = (f32[512,1792]{1,0:T(8,128)S(1)}, f32[512,1792]{1,0:T(8,128)}, u32[]{:S(2)}) copy-start(f32[512,1792]{1,0:T(8,128)} %curve_ref.3) | copy-start | bytes 11010052
  240.6 27.6 %copy-start.14 = (bf16[512,512]{1,0:T(8,128)(2,1)S(1)}, bf16[512,512]{1,0:T(8,128)(2,1)}, u32[]{:S(2)}) copy-start(bf16[512,512]{1,0:T(8,128)(2,1)} %get-tuple-element.59.turned) | copy-start | bytes 1572868
  240.8 27.5 %copy-start.3 = (f32[512,1792]{1,0:T(8,128)S(1)}, f32[512,1792]{1,0:T(8,128)}, u32[]{:S(2)}) copy-start(f32[512,1792]{1,0:T(8,128)} %moment_ref.3) | copy-start | bytes 11010052
  266.6 5.4 %copy-start.13 = (bf16[512,512]{1,0:T(8,128)(2,1)S(1)}, bf16[512,512]{1,0:T(8,128)(2,1)}, u32[]{:S(2)}) copy-start(bf16[512,512]{1,0:T(8,128)(2,1)} %get-tuple-element.51.turned) | copy-start | bytes 1572868
  266.6 5.4 %collective-permute-start.12 = (bf16[512,1792]{1,0:T(8,128)(2,1)S(1)}, bf16[512,1792]{1,0:T(8,128)(2,1)S(1)}, u32[]{:S(2)}, u32[]{:S(2)}) collective-permute-start(bf16[512,1792]{1,0:T(8,128)(2,1)S(1)} %bitcast.54), channel_id=1, source_target_pairs={{0,8},{8,0},{1,9},{9,1},{2,10},{10,2},{3,11},{11,3},{4,12},{12,4},... | collective-permute-start | bytes 5505032 | tf_op jit(solution)/shard_map/ppermute | solution.py:34
  272.0 3.8 %copy-start.1 = (bf16[512,1792]{1,0:T(8,128)(2,1)S(1)}, bf16[512,1792]{1,0:T(8,128)(2,1)}, u32[]{:S(2)}) copy-start(bf16[512,1792]{1,0:T(8,128)(2,1)} %param.10) | copy-start | bytes 5505028
  (12 other events, 18.8 us)

commit v10 on v9

--- a/solution.py
+++ b/solution.py
@@ -122,8 +122,8 @@
 
 def gate_up_pack(half_ref, own_gate, own_up, got_gate, got_up, labels, out):
     core = half_ref[0]
-    gate_sum = (own_gate[...] + got_gate[...].astype(f32)).astype(bf16)
-    up_sum = (own_up[...] + got_up[...].astype(f32)).astype(bf16)
+    gate_sum = (own_gate[...].astype(f32) + got_gate[...].astype(f32)).astype(bf16)
+    up_sum = (own_up[...].astype(f32) + got_up[...].astype(f32)).astype(bf16)
     for block in range(CHIPS):
         place = block + core * (CHIPS - 1 - 2 * block)
         rows = pl.ds(pl.multiple_of(place * BLOCK, BLOCK), BLOCK)
@@ -306,10 +306,11 @@
 
 def near_label_rows(rows):
     keep, send = own_part(rows, lax.axis_index("z") % 2, 1)
-    return keep + lax.ppermute(send, "z", [(0, 1), (1, 0), (2, 3), (3, 2)])
-
-
-def plane_label_rows(rows):
+    return keep, lax.ppermute(send, "z", [(0, 1), (1, 0), (2, 3), (3, 2)])
+
+
+def plane_label_rows(near, got):
+    rows = near + got
     keep, send = own_part(rows, lax.axis_index("z") // 2, 0)
     rows = keep + lax.ppermute(send, "z", [(0, 2), (2, 0), (1, 3), (3, 1)])
     return own_part(rows, lax.axis_index("xh"), 0)
@@ -350,10 +351,10 @@
     def gate_up(half):
         gate = lax.dynamic_slice_in_dim(gate_weight, half * FF_HALF, FF_HALF, 1)
         upper = lax.dynamic_slice_in_dim(up_weight, half * FF_HALF, FF_HALF, 1)
-        return dot(tokens, gate), dot(tokens, upper)
+        return dot(tokens, gate).astype(bf16), dot(tokens, upper).astype(bf16)
 
     far_gate, far_up = gate_up(far)
-    got_gate, got_up = other_core(far_gate.astype(bf16)), other_core(far_up.astype(bf16))
+    got_gate, got_up = other_core(far_gate), other_core(far_up)
     own_gate, own_up = gate_up(core)
     operands = (own_gate, own_up, got_gate, got_up, digits)
     both = on_core(
@@ -442,10 +443,9 @@
         exchange(packed, WIDTH_CHIPS),
         jnp.where(core == 0, turned, turned_reverse),
         jnp.where(core == 0, turned_reverse, turned),
-        plane_label_rows(label_row),
+        plane_label_rows(*label_row),
     )
     label_row, label_sent = label_row
-    label_row = label_row.astype(f32) + other_plane(label_sent).astype(f32)
     packed_own = packed_own.reshape(count, V_HALF + PAD)
     packed_far = other_core(packed_own)
     packed = on_core(
@@ -461,8 +461,11 @@
         [((count, width + PAD), bf16)],
         logit_flops,
     )
-    packed, label_row = together(packed, label_row)
-    packed = exchange(packed.reshape(CHIPS, BLOCK, width + PAD), UNIT_CHIPS)
+    packed, label_sent = together(packed, label_sent)
+    packed, label_got = together(
+        exchange(packed.reshape(CHIPS, BLOCK, width + PAD), UNIT_CHIPS), other_plane(label_sent)
+    )
+    label_row = label_row.astype(f32) + label_got.astype(f32)
     stats = from_three(packed[:, :, width:], N_STATS)
     row_top = jnp.max(stats[:, :, 0:1], axis=0, keepdims=True)
     weight = jnp.exp(stats[:, :, 0:1] - row_top)

time: 277 us -> 274 us (0.989)
  blocking collectives: 101 us -> 84.8 us
  waiting for transfers between devices: 57.9 us -> 65.7 us
  starting transfers between devices: 45.8 us -> 50.8 us
    all_to_all x5 -> x4, blocking collectives: 101 us -> 84.8 us  [exchange(): lax.all_to_all(blocks, tuple(MESH_SIZES), split_axis=0, concat_axis=0, ti...]
    all_to_all x5 -> x6, starting transfers between devices: 34.5 us -> 42.2 us  [exchange(): lax.all_to_all(blocks, tuple(MESH_SIZES), split_axis=0, concat_axis=0, ti...]
    ppermute x1, waiting for transfers between devices: 3.39 us -> 9.61 us  [other_plane(): return lax.ppermute(rows, 'xh', [(0, 1), (1, 0)])]
    ppermute x10, waiting for transfers between devices: 9.12 us -> 12 us  [other_core(): return lax.ppermute(value, 'core', [(0, 1), (1, 0)])]
    all_to_all x5 -> x6, waiting for transfers between devices: 32.2 us -> 30.9 us  [exchange(): lax.all_to_all(blocks, tuple(MESH_SIZES), split_axis=0, concat_axis=0, ti...]
    unnamed x53 -> x58, local copies, waits for them, and re-layouts: 9.79 us -> 10.6 us
  transfers between devices with their start and end apart: 18 -> 19, of which waited for: 10 -> 11; matrix products, arithmetic and copies ran while one was open for 13% -> 12% of each run, Pallas kernels for 1% -> 1%
where the time goes in v10:
time: 274 us; the launch traced here: 273 us
  blocking collectives  84.8 us (31%)
  waiting for transfers between devices  65.7 us (24%)
  starting transfers between devices  50.8 us (19%)
  local copies, waits for them, and re-layouts  26.6 us (10%)
  Pallas kernels  20.6 us (8%)
  other arithmetic  12.3 us (4%)
  matrix products  10.7 us (4%)
    all_to_all x4, blocking collectives, exchange(): lax.all_to_all(blocks, tuple(MESH_SIZES), split_axis=0, concat_axis=0, ti...  84.8 us
    all_to_all x6, starting transfers between devices, exchange(): lax.all_to_all(blocks, tuple(MESH_SIZES), split_axis=0, concat_axis=0, ti...  42.2 us
    all_to_all x6, waiting for transfers between devices, exchange(): lax.all_to_all(blocks, tuple(MESH_SIZES), split_axis=0, concat_axis=0, ti...  30.9 us
    ppermute x1, waiting for transfers between devices, near_label_rows(): return (keep, lax.ppermute(send, 'z', [(0, 1), (1, 0), (2, 3), (3, 2)]))  13.2 us
    pallas_call x7, Pallas kernels, on_core(): pl.pallas_call(kernel, out_shape=tuple((jax.ShapeDtypeStruct(shape, dtype...  13 us
    ppermute x10, waiting for transfers between devices, other_core(): return lax.ppermute(value, 'core', [(0, 1), (1, 0)])  12 us
    unnamed x58, local copies, waits for them, and re-layouts  10.6 us
    ppermute x1, waiting for transfers between devices, other_plane(): return lax.ppermute(rows, 'xh', [(0, 1), (1, 0)])  9.61 us
  transfers between devices with their start and end apart: 19, of which 11 were waited for; matrix products, arithmetic and copies ran while one was open for 12% of the time, Pallas kernels for 1%

profile of v10, /device:TPU:1, one launch (start us, length us, event | category | flops | bytes accessed | tf_op | source)
XLA Modules:
  0.0 272.5 jit_solution(16998974123333861767)
XLA Ops:
  2.9 3.0 %fusion.11 = bf16[512,896]{1,0:T(8,128)(2,1)} fusion(bf16[512,512]{1,0:T(8,128)(2,1)} %param.9, bf16[512,1792]{1,0:T(8,128)(2,1)} %param.11, s32[]{:T(128)S(6)} %select_n.97), kind=kOutput, calls=%fused_computation.16 | convolution fusion | flops 470220800 | bytes 2359300 | tf_op jit(solution)/shard_map/dot_general | solution.py:82
  16.9 8.1 %all-to-all-start = ((bf16[8,64,1920]{2,1,0:T(8,128)(2,1)}), bf16[8,64,1920]{2,1,0:T(8,128)(2,1)}, u32[]{:S(2)}, u32[]{:S(2)}) async-start(bf16[8,64,1920]{2,1,0:T(8,128)(2,1)} %bitcast.53), calls=%async_computation | async-start | bytes 3932160 | tf_op jit(solution)/shard_map/all_to_all | solution.py:49
  27.9 2.8 %collective-permute-done.4.down_got = bf16[896,512]{1,0:T(8,128)(2,1)} collective-permute-done((bf16[896,512]{1,0:T(8,128)(2,1)}, bf16[896,512]{1,0:T(8,128)(2,1)}, u32[]{:S(2)}, u32[]{:S(2)}) %collective-permute-start.4) | collective-permute-done | bytes 917536 | tf_op jit(solution)/shard_map/ppermute | solution.py:34
  30.7 17.5 %all-to-all-done.both = bf16[8,64,1920]{2,1,0:T(8,128)(2,1)} async-done(((bf16[8,64,1920]{2,1,0:T(8,128)(2,1)}), bf16[8,64,1920]{2,1,0:T(8,128)(2,1)}, u32[]{:S(2)}, u32[]{:S(2)}) %all-to-all-start) | async-done | bytes 1966112 | tf_op jit(solution)/shard_map/all_to_all | solution.py:49
  48.2 1.8 shard_map.113
  51.0 4.9 %all-to-all-start.1 = ((bf16[8,64,896]{2,1,0:T(8,128)(2,1)}), bf16[8,64,896]{2,1,0:T(8,128)(2,1)S(1)}, u32[]{:S(2)}, u32[]{:S(2)}) async-start(bf16[8,64,896]{2,1,0:T(8,128)(2,1)} %copy-done.16), calls=%async_computation.1 | async-start | bytes 1835008 | tf_op jit(solution)/shard_map/all_to_all | solution.py:49
  61.1 2.3 copy.77
  63.4 4.6 %all-to-all-done.1 = bf16[8,64,896]{2,1,0:T(8,128)(2,1)S(1)} async-done(((bf16[8,64,896]{2,1,0:T(8,128)(2,1)}), bf16[8,64,896]{2,1,0:T(8,128)(2,1)S(1)}, u32[]{:S(2)}, u32[]{:S(2)}) %all-to-all-start.1) | async-done | bytes 917536 | tf_op jit(solution)/shard_map/all_to_all | solution.py:49
  68.0 2.5 collective-permute-done.5.far
  72.0 2.0 shard_map.114
  74.0 10.1 %all-to-all-start.2 = ((bf16[8,64,512]{2,1,0:T(8,128)(2,1)}), bf16[8,64,512]{2,1,0:T(8,128)(2,1)}, u32[]{:S(2)}, u32[]{:S(2)}) async-start(bf16[8,64,512]{2,1,0:T(8,128)(2,1)} %bitcast.13), calls=%async_computation.2 | async-start | bytes 1048576 | tf_op jit(solution)/shard_map/all_to_all | solution.py:49
  84.1 7.9 %all-to-all-done.2 = bf16[8,64,512]{2,1,0:T(8,128)(2,1)} async-done(((bf16[8,64,512]{2,1,0:T(8,128)(2,1)}), bf16[8,64,512]{2,1,0:T(8,128)(2,1)}, u32[]{:S(2)}, u32[]{:S(2)}) %all-to-all-start.2) | async-done | bytes 524320 | tf_op jit(solution)/shard_map/all_to_all | solution.py:49
  94.2 13.4 %all_to_all.50 = bf16[8,64,512]{2,1,0:T(8,128)(2,1)S(1)} all-to-all(bf16[8,64,512]{2,1,0:T(8,128)(2,1)S(1)} %broadcast_in_dim.6), channel_id=1, replica_groups={{0,1,2,3,4,5,6,7},{15,14,13,12,11,10,9,8},{16,17,18,19,20,21,22,23},{31..., dimensions={0} | all-to-all | bytes 1048576 | tf_op jit(solution)/shard_map/all_to_all | solution.py:49
  113.2 5.6 %all-to-all-start.4 = ((s16[8,64,1152]{2,1,0:T(8,128)(2,1)}), s16[8,64,1152]{2,1,0:T(8,128)(2,1)S(1)}, u32[]{:S(2)}, u32[]{:S(2)}) async-start(s16[8,64,1152]{2,1,0:T(8,128)(2,1)} %bitcast.58), calls=%async_computation.4 | async-start | bytes 2359296 | tf_op jit(solution)/shard_map/all_to_all | solution.py:49
  118.8 2.3 dynamic-slice_bitcast_fusion
  121.0 13.2 %collective-permute-done.7 = bf16[2,2,64,1024]{3,2,1,0:T(8,128)(2,1)} collective-permute-done((bf16[2,2,64,1024]{3,2,1,0:T(8,128)(2,1)}, bf16[2,2,64,1024]{3,2,1,0:T(8,128)(2,1)}, u32[]{:S(2)}, u32[]{:S(2)}) %collective-permute-start.7) | collective-permute-done | bytes 524320 | tf_op jit(solution)/shard_map/ppermute | solution.py:309
  136.2 5.9 %all-to-all-start.5 = ((bf16[8,64,1152]{2,1,0:T(8,128)(2,1)}), bf16[8,64,1152]{2,1,0:T(8,128)(2,1)S(1)}, u32[]{:S(2)}, u32[]{:S(2)}) async-start(bf16[8,64,1152]{2,1,0:T(8,128)(2,1)} %copy-done.9), calls=%async_computation.5 | async-start | bytes 2359296 | tf_op jit(solution)/shard_map/all_to_all | solution.py:49
  146.2 2.1 copy.78
  148.2 1.9 rev.7
  150.1 2.0 copy.79
  152.1 2.3 select_bitcast_fusion
  156.9 2.8 %collective-permute-done.9.far = bf16[512,1152]{1,0:T(8,128)(2,1)S(1)} collective-permute-done((bf16[512,1152]{1,0:T(8,128)(2,1)S(1)}, bf16[512,1152]{1,0:T(8,128)(2,1)S(1)}, u32[]{:S(2)}, u32[]{:S(2)}) %collective-permute-start.9) | collective-permute-done | bytes 1179680 | tf_op jit(solution)/shard_map/ppermute | solution.py:34
  162.1 7.7 %all-to-all-start.6 = ((bf16[8,64,640]{2,1,0:T(8,128)(2,1)}), bf16[8,64,640]{2,1,0:T(8,128)(2,1)S(1)}, u32[]{:S(2)}, u32[]{:S(2)}) async-start(bf16[8,64,640]{2,1,0:T(8,128)(2,1)} %bitcast.61), calls=%async_computation.6 | async-start | bytes 1310720 | tf_op jit(solution)/shard_map/all_to_all | solution.py:49
  170.0 9.6 %collective-permute-done.10 = bf16[64,1024]{1,0:T(8,128)(2,1)S(1)} collective-permute-done((bf16[64,1024]{1,0:T(8,128)(2,1)}, bf16[64,1024]{1,0:T(8,128)(2,1)S(1)}, u32[]{:S(2)}, u32[]{:S(2)}) %collective-permute-start.10) | collective-permute-done | bytes 131104 | tf_op jit(solution)/shard_map/ppermute | solution.py:320
  183.4 19.4 %all_to_all.51 = bf16[8,64,1024]{2,1,0:T(8,128)(2,1)S(1)} all-to-all(bf16[8,64,1024]{2,1,0:T(8,128)(2,1)S(1)} %broadcast_in_dim.7), channel_id=1, replica_groups={{0,1,2,3,4,5,6,7},{15,14,13,12,11,10,9,8},{16,17,18,19,20,21,22,23},{31..., dimensions={0} | all-to-all | bytes 2097152 | tf_op jit(solution)/shard_map/all_to_all | solution.py:49
  202.8 2.0 collective-permute-start.11
  204.8 2.3 collective-permute-done.11.far_dsummed
  207.1 3.5 %shard_map.118 = bf16[512,1792]{1,0:T(8,128)(2,1)S(1)} custom-call(s32[1]{0:T(128)} %bitcast.2.half_ref, bf16[512,1024]{1,0:T(8,128)(2,1)S(1)} %bitcast.66, bf16[512,1024]{1,0:T(8,128)(2,1)S(1)} %collective-permute-done.11.far_dsummed, bf16[1792,512]{1,0:T(8,128)(2,1)S(1)} %copy-done.7, bf16[896,512]{1,0:T(8,128)(2,1)} %collective-permute-done.4.down_got), custom_call_target="tpu_custom_call" | custom-call | flops 1879048192 | bytes 4849664 | tf_op jit(solution)/shard_map/pallas_call | solution.py:108
  210.7 26.3 %all_to_all.52 = bf16[8,64,1792]{2,1,0:T(8,128)(2,1)S(1)} all-to-all(bf16[8,64,1792]{2,1,0:T(8,128)(2,1)S(1)} %bitcast.64), channel_id=1, replica_groups={{0,16,32,48,64,80,96,112},{1,17,33,49,65,81,97,113},{2,18,34,50,66,82,9..., dimensions={0} | all-to-all | bytes 3670016 | tf_op jit(solution)/shard_map/all_to_all | solution.py:49
  237.4 25.8 %all_to_all.53 = bf16[8,64,1792]{2,1,0:T(8,128)(2,1)S(1)} all-to-all(bf16[8,64,1792]{2,1,0:T(8,128)(2,1)S(1)} %broadcast_in_dim.8), channel_id=1, replica_groups={{0,16,32,48,64,80,96,112},{1,17,33,49,65,81,97,113},{2,18,34,50,66,82,9..., dimensions={0} | all-to-all | bytes 3670016 | tf_op jit(solution)/shard_map/all_to_all | solution.py:49
  264.9 3.8 %shard_map.119 = (f32[512,1792]{1,0:T(8,128)}, f32[512,1792]{1,0:T(8,128)}, f32[512,1792]{1,0:T(8,128)}) custom-call(s32[1]{0:T(128)} %bitcast.2.half_ref, bf16[512,512]{1,0:T(8,128)(2,1)S(1)} %copy-done.13, bf16[512,1792]{1,0:T(8,128)(2,1)S(1)} %bitcast.55, f32[512,1792]{1,0:T(8,128)S(1)} %copy-done.3, f32[512,1792]{1,0:T(8,128)S(1)} %copy-done.4), custom_call_target="tpu_custom_call" | custom-call | flops 950000000 | bytes 11000000 | tf_op jit(solution)/shard_map/pallas_call | solution.py:271
  268.7 3.8 %shard_map.120 = (f32[512,1792]{1,0:T(8,128)}, f32[512,1792]{1,0:T(8,128)}, f32[512,1792]{1,0:T(8,128)}) custom-call(s32[1]{0:T(128)} %bitcast.half_ref, bf16[512,512]{1,0:T(8,128)(2,1)S(1)} %copy-done.12, bf16[512,1792]{1,0:T(8,128)(2,1)S(1)} %collective-permute-done.12.cot, ...), custom_call_target="tpu_custom_call", output_to_operand_aliasing={{0}: (5, {}), {1}: (6, {}), {2}: (7, {})} | custom-call | flops 950000000 | bytes 11000000 | tf_op jit(solution)/shard_map/pallas_call | solution.py:271
  (127 shorter events, 48.3 us)
Async XLA Ops:
  0.6 5.3 %copy-start = (bf16[512,1792]{1,0:T(8,128)(2,1)S(1)}, bf16[512,1792]{1,0:T(8,128)(2,1)}, u32[]{:S(2)}) copy-start(bf16[512,1792]{1,0:T(8,128)(2,1)} %param.10) | copy-start | bytes 5505028
  0.6 5.3 %copy-start.19 = (bf16[512,512]{1,0:T(8,128)(2,1)S(1)}, bf16[512,512]{1,0:T(8,128)(2,1)}, u32[]{:S(2)}) copy-start(bf16[512,512]{1,0:T(8,128)(2,1)} %param.9) | copy-start | bytes 1572868
  1.5 9.9 %collective-permute-start.2 = (s32[32,2]{0,1:T(2,128)S(1)}, s32[32,2]{0,1:T(2,128)S(1)}, u32[]{:S(2)}, u32[]{:S(2)}) collective-permute-start(s32[32,2]{0,1:T(2,128)S(1)} %pad_add_fusion), channel_id=1, source_target_pairs={{0,8},{8,0},{1,9},{9,1},{2,10},{10,2},{3,11},{11,3},{4,12},{12,4},... | collective-permute-start | bytes 776 | tf_op jit(solution)/shard_map/ppermute | solution.py:34
  5.9 5.7 %collective-permute-start.1 = (bf16[512,896]{1,0:T(8,128)(2,1)}, bf16[512,896]{1,0:T(8,128)(2,1)S(1)}, u32[]{:S(2)}, u32[]{:S(2)}) collective-permute-start(bf16[512,896]{1,0:T(8,128)(2,1)} %fusion.11), channel_id=1, source_target_pairs={{0,8},{8,0},{1,9},{9,1},{2,10},{10,2},{3,11},{11,3},{4,12},{12,4},... | collective-permute-start | bytes 2752520 | tf_op jit(solution)/shard_map/ppermute | solution.py:34
  7.6 4.1 %collective-permute-start = (bf16[512,896]{1,0:T(8,128)(2,1)}, bf16[512,896]{1,0:T(8,128)(2,1)}, u32[]{:S(2)}, u32[]{:S(2)}) collective-permute-start(bf16[512,896]{1,0:T(8,128)(2,1)} %fusion.10), channel_id=1, source_target_pairs={{0,8},{8,0},{1,9},{9,1},{2,10},{10,2},{3,11},{11,3},{4,12},{12,4},... | collective-permute-start | bytes 2752520 | tf_op jit(solution)/shard_map/ppermute | solution.py:34
  16.9 8.1 %copy-start.2 = (bf16[512,2048]{1,0:T(8,128)(2,1)S(1)}, bf16[512,2048]{1,0:T(8,128)(2,1)}, u32[]{:S(2)}) copy-start(bf16[512,2048]{1,0:T(8,128)(2,1)} %head_far.1) | copy-start | bytes 6291460
  16.9 31.4 %all-to-all-start = ((bf16[8,64,1920]{2,1,0:T(8,128)(2,1)}), bf16[8,64,1920]{2,1,0:T(8,128)(2,1)}, u32[]{:S(2)}, u32[]{:S(2)}) async-start(bf16[8,64,1920]{2,1,0:T(8,128)(2,1)} %bitcast.53), calls=%async_computation | async-start | bytes 3932160 | tf_op jit(solution)/shard_map/all_to_all | solution.py:49
  26.1 4.6 %collective-permute-start.3 = (bf16[512,1024]{1,0:T(8,128)(2,1)}, bf16[512,1024]{1,0:T(8,128)(2,1)S(1)}, u32[]{:S(2)}, u32[]{:S(2)}) collective-permute-start(bf16[512,1024]{1,0:T(8,128)(2,1)} %constant_dynamic-slice_fusion.2), channel_id=1, source_target_pairs={{0,8},{8,0},{1,9},{9,1},{2,10},{10,2},{3,11},{11,3},{4,12},{12,4},... | collective-permute-start | bytes 3145736 | tf_op jit(solution)/shard_map/ppermute | solution.py:34
  27.9 2.8 %collective-permute-start.4 = (bf16[896,512]{1,0:T(8,128)(2,1)}, bf16[896,512]{1,0:T(8,128)(2,1)}, u32[]{:S(2)}, u32[]{:S(2)}) collective-permute-start(bf16[896,512]{1,0:T(8,128)(2,1)} %constant_dynamic-slice_fusion.1), channel_id=1, source_target_pairs={{0,8},{8,0},{1,9},{9,1},{2,10},{10,2},{3,11},{11,3},{4,12},{12,4},... | collective-permute-start | bytes 2752520 | tf_op jit(solution)/shard_map/ppermute | solution.py:34
  30.7 20.3 %copy-start.14 = (bf16[512,1024]{1,0:T(8,128)(2,1)}, bf16[512,1024]{1,0:T(8,128)(2,1)S(1)}, u32[]{:S(2)}) copy-start(bf16[512,1024]{1,0:T(8,128)(2,1)S(1)} %collective-permute-done.3.head_got) | copy-start | bytes 3145732
  51.0 17.0 %all-to-all-start.1 = ((bf16[8,64,896]{2,1,0:T(8,128)(2,1)}), bf16[8,64,896]{2,1,0:T(8,128)(2,1)S(1)}, u32[]{:S(2)}, u32[]{:S(2)}) async-start(bf16[8,64,896]{2,1,0:T(8,128)(2,1)} %copy-done.16), calls=%async_computation.1 | async-start | bytes 1835008 | tf_op jit(solution)/shard_map/all_to_all | solution.py:49
  68.0 2.5 collective-permute-start.5
  74.0 36.5 %copy-start.15 = (bf16[512,1024]{1,0:T(8,128)(2,1)S(1)}, bf16[512,1024]{1,0:T(8,128)(2,1)}, u32[]{:S(2)}) copy-start(bf16[512,1024]{1,0:T(8,128)(2,1)} %copy-done.14) | copy-start | bytes 3145732
  74.0 18.0 %all-to-all-start.2 = ((bf16[8,64,512]{2,1,0:T(8,128)(2,1)}), bf16[8,64,512]{2,1,0:T(8,128)(2,1)}, u32[]{:S(2)}, u32[]{:S(2)}) async-start(bf16[8,64,512]{2,1,0:T(8,128)(2,1)} %bitcast.13), calls=%async_computation.2 | async-start | bytes 1048576 | tf_op jit(solution)/shard_map/all_to_all | solution.py:49
  93.2 19.0 %copy-start.22 = (f32[64,512]{1,0:T(8,128)}, f32[64,512]{1,0:T(8,128)S(1)}, u32[]{:S(2)}) copy-start(f32[64,512]{1,0:T(8,128)S(1)} %convert_reduce_fusion.1) | copy-start | bytes 393220
  107.5 3.0 %collective-permute-start.6 = (bf16[512,512]{1,0:T(8,128)(2,1)S(1)}, bf16[512,512]{1,0:T(8,128)(2,1)S(1)}, u32[]{:S(2)}, u32[]{:S(2)}) collective-permute-start(bf16[512,512]{1,0:T(8,128)(2,1)S(1)} %bitcast.62), channel_id=1, source_target_pairs={{0,8},{8,0},{1,9},{9,1},{2,10},{10,2},{3,11},{11,3},{4,12},{12,4},... | collective-permute-start | bytes 1572872 | tf_op jit(solution)/shard_map/ppermute | solution.py:34
  113.2 21.0 %all-to-all-start.4 = ((s16[8,64,1152]{2,1,0:T(8,128)(2,1)}), s16[8,64,1152]{2,1,0:T(8,128)(2,1)S(1)}, u32[]{:S(2)}, u32[]{:S(2)}) async-start(s16[8,64,1152]{2,1,0:T(8,128)(2,1)} %bitcast.58), calls=%async_computation.4 | async-start | bytes 2359296 | tf_op jit(solution)/shard_map/all_to_all | solution.py:49
  121.0 13.2 %collective-permute-start.7 = (bf16[2,2,64,1024]{3,2,1,0:T(8,128)(2,1)}, bf16[2,2,64,1024]{3,2,1,0:T(8,128)(2,1)}, u32[]{:S(2)}, u32[]{:S(2)}) collective-permute-start(bf16[2,2,64,1024]{3,2,1,0:T(8,128)(2,1)} %get-tuple-element.84), channel_id=1, source_target_pairs={{0,2},{2,0},{4,6},{6,4},{1,3},{3,1},{5,7},{7,5},{8,10},{10,8},{12,... | collective-permute-start | bytes 1572872 | tf_op jit(solution)/shard_map/ppermute | solution.py:309
  136.2 20.8 %all-to-all-start.5 = ((bf16[8,64,1152]{2,1,0:T(8,128)(2,1)}), bf16[8,64,1152]{2,1,0:T(8,128)(2,1)S(1)}, u32[]{:S(2)}, u32[]{:S(2)}) async-start(bf16[8,64,1152]{2,1,0:T(8,128)(2,1)} %copy-done.9), calls=%async_computation.5 | async-start | bytes 2359296 | tf_op jit(solution)/shard_map/all_to_all | solution.py:49
  145.0 9.5 %collective-permute-start.8 = (bf16[2,64,1024]{2,1,0:T(8,128)(2,1)}, bf16[2,64,1024]{2,1,0:T(8,128)(2,1)}, u32[]{:S(2)}, u32[]{:S(2)}) collective-permute-start(bf16[2,64,1024]{2,1,0:T(8,128)(2,1)} %dynamic-slice_bitcast_fusion.2), channel_id=1, source_target_pairs={{0,4},{4,0},{2,6},{6,2},{1,5},{5,1},{3,7},{7,3},{8,12},{12,8},{10,... | collective-permute-start | bytes 786440 | tf_op jit(solution)/shard_map/ppermute | solution.py:315
  156.9 2.8 %collective-permute-start.9 = (bf16[512,1152]{1,0:T(8,128)(2,1)S(1)}, bf16[512,1152]{1,0:T(8,128)(2,1)S(1)}, u32[]{:S(2)}, u32[]{:S(2)}) collective-permute-start(bf16[512,1152]{1,0:T(8,128)(2,1)S(1)} %bitcast.56), channel_id=1, source_target_pairs={{0,8},{8,0},{1,9},{9,1},{2,10},{10,2},{3,11},{11,3},{4,12},{12,4},... | collective-permute-start | bytes 3538952 | tf_op jit(solution)/shard_map/ppermute | solution.py:34
  162.1 17.6 %all-to-all-start.6 = ((bf16[8,64,640]{2,1,0:T(8,128)(2,1)}), bf16[8,64,640]{2,1,0:T(8,128)(2,1)S(1)}, u32[]{:S(2)}, u32[]{:S(2)}) async-start(bf16[8,64,640]{2,1,0:T(8,128)(2,1)} %bitcast.61), calls=%async_computation.6 | async-start | bytes 1310720 | tf_op jit(solution)/shard_map/all_to_all | solution.py:49
  169.8 11.6 %copy-start.24 = (bf16[64,1024]{1,0:T(8,128)(2,1)S(1)}, bf16[64,1024]{1,0:T(8,128)(2,1)}, u32[]{:S(2)}) copy-start(bf16[64,1024]{1,0:T(8,128)(2,1)} %get-tuple-element.63) | copy-start | bytes 393220
  169.8 12.5 %copy-start.23 = (f32[64,512]{1,0:T(8,128)S(1)}, f32[64,512]{1,0:T(8,128)}, u32[]{:S(2)}) copy-start(f32[64,512]{1,0:T(8,128)} %copy-done.22) | copy-start | bytes 393220
  169.8 9.9 %collective-permute-start.10 = (bf16[64,1024]{1,0:T(8,128)(2,1)}, bf16[64,1024]{1,0:T(8,128)(2,1)S(1)}, u32[]{:S(2)}, u32[]{:S(2)}) collective-permute-start(bf16[64,1024]{1,0:T(8,128)(2,1)} %get-tuple-element.61), channel_id=1, source_target_pairs={{0,1},{1,0},{2,3},{3,2},{4,5},{5,4},{6,7},{7,6},{8,9},{9,8},{10,11... | collective-permute-start | bytes 393224 | tf_op jit(solution)/shard_map/ppermute | solution.py:320
  183.3 23.9 %copy-start.7 = (bf16[1792,512]{1,0:T(8,128)(2,1)S(1)}, bf16[1792,512]{1,0:T(8,128)(2,1)}, u32[]{:S(2)}) copy-start(bf16[1792,512]{1,0:T(8,128)(2,1)} %down.1) | copy-start | bytes 5505028
  202.8 4.3 %collective-permute-start.11 = (bf16[512,1024]{1,0:T(8,128)(2,1)S(1)}, bf16[512,1024]{1,0:T(8,128)(2,1)S(1)}, u32[]{:S(2)}, u32[]{:S(2)}) collective-permute-start(bf16[512,1024]{1,0:T(8,128)(2,1)S(1)} %bitcast.65), channel_id=1, source_target_pairs={{0,8},{8,0},{1,9},{9,1},{2,10},{10,2},{3,11},{11,3},{4,12},{12,4},... | collective-permute-start | bytes 3145736 | tf_op jit(solution)/shard_map/ppermute | solution.py:34
  237.0 27.9 %copy-start.4 = (f32[512,1792]{1,0:T(8,128)S(1)}, f32[512,1792]{1,0:T(8,128)}, u32[]{:S(2)}) copy-start(f32[512,1792]{1,0:T(8,128)} %curve_ref.3) | copy-start | bytes 11010052
  237.3 27.6 %copy-start.13 = (bf16[512,512]{1,0:T(8,128)(2,1)S(1)}, bf16[512,512]{1,0:T(8,128)(2,1)}, u32[]{:S(2)}) copy-start(bf16[512,512]{1,0:T(8,128)(2,1)} %get-tuple-element.67.turned) | copy-start | bytes 1572868
  237.4 27.5 %copy-start.3 = (f32[512,1792]{1,0:T(8,128)S(1)}, f32[512,1792]{1,0:T(8,128)}, u32[]{:S(2)}) copy-start(f32[512,1792]{1,0:T(8,128)} %moment_ref.3) | copy-start | bytes 11010052
  263.2 5.5 %copy-start.12 = (bf16[512,512]{1,0:T(8,128)(2,1)S(1)}, bf16[512,512]{1,0:T(8,128)(2,1)}, u32[]{:S(2)}) copy-start(bf16[512,512]{1,0:T(8,128)(2,1)} %get-tuple-element.57.turned) | copy-start | bytes 1572868
  263.2 5.5 %collective-permute-start.12 = (bf16[512,1792]{1,0:T(8,128)(2,1)S(1)}, bf16[512,1792]{1,0:T(8,128)(2,1)S(1)}, u32[]{:S(2)}, u32[]{:S(2)}) collective-permute-start(bf16[512,1792]{1,0:T(8,128)(2,1)S(1)} %bitcast.54), channel_id=1, source_target_pairs={{0,8},{8,0},{1,9},{9,1},{2,10},{10,2},{3,11},{11,3},{4,12},{12,4},... | collective-permute-start | bytes 5505032 | tf_op jit(solution)/shard_map/ppermute | solution.py:34
  (16 other events, 24.0 us)

commit v11 on v10

--- a/solution.py
+++ b/solution.py
@@ -124,16 +124,38 @@
     core = half_ref[0]
     gate_sum = (own_gate[...].astype(f32) + got_gate[...].astype(f32)).astype(bf16)
     up_sum = (own_up[...].astype(f32) + got_up[...].astype(f32)).astype(bf16)
-    for block in range(CHIPS):
-        place = block + core * (CHIPS - 1 - 2 * block)
+    blocks = own_gate.shape[0] // BLOCK
+    for block in range(blocks):
+        place = block + core * (blocks - 1 - 2 * block)
         rows = pl.ds(pl.multiple_of(place * BLOCK, BLOCK), BLOCK)
         out[rows, :FF_HALF] = gate_sum[block_rows(block)]
         out[rows, FF_HALF : 2 * FF_HALF] = up_sum[block_rows(block)]
         out[rows, 2 * FF_HALF :] = labels[...]
 
 
-def branch_kernel(half_ref, own, far, down_own, down_far, out):
-    out[...] = join_cores(dot(own[...], down_own[...]), dot(far[...], down_far[...])).astype(bf16)
+def pack_gate_up(core, own_gate, own_up, got_gate, got_up, labels):
+    steps = 4
+    count = own_gate.shape[0]
+    part = pl.BlockSpec((count // steps, FF_HALF), lambda step, half: (step, 0))
+    wide = 2 * FF_HALF + PAD
+    return pl.pallas_call(
+        gate_up_pack,
+        out_shape=jax.ShapeDtypeStruct((count, wide), bf16),
+        grid_spec=pltpu.PrefetchScalarGridSpec(
+            num_scalar_prefetch=1,
+            grid=(steps,),
+            in_specs=[part, part, part, part, whole(labels)],
+            out_specs=pl.BlockSpec(
+                (count // steps, wide), lambda step, half: (step + half[0] * (steps - 1 - 2 * step), 0)
+            ),
+        ),
+        compiler_params=pltpu.CompilerParams(vmem_limit_bytes=60 * 1024 * 1024),
+        cost_estimate=pl.CostEstimate(flops=2000000, bytes_accessed=6000000, transcendentals=0),
+    )(core.reshape(1), own_gate, own_up, got_gate, got_up, labels)
+
+
+def branch_kernel(half_ref, own_part, far, down_far, out):
+    out[...] = join_cores(own_part[...], dot(far[...], down_far[...])).astype(bf16)
 
 
 def hidden_kernel(half_ref, both, hidden, silu_out):
@@ -336,6 +358,17 @@
     unit_chip = lax.axis_index(UNIT_CHIPS)
     count, width = tokens.shape
 
+    gate_up_flops = 4 * count * width * FF_HALF
+
+    def gate_up(half):
+        gate = lax.dynamic_slice_in_dim(gate_weight, half * FF_HALF, FF_HALF, 1)
+        upper = lax.dynamic_slice_in_dim(up_weight, half * FF_HALF, FF_HALF, 1)
+        return dot(tokens, gate).astype(bf16), dot(tokens, upper).astype(bf16)
+
+    far_gate, far_up = gate_up(far)
+    far_gate, true_labels, sampled_labels = together(far_gate, true_labels, sampled_labels)
+    got_gate, got_up = other_core(far_gate), other_core(far_up)
+    own_gate, own_up = gate_up(core)
     labels = jnp.stack([true_labels, sampled_labels], axis=1)
     far_labels = other_core(labels)
     labels = jnp.where(
@@ -346,25 +379,7 @@
     digits = jnp.concatenate([labels // PAD, labels % PAD], axis=1).astype(bf16)
     digits = jnp.pad(digits, ((0, 0), (0, PAD - 4)))
 
-    gate_up_flops = 4 * count * width * FF_HALF
-
-    def gate_up(half):
-        gate = lax.dynamic_slice_in_dim(gate_weight, half * FF_HALF, FF_HALF, 1)
-        upper = lax.dynamic_slice_in_dim(up_weight, half * FF_HALF, FF_HALF, 1)
-        return dot(tokens, gate).astype(bf16), dot(tokens, upper).astype(bf16)
-
-    far_gate, far_up = gate_up(far)
-    got_gate, got_up = other_core(far_gate), other_core(far_up)
-    own_gate, own_up = gate_up(core)
-    operands = (own_gate, own_up, got_gate, got_up, digits)
-    both = on_core(
-        gate_up_pack,
-        core,
-        operands,
-        [whole(operand) for operand in operands],
-        [((count, 2 * FF_HALF + PAD), bf16)],
-        1000000,
-    )
+    both = pack_gate_up(core, own_gate, own_up, got_gate, got_up, digits)
     both, sent_head, sent_down = together(both, head_weight, down_weight)
     head_send = lax.dynamic_slice_in_dim(sent_head, far * V_HALF, V_HALF, 1)
     down_send = lax.dynamic_slice_in_dim(sent_down, far * FF_HALF, FF_HALF, 0)
@@ -394,14 +409,14 @@
     )
     hidden_own = hidden_own.reshape(count, FF_HALF)
     hidden_far = other_core(hidden_own)
+    own_part = dot(hidden_own, lax.dynamic_slice_in_dim(down_weight, core * FF_HALF, FF_HALF, 0))
     branch = on_core(
         branch_kernel,
         core,
-        (hidden_own, hidden_far, down_weight, down_weight),
+        (own_part, hidden_far, down_weight),
         [
-            whole(hidden_own),
+            whole(own_part),
             whole(hidden_far),
-            rows_of(down_weight, FF_HALF),
             pl.BlockSpec((FF_HALF, width), lambda step, half: (1 - half[0], 0)),
         ],
         [((count, width), bf16)],

time: 274 us -> 272 us (level)
  waiting for transfers between devices: 65.7 us -> 62.3 us
    pallas_call x0 -> x1, Pallas kernels: none -> 4.27 us  [pack_gate_up(): pl.pallas_call(gate_up_pack, out_shape=jax.ShapeDtypeStruct((count, wide)...]
    dot_general x4 -> x5, matrix products: 7.91 us -> 10.1 us  [dot(): return jnp.dot(left, right, preferred_element_type=f32)]
    pallas_call x7 -> x6, Pallas kernels: 13 us -> 10.9 us  [on_core(): pl.pallas_call(kernel, out_shape=tuple((jax.ShapeDtypeStruct(shape, dtype...]
    unnamed x58 -> x52, local copies, waits for them, and re-layouts: 10.6 us -> 8.58 us
where the time goes in v11:
time: 272 us; the launch traced here: 271 us
  blocking collectives  84.8 us (31%)
  waiting for transfers between devices  62.3 us (23%)
  starting transfers between devices  50.7 us (19%)
  local copies, waits for them, and re-layouts  25.9 us (10%)
  Pallas kernels  22.8 us (8%)
  matrix products  12.8 us (5%)
  other arithmetic  10.6 us (4%)
    all_to_all x4, blocking collectives, exchange(): lax.all_to_all(blocks, tuple(MESH_SIZES), split_axis=0, concat_axis=0, ti...  84.8 us
    all_to_all x6, starting transfers between devices, exchange(): lax.all_to_all(blocks, tuple(MESH_SIZES), split_axis=0, concat_axis=0, ti...  42 us
    all_to_all x6, waiting for transfers between devices, exchange(): lax.all_to_all(blocks, tuple(MESH_SIZES), split_axis=0, concat_axis=0, ti...  29.6 us
    ppermute x1, waiting for transfers between devices, near_label_rows(): return (keep, lax.ppermute(send, 'z', [(0, 1), (1, 0), (2, 3), (3, 2)]))  13.2 us
    pallas_call x6, Pallas kernels, on_core(): pl.pallas_call(kernel, out_shape=tuple((jax.ShapeDtypeStruct(shape, dtype...  10.9 us
    dot_general x5, matrix products, dot(): return jnp.dot(left, right, preferred_element_type=f32)  10.1 us
    ppermute x10, waiting for transfers between devices, other_core(): return lax.ppermute(value, 'core', [(0, 1), (1, 0)])  9.87 us
    ppermute x1, waiting for transfers between devices, other_plane(): return lax.ppermute(rows, 'xh', [(0, 1), (1, 0)])  9.61 us
  transfers between devices with their start and end apart: 19, of which 11 were waited for; matrix products, arithmetic and copies ran while one was open for 12% of the time, Pallas kernels for 1%

profile of v11, /device:TPU:1, one launch (start us, length us, event | category | flops | bytes accessed | tf_op | source)
XLA Modules:
  0.0 271.0 jit_solution(7311431020301047947)
XLA Ops:
  2.2 2.8 %fusion.10 = bf16[512,896]{1,0:T(8,128)(2,1)} fusion(bf16[512,512]{1,0:T(8,128)(2,1)} %param.9, bf16[512,1792]{1,0:T(8,128)(2,1)S(1)} %copy-done, s32[]{:T(128)S(6)} %select_n.98), kind=kOutput, calls=%fused_computation.15 | convolution fusion | flops 470220800 | bytes 2359300 | tf_op jit(solution)/shard_map/dot_general | solution.py:82
  13.8 4.3 %shard_map.112 = bf16[512,1920]{1,0:T(8,128)(2,1)} custom-call(s32[1]{0:T(128)} %bitcast.2.half_ref, bf16[512,896]{1,0:T(8,128)(2,1)} %fusion.8.own_gate, bf16[512,896]{1,0:T(8,128)(2,1)} %fusion.9.own_up, bf16[512,896]{1,0:T(8,128)(2,1)} %collective-permute-done.got_gate, bf16[512,896]{1,0:T(8,128)(2,1)} %copy-done.20, bf16[64,128]{1,0:T(8,128)(2,1)} %pad.4.labels), custom_call_target="tpu_custom_call" | custom-call | flops 2000000 | bytes 6000000 | tf_op jit(solution)/shard_map/pallas_call | solution.py:141
  18.1 8.1 %all-to-all-start = ((bf16[8,64,1920]{2,1,0:T(8,128)(2,1)}), bf16[8,64,1920]{2,1,0:T(8,128)(2,1)}, u32[]{:S(2)}, u32[]{:S(2)}) async-start(bf16[8,64,1920]{2,1,0:T(8,128)(2,1)} %bitcast.65), calls=%async_computation | async-start | bytes 3932160 | tf_op jit(solution)/shard_map/all_to_all | solution.py:49
  29.1 2.8 %collective-permute-done.4.down_got = bf16[896,512]{1,0:T(8,128)(2,1)} collective-permute-done((bf16[896,512]{1,0:T(8,128)(2,1)}, bf16[896,512]{1,0:T(8,128)(2,1)}, u32[]{:S(2)}, u32[]{:S(2)}) %collective-permute-start.4) | collective-permute-done | bytes 917536 | tf_op jit(solution)/shard_map/ppermute | solution.py:34
  31.9 17.6 %all-to-all-done.both = bf16[8,64,1920]{2,1,0:T(8,128)(2,1)} async-done(((bf16[8,64,1920]{2,1,0:T(8,128)(2,1)}), bf16[8,64,1920]{2,1,0:T(8,128)(2,1)}, u32[]{:S(2)}, u32[]{:S(2)}) %all-to-all-start) | async-done | bytes 1966112 | tf_op jit(solution)/shard_map/all_to_all | solution.py:49
  49.5 1.8 shard_map.113
  52.3 4.8 %all-to-all-start.1 = ((bf16[8,64,896]{2,1,0:T(8,128)(2,1)}), bf16[8,64,896]{2,1,0:T(8,128)(2,1)}, u32[]{:S(2)}, u32[]{:S(2)}) async-start(bf16[8,64,896]{2,1,0:T(8,128)(2,1)} %copy-done.13), calls=%async_computation.1 | async-start | bytes 1835008 | tf_op jit(solution)/shard_map/all_to_all | solution.py:49
  63.0 2.3 copy.77
  66.0 3.3 %all-to-all-done.1 = bf16[8,64,896]{2,1,0:T(8,128)(2,1)} async-done(((bf16[8,64,896]{2,1,0:T(8,128)(2,1)}), bf16[8,64,896]{2,1,0:T(8,128)(2,1)}, u32[]{:S(2)}, u32[]{:S(2)}) %all-to-all-start.1) | async-done | bytes 917536 | tf_op jit(solution)/shard_map/all_to_all | solution.py:49
  69.3 2.3 fusion.18.own_part
  73.5 10.0 %all-to-all-start.2 = ((bf16[8,64,512]{2,1,0:T(8,128)(2,1)}), bf16[8,64,512]{2,1,0:T(8,128)(2,1)}, u32[]{:S(2)}, u32[]{:S(2)}) async-start(bf16[8,64,512]{2,1,0:T(8,128)(2,1)} %bitcast.13), calls=%async_computation.2 | async-start | bytes 1048576 | tf_op jit(solution)/shard_map/all_to_all | solution.py:49
  83.5 7.9 %all-to-all-done.2 = bf16[8,64,512]{2,1,0:T(8,128)(2,1)} async-done(((bf16[8,64,512]{2,1,0:T(8,128)(2,1)}), bf16[8,64,512]{2,1,0:T(8,128)(2,1)}, u32[]{:S(2)}, u32[]{:S(2)}) %all-to-all-start.2) | async-done | bytes 524320 | tf_op jit(solution)/shard_map/all_to_all | solution.py:49
  93.5 13.4 %all_to_all.50 = bf16[8,64,512]{2,1,0:T(8,128)(2,1)S(1)} all-to-all(bf16[8,64,512]{2,1,0:T(8,128)(2,1)S(1)} %broadcast_in_dim.6), channel_id=1, replica_groups={{0,1,2,3,4,5,6,7},{15,14,13,12,11,10,9,8},{16,17,18,19,20,21,22,23},{31..., dimensions={0} | all-to-all | bytes 1048576 | tf_op jit(solution)/shard_map/all_to_all | solution.py:49
  112.6 5.5 %all-to-all-start.4 = ((s16[8,64,1152]{2,1,0:T(8,128)(2,1)}), s16[8,64,1152]{2,1,0:T(8,128)(2,1)S(1)}, u32[]{:S(2)}, u32[]{:S(2)}) async-start(s16[8,64,1152]{2,1,0:T(8,128)(2,1)} %bitcast.58), calls=%async_computation.4 | async-start | bytes 2359296 | tf_op jit(solution)/shard_map/all_to_all | solution.py:49
  118.1 2.2 dynamic-slice_bitcast_fusion
  120.4 13.2 %collective-permute-done.7 = bf16[2,2,64,1024]{3,2,1,0:T(8,128)(2,1)} collective-permute-done((bf16[2,2,64,1024]{3,2,1,0:T(8,128)(2,1)}, bf16[2,2,64,1024]{3,2,1,0:T(8,128)(2,1)}, u32[]{:S(2)}, u32[]{:S(2)}) %collective-permute-start.7) | collective-permute-done | bytes 524320 | tf_op jit(solution)/shard_map/ppermute | solution.py:331
  135.5 5.9 %all-to-all-start.5 = ((bf16[8,64,1152]{2,1,0:T(8,128)(2,1)}), bf16[8,64,1152]{2,1,0:T(8,128)(2,1)S(1)}, u32[]{:S(2)}, u32[]{:S(2)}) async-start(bf16[8,64,1152]{2,1,0:T(8,128)(2,1)} %copy-done.5), calls=%async_computation.5 | async-start | bytes 2359296 | tf_op jit(solution)/shard_map/all_to_all | solution.py:49
  145.5 2.1 copy.78
  147.6 1.9 rev.7
  149.4 2.0 copy.79
  151.5 2.3 select_bitcast_fusion
  156.3 2.8 %collective-permute-done.9.far = bf16[512,1152]{1,0:T(8,128)(2,1)S(1)} collective-permute-done((bf16[512,1152]{1,0:T(8,128)(2,1)S(1)}, bf16[512,1152]{1,0:T(8,128)(2,1)S(1)}, u32[]{:S(2)}, u32[]{:S(2)}) %collective-permute-start.9) | collective-permute-done | bytes 1179680 | tf_op jit(solution)/shard_map/ppermute | solution.py:34
  161.4 7.7 %all-to-all-start.6 = ((bf16[8,64,640]{2,1,0:T(8,128)(2,1)}), bf16[8,64,640]{2,1,0:T(8,128)(2,1)S(1)}, u32[]{:S(2)}, u32[]{:S(2)}) async-start(bf16[8,64,640]{2,1,0:T(8,128)(2,1)} %bitcast.59), calls=%async_computation.6 | async-start | bytes 1310720 | tf_op jit(solution)/shard_map/all_to_all | solution.py:49
  169.4 9.6 %collective-permute-done.10 = bf16[64,1024]{1,0:T(8,128)(2,1)S(1)} collective-permute-done((bf16[64,1024]{1,0:T(8,128)(2,1)}, bf16[64,1024]{1,0:T(8,128)(2,1)S(1)}, u32[]{:S(2)}, u32[]{:S(2)}) %collective-permute-start.10) | collective-permute-done | bytes 131104 | tf_op jit(solution)/shard_map/ppermute | solution.py:342
  181.9 19.4 %all_to_all.51 = bf16[8,64,1024]{2,1,0:T(8,128)(2,1)S(1)} all-to-all(bf16[8,64,1024]{2,1,0:T(8,128)(2,1)S(1)} %broadcast_in_dim.7), channel_id=1, replica_groups={{0,1,2,3,4,5,6,7},{15,14,13,12,11,10,9,8},{16,17,18,19,20,21,22,23},{31..., dimensions={0} | all-to-all | bytes 2097152 | tf_op jit(solution)/shard_map/all_to_all | solution.py:49
  201.3 2.0 collective-permute-start.11
  203.3 2.3 collective-permute-done.11.far_dsummed
  205.6 3.5 %shard_map.118 = bf16[512,1792]{1,0:T(8,128)(2,1)S(1)} custom-call(s32[1]{0:T(128)} %bitcast.2.half_ref, bf16[512,1024]{1,0:T(8,128)(2,1)S(1)} %bitcast.64, bf16[512,1024]{1,0:T(8,128)(2,1)S(1)} %collective-permute-done.11.far_dsummed, bf16[1792,512]{1,0:T(8,128)(2,1)S(1)} %copy-done.9, bf16[896,512]{1,0:T(8,128)(2,1)} %collective-permute-done.4.down_got), custom_call_target="tpu_custom_call" | custom-call | flops 1879048192 | bytes 4849664 | tf_op jit(solution)/shard_map/pallas_call | solution.py:108
  209.1 26.3 %all_to_all.52 = bf16[8,64,1792]{2,1,0:T(8,128)(2,1)S(1)} all-to-all(bf16[8,64,1792]{2,1,0:T(8,128)(2,1)S(1)} %bitcast.62), channel_id=1, replica_groups={{0,16,32,48,64,80,96,112},{1,17,33,49,65,81,97,113},{2,18,34,50,66,82,9..., dimensions={0} | all-to-all | bytes 3670016 | tf_op jit(solution)/shard_map/all_to_all | solution.py:49
  235.9 25.8 %all_to_all.53 = bf16[8,64,1792]{2,1,0:T(8,128)(2,1)S(1)} all-to-all(bf16[8,64,1792]{2,1,0:T(8,128)(2,1)S(1)} %broadcast_in_dim.8), channel_id=1, replica_groups={{0,16,32,48,64,80,96,112},{1,17,33,49,65,81,97,113},{2,18,34,50,66,82,9..., dimensions={0} | all-to-all | bytes 3670016 | tf_op jit(solution)/shard_map/all_to_all | solution.py:49
  263.4 3.8 %shard_map.119 = (f32[512,1792]{1,0:T(8,128)}, f32[512,1792]{1,0:T(8,128)}, f32[512,1792]{1,0:T(8,128)}) custom-call(s32[1]{0:T(128)} %bitcast.2.half_ref, bf16[512,512]{1,0:T(8,128)(2,1)S(1)} %copy-done.12, bf16[512,1792]{1,0:T(8,128)(2,1)S(1)} %bitcast.55, f32[512,1792]{1,0:T(8,128)S(1)} %copy-done.3, f32[512,1792]{1,0:T(8,128)S(1)} %copy-done.4), custom_call_target="tpu_custom_call" | custom-call | flops 950000000 | bytes 11000000 | tf_op jit(solution)/shard_map/pallas_call | solution.py:293
  267.2 3.8 %shard_map.120 = (f32[512,1792]{1,0:T(8,128)}, f32[512,1792]{1,0:T(8,128)}, f32[512,1792]{1,0:T(8,128)}) custom-call(s32[1]{0:T(128)} %bitcast.half_ref, bf16[512,512]{1,0:T(8,128)(2,1)S(1)} %copy-done.11, bf16[512,1792]{1,0:T(8,128)(2,1)S(1)} %collective-permute-done.12.cot, ...), custom_call_target="tpu_custom_call", output_to_operand_aliasing={{0}: (5, {}), {1}: (6, {}), {2}: (7, {})} | custom-call | flops 950000000 | bytes 11000000 | tf_op jit(solution)/shard_map/pallas_call | solution.py:293
  (122 shorter events, 46.4 us)
Async XLA Ops:
  0.6 5.9 %copy-start.14 = (bf16[512,512]{1,0:T(8,128)(2,1)S(1)}, bf16[512,512]{1,0:T(8,128)(2,1)}, u32[]{:S(2)}) copy-start(bf16[512,512]{1,0:T(8,128)(2,1)} %param.9) | copy-start | bytes 1572868
  0.7 4.3 %copy-start.22 = (s32[32]{0:T(128)S(1)}, s32[32]{0:T(128)}, u32[]{:S(2)}) copy-start(s32[32]{0:T(128)} %param.17) | copy-start | bytes 388
  0.7 4.3 %copy-start.23 = (s32[32]{0:T(128)S(1)}, s32[32]{0:T(128)}, u32[]{:S(2)}) copy-start(s32[32]{0:T(128)} %param.16) | copy-start | bytes 388
  2.2 4.3 %copy-start.24 = (bf16[512,1792]{1,0:T(8,128)(2,1)S(1)}, bf16[512,1792]{1,0:T(8,128)(2,1)}, u32[]{:S(2)}) copy-start(bf16[512,1792]{1,0:T(8,128)(2,1)} %param.11) | copy-start | bytes 5505028
  5.0 7.0 %collective-permute-start.2 = (s32[32,2]{0,1:T(2,128)S(1)}, s32[32,2]{0,1:T(2,128)S(1)}, u32[]{:S(2)}, u32[]{:S(2)}) collective-permute-start(s32[32,2]{0,1:T(2,128)S(1)} %pad_add_fusion), channel_id=1, source_target_pairs={{0,8},{8,0},{1,9},{9,1},{2,10},{10,2},{3,11},{11,3},{4,12},{12,4},... | collective-permute-start | bytes 776 | tf_op jit(solution)/shard_map/ppermute | solution.py:34
  8.2 4.7 %collective-permute-start.1 = (bf16[512,896]{1,0:T(8,128)(2,1)}, bf16[512,896]{1,0:T(8,128)(2,1)S(1)}, u32[]{:S(2)}, u32[]{:S(2)}) collective-permute-start(bf16[512,896]{1,0:T(8,128)(2,1)} %fusion.11), channel_id=1, source_target_pairs={{0,8},{8,0},{1,9},{9,1},{2,10},{10,2},{3,11},{11,3},{4,12},{12,4},... | collective-permute-start | bytes 2752520 | tf_op jit(solution)/shard_map/ppermute | solution.py:34
  8.2 4.6 %collective-permute-start = (bf16[512,896]{1,0:T(8,128)(2,1)}, bf16[512,896]{1,0:T(8,128)(2,1)}, u32[]{:S(2)}, u32[]{:S(2)}) collective-permute-start(bf16[512,896]{1,0:T(8,128)(2,1)} %fusion.10), channel_id=1, source_target_pairs={{0,8},{8,0},{1,9},{9,1},{2,10},{10,2},{3,11},{11,3},{4,12},{12,4},... | collective-permute-start | bytes 2752520 | tf_op jit(solution)/shard_map/ppermute | solution.py:34
  18.1 8.1 %copy-start.2 = (bf16[512,2048]{1,0:T(8,128)(2,1)S(1)}, bf16[512,2048]{1,0:T(8,128)(2,1)}, u32[]{:S(2)}) copy-start(bf16[512,2048]{1,0:T(8,128)(2,1)} %head_far.1) | copy-start | bytes 6291460
  18.1 31.4 %all-to-all-start = ((bf16[8,64,1920]{2,1,0:T(8,128)(2,1)}), bf16[8,64,1920]{2,1,0:T(8,128)(2,1)}, u32[]{:S(2)}, u32[]{:S(2)}) async-start(bf16[8,64,1920]{2,1,0:T(8,128)(2,1)} %bitcast.65), calls=%async_computation | async-start | bytes 3932160 | tf_op jit(solution)/shard_map/all_to_all | solution.py:49
  27.3 4.6 %collective-permute-start.3 = (bf16[512,1024]{1,0:T(8,128)(2,1)}, bf16[512,1024]{1,0:T(8,128)(2,1)S(1)}, u32[]{:S(2)}, u32[]{:S(2)}) collective-permute-start(bf16[512,1024]{1,0:T(8,128)(2,1)} %constant_dynamic-slice_fusion.2), channel_id=1, source_target_pairs={{0,8},{8,0},{1,9},{9,1},{2,10},{10,2},{3,11},{11,3},{4,12},{12,4},... | collective-permute-start | bytes 3145736 | tf_op jit(solution)/shard_map/ppermute | solution.py:34
  29.1 2.8 %collective-permute-start.4 = (bf16[896,512]{1,0:T(8,128)(2,1)}, bf16[896,512]{1,0:T(8,128)(2,1)}, u32[]{:S(2)}, u32[]{:S(2)}) collective-permute-start(bf16[896,512]{1,0:T(8,128)(2,1)} %constant_dynamic-slice_fusion.1), channel_id=1, source_target_pairs={{0,8},{8,0},{1,9},{9,1},{2,10},{10,2},{3,11},{11,3},{4,12},{12,4},... | collective-permute-start | bytes 2752520 | tf_op jit(solution)/shard_map/ppermute | solution.py:34
  52.3 17.1 %all-to-all-start.1 = ((bf16[8,64,896]{2,1,0:T(8,128)(2,1)}), bf16[8,64,896]{2,1,0:T(8,128)(2,1)}, u32[]{:S(2)}, u32[]{:S(2)}) async-start(bf16[8,64,896]{2,1,0:T(8,128)(2,1)} %copy-done.13), calls=%async_computation.1 | async-start | bytes 1835008 | tf_op jit(solution)/shard_map/all_to_all | solution.py:49
  69.3 2.7 collective-permute-start.5
  73.5 17.9 %all-to-all-start.2 = ((bf16[8,64,512]{2,1,0:T(8,128)(2,1)}), bf16[8,64,512]{2,1,0:T(8,128)(2,1)}, u32[]{:S(2)}, u32[]{:S(2)}) async-start(bf16[8,64,512]{2,1,0:T(8,128)(2,1)} %bitcast.13), calls=%async_computation.2 | async-start | bytes 1048576 | tf_op jit(solution)/shard_map/all_to_all | solution.py:49
  92.6 19.0 %copy-start.18 = (f32[64,512]{1,0:T(8,128)}, f32[64,512]{1,0:T(8,128)S(1)}, u32[]{:S(2)}) copy-start(f32[64,512]{1,0:T(8,128)S(1)} %convert_reduce_fusion.1) | copy-start | bytes 393220
  106.9 3.0 %collective-permute-start.6 = (bf16[512,512]{1,0:T(8,128)(2,1)S(1)}, bf16[512,512]{1,0:T(8,128)(2,1)S(1)}, u32[]{:S(2)}, u32[]{:S(2)}) collective-permute-start(bf16[512,512]{1,0:T(8,128)(2,1)S(1)} %bitcast.60), channel_id=1, source_target_pairs={{0,8},{8,0},{1,9},{9,1},{2,10},{10,2},{3,11},{11,3},{4,12},{12,4},... | collective-permute-start | bytes 1572872 | tf_op jit(solution)/shard_map/ppermute | solution.py:34
  112.6 21.0 %all-to-all-start.4 = ((s16[8,64,1152]{2,1,0:T(8,128)(2,1)}), s16[8,64,1152]{2,1,0:T(8,128)(2,1)S(1)}, u32[]{:S(2)}, u32[]{:S(2)}) async-start(s16[8,64,1152]{2,1,0:T(8,128)(2,1)} %bitcast.58), calls=%async_computation.4 | async-start | bytes 2359296 | tf_op jit(solution)/shard_map/all_to_all | solution.py:49
  120.4 13.2 %collective-permute-start.7 = (bf16[2,2,64,1024]{3,2,1,0:T(8,128)(2,1)}, bf16[2,2,64,1024]{3,2,1,0:T(8,128)(2,1)}, u32[]{:S(2)}, u32[]{:S(2)}) collective-permute-start(bf16[2,2,64,1024]{3,2,1,0:T(8,128)(2,1)} %get-tuple-element.90), channel_id=1, source_target_pairs={{0,2},{2,0},{4,6},{6,4},{1,3},{3,1},{5,7},{7,5},{8,10},{10,8},{12,... | collective-permute-start | bytes 1572872 | tf_op jit(solution)/shard_map/ppermute | solution.py:331
  135.5 20.8 %all-to-all-start.5 = ((bf16[8,64,1152]{2,1,0:T(8,128)(2,1)}), bf16[8,64,1152]{2,1,0:T(8,128)(2,1)S(1)}, u32[]{:S(2)}, u32[]{:S(2)}) async-start(bf16[8,64,1152]{2,1,0:T(8,128)(2,1)} %copy-done.5), calls=%async_computation.5 | async-start | bytes 2359296 | tf_op jit(solution)/shard_map/all_to_all | solution.py:49
  144.3 9.5 %collective-permute-start.8 = (bf16[2,64,1024]{2,1,0:T(8,128)(2,1)}, bf16[2,64,1024]{2,1,0:T(8,128)(2,1)}, u32[]{:S(2)}, u32[]{:S(2)}) collective-permute-start(bf16[2,64,1024]{2,1,0:T(8,128)(2,1)} %dynamic-slice_bitcast_fusion.2), channel_id=1, source_target_pairs={{0,4},{4,0},{2,6},{6,2},{1,5},{5,1},{3,7},{7,3},{8,12},{12,8},{10,... | collective-permute-start | bytes 786440 | tf_op jit(solution)/shard_map/ppermute | solution.py:337
  156.3 2.8 %collective-permute-start.9 = (bf16[512,1152]{1,0:T(8,128)(2,1)S(1)}, bf16[512,1152]{1,0:T(8,128)(2,1)S(1)}, u32[]{:S(2)}, u32[]{:S(2)}) collective-permute-start(bf16[512,1152]{1,0:T(8,128)(2,1)S(1)} %bitcast.56), channel_id=1, source_target_pairs={{0,8},{8,0},{1,9},{9,1},{2,10},{10,2},{3,11},{11,3},{4,12},{12,4},... | collective-permute-start | bytes 3538952 | tf_op jit(solution)/shard_map/ppermute | solution.py:34
  161.4 17.6 %all-to-all-start.6 = ((bf16[8,64,640]{2,1,0:T(8,128)(2,1)}), bf16[8,64,640]{2,1,0:T(8,128)(2,1)S(1)}, u32[]{:S(2)}, u32[]{:S(2)}) async-start(bf16[8,64,640]{2,1,0:T(8,128)(2,1)} %bitcast.59), calls=%async_computation.6 | async-start | bytes 1310720 | tf_op jit(solution)/shard_map/all_to_all | solution.py:49
  169.1 11.5 %copy-start.21 = (bf16[64,1024]{1,0:T(8,128)(2,1)S(1)}, bf16[64,1024]{1,0:T(8,128)(2,1)}, u32[]{:S(2)}) copy-start(bf16[64,1024]{1,0:T(8,128)(2,1)} %get-tuple-element.69) | copy-start | bytes 393220
  169.1 11.6 %copy-start.19 = (f32[64,512]{1,0:T(8,128)S(1)}, f32[64,512]{1,0:T(8,128)}, u32[]{:S(2)}) copy-start(f32[64,512]{1,0:T(8,128)} %copy-done.18) | copy-start | bytes 393220
  169.1 9.9 %collective-permute-start.10 = (bf16[64,1024]{1,0:T(8,128)(2,1)}, bf16[64,1024]{1,0:T(8,128)(2,1)S(1)}, u32[]{:S(2)}, u32[]{:S(2)}) collective-permute-start(bf16[64,1024]{1,0:T(8,128)(2,1)} %get-tuple-element.67), channel_id=1, source_target_pairs={{0,1},{1,0},{2,3},{3,2},{4,5},{5,4},{6,7},{7,6},{8,9},{9,8},{10,11... | collective-permute-start | bytes 393224 | tf_op jit(solution)/shard_map/ppermute | solution.py:342
  181.7 23.9 %copy-start.9 = (bf16[1792,512]{1,0:T(8,128)(2,1)S(1)}, bf16[1792,512]{1,0:T(8,128)(2,1)}, u32[]{:S(2)}) copy-start(bf16[1792,512]{1,0:T(8,128)(2,1)} %down.1) | copy-start | bytes 5505028
  201.3 4.3 %collective-permute-start.11 = (bf16[512,1024]{1,0:T(8,128)(2,1)S(1)}, bf16[512,1024]{1,0:T(8,128)(2,1)S(1)}, u32[]{:S(2)}, u32[]{:S(2)}) collective-permute-start(bf16[512,1024]{1,0:T(8,128)(2,1)S(1)} %bitcast.63), channel_id=1, source_target_pairs={{0,8},{8,0},{1,9},{9,1},{2,10},{10,2},{3,11},{11,3},{4,12},{12,4},... | collective-permute-start | bytes 3145736 | tf_op jit(solution)/shard_map/ppermute | solution.py:34
  235.4 27.9 %copy-start.4 = (f32[512,1792]{1,0:T(8,128)S(1)}, f32[512,1792]{1,0:T(8,128)}, u32[]{:S(2)}) copy-start(f32[512,1792]{1,0:T(8,128)} %curve_ref.3) | copy-start | bytes 11010052
  235.7 27.6 %copy-start.12 = (bf16[512,512]{1,0:T(8,128)(2,1)S(1)}, bf16[512,512]{1,0:T(8,128)(2,1)}, u32[]{:S(2)}) copy-start(bf16[512,512]{1,0:T(8,128)(2,1)} %get-tuple-element.73.turned) | copy-start | bytes 1572868
  235.9 27.5 %copy-start.3 = (f32[512,1792]{1,0:T(8,128)S(1)}, f32[512,1792]{1,0:T(8,128)}, u32[]{:S(2)}) copy-start(f32[512,1792]{1,0:T(8,128)} %moment_ref.3) | copy-start | bytes 11010052
  261.6 5.6 %copy-start.11 = (bf16[512,512]{1,0:T(8,128)(2,1)S(1)}, bf16[512,512]{1,0:T(8,128)(2,1)}, u32[]{:S(2)}) copy-start(bf16[512,512]{1,0:T(8,128)(2,1)} %get-tuple-element.63.turned) | copy-start | bytes 1572868
  261.6 5.6 %collective-permute-start.12 = (bf16[512,1792]{1,0:T(8,128)(2,1)S(1)}, bf16[512,1792]{1,0:T(8,128)(2,1)S(1)}, u32[]{:S(2)}, u32[]{:S(2)}) collective-permute-start(bf16[512,1792]{1,0:T(8,128)(2,1)S(1)} %bitcast.54), channel_id=1, source_target_pairs={{0,8},{8,0},{1,9},{9,1},{2,10},{10,2},{3,11},{11,3},{4,12},{12,4},... | collective-permute-start | bytes 5505032 | tf_op jit(solution)/shard_map/ppermute | solution.py:34
  (13 other events, 20.2 us)

commit v12 on v10

--- a/solution.py
+++ b/solution.py
@@ -132,8 +132,8 @@
         out[rows, 2 * FF_HALF :] = labels[...]
 
 
-def branch_kernel(half_ref, own, far, down_own, down_far, out):
-    out[...] = join_cores(dot(own[...], down_own[...]), dot(far[...], down_far[...])).astype(bf16)
+def branch_kernel(half_ref, own_part, far, down_far, out):
+    out[...] = join_cores(own_part[...], dot(far[...], down_far[...])).astype(bf16)
 
 
 def hidden_kernel(half_ref, both, hidden, silu_out):
@@ -259,7 +259,10 @@
     curve = beta_two * curve_ref[...] + (1.0 - beta_two) * grad_sampled * grad_sampled
     new_moment[...] = moment
     new_curve[...] = curve
-    update[...] = jnp.clip(moment / (rho_scale * curve), -1.0, 1.0)
+    divisor = rho_scale * curve
+    inverse = pl.reciprocal(divisor, approx=True)
+    inverse = inverse * (2.0 - divisor * inverse)
+    update[...] = jnp.clip(moment * inverse, -1.0, 1.0)
 
 
 def sophia_half(half, turned, cot, moment, curve, done):
@@ -394,14 +397,14 @@
     )
     hidden_own = hidden_own.reshape(count, FF_HALF)
     hidden_far = other_core(hidden_own)
+    own_part = dot(hidden_own, lax.dynamic_slice_in_dim(down_weight, core * FF_HALF, FF_HALF, 0))
     branch = on_core(
         branch_kernel,
         core,
-        (hidden_own, hidden_far, down_weight, down_weight),
+        (own_part, hidden_far, down_weight),
         [
-            whole(hidden_own),
+            whole(own_part),
             whole(hidden_far),
-            rows_of(down_weight, FF_HALF),
             pl.BlockSpec((FF_HALF, width), lambda step, half: (1 - half[0], 0)),
         ],
         [((count, width), bf16)],

time: 274 us -> 268 us (0.978)
  waiting for transfers between devices: 65.7 us -> 62.3 us
    unnamed x58 -> x52, local copies, waits for them, and re-layouts: 10.6 us -> 7.58 us
    dot_general x4 -> x5, matrix products: 7.91 us -> 9.28 us  [dot(): return jnp.dot(left, right, preferred_element_type=f32)]
  transfers between devices with their start and end apart: 19 -> 19, of which waited for: 11 -> 11; matrix products, arithmetic and copies ran while one was open for 12% -> 13% of each run, Pallas kernels for 1% -> 1%
where the time goes in v12:
time: 268 us; the launch traced here: 267 us
  blocking collectives  84.8 us (32%)
  waiting for transfers between devices  62.3 us (23%)
  starting transfers between devices  50.6 us (19%)
  local copies, waits for them, and re-layouts  24.3 us (9%)
  Pallas kernels  20 us (7%)
  matrix products  12 us (4%)
  other arithmetic  11.4 us (4%)
    all_to_all x4, blocking collectives, exchange(): lax.all_to_all(blocks, tuple(MESH_SIZES), split_axis=0, concat_axis=0, ti...  84.8 us
    all_to_all x6, starting transfers between devices, exchange(): lax.all_to_all(blocks, tuple(MESH_SIZES), split_axis=0, concat_axis=0, ti...  42 us
    all_to_all x6, waiting for transfers between devices, exchange(): lax.all_to_all(blocks, tuple(MESH_SIZES), split_axis=0, concat_axis=0, ti...  29.6 us
    ppermute x1, waiting for transfers between devices, near_label_rows(): return (keep, lax.ppermute(send, 'z', [(0, 1), (1, 0), (2, 3), (3, 2)]))  13.2 us
    pallas_call x7, Pallas kernels, on_core(): pl.pallas_call(kernel, out_shape=tuple((jax.ShapeDtypeStruct(shape, dtype...  12.5 us
    ppermute x10, waiting for transfers between devices, other_core(): return lax.ppermute(value, 'core', [(0, 1), (1, 0)])  9.87 us
    ppermute x1, waiting for transfers between devices, other_plane(): return lax.ppermute(rows, 'xh', [(0, 1), (1, 0)])  9.61 us
    dot_general x5, matrix products, dot(): return jnp.dot(left, right, preferred_element_type=f32)  9.28 us
  transfers between devices with their start and end apart: 19, of which 11 were waited for; matrix products, arithmetic and copies ran while one was open for 13% of the time, Pallas kernels for 1%

profile of v12, /device:TPU:1, one launch (start us, length us, event | category | flops | bytes accessed | tf_op | source)
XLA Modules:
  0.0 266.6 jit_solution(15970953033686171652)
XLA Ops:
  2.9 3.0 %fusion.11 = bf16[512,896]{1,0:T(8,128)(2,1)} fusion(bf16[512,512]{1,0:T(8,128)(2,1)} %param.9, bf16[512,1792]{1,0:T(8,128)(2,1)} %param.11, s32[]{:T(128)S(6)} %select_n.98), kind=kOutput, calls=%fused_computation.16 | convolution fusion | flops 470220800 | bytes 2359300 | tf_op jit(solution)/shard_map/dot_general | solution.py:82
  13.8 8.1 %all-to-all-start = ((bf16[8,64,1920]{2,1,0:T(8,128)(2,1)}), bf16[8,64,1920]{2,1,0:T(8,128)(2,1)}, u32[]{:S(2)}, u32[]{:S(2)}) async-start(bf16[8,64,1920]{2,1,0:T(8,128)(2,1)} %bitcast.54), calls=%async_computation | async-start | bytes 3932160 | tf_op jit(solution)/shard_map/all_to_all | solution.py:49
  24.8 2.8 %collective-permute-done.4.down_got = bf16[896,512]{1,0:T(8,128)(2,1)} collective-permute-done((bf16[896,512]{1,0:T(8,128)(2,1)}, bf16[896,512]{1,0:T(8,128)(2,1)}, u32[]{:S(2)}, u32[]{:S(2)}) %collective-permute-start.4) | collective-permute-done | bytes 917536 | tf_op jit(solution)/shard_map/ppermute | solution.py:34
  27.6 17.6 %all-to-all-done.both = bf16[8,64,1920]{2,1,0:T(8,128)(2,1)} async-done(((bf16[8,64,1920]{2,1,0:T(8,128)(2,1)}), bf16[8,64,1920]{2,1,0:T(8,128)(2,1)}, u32[]{:S(2)}, u32[]{:S(2)}) %all-to-all-start) | async-done | bytes 1966112 | tf_op jit(solution)/shard_map/all_to_all | solution.py:49
  45.2 1.8 shard_map.113
  47.9 4.8 %all-to-all-start.1 = ((bf16[8,64,896]{2,1,0:T(8,128)(2,1)}), bf16[8,64,896]{2,1,0:T(8,128)(2,1)}, u32[]{:S(2)}, u32[]{:S(2)}) async-start(bf16[8,64,896]{2,1,0:T(8,128)(2,1)} %copy-done.14), calls=%async_computation.1 | async-start | bytes 1835008 | tf_op jit(solution)/shard_map/all_to_all | solution.py:49
  58.7 2.3 copy.77
  61.7 3.3 %all-to-all-done.1 = bf16[8,64,896]{2,1,0:T(8,128)(2,1)} async-done(((bf16[8,64,896]{2,1,0:T(8,128)(2,1)}), bf16[8,64,896]{2,1,0:T(8,128)(2,1)}, u32[]{:S(2)}, u32[]{:S(2)}) %all-to-all-start.1) | async-done | bytes 917536 | tf_op jit(solution)/shard_map/all_to_all | solution.py:49
  65.0 2.3 fusion.18.own_part
  69.2 10.0 %all-to-all-start.2 = ((bf16[8,64,512]{2,1,0:T(8,128)(2,1)}), bf16[8,64,512]{2,1,0:T(8,128)(2,1)}, u32[]{:S(2)}, u32[]{:S(2)}) async-start(bf16[8,64,512]{2,1,0:T(8,128)(2,1)} %bitcast.13), calls=%async_computation.2 | async-start | bytes 1048576 | tf_op jit(solution)/shard_map/all_to_all | solution.py:49
  79.2 7.9 %all-to-all-done.2 = bf16[8,64,512]{2,1,0:T(8,128)(2,1)} async-done(((bf16[8,64,512]{2,1,0:T(8,128)(2,1)}), bf16[8,64,512]{2,1,0:T(8,128)(2,1)}, u32[]{:S(2)}, u32[]{:S(2)}) %all-to-all-start.2) | async-done | bytes 524320 | tf_op jit(solution)/shard_map/all_to_all | solution.py:49
  89.2 13.4 %all_to_all.50 = bf16[8,64,512]{2,1,0:T(8,128)(2,1)S(1)} all-to-all(bf16[8,64,512]{2,1,0:T(8,128)(2,1)S(1)} %broadcast_in_dim.6), channel_id=1, replica_groups={{0,1,2,3,4,5,6,7},{15,14,13,12,11,10,9,8},{16,17,18,19,20,21,22,23},{31..., dimensions={0} | all-to-all | bytes 1048576 | tf_op jit(solution)/shard_map/all_to_all | solution.py:49
  108.3 5.5 %all-to-all-start.4 = ((s16[8,64,1152]{2,1,0:T(8,128)(2,1)}), s16[8,64,1152]{2,1,0:T(8,128)(2,1)S(1)}, u32[]{:S(2)}, u32[]{:S(2)}) async-start(s16[8,64,1152]{2,1,0:T(8,128)(2,1)} %bitcast.59), calls=%async_computation.4 | async-start | bytes 2359296 | tf_op jit(solution)/shard_map/all_to_all | solution.py:49
  113.8 2.2 dynamic-slice_bitcast_fusion
  116.1 13.2 %collective-permute-done.7 = bf16[2,2,64,1024]{3,2,1,0:T(8,128)(2,1)} collective-permute-done((bf16[2,2,64,1024]{3,2,1,0:T(8,128)(2,1)}, bf16[2,2,64,1024]{3,2,1,0:T(8,128)(2,1)}, u32[]{:S(2)}, u32[]{:S(2)}) %collective-permute-start.7) | collective-permute-done | bytes 524320 | tf_op jit(solution)/shard_map/ppermute | solution.py:312
  131.2 5.9 %all-to-all-start.5 = ((bf16[8,64,1152]{2,1,0:T(8,128)(2,1)}), bf16[8,64,1152]{2,1,0:T(8,128)(2,1)S(1)}, u32[]{:S(2)}, u32[]{:S(2)}) async-start(bf16[8,64,1152]{2,1,0:T(8,128)(2,1)} %copy-done.6), calls=%async_computation.5 | async-start | bytes 2359296 | tf_op jit(solution)/shard_map/all_to_all | solution.py:49
  141.2 2.1 copy.78
  143.2 1.9 rev.7
  145.1 2.0 copy.79
  147.2 2.3 select_bitcast_fusion
  152.0 2.8 %collective-permute-done.9.far = bf16[512,1152]{1,0:T(8,128)(2,1)S(1)} collective-permute-done((bf16[512,1152]{1,0:T(8,128)(2,1)S(1)}, bf16[512,1152]{1,0:T(8,128)(2,1)S(1)}, u32[]{:S(2)}, u32[]{:S(2)}) %collective-permute-start.9) | collective-permute-done | bytes 1179680 | tf_op jit(solution)/shard_map/ppermute | solution.py:34
  157.1 7.7 %all-to-all-start.6 = ((bf16[8,64,640]{2,1,0:T(8,128)(2,1)}), bf16[8,64,640]{2,1,0:T(8,128)(2,1)S(1)}, u32[]{:S(2)}, u32[]{:S(2)}) async-start(bf16[8,64,640]{2,1,0:T(8,128)(2,1)} %bitcast.60), calls=%async_computation.6 | async-start | bytes 1310720 | tf_op jit(solution)/shard_map/all_to_all | solution.py:49
  165.1 9.6 %collective-permute-done.10 = bf16[64,1024]{1,0:T(8,128)(2,1)S(1)} collective-permute-done((bf16[64,1024]{1,0:T(8,128)(2,1)}, bf16[64,1024]{1,0:T(8,128)(2,1)S(1)}, u32[]{:S(2)}, u32[]{:S(2)}) %collective-permute-start.10) | collective-permute-done | bytes 131104 | tf_op jit(solution)/shard_map/ppermute | solution.py:323
  177.6 19.4 %all_to_all.51 = bf16[8,64,1024]{2,1,0:T(8,128)(2,1)S(1)} all-to-all(bf16[8,64,1024]{2,1,0:T(8,128)(2,1)S(1)} %broadcast_in_dim.7), channel_id=1, replica_groups={{0,1,2,3,4,5,6,7},{15,14,13,12,11,10,9,8},{16,17,18,19,20,21,22,23},{31..., dimensions={0} | all-to-all | bytes 2097152 | tf_op jit(solution)/shard_map/all_to_all | solution.py:49
  197.0 2.0 collective-permute-start.11
  199.0 2.3 collective-permute-done.11.far_dsummed
  201.3 3.5 %shard_map.118 = bf16[512,1792]{1,0:T(8,128)(2,1)S(1)} custom-call(s32[1]{0:T(128)} %bitcast.2.half_ref, bf16[512,1024]{1,0:T(8,128)(2,1)S(1)} %bitcast.65, bf16[512,1024]{1,0:T(8,128)(2,1)S(1)} %collective-permute-done.11.far_dsummed, bf16[1792,512]{1,0:T(8,128)(2,1)S(1)} %copy-done.10, bf16[896,512]{1,0:T(8,128)(2,1)} %collective-permute-done.4.down_got), custom_call_target="tpu_custom_call" | custom-call | flops 1879048192 | bytes 4849664 | tf_op jit(solution)/shard_map/pallas_call | solution.py:108
  204.8 26.3 %all_to_all.52 = bf16[8,64,1792]{2,1,0:T(8,128)(2,1)S(1)} all-to-all(bf16[8,64,1792]{2,1,0:T(8,128)(2,1)S(1)} %bitcast.63), channel_id=1, replica_groups={{0,16,32,48,64,80,96,112},{1,17,33,49,65,81,97,113},{2,18,34,50,66,82,9..., dimensions={0} | all-to-all | bytes 3670016 | tf_op jit(solution)/shard_map/all_to_all | solution.py:49
  231.6 25.8 %all_to_all.53 = bf16[8,64,1792]{2,1,0:T(8,128)(2,1)S(1)} all-to-all(bf16[8,64,1792]{2,1,0:T(8,128)(2,1)S(1)} %broadcast_in_dim.8), channel_id=1, replica_groups={{0,16,32,48,64,80,96,112},{1,17,33,49,65,81,97,113},{2,18,34,50,66,82,9..., dimensions={0} | all-to-all | bytes 3670016 | tf_op jit(solution)/shard_map/all_to_all | solution.py:49
  257.3 1.7 collective-permute-start.12
  259.1 3.8 %shard_map.119 = (f32[512,1792]{1,0:T(8,128)}, f32[512,1792]{1,0:T(8,128)}, f32[512,1792]{1,0:T(8,128)}) custom-call(s32[1]{0:T(128)} %bitcast.2.half_ref, bf16[512,512]{1,0:T(8,128)(2,1)S(1)} %copy-done.13, bf16[512,1792]{1,0:T(8,128)(2,1)S(1)} %bitcast.56, f32[512,1792]{1,0:T(8,128)S(1)} %copy-done.3, f32[512,1792]{1,0:T(8,128)S(1)} %copy-done.4), custom_call_target="tpu_custom_call" | custom-call | flops 950000000 | bytes 11000000 | tf_op jit(solution)/shard_map/pallas_call | solution.py:274
  262.8 3.8 %shard_map.120 = (f32[512,1792]{1,0:T(8,128)}, f32[512,1792]{1,0:T(8,128)}, f32[512,1792]{1,0:T(8,128)}) custom-call(s32[1]{0:T(128)} %bitcast.half_ref, bf16[512,512]{1,0:T(8,128)(2,1)S(1)} %copy-done.12, bf16[512,1792]{1,0:T(8,128)(2,1)S(1)} %collective-permute-done.12.cot, ...), custom_call_target="tpu_custom_call", output_to_operand_aliasing={{0}: (5, {}), {1}: (6, {}), {2}: (7, {})} | custom-call | flops 950000000 | bytes 11000000 | tf_op jit(solution)/shard_map/pallas_call | solution.py:274
  (122 shorter events, 44.5 us)
Async XLA Ops:
  0.6 5.3 %copy-start = (bf16[512,1792]{1,0:T(8,128)(2,1)S(1)}, bf16[512,1792]{1,0:T(8,128)(2,1)}, u32[]{:S(2)}) copy-start(bf16[512,1792]{1,0:T(8,128)(2,1)} %param.10) | copy-start | bytes 5505028
  0.6 5.3 %copy-start.16 = (bf16[512,512]{1,0:T(8,128)(2,1)S(1)}, bf16[512,512]{1,0:T(8,128)(2,1)}, u32[]{:S(2)}) copy-start(bf16[512,512]{1,0:T(8,128)(2,1)} %param.9) | copy-start | bytes 1572868
  1.5 9.0 %collective-permute-start.2 = (s32[32,2]{0,1:T(2,128)S(1)}, s32[32,2]{0,1:T(2,128)S(1)}, u32[]{:S(2)}, u32[]{:S(2)}) collective-permute-start(s32[32,2]{0,1:T(2,128)S(1)} %pad_add_fusion), channel_id=1, source_target_pairs={{0,8},{8,0},{1,9},{9,1},{2,10},{10,2},{3,11},{11,3},{4,12},{12,4},... | collective-permute-start | bytes 776 | tf_op jit(solution)/shard_map/ppermute | solution.py:34
  5.9 4.8 %collective-permute-start.1 = (bf16[512,896]{1,0:T(8,128)(2,1)}, bf16[512,896]{1,0:T(8,128)(2,1)S(1)}, u32[]{:S(2)}, u32[]{:S(2)}) collective-permute-start(bf16[512,896]{1,0:T(8,128)(2,1)} %fusion.11), channel_id=1, source_target_pairs={{0,8},{8,0},{1,9},{9,1},{2,10},{10,2},{3,11},{11,3},{4,12},{12,4},... | collective-permute-start | bytes 2752520 | tf_op jit(solution)/shard_map/ppermute | solution.py:34
  7.6 3.2 %collective-permute-start = (bf16[512,896]{1,0:T(8,128)(2,1)}, bf16[512,896]{1,0:T(8,128)(2,1)}, u32[]{:S(2)}, u32[]{:S(2)}) collective-permute-start(bf16[512,896]{1,0:T(8,128)(2,1)} %fusion.10), channel_id=1, source_target_pairs={{0,8},{8,0},{1,9},{9,1},{2,10},{10,2},{3,11},{11,3},{4,12},{12,4},... | collective-permute-start | bytes 2752520 | tf_op jit(solution)/shard_map/ppermute | solution.py:34
  13.8 8.1 %copy-start.2 = (bf16[512,2048]{1,0:T(8,128)(2,1)S(1)}, bf16[512,2048]{1,0:T(8,128)(2,1)}, u32[]{:S(2)}) copy-start(bf16[512,2048]{1,0:T(8,128)(2,1)} %head_far.1) | copy-start | bytes 6291460
  13.8 31.4 %all-to-all-start = ((bf16[8,64,1920]{2,1,0:T(8,128)(2,1)}), bf16[8,64,1920]{2,1,0:T(8,128)(2,1)}, u32[]{:S(2)}, u32[]{:S(2)}) async-start(bf16[8,64,1920]{2,1,0:T(8,128)(2,1)} %bitcast.54), calls=%async_computation | async-start | bytes 3932160 | tf_op jit(solution)/shard_map/all_to_all | solution.py:49
  23.0 4.6 %collective-permute-start.3 = (bf16[512,1024]{1,0:T(8,128)(2,1)}, bf16[512,1024]{1,0:T(8,128)(2,1)S(1)}, u32[]{:S(2)}, u32[]{:S(2)}) collective-permute-start(bf16[512,1024]{1,0:T(8,128)(2,1)} %constant_dynamic-slice_fusion.2), channel_id=1, source_target_pairs={{0,8},{8,0},{1,9},{9,1},{2,10},{10,2},{3,11},{11,3},{4,12},{12,4},... | collective-permute-start | bytes 3145736 | tf_op jit(solution)/shard_map/ppermute | solution.py:34
  24.8 2.8 %collective-permute-start.4 = (bf16[896,512]{1,0:T(8,128)(2,1)}, bf16[896,512]{1,0:T(8,128)(2,1)}, u32[]{:S(2)}, u32[]{:S(2)}) collective-permute-start(bf16[896,512]{1,0:T(8,128)(2,1)} %constant_dynamic-slice_fusion.1), channel_id=1, source_target_pairs={{0,8},{8,0},{1,9},{9,1},{2,10},{10,2},{3,11},{11,3},{4,12},{12,4},... | collective-permute-start | bytes 2752520 | tf_op jit(solution)/shard_map/ppermute | solution.py:34
  47.9 17.1 %all-to-all-start.1 = ((bf16[8,64,896]{2,1,0:T(8,128)(2,1)}), bf16[8,64,896]{2,1,0:T(8,128)(2,1)}, u32[]{:S(2)}, u32[]{:S(2)}) async-start(bf16[8,64,896]{2,1,0:T(8,128)(2,1)} %copy-done.14), calls=%async_computation.1 | async-start | bytes 1835008 | tf_op jit(solution)/shard_map/all_to_all | solution.py:49
  65.0 2.7 %copy-start.9 = (bf16[1792,512]{1,0:T(8,128)(2,1)S(1)}, bf16[1792,512]{1,0:T(8,128)(2,1)}, u32[]{:S(2)}) copy-start(bf16[1792,512]{1,0:T(8,128)(2,1)} %down.1) | copy-start | bytes 5505028
  65.0 2.7 %collective-permute-start.5 = (bf16[512,896]{1,0:T(8,128)(2,1)}, bf16[512,896]{1,0:T(8,128)(2,1)S(1)}, u32[]{:S(2)}, u32[]{:S(2)}) collective-permute-start(bf16[512,896]{1,0:T(8,128)(2,1)} %bitcast.12), channel_id=1, source_target_pairs={{0,8},{8,0},{1,9},{9,1},{2,10},{10,2},{3,11},{11,3},{4,12},{12,4},... | collective-permute-start | bytes 2752520 | tf_op jit(solution)/shard_map/ppermute | solution.py:34
  69.2 17.9 %all-to-all-start.2 = ((bf16[8,64,512]{2,1,0:T(8,128)(2,1)}), bf16[8,64,512]{2,1,0:T(8,128)(2,1)}, u32[]{:S(2)}, u32[]{:S(2)}) async-start(bf16[8,64,512]{2,1,0:T(8,128)(2,1)} %bitcast.13), calls=%async_computation.2 | async-start | bytes 1048576 | tf_op jit(solution)/shard_map/all_to_all | solution.py:49
  88.2 19.0 %copy-start.20 = (f32[64,512]{1,0:T(8,128)}, f32[64,512]{1,0:T(8,128)S(1)}, u32[]{:S(2)}) copy-start(f32[64,512]{1,0:T(8,128)S(1)} %convert_reduce_fusion.1) | copy-start | bytes 393220
  102.6 3.0 %collective-permute-start.6 = (bf16[512,512]{1,0:T(8,128)(2,1)S(1)}, bf16[512,512]{1,0:T(8,128)(2,1)S(1)}, u32[]{:S(2)}, u32[]{:S(2)}) collective-permute-start(bf16[512,512]{1,0:T(8,128)(2,1)S(1)} %bitcast.61), channel_id=1, source_target_pairs={{0,8},{8,0},{1,9},{9,1},{2,10},{10,2},{3,11},{11,3},{4,12},{12,4},... | collective-permute-start | bytes 1572872 | tf_op jit(solution)/shard_map/ppermute | solution.py:34
  108.3 21.0 %all-to-all-start.4 = ((s16[8,64,1152]{2,1,0:T(8,128)(2,1)}), s16[8,64,1152]{2,1,0:T(8,128)(2,1)S(1)}, u32[]{:S(2)}, u32[]{:S(2)}) async-start(s16[8,64,1152]{2,1,0:T(8,128)(2,1)} %bitcast.59), calls=%async_computation.4 | async-start | bytes 2359296 | tf_op jit(solution)/shard_map/all_to_all | solution.py:49
  116.1 13.2 %collective-permute-start.7 = (bf16[2,2,64,1024]{3,2,1,0:T(8,128)(2,1)}, bf16[2,2,64,1024]{3,2,1,0:T(8,128)(2,1)}, u32[]{:S(2)}, u32[]{:S(2)}) collective-permute-start(bf16[2,2,64,1024]{3,2,1,0:T(8,128)(2,1)} %get-tuple-element.84), channel_id=1, source_target_pairs={{0,2},{2,0},{4,6},{6,4},{1,3},{3,1},{5,7},{7,5},{8,10},{10,8},{12,... | collective-permute-start | bytes 1572872 | tf_op jit(solution)/shard_map/ppermute | solution.py:312
  131.2 20.8 %all-to-all-start.5 = ((bf16[8,64,1152]{2,1,0:T(8,128)(2,1)}), bf16[8,64,1152]{2,1,0:T(8,128)(2,1)S(1)}, u32[]{:S(2)}, u32[]{:S(2)}) async-start(bf16[8,64,1152]{2,1,0:T(8,128)(2,1)} %copy-done.6), calls=%async_computation.5 | async-start | bytes 2359296 | tf_op jit(solution)/shard_map/all_to_all | solution.py:49
  140.0 9.5 %collective-permute-start.8 = (bf16[2,64,1024]{2,1,0:T(8,128)(2,1)}, bf16[2,64,1024]{2,1,0:T(8,128)(2,1)}, u32[]{:S(2)}, u32[]{:S(2)}) collective-permute-start(bf16[2,64,1024]{2,1,0:T(8,128)(2,1)} %dynamic-slice_bitcast_fusion.2), channel_id=1, source_target_pairs={{0,4},{4,0},{2,6},{6,2},{1,5},{5,1},{3,7},{7,3},{8,12},{12,8},{10,... | collective-permute-start | bytes 786440 | tf_op jit(solution)/shard_map/ppermute | solution.py:318
  152.0 2.8 %collective-permute-start.9 = (bf16[512,1152]{1,0:T(8,128)(2,1)S(1)}, bf16[512,1152]{1,0:T(8,128)(2,1)S(1)}, u32[]{:S(2)}, u32[]{:S(2)}) collective-permute-start(bf16[512,1152]{1,0:T(8,128)(2,1)S(1)} %bitcast.57), channel_id=1, source_target_pairs={{0,8},{8,0},{1,9},{9,1},{2,10},{10,2},{3,11},{11,3},{4,12},{12,4},... | collective-permute-start | bytes 3538952 | tf_op jit(solution)/shard_map/ppermute | solution.py:34
  157.1 17.6 %all-to-all-start.6 = ((bf16[8,64,640]{2,1,0:T(8,128)(2,1)}), bf16[8,64,640]{2,1,0:T(8,128)(2,1)S(1)}, u32[]{:S(2)}, u32[]{:S(2)}) async-start(bf16[8,64,640]{2,1,0:T(8,128)(2,1)} %bitcast.60), calls=%async_computation.6 | async-start | bytes 1310720 | tf_op jit(solution)/shard_map/all_to_all | solution.py:49
  164.8 11.5 %copy-start.22 = (bf16[64,1024]{1,0:T(8,128)(2,1)S(1)}, bf16[64,1024]{1,0:T(8,128)(2,1)}, u32[]{:S(2)}) copy-start(bf16[64,1024]{1,0:T(8,128)(2,1)} %get-tuple-element.63) | copy-start | bytes 393220
  164.8 11.6 %copy-start.21 = (f32[64,512]{1,0:T(8,128)S(1)}, f32[64,512]{1,0:T(8,128)}, u32[]{:S(2)}) copy-start(f32[64,512]{1,0:T(8,128)} %copy-done.20) | copy-start | bytes 393220
  164.8 9.9 %collective-permute-start.10 = (bf16[64,1024]{1,0:T(8,128)(2,1)}, bf16[64,1024]{1,0:T(8,128)(2,1)S(1)}, u32[]{:S(2)}, u32[]{:S(2)}) collective-permute-start(bf16[64,1024]{1,0:T(8,128)(2,1)} %get-tuple-element.61), channel_id=1, source_target_pairs={{0,1},{1,0},{2,3},{3,2},{4,5},{5,4},{6,7},{7,6},{8,9},{9,8},{10,11... | collective-permute-start | bytes 393224 | tf_op jit(solution)/shard_map/ppermute | solution.py:323
  177.4 23.9 %copy-start.10 = (bf16[1792,512]{1,0:T(8,128)(2,1)S(1)}, bf16[1792,512]{1,0:T(8,128)(2,1)}, u32[]{:S(2)}) copy-start(bf16[1792,512]{1,0:T(8,128)(2,1)} %down.1) | copy-start | bytes 5505028
  197.0 4.3 %collective-permute-start.11 = (bf16[512,1024]{1,0:T(8,128)(2,1)S(1)}, bf16[512,1024]{1,0:T(8,128)(2,1)S(1)}, u32[]{:S(2)}, u32[]{:S(2)}) collective-permute-start(bf16[512,1024]{1,0:T(8,128)(2,1)S(1)} %bitcast.64), channel_id=1, source_target_pairs={{0,8},{8,0},{1,9},{9,1},{2,10},{10,2},{3,11},{11,3},{4,12},{12,4},... | collective-permute-start | bytes 3145736 | tf_op jit(solution)/shard_map/ppermute | solution.py:34
  231.1 27.9 %copy-start.4 = (f32[512,1792]{1,0:T(8,128)S(1)}, f32[512,1792]{1,0:T(8,128)}, u32[]{:S(2)}) copy-start(f32[512,1792]{1,0:T(8,128)} %curve_ref.3) | copy-start | bytes 11010052
  231.4 27.6 %copy-start.13 = (bf16[512,512]{1,0:T(8,128)(2,1)S(1)}, bf16[512,512]{1,0:T(8,128)(2,1)}, u32[]{:S(2)}) copy-start(bf16[512,512]{1,0:T(8,128)(2,1)} %get-tuple-element.67.turned) | copy-start | bytes 1572868
  231.6 27.5 %copy-start.3 = (f32[512,1792]{1,0:T(8,128)S(1)}, f32[512,1792]{1,0:T(8,128)}, u32[]{:S(2)}) copy-start(f32[512,1792]{1,0:T(8,128)} %moment_ref.3) | copy-start | bytes 11010052
  257.3 5.5 %copy-start.12 = (bf16[512,512]{1,0:T(8,128)(2,1)S(1)}, bf16[512,512]{1,0:T(8,128)(2,1)}, u32[]{:S(2)}) copy-start(bf16[512,512]{1,0:T(8,128)(2,1)} %get-tuple-element.57.turned) | copy-start | bytes 1572868
  257.3 5.5 %collective-permute-start.12 = (bf16[512,1792]{1,0:T(8,128)(2,1)S(1)}, bf16[512,1792]{1,0:T(8,128)(2,1)S(1)}, u32[]{:S(2)}, u32[]{:S(2)}) collective-permute-start(bf16[512,1792]{1,0:T(8,128)(2,1)S(1)} %bitcast.55), channel_id=1, source_target_pairs={{0,8},{8,0},{1,9},{9,1},{2,10},{10,2},{3,11},{11,3},{4,12},{12,4},... | collective-permute-start | bytes 5505032 | tf_op jit(solution)/shard_map/ppermute | solution.py:34
  262.8 3.8 %copy-start.1 = (bf16[512,1792]{1,0:T(8,128)(2,1)S(1)}, bf16[512,1792]{1,0:T(8,128)(2,1)}, u32[]{:S(2)}) copy-start(bf16[512,1792]{1,0:T(8,128)(2,1)} %param.10) | copy-start | bytes 5505028
  (13 other events, 15.2 us)

commit v13 on v12

--- a/solution.py
+++ b/solution.py
@@ -120,7 +120,7 @@
     return results if len(outs) > 1 else results[0]
 
 
-def gate_up_pack(half_ref, own_gate, own_up, got_gate, got_up, labels, out):
+def gate_up_pack(half_ref, own_gate, own_up, got_gate, got_up, out):
     core = half_ref[0]
     gate_sum = (own_gate[...].astype(f32) + got_gate[...].astype(f32)).astype(bf16)
     up_sum = (own_up[...].astype(f32) + got_up[...].astype(f32)).astype(bf16)
@@ -129,14 +129,13 @@
         rows = pl.ds(pl.multiple_of(place * BLOCK, BLOCK), BLOCK)
         out[rows, :FF_HALF] = gate_sum[block_rows(block)]
         out[rows, FF_HALF : 2 * FF_HALF] = up_sum[block_rows(block)]
-        out[rows, 2 * FF_HALF :] = labels[...]
 
 
 def branch_kernel(half_ref, own_part, far, down_far, out):
-    out[...] = join_cores(own_part[...], dot(far[...], down_far[...])).astype(bf16)
-
-
-def hidden_kernel(half_ref, both, hidden, silu_out):
+    out[...] = join_cores(own_part[...], dot(far[:, :FF_HALF], down_far[...])).astype(bf16)
+
+
+def hidden_kernel(half_ref, both, labels, hidden, silu_out):
     gate = jnp.zeros((BLOCK, FF_HALF), f32)
     upper = jnp.zeros((BLOCK, FF_HALF), f32)
     for chip in range(CHIPS):
@@ -146,7 +145,8 @@
     silu_out[...] = silu_gate
     rounded = (silu_gate * upper).astype(bf16)
     for chip in range(CHIPS):
-        hidden[chip] = rounded
+        hidden[chip, :, :FF_HALF] = rounded
+        hidden[chip, :, FF_HALF:] = labels[...]
 
 
 def squares_of(rows):
@@ -359,45 +359,35 @@
     far_gate, far_up = gate_up(far)
     got_gate, got_up = other_core(far_gate), other_core(far_up)
     own_gate, own_up = gate_up(core)
-    operands = (own_gate, own_up, got_gate, got_up, digits)
+    operands = (own_gate, own_up, got_gate, got_up)
     both = on_core(
         gate_up_pack,
         core,
         operands,
         [whole(operand) for operand in operands],
-        [((count, 2 * FF_HALF + PAD), bf16)],
+        [((count, 2 * FF_HALF), bf16)],
         1000000,
     )
     both, sent_head, sent_down = together(both, head_weight, down_weight)
     head_send = lax.dynamic_slice_in_dim(sent_head, far * V_HALF, V_HALF, 1)
     down_send = lax.dynamic_slice_in_dim(sent_down, far * FF_HALF, FF_HALF, 0)
     both, head_got, down_got = together(
-        exchange(both.reshape(CHIPS, BLOCK, 2 * FF_HALF + PAD), WIDTH_CHIPS),
+        exchange(both.reshape(CHIPS, BLOCK, 2 * FF_HALF), WIDTH_CHIPS),
         other_core(head_send),
         other_core(down_send),
     )
     hidden, silu_gate = on_core(
         hidden_kernel,
         core,
-        (both,),
-        [whole(both)],
-        [((CHIPS, BLOCK, FF_HALF), bf16), ((BLOCK, FF_HALF), f32)],
+        (both, digits),
+        [whole(both), whole(digits)],
+        [((CHIPS, BLOCK, FF_HALF + PAD), bf16), ((BLOCK, FF_HALF), f32)],
         1000000,
     )
 
-    hidden, digits = together(hidden, both)
-    digits = digits[:, :, 2 * FF_HALF : 2 * FF_HALF + 4].astype(jnp.int32)
-    all_labels = digits[:, :, :2] * PAD + digits[:, :, 2:]
-    all_labels = jnp.where(core == 0, all_labels, all_labels[::-1]).reshape(count, 2)
-    width_chip = lax.axis_index(WIDTH_CHIPS)
-    hidden_own, label_row, labels = together(
-        exchange(hidden, WIDTH_CHIPS),
-        label_rows(all_labels, head_weight, unit_chip),
-        lax.dynamic_slice_in_dim(all_labels, width_chip * BLOCK, BLOCK, 0),
-    )
-    hidden_own = hidden_own.reshape(count, FF_HALF)
+    hidden_own = exchange(hidden, WIDTH_CHIPS).reshape(count, FF_HALF + PAD)
     hidden_far = other_core(hidden_own)
-    own_part = dot(hidden_own, lax.dynamic_slice_in_dim(down_weight, core * FF_HALF, FF_HALF, 0))
+    own_part = dot(hidden_own[:, :FF_HALF], lax.dynamic_slice_in_dim(down_weight, core * FF_HALF, FF_HALF, 0))
     branch = on_core(
         branch_kernel,
         core,
@@ -410,7 +400,16 @@
         [((count, width), bf16)],
         gate_up_flops,
     )
-    branch = exchange(branch.reshape(CHIPS, BLOCK, width), UNIT_CHIPS)
+    branch, hidden_own = together(branch, hidden_own)
+    digits = hidden_own[:, FF_HALF : FF_HALF + 4].astype(jnp.int32)
+    all_labels = digits[:, :2] * PAD + digits[:, 2:]
+    all_labels = jnp.where(core == 0, all_labels, reverse_blocks(all_labels))
+    width_chip = lax.axis_index(WIDTH_CHIPS)
+    branch, label_row, labels = together(
+        exchange(branch.reshape(CHIPS, BLOCK, width), UNIT_CHIPS),
+        label_rows(all_labels, head_weight, unit_chip),
+        lax.dynamic_slice_in_dim(all_labels, width_chip * BLOCK, BLOCK, 0),
+    )
     branch = jnp.sum(branch.astype(f32), axis=0)
     own_tokens = lax.dynamic_slice_in_dim(tokens, unit_chip * BLOCK, BLOCK, 0)
     summed = own_tokens.astype(f32) + branch

time: 268 us -> 266 us (level)
  blocking collectives: 84.8 us -> 102 us
  waiting for transfers between devices: 62.3 us -> 50.7 us
  starting transfers between devices: 50.6 us -> 47.3 us
    all_to_all x4 -> x5, blocking collectives: 84.8 us -> 102 us  [exchange(): lax.all_to_all(blocks, tuple(MESH_SIZES), split_axis=0, concat_axis=0, ti...]
    all_to_all x6 -> x5, waiting for transfers between devices: 29.6 us -> 18.4 us  [exchange(): lax.all_to_all(blocks, tuple(MESH_SIZES), split_axis=0, concat_axis=0, ti...]
    all_to_all x6 -> x5, starting transfers between devices: 42 us -> 36.8 us  [exchange(): lax.all_to_all(blocks, tuple(MESH_SIZES), split_axis=0, concat_axis=0, ti...]
    unnamed x52 -> x54, local copies, waits for them, and re-layouts: 7.58 us -> 6.52 us
  transfers between devices with their start and end apart: 19 -> 18, of which waited for: 11 -> 12; matrix products, arithmetic and copies ran while one was open for 13% -> 11% of each run, Pallas kernels for 1% -> 1%
where the time goes in v13:
time: 266 us; the launch traced here: 265 us
  blocking collectives  102 us (38%)
  waiting for transfers between devices  50.7 us (19%)
  starting transfers between devices  47.3 us (18%)
  local copies, waits for them, and re-layouts  22.5 us (8%)
  Pallas kernels  19.9 us (7%)
  matrix products  11.2 us (4%)
  other arithmetic  10.6 us (4%)
    all_to_all x5, blocking collectives, exchange(): lax.all_to_all(blocks, tuple(MESH_SIZES), split_axis=0, concat_axis=0, ti...  102 us
    all_to_all x5, starting transfers between devices, exchange(): lax.all_to_all(blocks, tuple(MESH_SIZES), split_axis=0, concat_axis=0, ti...  36.8 us
    all_to_all x5, waiting for transfers between devices, exchange(): lax.all_to_all(blocks, tuple(MESH_SIZES), split_axis=0, concat_axis=0, ti...  18.4 us
    ppermute x1, waiting for transfers between devices, near_label_rows(): return (keep, lax.ppermute(send, 'z', [(0, 1), (1, 0), (2, 3), (3, 2)]))  13.4 us
    pallas_call x7, Pallas kernels, on_core(): pl.pallas_call(kernel, out_shape=tuple((jax.ShapeDtypeStruct(shape, dtype...  12.4 us
    ppermute x1, waiting for transfers between devices, other_plane(): return lax.ppermute(rows, 'xh', [(0, 1), (1, 0)])  9.61 us
    ppermute x10, waiting for transfers between devices, other_core(): return lax.ppermute(value, 'core', [(0, 1), (1, 0)])  9.39 us
    ppermute x10, starting transfers between devices, other_core(): return lax.ppermute(value, 'core', [(0, 1), (1, 0)])  9.1 us
  transfers between devices with their start and end apart: 18, of which 12 were waited for; matrix products, arithmetic and copies ran while one was open for 11% of the time, Pallas kernels for 1%

profile of v13, /device:TPU:1, one launch (start us, length us, event | category | flops | bytes accessed | tf_op | source)
XLA Modules:
  0.0 265.2 jit_solution(8319528438195418128)
XLA Ops:
  0.7 3.1 %fusion.11 = bf16[512,896]{1,0:T(8,128)(2,1)} fusion(bf16[512,512]{1,0:T(8,128)(2,1)} %param.9, bf16[512,1792]{1,0:T(8,128)(2,1)} %param.11, s32[]{:T(128)S(6)} %select_n.98), kind=kOutput, calls=%fused_computation.16 | convolution fusion | flops 470220800 | bytes 2359300 | tf_op jit(solution)/shard_map/dot_general | solution.py:82
  5.2 1.6 fusion.10
  9.7 1.6 shard_map.112
  12.5 8.1 %all-to-all-start = ((bf16[8,64,1792]{2,1,0:T(8,128)(2,1)}), bf16[8,64,1792]{2,1,0:T(8,128)(2,1)}, u32[]{:S(2)}, u32[]{:S(2)}) async-start(bf16[8,64,1792]{2,1,0:T(8,128)(2,1)} %bitcast.57), calls=%async_computation | async-start | bytes 3670016 | tf_op jit(solution)/shard_map/all_to_all | solution.py:49
  26.3 16.3 %all-to-all-done.both = bf16[8,64,1792]{2,1,0:T(8,128)(2,1)} async-done(((bf16[8,64,1792]{2,1,0:T(8,128)(2,1)}), bf16[8,64,1792]{2,1,0:T(8,128)(2,1)}, u32[]{:S(2)}, u32[]{:S(2)}) %all-to-all-start) | async-done | bytes 1835040 | tf_op jit(solution)/shard_map/all_to_all | solution.py:49
  42.6 1.8 shard_map.113
  44.4 17.6 %all_to_all.50 = bf16[8,64,1024]{2,1,0:T(8,128)(2,1)} all-to-all(bf16[8,64,1024]{2,1,0:T(8,128)(2,1)S(1)} %get-tuple-element.41), channel_id=1, replica_groups={{0,16,32,48,64,80,96,112},{1,17,33,49,65,81,97,113},{2,18,34,50,66,82,9..., dimensions={0} | all-to-all | bytes 2097152 | tf_op jit(solution)/shard_map/all_to_all | solution.py:49
  62.9 2.3 fusion.18.own_part
  66.9 10.0 %all-to-all-start.2 = ((bf16[8,64,512]{2,1,0:T(8,128)(2,1)}), bf16[8,64,512]{2,1,0:T(8,128)(2,1)}, u32[]{:S(2)}, u32[]{:S(2)}) async-start(bf16[8,64,512]{2,1,0:T(8,128)(2,1)} %bitcast.11), calls=%async_computation.2 | async-start | bytes 1048576 | tf_op jit(solution)/shard_map/all_to_all | solution.py:49
  86.9 12.6 %all_to_all.51 = bf16[8,64,512]{2,1,0:T(8,128)(2,1)S(1)} all-to-all(bf16[8,64,512]{2,1,0:T(8,128)(2,1)S(1)} %broadcast_in_dim.6), channel_id=1, replica_groups={{0,1,2,3,4,5,6,7},{15,14,13,12,11,10,9,8},{16,17,18,19,20,21,22,23},{31..., dimensions={0} | all-to-all | bytes 1048576 | tf_op jit(solution)/shard_map/all_to_all | solution.py:49
  99.5 2.5 collective-permute-start.6
  103.6 1.7 shard_map.115
  106.2 5.3 %all-to-all-start.4 = ((s16[8,64,1152]{2,1,0:T(8,128)(2,1)}), s16[8,64,1152]{2,1,0:T(8,128)(2,1)S(1)}, u32[]{:S(2)}, u32[]{:S(2)}) async-start(s16[8,64,1152]{2,1,0:T(8,128)(2,1)} %bitcast.60), calls=%async_computation.4 | async-start | bytes 2359296 | tf_op jit(solution)/shard_map/all_to_all | solution.py:49
  111.5 2.2 dynamic-slice_bitcast_fusion
  113.8 13.4 %collective-permute-done.7 = bf16[2,2,64,1024]{3,2,1,0:T(8,128)(2,1)} collective-permute-done((bf16[2,2,64,1024]{3,2,1,0:T(8,128)(2,1)}, bf16[2,2,64,1024]{3,2,1,0:T(8,128)(2,1)}, u32[]{:S(2)}, u32[]{:S(2)}) %collective-permute-start.7) | collective-permute-done | bytes 524320 | tf_op jit(solution)/shard_map/ppermute | solution.py:312
  129.1 5.5 %all-to-all-start.5 = ((bf16[8,64,1152]{2,1,0:T(8,128)(2,1)}), bf16[8,64,1152]{2,1,0:T(8,128)(2,1)S(1)}, u32[]{:S(2)}, u32[]{:S(2)}) async-start(bf16[8,64,1152]{2,1,0:T(8,128)(2,1)} %copy-done.6), calls=%async_computation.5 | async-start | bytes 2359296 | tf_op jit(solution)/shard_map/all_to_all | solution.py:49
  138.7 2.1 copy.78
  140.7 1.9 rev.7
  142.6 2.0 copy.79
  144.7 2.3 select_bitcast_fusion
  149.5 2.8 %collective-permute-done.9.far = bf16[512,1152]{1,0:T(8,128)(2,1)S(1)} collective-permute-done((bf16[512,1152]{1,0:T(8,128)(2,1)S(1)}, bf16[512,1152]{1,0:T(8,128)(2,1)S(1)}, u32[]{:S(2)}, u32[]{:S(2)}) %collective-permute-start.9) | collective-permute-done | bytes 1179680 | tf_op jit(solution)/shard_map/ppermute | solution.py:34
  154.6 7.9 %all-to-all-start.6 = ((bf16[8,64,640]{2,1,0:T(8,128)(2,1)}), bf16[8,64,640]{2,1,0:T(8,128)(2,1)S(1)}, u32[]{:S(2)}, u32[]{:S(2)}) async-start(bf16[8,64,640]{2,1,0:T(8,128)(2,1)} %bitcast.61), calls=%async_computation.6 | async-start | bytes 1310720 | tf_op jit(solution)/shard_map/all_to_all | solution.py:49
  162.8 9.6 %collective-permute-done.10 = bf16[64,1024]{1,0:T(8,128)(2,1)S(1)} collective-permute-done((bf16[64,1024]{1,0:T(8,128)(2,1)}, bf16[64,1024]{1,0:T(8,128)(2,1)S(1)}, u32[]{:S(2)}, u32[]{:S(2)}) %collective-permute-start.10) | collective-permute-done | bytes 131104 | tf_op jit(solution)/shard_map/ppermute | solution.py:323
  176.2 19.4 %all_to_all.52 = bf16[8,64,1024]{2,1,0:T(8,128)(2,1)S(1)} all-to-all(bf16[8,64,1024]{2,1,0:T(8,128)(2,1)S(1)} %broadcast_in_dim.7), channel_id=1, replica_groups={{0,1,2,3,4,5,6,7},{15,14,13,12,11,10,9,8},{16,17,18,19,20,21,22,23},{31..., dimensions={0} | all-to-all | bytes 2097152 | tf_op jit(solution)/shard_map/all_to_all | solution.py:49
  195.6 2.0 collective-permute-start.11
  197.6 2.3 collective-permute-done.11.far_dsummed
  199.9 3.5 %shard_map.118 = bf16[512,1792]{1,0:T(8,128)(2,1)S(1)} custom-call(s32[1]{0:T(128)} %bitcast.2.half_ref, bf16[512,1024]{1,0:T(8,128)(2,1)S(1)} %bitcast.66, bf16[512,1024]{1,0:T(8,128)(2,1)S(1)} %collective-permute-done.11.far_dsummed, bf16[1792,512]{1,0:T(8,128)(2,1)S(1)} %copy-done.10, bf16[896,512]{1,0:T(8,128)(2,1)} %collective-permute-done.3.down_got), custom_call_target="tpu_custom_call" | custom-call | flops 1879048192 | bytes 4849664 | tf_op jit(solution)/shard_map/pallas_call | solution.py:108
  203.4 26.3 %all_to_all.53 = bf16[8,64,1792]{2,1,0:T(8,128)(2,1)S(1)} all-to-all(bf16[8,64,1792]{2,1,0:T(8,128)(2,1)S(1)} %bitcast.64), channel_id=1, replica_groups={{0,16,32,48,64,80,96,112},{1,17,33,49,65,81,97,113},{2,18,34,50,66,82,9..., dimensions={0} | all-to-all | bytes 3670016 | tf_op jit(solution)/shard_map/all_to_all | solution.py:49
  230.2 25.8 %all_to_all.54 = bf16[8,64,1792]{2,1,0:T(8,128)(2,1)S(1)} all-to-all(bf16[8,64,1792]{2,1,0:T(8,128)(2,1)S(1)} %broadcast_in_dim.8), channel_id=1, replica_groups={{0,16,32,48,64,80,96,112},{1,17,33,49,65,81,97,113},{2,18,34,50,66,82,9..., dimensions={0} | all-to-all | bytes 3670016 | tf_op jit(solution)/shard_map/all_to_all | solution.py:49
  256.0 1.7 collective-permute-start.12
  257.7 3.7 %shard_map.119 = (f32[512,1792]{1,0:T(8,128)}, f32[512,1792]{1,0:T(8,128)}, f32[512,1792]{1,0:T(8,128)}) custom-call(s32[1]{0:T(128)} %bitcast.2.half_ref, bf16[512,512]{1,0:T(8,128)(2,1)S(1)} %copy-done.13, bf16[512,1792]{1,0:T(8,128)(2,1)S(1)} %bitcast.56, f32[512,1792]{1,0:T(8,128)S(1)} %copy-done.3, f32[512,1792]{1,0:T(8,128)S(1)} %copy-done.4), custom_call_target="tpu_custom_call" | custom-call | flops 950000000 | bytes 11000000 | tf_op jit(solution)/shard_map/pallas_call | solution.py:274
  261.4 3.7 %shard_map.120 = (f32[512,1792]{1,0:T(8,128)}, f32[512,1792]{1,0:T(8,128)}, f32[512,1792]{1,0:T(8,128)}) custom-call(s32[1]{0:T(128)} %bitcast.half_ref, bf16[512,512]{1,0:T(8,128)(2,1)S(1)} %copy-done.12, bf16[512,1792]{1,0:T(8,128)(2,1)S(1)} %collective-permute-done.12.cot, ...), custom_call_target="tpu_custom_call", output_to_operand_aliasing={{0}: (5, {}), {1}: (6, {}), {2}: (7, {})} | custom-call | flops 950000000 | bytes 11000000 | tf_op jit(solution)/shard_map/pallas_call | solution.py:274
  (124 shorter events, 41.3 us)
Async XLA Ops:
  0.6 4.6 %copy-start = (bf16[512,1792]{1,0:T(8,128)(2,1)S(1)}, bf16[512,1792]{1,0:T(8,128)(2,1)}, u32[]{:S(2)}) copy-start(bf16[512,1792]{1,0:T(8,128)(2,1)} %param.10) | copy-start | bytes 5505028
  0.6 4.6 %copy-start.16 = (bf16[512,512]{1,0:T(8,128)(2,1)S(1)}, bf16[512,512]{1,0:T(8,128)(2,1)}, u32[]{:S(2)}) copy-start(bf16[512,512]{1,0:T(8,128)(2,1)} %param.9) | copy-start | bytes 1572868
  3.8 5.3 %collective-permute-start.1 = (bf16[512,896]{1,0:T(8,128)(2,1)}, bf16[512,896]{1,0:T(8,128)(2,1)S(1)}, u32[]{:S(2)}, u32[]{:S(2)}) collective-permute-start(bf16[512,896]{1,0:T(8,128)(2,1)} %fusion.11), channel_id=1, source_target_pairs={{0,8},{8,0},{1,9},{9,1},{2,10},{10,2},{3,11},{11,3},{4,12},{12,4},... | collective-permute-start | bytes 2752520 | tf_op jit(solution)/shard_map/ppermute | solution.py:34
  6.9 2.8 %collective-permute-start = (bf16[512,896]{1,0:T(8,128)(2,1)}, bf16[512,896]{1,0:T(8,128)(2,1)}, u32[]{:S(2)}, u32[]{:S(2)}) collective-permute-start(bf16[512,896]{1,0:T(8,128)(2,1)} %fusion.10), channel_id=1, source_target_pairs={{0,8},{8,0},{1,9},{9,1},{2,10},{10,2},{3,11},{11,3},{4,12},{12,4},... | collective-permute-start | bytes 2752520 | tf_op jit(solution)/shard_map/ppermute | solution.py:34
  12.5 8.1 %copy-start.2 = (bf16[512,2048]{1,0:T(8,128)(2,1)S(1)}, bf16[512,2048]{1,0:T(8,128)(2,1)}, u32[]{:S(2)}) copy-start(bf16[512,2048]{1,0:T(8,128)(2,1)} %head_far.1) | copy-start | bytes 6291460
  12.5 30.1 %all-to-all-start = ((bf16[8,64,1792]{2,1,0:T(8,128)(2,1)}), bf16[8,64,1792]{2,1,0:T(8,128)(2,1)}, u32[]{:S(2)}, u32[]{:S(2)}) async-start(bf16[8,64,1792]{2,1,0:T(8,128)(2,1)} %bitcast.57), calls=%async_computation | async-start | bytes 3670016 | tf_op jit(solution)/shard_map/all_to_all | solution.py:49
  21.7 4.6 %collective-permute-start.2 = (bf16[512,1024]{1,0:T(8,128)(2,1)}, bf16[512,1024]{1,0:T(8,128)(2,1)S(1)}, u32[]{:S(2)}, u32[]{:S(2)}) collective-permute-start(bf16[512,1024]{1,0:T(8,128)(2,1)} %constant_dynamic-slice_fusion.2), channel_id=1, source_target_pairs={{0,8},{8,0},{1,9},{9,1},{2,10},{10,2},{3,11},{11,3},{4,12},{12,4},... | collective-permute-start | bytes 3145736 | tf_op jit(solution)/shard_map/ppermute | solution.py:34
  23.5 2.8 %collective-permute-start.3 = (bf16[896,512]{1,0:T(8,128)(2,1)}, bf16[896,512]{1,0:T(8,128)(2,1)}, u32[]{:S(2)}, u32[]{:S(2)}) collective-permute-start(bf16[896,512]{1,0:T(8,128)(2,1)} %constant_dynamic-slice_fusion.1), channel_id=1, source_target_pairs={{0,8},{8,0},{1,9},{9,1},{2,10},{10,2},{3,11},{11,3},{4,12},{12,4},... | collective-permute-start | bytes 2752520 | tf_op jit(solution)/shard_map/ppermute | solution.py:34
  23.5 2.2 collective-permute-start.4
  26.3 35.8 %copy-start.14 = (bf16[512,1024]{1,0:T(8,128)(2,1)}, bf16[512,1024]{1,0:T(8,128)(2,1)S(1)}, u32[]{:S(2)}) copy-start(bf16[512,1024]{1,0:T(8,128)(2,1)S(1)} %collective-permute-done.2.head_got) | copy-start | bytes 3145732
  62.1 3.4 %collective-permute-start.5 = (bf16[512,1024]{1,0:T(8,128)(2,1)}, bf16[512,1024]{1,0:T(8,128)(2,1)S(1)}, u32[]{:S(2)}, u32[]{:S(2)}) collective-permute-start(bf16[512,1024]{1,0:T(8,128)(2,1)} %bitcast.10), channel_id=1, source_target_pairs={{0,8},{8,0},{1,9},{9,1},{2,10},{10,2},{3,11},{11,3},{4,12},{12,4},... | collective-permute-start | bytes 3145736 | tf_op jit(solution)/shard_map/ppermute | solution.py:34
  66.9 17.8 %all-to-all-start.2 = ((bf16[8,64,512]{2,1,0:T(8,128)(2,1)}), bf16[8,64,512]{2,1,0:T(8,128)(2,1)}, u32[]{:S(2)}, u32[]{:S(2)}) async-start(bf16[8,64,512]{2,1,0:T(8,128)(2,1)} %bitcast.11), calls=%async_computation.2 | async-start | bytes 1048576 | tf_op jit(solution)/shard_map/all_to_all | solution.py:49
  82.6 20.9 %copy-start.15 = (bf16[512,1024]{1,0:T(8,128)(2,1)S(1)}, bf16[512,1024]{1,0:T(8,128)(2,1)}, u32[]{:S(2)}) copy-start(bf16[512,1024]{1,0:T(8,128)(2,1)} %copy-done.14) | copy-start | bytes 3145732
  85.9 19.3 %copy-start.20 = (f32[64,512]{1,0:T(8,128)}, f32[64,512]{1,0:T(8,128)S(1)}, u32[]{:S(2)}) copy-start(f32[64,512]{1,0:T(8,128)S(1)} %convert_reduce_fusion.1) | copy-start | bytes 393220
  99.5 4.0 %collective-permute-start.6 = (bf16[512,512]{1,0:T(8,128)(2,1)S(1)}, bf16[512,512]{1,0:T(8,128)(2,1)S(1)}, u32[]{:S(2)}, u32[]{:S(2)}) collective-permute-start(bf16[512,512]{1,0:T(8,128)(2,1)S(1)} %bitcast.62), channel_id=1, source_target_pairs={{0,8},{8,0},{1,9},{9,1},{2,10},{10,2},{3,11},{11,3},{4,12},{12,4},... | collective-permute-start | bytes 1572872 | tf_op jit(solution)/shard_map/ppermute | solution.py:34
  106.2 20.9 %all-to-all-start.4 = ((s16[8,64,1152]{2,1,0:T(8,128)(2,1)}), s16[8,64,1152]{2,1,0:T(8,128)(2,1)S(1)}, u32[]{:S(2)}, u32[]{:S(2)}) async-start(s16[8,64,1152]{2,1,0:T(8,128)(2,1)} %bitcast.60), calls=%async_computation.4 | async-start | bytes 2359296 | tf_op jit(solution)/shard_map/all_to_all | solution.py:49
  113.8 13.4 %collective-permute-start.7 = (bf16[2,2,64,1024]{3,2,1,0:T(8,128)(2,1)}, bf16[2,2,64,1024]{3,2,1,0:T(8,128)(2,1)}, u32[]{:S(2)}, u32[]{:S(2)}) collective-permute-start(bf16[2,2,64,1024]{3,2,1,0:T(8,128)(2,1)} %get-tuple-element.84), channel_id=1, source_target_pairs={{0,2},{2,0},{4,6},{6,4},{1,3},{3,1},{5,7},{7,5},{8,10},{10,8},{12,... | collective-permute-start | bytes 1572872 | tf_op jit(solution)/shard_map/ppermute | solution.py:312
  129.1 20.4 %all-to-all-start.5 = ((bf16[8,64,1152]{2,1,0:T(8,128)(2,1)}), bf16[8,64,1152]{2,1,0:T(8,128)(2,1)S(1)}, u32[]{:S(2)}, u32[]{:S(2)}) async-start(bf16[8,64,1152]{2,1,0:T(8,128)(2,1)} %copy-done.6), calls=%async_computation.5 | async-start | bytes 2359296 | tf_op jit(solution)/shard_map/all_to_all | solution.py:49
  137.5 9.5 %collective-permute-start.8 = (bf16[2,64,1024]{2,1,0:T(8,128)(2,1)}, bf16[2,64,1024]{2,1,0:T(8,128)(2,1)}, u32[]{:S(2)}, u32[]{:S(2)}) collective-permute-start(bf16[2,64,1024]{2,1,0:T(8,128)(2,1)} %dynamic-slice_bitcast_fusion.2), channel_id=1, source_target_pairs={{0,4},{4,0},{2,6},{6,2},{1,5},{5,1},{3,7},{7,3},{8,12},{12,8},{10,... | collective-permute-start | bytes 786440 | tf_op jit(solution)/shard_map/ppermute | solution.py:318
  149.5 2.8 %collective-permute-start.9 = (bf16[512,1152]{1,0:T(8,128)(2,1)S(1)}, bf16[512,1152]{1,0:T(8,128)(2,1)S(1)}, u32[]{:S(2)}, u32[]{:S(2)}) collective-permute-start(bf16[512,1152]{1,0:T(8,128)(2,1)S(1)} %bitcast.58), channel_id=1, source_target_pairs={{0,8},{8,0},{1,9},{9,1},{2,10},{10,2},{3,11},{11,3},{4,12},{12,4},... | collective-permute-start | bytes 3538952 | tf_op jit(solution)/shard_map/ppermute | solution.py:34
  154.6 17.8 %all-to-all-start.6 = ((bf16[8,64,640]{2,1,0:T(8,128)(2,1)}), bf16[8,64,640]{2,1,0:T(8,128)(2,1)S(1)}, u32[]{:S(2)}, u32[]{:S(2)}) async-start(bf16[8,64,640]{2,1,0:T(8,128)(2,1)} %bitcast.61), calls=%async_computation.6 | async-start | bytes 1310720 | tf_op jit(solution)/shard_map/all_to_all | solution.py:49
  162.5 11.6 %copy-start.22 = (bf16[64,1024]{1,0:T(8,128)(2,1)S(1)}, bf16[64,1024]{1,0:T(8,128)(2,1)}, u32[]{:S(2)}) copy-start(bf16[64,1024]{1,0:T(8,128)(2,1)} %get-tuple-element.63) | copy-start | bytes 393220
  162.5 12.5 %copy-start.21 = (f32[64,512]{1,0:T(8,128)S(1)}, f32[64,512]{1,0:T(8,128)}, u32[]{:S(2)}) copy-start(f32[64,512]{1,0:T(8,128)} %copy-done.20) | copy-start | bytes 393220
  162.5 9.9 %collective-permute-start.10 = (bf16[64,1024]{1,0:T(8,128)(2,1)}, bf16[64,1024]{1,0:T(8,128)(2,1)S(1)}, u32[]{:S(2)}, u32[]{:S(2)}) collective-permute-start(bf16[64,1024]{1,0:T(8,128)(2,1)} %get-tuple-element.61), channel_id=1, source_target_pairs={{0,1},{1,0},{2,3},{3,2},{4,5},{5,4},{6,7},{7,6},{8,9},{9,8},{10,11... | collective-permute-start | bytes 393224 | tf_op jit(solution)/shard_map/ppermute | solution.py:323
  176.0 23.9 %copy-start.10 = (bf16[1792,512]{1,0:T(8,128)(2,1)S(1)}, bf16[1792,512]{1,0:T(8,128)(2,1)}, u32[]{:S(2)}) copy-start(bf16[1792,512]{1,0:T(8,128)(2,1)} %down.1) | copy-start | bytes 5505028
  195.6 4.3 %collective-permute-start.11 = (bf16[512,1024]{1,0:T(8,128)(2,1)S(1)}, bf16[512,1024]{1,0:T(8,128)(2,1)S(1)}, u32[]{:S(2)}, u32[]{:S(2)}) collective-permute-start(bf16[512,1024]{1,0:T(8,128)(2,1)S(1)} %bitcast.65), channel_id=1, source_target_pairs={{0,8},{8,0},{1,9},{9,1},{2,10},{10,2},{3,11},{11,3},{4,12},{12,4},... | collective-permute-start | bytes 3145736 | tf_op jit(solution)/shard_map/ppermute | solution.py:34
  229.7 27.9 %copy-start.4 = (f32[512,1792]{1,0:T(8,128)S(1)}, f32[512,1792]{1,0:T(8,128)}, u32[]{:S(2)}) copy-start(f32[512,1792]{1,0:T(8,128)} %curve_ref.3) | copy-start | bytes 11010052
  230.0 27.6 %copy-start.13 = (bf16[512,512]{1,0:T(8,128)(2,1)S(1)}, bf16[512,512]{1,0:T(8,128)(2,1)}, u32[]{:S(2)}) copy-start(bf16[512,512]{1,0:T(8,128)(2,1)} %get-tuple-element.67.turned) | copy-start | bytes 1572868
  230.2 27.5 %copy-start.3 = (f32[512,1792]{1,0:T(8,128)S(1)}, f32[512,1792]{1,0:T(8,128)}, u32[]{:S(2)}) copy-start(f32[512,1792]{1,0:T(8,128)} %moment_ref.3) | copy-start | bytes 11010052
  256.0 5.4 %copy-start.12 = (bf16[512,512]{1,0:T(8,128)(2,1)S(1)}, bf16[512,512]{1,0:T(8,128)(2,1)}, u32[]{:S(2)}) copy-start(bf16[512,512]{1,0:T(8,128)(2,1)} %get-tuple-element.57.turned) | copy-start | bytes 1572868
  256.0 5.4 %collective-permute-start.12 = (bf16[512,1792]{1,0:T(8,128)(2,1)S(1)}, bf16[512,1792]{1,0:T(8,128)(2,1)S(1)}, u32[]{:S(2)}, u32[]{:S(2)}) collective-permute-start(bf16[512,1792]{1,0:T(8,128)(2,1)S(1)} %bitcast.55), channel_id=1, source_target_pairs={{0,8},{8,0},{1,9},{9,1},{2,10},{10,2},{3,11},{11,3},{4,12},{12,4},... | collective-permute-start | bytes 5505032 | tf_op jit(solution)/shard_map/ppermute | solution.py:34
  261.4 3.8 %copy-start.1 = (bf16[512,1792]{1,0:T(8,128)(2,1)S(1)}, bf16[512,1792]{1,0:T(8,128)(2,1)}, u32[]{:S(2)}) copy-start(bf16[512,1792]{1,0:T(8,128)(2,1)} %param.10) | copy-start | bytes 5505028
  (13 other events, 21.8 us)

commit v14 on v13

--- a/solution.py
+++ b/solution.py
@@ -464,9 +464,8 @@
         logit_flops,
     )
     packed, label_sent = together(packed, label_sent)
-    packed, label_got = together(
-        exchange(packed.reshape(CHIPS, BLOCK, width + PAD), UNIT_CHIPS), other_plane(label_sent)
-    )
+    label_got = other_plane(label_sent)
+    packed = exchange(packed.reshape(CHIPS, BLOCK, width + PAD), UNIT_CHIPS)
     label_row = label_row.astype(f32) + label_got.astype(f32)
     stats = from_three(packed[:, :, width:], N_STATS)
     row_top = jnp.max(stats[:, :, 0:1], axis=0, keepdims=True)

time: 266 us -> 265 us (level)
    unnamed x54 -> x51, local copies, waits for them, and re-layouts: 6.52 us -> 6.7 us
where the time goes in v14:
time: 265 us; the launch traced here: 264 us
  blocking collectives  102 us (38%)
  waiting for transfers between devices  50.7 us (19%)
  starting transfers between devices  47.5 us (18%)
  local copies, waits for them, and re-layouts  21.3 us (8%)
  Pallas kernels  19.9 us (8%)
  matrix products  11.2 us (4%)
  other arithmetic  10.6 us (4%)
    all_to_all x5, blocking collectives, exchange(): lax.all_to_all(blocks, tuple(MESH_SIZES), split_axis=0, concat_axis=0, ti...  102 us
    all_to_all x5, starting transfers between devices, exchange(): lax.all_to_all(blocks, tuple(MESH_SIZES), split_axis=0, concat_axis=0, ti...  36.9 us
    all_to_all x5, waiting for transfers between devices, exchange(): lax.all_to_all(blocks, tuple(MESH_SIZES), split_axis=0, concat_axis=0, ti...  18.4 us
    ppermute x1, waiting for transfers between devices, near_label_rows(): return (keep, lax.ppermute(send, 'z', [(0, 1), (1, 0), (2, 3), (3, 2)]))  13.4 us
    pallas_call x7, Pallas kernels, on_core(): pl.pallas_call(kernel, out_shape=tuple((jax.ShapeDtypeStruct(shape, dtype...  12.4 us
    ppermute x1, waiting for transfers between devices, other_plane(): return lax.ppermute(rows, 'xh', [(0, 1), (1, 0)])  9.61 us
    ppermute x10, waiting for transfers between devices, other_core(): return lax.ppermute(value, 'core', [(0, 1), (1, 0)])  9.39 us
    ppermute x10, starting transfers between devices, other_core(): return lax.ppermute(value, 'core', [(0, 1), (1, 0)])  9.11 us
  transfers between devices with their start and end apart: 18, of which 12 were waited for; matrix products, arithmetic and copies ran while one was open for 11% of the time, Pallas kernels for 1%

profile of v14, /device:TPU:1, one launch (start us, length us, event | category | flops | bytes accessed | tf_op | source)
XLA Modules:
  0.0 264.2 jit_solution(15222746596334616655)
XLA Ops:
  0.7 3.1 %fusion.11 = bf16[512,896]{1,0:T(8,128)(2,1)} fusion(bf16[512,512]{1,0:T(8,128)(2,1)} %param.9, bf16[512,1792]{1,0:T(8,128)(2,1)} %param.11, s32[]{:T(128)S(6)} %select_n.98), kind=kOutput, calls=%fused_computation.16 | convolution fusion | flops 470220800 | bytes 2359300 | tf_op jit(solution)/shard_map/dot_general | solution.py:82
  5.2 1.6 fusion.10
  9.7 1.6 shard_map.112
  12.5 8.1 %all-to-all-start = ((bf16[8,64,1792]{2,1,0:T(8,128)(2,1)}), bf16[8,64,1792]{2,1,0:T(8,128)(2,1)}, u32[]{:S(2)}, u32[]{:S(2)}) async-start(bf16[8,64,1792]{2,1,0:T(8,128)(2,1)} %bitcast.57), calls=%async_computation | async-start | bytes 3670016 | tf_op jit(solution)/shard_map/all_to_all | solution.py:49
  26.3 16.3 %all-to-all-done.both = bf16[8,64,1792]{2,1,0:T(8,128)(2,1)} async-done(((bf16[8,64,1792]{2,1,0:T(8,128)(2,1)}), bf16[8,64,1792]{2,1,0:T(8,128)(2,1)}, u32[]{:S(2)}, u32[]{:S(2)}) %all-to-all-start) | async-done | bytes 1835040 | tf_op jit(solution)/shard_map/all_to_all | solution.py:49
  42.6 1.8 shard_map.113
  44.4 17.6 %all_to_all.50 = bf16[8,64,1024]{2,1,0:T(8,128)(2,1)} all-to-all(bf16[8,64,1024]{2,1,0:T(8,128)(2,1)S(1)} %get-tuple-element.39), channel_id=1, replica_groups={{0,16,32,48,64,80,96,112},{1,17,33,49,65,81,97,113},{2,18,34,50,66,82,9..., dimensions={0} | all-to-all | bytes 2097152 | tf_op jit(solution)/shard_map/all_to_all | solution.py:49
  62.9 2.3 fusion.18.own_part
  66.9 10.0 %all-to-all-start.2 = ((bf16[8,64,512]{2,1,0:T(8,128)(2,1)}), bf16[8,64,512]{2,1,0:T(8,128)(2,1)}, u32[]{:S(2)}, u32[]{:S(2)}) async-start(bf16[8,64,512]{2,1,0:T(8,128)(2,1)} %bitcast.11), calls=%async_computation.2 | async-start | bytes 1048576 | tf_op jit(solution)/shard_map/all_to_all | solution.py:49
  86.9 12.6 %all_to_all.51 = bf16[8,64,512]{2,1,0:T(8,128)(2,1)S(1)} all-to-all(bf16[8,64,512]{2,1,0:T(8,128)(2,1)S(1)} %broadcast_in_dim.6), channel_id=1, replica_groups={{0,1,2,3,4,5,6,7},{15,14,13,12,11,10,9,8},{16,17,18,19,20,21,22,23},{31..., dimensions={0} | all-to-all | bytes 1048576 | tf_op jit(solution)/shard_map/all_to_all | solution.py:49
  99.5 2.5 collective-permute-start.6
  103.6 1.7 shard_map.115
  106.2 5.3 %all-to-all-start.4 = ((s16[8,64,1152]{2,1,0:T(8,128)(2,1)}), s16[8,64,1152]{2,1,0:T(8,128)(2,1)S(1)}, u32[]{:S(2)}, u32[]{:S(2)}) async-start(s16[8,64,1152]{2,1,0:T(8,128)(2,1)} %bitcast.60), calls=%async_computation.4 | async-start | bytes 2359296 | tf_op jit(solution)/shard_map/all_to_all | solution.py:49
  111.5 2.2 dynamic-slice_bitcast_fusion
  113.8 13.4 %collective-permute-done.7 = bf16[2,2,64,1024]{3,2,1,0:T(8,128)(2,1)} collective-permute-done((bf16[2,2,64,1024]{3,2,1,0:T(8,128)(2,1)}, bf16[2,2,64,1024]{3,2,1,0:T(8,128)(2,1)}, u32[]{:S(2)}, u32[]{:S(2)}) %collective-permute-start.7) | collective-permute-done | bytes 524320 | tf_op jit(solution)/shard_map/ppermute | solution.py:312
  129.1 5.5 %all-to-all-start.5 = ((bf16[8,64,1152]{2,1,0:T(8,128)(2,1)}), bf16[8,64,1152]{2,1,0:T(8,128)(2,1)S(1)}, u32[]{:S(2)}, u32[]{:S(2)}) async-start(bf16[8,64,1152]{2,1,0:T(8,128)(2,1)} %copy-done.6), calls=%async_computation.5 | async-start | bytes 2359296 | tf_op jit(solution)/shard_map/all_to_all | solution.py:49
  138.7 2.1 copy.78
  140.8 1.9 rev.7
  142.6 2.0 copy.79
  144.7 2.3 select_bitcast_fusion
  149.5 2.8 %collective-permute-done.9.far = bf16[512,1152]{1,0:T(8,128)(2,1)S(1)} collective-permute-done((bf16[512,1152]{1,0:T(8,128)(2,1)S(1)}, bf16[512,1152]{1,0:T(8,128)(2,1)S(1)}, u32[]{:S(2)}, u32[]{:S(2)}) %collective-permute-start.9) | collective-permute-done | bytes 1179680 | tf_op jit(solution)/shard_map/ppermute | solution.py:34
  154.6 8.0 %all-to-all-start.6 = ((bf16[8,64,640]{2,1,0:T(8,128)(2,1)}), bf16[8,64,640]{2,1,0:T(8,128)(2,1)S(1)}, u32[]{:S(2)}, u32[]{:S(2)}) async-start(bf16[8,64,640]{2,1,0:T(8,128)(2,1)} %bitcast.61), calls=%async_computation.6 | async-start | bytes 1310720 | tf_op jit(solution)/shard_map/all_to_all | solution.py:49
  162.9 9.6 %collective-permute-done.10 = bf16[64,1024]{1,0:T(8,128)(2,1)S(1)} collective-permute-done((bf16[64,1024]{1,0:T(8,128)(2,1)}, bf16[64,1024]{1,0:T(8,128)(2,1)S(1)}, u32[]{:S(2)}, u32[]{:S(2)}) %collective-permute-start.10) | collective-permute-done | bytes 131104 | tf_op jit(solution)/shard_map/ppermute | solution.py:323
  175.2 19.4 %all_to_all.52 = bf16[8,64,1024]{2,1,0:T(8,128)(2,1)S(1)} all-to-all(bf16[8,64,1024]{2,1,0:T(8,128)(2,1)S(1)} %broadcast_in_dim.7), channel_id=1, replica_groups={{0,1,2,3,4,5,6,7},{15,14,13,12,11,10,9,8},{16,17,18,19,20,21,22,23},{31..., dimensions={0} | all-to-all | bytes 2097152 | tf_op jit(solution)/shard_map/all_to_all | solution.py:49
  194.6 2.0 collective-permute-start.11
  196.6 2.3 collective-permute-done.11.far_dsummed
  198.9 3.5 %shard_map.118 = bf16[512,1792]{1,0:T(8,128)(2,1)S(1)} custom-call(s32[1]{0:T(128)} %bitcast.2.half_ref, bf16[512,1024]{1,0:T(8,128)(2,1)S(1)} %bitcast.66, bf16[512,1024]{1,0:T(8,128)(2,1)S(1)} %collective-permute-done.11.far_dsummed, bf16[1792,512]{1,0:T(8,128)(2,1)S(1)} %copy-done.10, bf16[896,512]{1,0:T(8,128)(2,1)} %collective-permute-done.3.down_got), custom_call_target="tpu_custom_call" | custom-call | flops 1879048192 | bytes 4849664 | tf_op jit(solution)/shard_map/pallas_call | solution.py:108
  202.4 26.3 %all_to_all.53 = bf16[8,64,1792]{2,1,0:T(8,128)(2,1)S(1)} all-to-all(bf16[8,64,1792]{2,1,0:T(8,128)(2,1)S(1)} %bitcast.64), channel_id=1, replica_groups={{0,16,32,48,64,80,96,112},{1,17,33,49,65,81,97,113},{2,18,34,50,66,82,9..., dimensions={0} | all-to-all | bytes 3670016 | tf_op jit(solution)/shard_map/all_to_all | solution.py:49
  229.2 25.8 %all_to_all.54 = bf16[8,64,1792]{2,1,0:T(8,128)(2,1)S(1)} all-to-all(bf16[8,64,1792]{2,1,0:T(8,128)(2,1)S(1)} %broadcast_in_dim.8), channel_id=1, replica_groups={{0,16,32,48,64,80,96,112},{1,17,33,49,65,81,97,113},{2,18,34,50,66,82,9..., dimensions={0} | all-to-all | bytes 3670016 | tf_op jit(solution)/shard_map/all_to_all | solution.py:49
  255.0 1.7 collective-permute-start.12
  256.7 3.7 %shard_map.119 = (f32[512,1792]{1,0:T(8,128)}, f32[512,1792]{1,0:T(8,128)}, f32[512,1792]{1,0:T(8,128)}) custom-call(s32[1]{0:T(128)} %bitcast.2.half_ref, bf16[512,512]{1,0:T(8,128)(2,1)S(1)} %copy-done.13, bf16[512,1792]{1,0:T(8,128)(2,1)S(1)} %bitcast.56, f32[512,1792]{1,0:T(8,128)S(1)} %copy-done.3, f32[512,1792]{1,0:T(8,128)S(1)} %copy-done.4), custom_call_target="tpu_custom_call" | custom-call | flops 950000000 | bytes 11000000 | tf_op jit(solution)/shard_map/pallas_call | solution.py:274
  260.4 3.7 %shard_map.120 = (f32[512,1792]{1,0:T(8,128)}, f32[512,1792]{1,0:T(8,128)}, f32[512,1792]{1,0:T(8,128)}) custom-call(s32[1]{0:T(128)} %bitcast.half_ref, bf16[512,512]{1,0:T(8,128)(2,1)S(1)} %copy-done.12, bf16[512,1792]{1,0:T(8,128)(2,1)S(1)} %collective-permute-done.12.cot, ...), custom_call_target="tpu_custom_call", output_to_operand_aliasing={{0}: (5, {}), {1}: (6, {}), {2}: (7, {})} | custom-call | flops 950000000 | bytes 11000000 | tf_op jit(solution)/shard_map/pallas_call | solution.py:274
  (121 shorter events, 40.2 us)
Async XLA Ops:
  0.6 4.6 %copy-start = (bf16[512,1792]{1,0:T(8,128)(2,1)S(1)}, bf16[512,1792]{1,0:T(8,128)(2,1)}, u32[]{:S(2)}) copy-start(bf16[512,1792]{1,0:T(8,128)(2,1)} %param.10) | copy-start | bytes 5505028
  0.6 4.6 %copy-start.16 = (bf16[512,512]{1,0:T(8,128)(2,1)S(1)}, bf16[512,512]{1,0:T(8,128)(2,1)}, u32[]{:S(2)}) copy-start(bf16[512,512]{1,0:T(8,128)(2,1)} %param.9) | copy-start | bytes 1572868
  3.8 5.3 %collective-permute-start.1 = (bf16[512,896]{1,0:T(8,128)(2,1)}, bf16[512,896]{1,0:T(8,128)(2,1)S(1)}, u32[]{:S(2)}, u32[]{:S(2)}) collective-permute-start(bf16[512,896]{1,0:T(8,128)(2,1)} %fusion.11), channel_id=1, source_target_pairs={{0,8},{8,0},{1,9},{9,1},{2,10},{10,2},{3,11},{11,3},{4,12},{12,4},... | collective-permute-start | bytes 2752520 | tf_op jit(solution)/shard_map/ppermute | solution.py:34
  6.9 2.8 %collective-permute-start = (bf16[512,896]{1,0:T(8,128)(2,1)}, bf16[512,896]{1,0:T(8,128)(2,1)}, u32[]{:S(2)}, u32[]{:S(2)}) collective-permute-start(bf16[512,896]{1,0:T(8,128)(2,1)} %fusion.10), channel_id=1, source_target_pairs={{0,8},{8,0},{1,9},{9,1},{2,10},{10,2},{3,11},{11,3},{4,12},{12,4},... | collective-permute-start | bytes 2752520 | tf_op jit(solution)/shard_map/ppermute | solution.py:34
  12.5 8.1 %copy-start.2 = (bf16[512,2048]{1,0:T(8,128)(2,1)S(1)}, bf16[512,2048]{1,0:T(8,128)(2,1)}, u32[]{:S(2)}) copy-start(bf16[512,2048]{1,0:T(8,128)(2,1)} %head_far.1) | copy-start | bytes 6291460
  12.5 30.1 %all-to-all-start = ((bf16[8,64,1792]{2,1,0:T(8,128)(2,1)}), bf16[8,64,1792]{2,1,0:T(8,128)(2,1)}, u32[]{:S(2)}, u32[]{:S(2)}) async-start(bf16[8,64,1792]{2,1,0:T(8,128)(2,1)} %bitcast.57), calls=%async_computation | async-start | bytes 3670016 | tf_op jit(solution)/shard_map/all_to_all | solution.py:49
  20.6 2.9 %copy-start.22 = (s32[32]{0:T(128)S(1)}, s32[32]{0:T(128)}, u32[]{:S(2)}) copy-start(s32[32]{0:T(128)} %param.17) | copy-start | bytes 388
  21.7 4.6 %collective-permute-start.2 = (bf16[512,1024]{1,0:T(8,128)(2,1)}, bf16[512,1024]{1,0:T(8,128)(2,1)S(1)}, u32[]{:S(2)}, u32[]{:S(2)}) collective-permute-start(bf16[512,1024]{1,0:T(8,128)(2,1)} %constant_dynamic-slice_fusion.2), channel_id=1, source_target_pairs={{0,8},{8,0},{1,9},{9,1},{2,10},{10,2},{3,11},{11,3},{4,12},{12,4},... | collective-permute-start | bytes 3145736 | tf_op jit(solution)/shard_map/ppermute | solution.py:34
  23.5 2.8 %collective-permute-start.3 = (bf16[896,512]{1,0:T(8,128)(2,1)}, bf16[896,512]{1,0:T(8,128)(2,1)}, u32[]{:S(2)}, u32[]{:S(2)}) collective-permute-start(bf16[896,512]{1,0:T(8,128)(2,1)} %constant_dynamic-slice_fusion.1), channel_id=1, source_target_pairs={{0,8},{8,0},{1,9},{9,1},{2,10},{10,2},{3,11},{11,3},{4,12},{12,4},... | collective-permute-start | bytes 2752520 | tf_op jit(solution)/shard_map/ppermute | solution.py:34
  23.5 2.2 collective-permute-start.4
  26.3 35.8 %copy-start.14 = (bf16[512,1024]{1,0:T(8,128)(2,1)}, bf16[512,1024]{1,0:T(8,128)(2,1)S(1)}, u32[]{:S(2)}) copy-start(bf16[512,1024]{1,0:T(8,128)(2,1)S(1)} %collective-permute-done.2.head_got) | copy-start | bytes 3145732
  62.1 3.4 %collective-permute-start.5 = (bf16[512,1024]{1,0:T(8,128)(2,1)}, bf16[512,1024]{1,0:T(8,128)(2,1)S(1)}, u32[]{:S(2)}, u32[]{:S(2)}) collective-permute-start(bf16[512,1024]{1,0:T(8,128)(2,1)} %bitcast.10), channel_id=1, source_target_pairs={{0,8},{8,0},{1,9},{9,1},{2,10},{10,2},{3,11},{11,3},{4,12},{12,4},... | collective-permute-start | bytes 3145736 | tf_op jit(solution)/shard_map/ppermute | solution.py:34
  66.9 17.8 %all-to-all-start.2 = ((bf16[8,64,512]{2,1,0:T(8,128)(2,1)}), bf16[8,64,512]{2,1,0:T(8,128)(2,1)}, u32[]{:S(2)}, u32[]{:S(2)}) async-start(bf16[8,64,512]{2,1,0:T(8,128)(2,1)} %bitcast.11), calls=%async_computation.2 | async-start | bytes 1048576 | tf_op jit(solution)/shard_map/all_to_all | solution.py:49
  82.6 20.9 %copy-start.15 = (bf16[512,1024]{1,0:T(8,128)(2,1)S(1)}, bf16[512,1024]{1,0:T(8,128)(2,1)}, u32[]{:S(2)}) copy-start(bf16[512,1024]{1,0:T(8,128)(2,1)} %copy-done.14) | copy-start | bytes 3145732
  85.9 19.3 %copy-start.20 = (f32[64,512]{1,0:T(8,128)}, f32[64,512]{1,0:T(8,128)S(1)}, u32[]{:S(2)}) copy-start(f32[64,512]{1,0:T(8,128)S(1)} %convert_reduce_fusion.1) | copy-start | bytes 393220
  99.5 4.0 %collective-permute-start.6 = (bf16[512,512]{1,0:T(8,128)(2,1)S(1)}, bf16[512,512]{1,0:T(8,128)(2,1)S(1)}, u32[]{:S(2)}, u32[]{:S(2)}) collective-permute-start(bf16[512,512]{1,0:T(8,128)(2,1)S(1)} %bitcast.62), channel_id=1, source_target_pairs={{0,8},{8,0},{1,9},{9,1},{2,10},{10,2},{3,11},{11,3},{4,12},{12,4},... | collective-permute-start | bytes 1572872 | tf_op jit(solution)/shard_map/ppermute | solution.py:34
  106.2 20.9 %all-to-all-start.4 = ((s16[8,64,1152]{2,1,0:T(8,128)(2,1)}), s16[8,64,1152]{2,1,0:T(8,128)(2,1)S(1)}, u32[]{:S(2)}, u32[]{:S(2)}) async-start(s16[8,64,1152]{2,1,0:T(8,128)(2,1)} %bitcast.60), calls=%async_computation.4 | async-start | bytes 2359296 | tf_op jit(solution)/shard_map/all_to_all | solution.py:49
  113.8 13.4 %collective-permute-start.7 = (bf16[2,2,64,1024]{3,2,1,0:T(8,128)(2,1)}, bf16[2,2,64,1024]{3,2,1,0:T(8,128)(2,1)}, u32[]{:S(2)}, u32[]{:S(2)}) collective-permute-start(bf16[2,2,64,1024]{3,2,1,0:T(8,128)(2,1)} %get-tuple-element.80), channel_id=1, source_target_pairs={{0,2},{2,0},{4,6},{6,4},{1,3},{3,1},{5,7},{7,5},{8,10},{10,8},{12,... | collective-permute-start | bytes 1572872 | tf_op jit(solution)/shard_map/ppermute | solution.py:312
  129.1 20.4 %all-to-all-start.5 = ((bf16[8,64,1152]{2,1,0:T(8,128)(2,1)}), bf16[8,64,1152]{2,1,0:T(8,128)(2,1)S(1)}, u32[]{:S(2)}, u32[]{:S(2)}) async-start(bf16[8,64,1152]{2,1,0:T(8,128)(2,1)} %copy-done.6), calls=%async_computation.5 | async-start | bytes 2359296 | tf_op jit(solution)/shard_map/all_to_all | solution.py:49
  137.5 9.5 %collective-permute-start.8 = (bf16[2,64,1024]{2,1,0:T(8,128)(2,1)}, bf16[2,64,1024]{2,1,0:T(8,128)(2,1)}, u32[]{:S(2)}, u32[]{:S(2)}) collective-permute-start(bf16[2,64,1024]{2,1,0:T(8,128)(2,1)} %dynamic-slice_bitcast_fusion.2), channel_id=1, source_target_pairs={{0,4},{4,0},{2,6},{6,2},{1,5},{5,1},{3,7},{7,3},{8,12},{12,8},{10,... | collective-permute-start | bytes 786440 | tf_op jit(solution)/shard_map/ppermute | solution.py:318
  149.5 2.8 %collective-permute-start.9 = (bf16[512,1152]{1,0:T(8,128)(2,1)S(1)}, bf16[512,1152]{1,0:T(8,128)(2,1)S(1)}, u32[]{:S(2)}, u32[]{:S(2)}) collective-permute-start(bf16[512,1152]{1,0:T(8,128)(2,1)S(1)} %bitcast.58), channel_id=1, source_target_pairs={{0,8},{8,0},{1,9},{9,1},{2,10},{10,2},{3,11},{11,3},{4,12},{12,4},... | collective-permute-start | bytes 3538952 | tf_op jit(solution)/shard_map/ppermute | solution.py:34
  154.6 19.5 %copy-start.21 = (f32[64,512]{1,0:T(8,128)S(1)}, f32[64,512]{1,0:T(8,128)}, u32[]{:S(2)}) copy-start(f32[64,512]{1,0:T(8,128)} %copy-done.20) | copy-start | bytes 393220
  154.6 18.9 %all-to-all-start.6 = ((bf16[8,64,640]{2,1,0:T(8,128)(2,1)}), bf16[8,64,640]{2,1,0:T(8,128)(2,1)S(1)}, u32[]{:S(2)}, u32[]{:S(2)}) async-start(bf16[8,64,640]{2,1,0:T(8,128)(2,1)} %bitcast.61), calls=%async_computation.6 | async-start | bytes 1310720 | tf_op jit(solution)/shard_map/all_to_all | solution.py:49
  162.6 9.9 %collective-permute-start.10 = (bf16[64,1024]{1,0:T(8,128)(2,1)}, bf16[64,1024]{1,0:T(8,128)(2,1)S(1)}, u32[]{:S(2)}, u32[]{:S(2)}) collective-permute-start(bf16[64,1024]{1,0:T(8,128)(2,1)} %get-tuple-element.60), channel_id=1, source_target_pairs={{0,1},{1,0},{2,3},{3,2},{4,5},{5,4},{6,7},{7,6},{8,9},{9,8},{10,11... | collective-permute-start | bytes 393224 | tf_op jit(solution)/shard_map/ppermute | solution.py:323
  175.0 23.9 %copy-start.10 = (bf16[1792,512]{1,0:T(8,128)(2,1)S(1)}, bf16[1792,512]{1,0:T(8,128)(2,1)}, u32[]{:S(2)}) copy-start(bf16[1792,512]{1,0:T(8,128)(2,1)} %down.1) | copy-start | bytes 5505028
  194.6 4.3 %collective-permute-start.11 = (bf16[512,1024]{1,0:T(8,128)(2,1)S(1)}, bf16[512,1024]{1,0:T(8,128)(2,1)S(1)}, u32[]{:S(2)}, u32[]{:S(2)}) collective-permute-start(bf16[512,1024]{1,0:T(8,128)(2,1)S(1)} %bitcast.65), channel_id=1, source_target_pairs={{0,8},{8,0},{1,9},{9,1},{2,10},{10,2},{3,11},{11,3},{4,12},{12,4},... | collective-permute-start | bytes 3145736 | tf_op jit(solution)/shard_map/ppermute | solution.py:34
  228.7 27.9 %copy-start.4 = (f32[512,1792]{1,0:T(8,128)S(1)}, f32[512,1792]{1,0:T(8,128)}, u32[]{:S(2)}) copy-start(f32[512,1792]{1,0:T(8,128)} %curve_ref.3) | copy-start | bytes 11010052
  229.0 27.6 %copy-start.13 = (bf16[512,512]{1,0:T(8,128)(2,1)S(1)}, bf16[512,512]{1,0:T(8,128)(2,1)}, u32[]{:S(2)}) copy-start(bf16[512,512]{1,0:T(8,128)(2,1)} %get-tuple-element.63.turned) | copy-start | bytes 1572868
  229.2 27.5 %copy-start.3 = (f32[512,1792]{1,0:T(8,128)S(1)}, f32[512,1792]{1,0:T(8,128)}, u32[]{:S(2)}) copy-start(f32[512,1792]{1,0:T(8,128)} %moment_ref.3) | copy-start | bytes 11010052
  255.0 5.5 %copy-start.12 = (bf16[512,512]{1,0:T(8,128)(2,1)S(1)}, bf16[512,512]{1,0:T(8,128)(2,1)}, u32[]{:S(2)}) copy-start(bf16[512,512]{1,0:T(8,128)(2,1)} %get-tuple-element.55.turned) | copy-start | bytes 1572868
  255.0 5.5 %collective-permute-start.12 = (bf16[512,1792]{1,0:T(8,128)(2,1)S(1)}, bf16[512,1792]{1,0:T(8,128)(2,1)S(1)}, u32[]{:S(2)}, u32[]{:S(2)}) collective-permute-start(bf16[512,1792]{1,0:T(8,128)(2,1)S(1)} %bitcast.55), channel_id=1, source_target_pairs={{0,8},{8,0},{1,9},{9,1},{2,10},{10,2},{3,11},{11,3},{4,12},{12,4},... | collective-permute-start | bytes 5505032 | tf_op jit(solution)/shard_map/ppermute | solution.py:34
  260.4 3.8 %copy-start.1 = (bf16[512,1792]{1,0:T(8,128)(2,1)S(1)}, bf16[512,1792]{1,0:T(8,128)(2,1)}, u32[]{:S(2)}) copy-start(bf16[512,1792]{1,0:T(8,128)(2,1)} %param.10) | copy-start | bytes 5505028
  (11 other events, 17.7 us)
